TPU v7x, 32 devices: a whole 2x2x4 slice. The times are simulated.
32 devices in a mesh: seq: 4 (over y, core), fsdp: 8 (over z, x).
Axes of the slice: x: 2, y: 2, z: 4, core: 2. Of those that a mesh axis runs over, the one named last changes fastest.
Arguments:
- tokens: bfloat16 [12288, 896], P(('fsdp', 'seq')), may hold values from -6 to 6
- segment_ids: int32 [12288], P(('fsdp', 'seq')), may hold values from 0 to 23, as said below
- positions: int32 [12288], P(('fsdp', 'seq')), may hold values from 0 to 1533, as said below
- norm_one: bfloat16 [896], P('fsdp'), may hold values from 0.5 to 1.5
- qkv_weight: bfloat16 [896, 1152], P('seq', 'fsdp'), may hold values from -0.1875 to 0.1875
- qkv_bias: bfloat16 [1152], P('fsdp'), may hold values from -3 to 3
- out_weight: bfloat16 [896, 896], P('fsdp', 'seq'), may hold values from -3 to 3
- norm_two: bfloat16 [896], P('fsdp'), may hold values from 0.5 to 1.5
- gate_up_weight: bfloat16 [896, 9728], P('seq', 'fsdp'), may hold values from -0.1875 to 0.1875
- down_weight: bfloat16 [4864, 896], P('fsdp', 'seq'), may hold values from -0.078125 to 0.078125
- cotangent: bfloat16 [12288, 896], P(('fsdp', 'seq')), may hold values from -6 to 6
Outputs:
- layer_out: bfloat16 [12288, 896], P(('fsdp', 'seq'))
- grad_tokens: float32 [12288, 896], P(('fsdp', 'seq'))
- grad_norm_one: float32 [896], P('fsdp')
- grad_qkv_weight: float32 [896, 1152], P('seq', 'fsdp')
- grad_qk_bias: float32 [1024], P('fsdp')
- grad_value_bias: float32 [128], P('fsdp')
- grad_out_weight: float32 [896, 896], P('fsdp', 'seq')
- grad_norm_two: float32 [896], P('fsdp')
- grad_gate_up: float32 [896, 9728], P('seq', 'fsdp')
- grad_down: float32 [4864, 896], P('fsdp', 'seq')
Inputs may be any that keep to these rules, and one draw needn't show every extreme that they name: `segment_ids`: the tokens come in aligned groups of 1536 (one index of fsdp each). Group g holds three documents numbered 3 g, 3 g + 1 and 3 g + 2 in order; the first and the last are shorter than 384 tokens and at least one token long. `positions`: each token's place in its document, counted from 0 at the document's first token; in one group the first and the last documents are one token long each.
All inputs are finite; a program needn't handle non-finite values.
Results may differ from a plain program's by a relative error of at most 0.015.
Values may be sent and summed in bfloat16 or wider, within the bound.
No kernel may reach another device: no remote copies, remote signals or barrier semaphores. Data moves between devices by JAX's collectives and lax.ppermute only.
A program may use at most 192 MiB of HBM per device.

v0:
```python
import jax
import jax.numpy as jnp
from jax import lax
from jax.sharding import PartitionSpec as P

HEADS = 14
KV_HEADS = 2
HEAD = 64
FF = 4864
QW = 896
KVW = 128


EPSILON = 1e-06
ROPE_BASE = 1000000.0


def rms_scale(values_in):
    return lax.rsqrt(jnp.mean(values_in * values_in, axis=-1, keepdims=True) + EPSILON)


def angles(places):
    exponent = jnp.arange(HEAD // 2, dtype=jnp.float32) * 2.0 / HEAD
    frequency = ROPE_BASE ** (-exponent)
    turn = places.astype(jnp.float32)[:, None] * frequency[None, :]
    turn = jnp.concatenate([turn, turn], axis=-1)
    return (jnp.cos(turn)[:, None, :], jnp.sin(turn)[:, None, :])


def rotate(tensor, cos_table, sine_table):
    half_size = HEAD // 2
    turned = jnp.concatenate([-tensor[..., half_size:], tensor[..., :half_size]], axis=-1)
    return tensor * cos_table + turned * sine_table


def rotate_back(grad_in, cos_table, sine_table):
    half_size = HEAD // 2
    scaled = grad_in * sine_table
    return grad_in * cos_table + jnp.concatenate(
        [scaled[..., half_size:], -scaled[..., :half_size]], axis=-1
    )


def norm_back(grad_in, row_data, scale_in, gain_in):
    gain_term = jnp.sum(grad_in * row_data * scale_in, axis=0)
    grad_normed = grad_in * gain_in
    inner_mean = jnp.mean(grad_normed * row_data, axis=-1, keepdims=True)
    return (
        scale_in * grad_normed - row_data * scale_in * scale_in * scale_in * inner_mean,
        gain_term,
    )


def collect(qkv_weight, out_weight, gate_up_weight, down_weight, norm_one, qkv_bias, norm_two):
    section_one = (
        lax.all_gather(qkv_weight, "seq", axis=0, tiled=True),
        lax.all_gather(out_weight, "seq", axis=1, tiled=True),
        lax.all_gather(gate_up_weight, "seq", axis=0, tiled=True),
        lax.all_gather(down_weight, "seq", axis=1, tiled=True),
    )
    return (
        lax.all_gather(section_one[0], "fsdp", axis=1, tiled=True),
        lax.all_gather(section_one[1], "fsdp", axis=0, tiled=True),
        lax.all_gather(section_one[2], "fsdp", axis=1, tiled=True),
        lax.all_gather(section_one[3], "fsdp", axis=0, tiled=True),
        lax.all_gather(norm_one, "fsdp", axis=0, tiled=True),
        lax.all_gather(qkv_bias, "fsdp", axis=0, tiled=True),
        lax.all_gather(norm_two, "fsdp", axis=0, tiled=True),
    )


def reduce_grads(
    qkv_term, out_term, gate_up_term, down_term, norm_one_term, bias_term, norm_two_term
):
    small_sums = lax.psum((norm_one_term, bias_term, norm_two_term), "seq")
    query_key_sum = small_sums[1][: QW + KVW]
    value_sum = small_sums[1][QW + KVW :]
    section_one = (
        lax.psum_scatter(qkv_term, "fsdp", scatter_dimension=1, tiled=True),
        lax.psum_scatter(out_term, "fsdp", scatter_dimension=0, tiled=True),
        lax.psum_scatter(gate_up_term, "fsdp", scatter_dimension=1, tiled=True),
        lax.psum_scatter(down_term, "fsdp", scatter_dimension=0, tiled=True),
        lax.psum_scatter(small_sums[0], "fsdp", scatter_dimension=0, tiled=True),
        lax.psum_scatter(query_key_sum, "fsdp", scatter_dimension=0, tiled=True),
        lax.psum_scatter(value_sum, "fsdp", scatter_dimension=0, tiled=True),
        lax.psum_scatter(small_sums[2], "fsdp", scatter_dimension=0, tiled=True),
    )
    section_two = (
        lax.psum_scatter(section_one[0], "seq", scatter_dimension=0, tiled=True),
        lax.psum_scatter(section_one[1], "seq", scatter_dimension=1, tiled=True),
        lax.psum_scatter(section_one[2], "seq", scatter_dimension=0, tiled=True),
        lax.psum_scatter(section_one[3], "seq", scatter_dimension=1, tiled=True),
    )
    return (
        section_two[0],
        section_two[1],
        section_two[2],
        section_two[3],
        section_one[4],
        section_one[5],
        section_one[6],
        section_one[7],
    )


def head_scores(query_block, key_block, allowed):
    scores = (
        jnp.einsum("qd,kd->qk", query_block, key_block, preferred_element_type=jnp.float32) * 0.125
    )
    return jnp.where(allowed, scores, -jnp.inf)


def attend(query_heads, keys_all, values_all, allowed):
    head_share = HEADS // KV_HEADS

    def one_head(head_index):
        key_block = keys_all[head_index // head_share]
        scores = head_scores(query_heads[head_index], key_block, allowed)
        max_score = jnp.max(scores, axis=1, keepdims=True)
        exp_score = jnp.exp(scores - max_score)
        denominator = jnp.sum(exp_score, axis=1, keepdims=True)
        attn_probs = (exp_score / denominator).astype(jnp.bfloat16)
        head_result = jnp.einsum(
            "qk,kd->qd",
            attn_probs,
            values_all[head_index // head_share],
            preferred_element_type=jnp.float32,
        )
        return (head_result, max_score[:, 0] + jnp.log(denominator[:, 0]))

    return lax.map(one_head, jnp.arange(HEADS))


def attend_back(query_heads, keys_all, values_all, allowed, grad_heads, log_totals):
    head_share = HEADS // KV_HEADS

    def one_head(head_index):
        query_block = query_heads[head_index]
        key_block = keys_all[head_index // head_share]
        value_block = values_all[head_index // head_share]
        grad_block = grad_heads[head_index]
        scores = head_scores(query_block, key_block, allowed)
        attn_probs = jnp.exp(scores - log_totals[head_index][:, None])
        grad_probs = jnp.einsum(
            "qd,kd->qk", grad_block, value_block, preferred_element_type=jnp.float32
        )
        delta_rows = jnp.sum(attn_probs * grad_probs, axis=1, keepdims=True)
        grad_scores = (attn_probs * (grad_probs - delta_rows)).astype(jnp.bfloat16)
        grad_query = (
            jnp.einsum("qk,kd->qd", grad_scores, key_block, preferred_element_type=jnp.float32)
            * 0.125
        )
        grad_key = (
            jnp.einsum("qk,qd->kd", grad_scores, query_block, preferred_element_type=jnp.float32)
            * 0.125
        )
        grad_value = jnp.einsum(
            "qk,qd->kd",
            attn_probs.astype(jnp.bfloat16),
            grad_block,
            preferred_element_type=jnp.float32,
        )
        return (grad_query, grad_key, grad_value)

    grad_queries, grad_keys, grad_values = lax.map(one_head, jnp.arange(HEADS))
    key_count = keys_all.shape[1]
    grad_keys = jnp.sum(grad_keys.reshape(KV_HEADS, head_share, key_count, HEAD), axis=1)
    grad_values = jnp.sum(grad_values.reshape(KV_HEADS, head_share, key_count, HEAD), axis=1)
    return (grad_queries, grad_keys, grad_values)


def per_device(
    tokens,
    segment_ids,
    positions,
    norm_one,
    qkv_weight,
    qkv_bias,
    out_weight,
    norm_two,
    gate_up_weight,
    down_weight,
    cotangent,
):
    gathered = collect(
        qkv_weight, out_weight, gate_up_weight, down_weight, norm_one, qkv_bias, norm_two
    )
    qkv_full, out_full, gate_up_full, down_full = (
        gathered[0],
        gathered[1],
        gathered[2],
        gathered[3],
    )
    gain_one = gathered[4].astype(jnp.float32)
    bias_full = gathered[5].astype(jnp.float32)
    gain_two = gathered[6].astype(jnp.float32)
    inputs = tokens.astype(jnp.float32)
    row_count = inputs.shape[0]
    scale_one = rms_scale(inputs)
    normed_one = (inputs * scale_one * gain_one).astype(jnp.bfloat16)
    joined = jnp.dot(normed_one, qkv_full, preferred_element_type=jnp.float32) + bias_full
    cos_table, sine_table = angles(positions)
    queries = rotate(joined[:, :QW].reshape(row_count, HEADS, HEAD), cos_table, sine_table).astype(
        jnp.bfloat16
    )
    keys_local = rotate(
        joined[:, QW : QW + KVW].reshape(row_count, KV_HEADS, HEAD), cos_table, sine_table
    ).astype(jnp.bfloat16)
    values_local = joined[:, QW + KVW :].astype(jnp.bfloat16)
    packed = jnp.concatenate([keys_local.reshape(row_count, KVW), values_local], axis=1)
    kv_all, seg_all, pos_all = (
        lax.all_gather(packed, "seq", axis=0, tiled=True),
        lax.all_gather(segment_ids, "seq", axis=0, tiled=True),
        lax.all_gather(positions, "seq", axis=0, tiled=True),
    )
    key_count = kv_all.shape[0]
    keys_all = jnp.transpose(kv_all[:, :KVW].reshape(key_count, KV_HEADS, HEAD), (1, 0, 2))
    values_all = jnp.transpose(kv_all[:, KVW:].reshape(key_count, KV_HEADS, HEAD), (1, 0, 2))
    allowed = (segment_ids[:, None] == seg_all[None, :]) & (pos_all[None, :] <= positions[:, None])
    query_heads = jnp.transpose(queries, (1, 0, 2))
    head_out, log_totals = attend(query_heads, keys_all, values_all, allowed)
    attn_flat = jnp.transpose(head_out, (1, 0, 2)).reshape(row_count, QW).astype(jnp.bfloat16)
    residual = inputs + jnp.dot(attn_flat, out_full, preferred_element_type=jnp.float32)
    scale_two = rms_scale(residual)
    normed_two = (residual * scale_two * gain_two).astype(jnp.bfloat16)
    gate_up = jnp.dot(normed_two, gate_up_full, preferred_element_type=jnp.float32)
    gate_part = gate_up[:, :FF]
    up_part = gate_up[:, FF:]
    sigmoid_gate = jax.nn.sigmoid(gate_part)
    silu_gate = gate_part * sigmoid_gate
    hidden = (silu_gate * up_part).astype(jnp.bfloat16)
    layer_out = residual + jnp.dot(hidden, down_full, preferred_element_type=jnp.float32)
    gathered = collect(
        qkv_weight, out_weight, gate_up_weight, down_weight, norm_one, qkv_bias, norm_two
    )
    qkv_full, out_full, gate_up_full, down_full = (
        gathered[0],
        gathered[1],
        gathered[2],
        gathered[3],
    )
    gain_one = gathered[4].astype(jnp.float32)
    gain_two = gathered[6].astype(jnp.float32)
    grad_out = cotangent.astype(jnp.float32)
    down_term = jnp.einsum("rf,rd->fd", hidden, cotangent, preferred_element_type=jnp.float32)
    grad_hidden = jnp.einsum("rd,fd->rf", cotangent, down_full, preferred_element_type=jnp.float32)
    grad_gate = grad_hidden * up_part * sigmoid_gate * (1.0 + gate_part * (1.0 - sigmoid_gate))
    grad_up = grad_hidden * silu_gate
    grad_gate_up = jnp.concatenate([grad_gate, grad_up], axis=1).astype(jnp.bfloat16)
    gate_up_term = jnp.einsum(
        "rd,rc->dc", normed_two, grad_gate_up, preferred_element_type=jnp.float32
    )
    grad_normed_two = jnp.einsum(
        "rc,dc->rd", grad_gate_up, gate_up_full, preferred_element_type=jnp.float32
    )
    grad_norm_path, norm_two_term = norm_back(grad_normed_two, residual, scale_two, gain_two)
    grad_residual = grad_out + grad_norm_path
    grad_branch = grad_residual.astype(jnp.bfloat16)
    out_term = jnp.einsum("rq,rd->qd", attn_flat, grad_branch, preferred_element_type=jnp.float32)
    grad_attn = jnp.einsum(
        "rd,qd->rq", grad_branch, out_full, preferred_element_type=jnp.float32
    ).astype(jnp.bfloat16)
    grad_heads = jnp.transpose(grad_attn.reshape(row_count, HEADS, HEAD), (1, 0, 2))
    grad_queries, grad_keys, grad_values = attend_back(
        query_heads, keys_all, values_all, allowed, grad_heads, log_totals
    )
    kv_terms = jnp.concatenate(
        [
            jnp.transpose(grad_keys, (1, 0, 2)).reshape(key_count, KVW),
            jnp.transpose(grad_values, (1, 0, 2)).reshape(key_count, KVW),
        ],
        axis=1,
    )
    kv_local = lax.psum_scatter(kv_terms, "seq", scatter_dimension=0, tiled=True)
    grad_query_lin = rotate_back(
        jnp.transpose(grad_queries, (1, 0, 2)), cos_table, sine_table
    ).reshape(row_count, QW)
    grad_key_lin = rotate_back(
        kv_local[:, :KVW].reshape(row_count, KV_HEADS, HEAD), cos_table, sine_table
    ).reshape(row_count, KVW)
    grad_joined = jnp.concatenate([grad_query_lin, grad_key_lin, kv_local[:, KVW:]], axis=1).astype(
        jnp.bfloat16
    )
    qkv_term = jnp.einsum("rd,rc->dc", normed_one, grad_joined, preferred_element_type=jnp.float32)
    bias_term = jnp.sum(grad_joined.astype(jnp.float32), axis=0)
    grad_normed_one = jnp.einsum(
        "rc,dc->rd", grad_joined, qkv_full, preferred_element_type=jnp.float32
    )
    grad_input_path, norm_one_term = norm_back(grad_normed_one, inputs, scale_one, gain_one)
    grad_tokens = grad_residual + grad_input_path
    reduced = reduce_grads(
        qkv_term, out_term, gate_up_term, down_term, norm_one_term, bias_term, norm_two_term
    )
    return (
        layer_out.astype(jnp.bfloat16),
        grad_tokens,
        reduced[4],
        reduced[0],
        reduced[5],
        reduced[6],
        reduced[1],
        reduced[7],
        reduced[2],
        reduced[3],
    )


def solution(mesh):
    return jax.shard_map(
        per_device,
        mesh=mesh,
        in_specs=(
            P(("fsdp", "seq"), None),
            P(("fsdp", "seq")),
            P(("fsdp", "seq")),
            P("fsdp"),
            P("seq", "fsdp"),
            P("fsdp"),
            P("fsdp", "seq"),
            P("fsdp"),
            P("seq", "fsdp"),
            P("fsdp", "seq"),
            P(("fsdp", "seq"), None),
        ),
        out_specs=(
            P(("fsdp", "seq"), None),
            P(("fsdp", "seq"), None),
            P("fsdp"),
            P("seq", "fsdp"),
            P("fsdp"),
            P("fsdp"),
            P("fsdp", "seq"),
            P("fsdp"),
            P("seq", "fsdp"),
            P("fsdp", "seq"),
        ),
        check_vma=False,
    )
```

profile of v0, /device:TPU:0, one launch (start us, length us, event | category | flops | bytes accessed | tf_op | source)
XLA Modules:
  0.0 2065.3 jit_solution(2635598276269399068)
XLA Ops:
  8.7 7.6 all-gather
  24.7 11.6 all-gather.14.cloned.1.call-done
  43.8 21.9 %all-reduce.9 = (bf16[1152]{0:T(1024)(128)(2,1)S(1)}, bf16[896]{0:T(1024)(128)(2,1)S(1)}, bf16[896]{0:T(1024)(128)(2,1)S(1)}) all-reduce(bf16[1152]{0:T(1024)(128)(2,1)S(1)} %dynamic-update-slice.1, bf16[896]{0:T(1024)(128)(2,1)S(1)} %dynamic-update-slice, ...), channel_id=1, replica_groups=mesh['seq'=4,'fsdp'=8] {'fsdp'}, use_global_device_ids=true, to_apply=%add.1 | all-reduce | flops 2944 | bytes 11776
  81.4 26.8 %all-gather.10.cloned.1.call-done = bf16[896,1152]{0,1:T(8,128)(2,1)} async-done(((bf16[896,144]{0,1:T(8,128)(2,1)}), bf16[896,1152]{0,1:T(8,128)(2,1)}) %all-gather.10.cloned.1.call-update) | async-done | bytes 2064400 | tf_op jit(solution)/shard_map/all_gather | solution.py:62
  115.9 8.7 all_gather.56
  126.0 121.3 %while.34 = (s32[]{:T(128)}, bf16[14,384,64]{1,2,0:T(8,128)(2,1)S(1)}, f32[14,384]{1,0:T(8,128)}, s32[14]{0:T(128)S(1)}, bf16[14,384,64]{2,1,0:T(8,128)(2,1)}, /...) while((s32[]{:T(128)}, ...), condition=%wide.region_4.5_spmd.clone.clone, body=%wide.region_1.4_spmd.clone.sunk.clone | while | flops 157482640 | bytes 8101159 | solution.py:131
  251.1 237.6 %all-gather.16.cloned.1.call-done = bf16[896,9728]{0,1:T(8,128)(2,1)} async-done(((bf16[896,1216]{0,1:T(8,128)(2,1)}), bf16[896,9728]{0,1:T(8,128)(2,1)}) %all-gather.16.cloned.1.call-update) | async-done | bytes 17432592 | tf_op jit(solution)/shard_map/all_gather | solution.py:64
  488.7 15.0 fusion.76
  503.7 116.8 %all-gather.20.cloned.1.call-done = bf16[4864,896]{1,0:T(8,128)(2,1)} async-done(((bf16[608,896]{1,0:T(8,128)(2,1)}), bf16[4864,896]{1,0:T(8,128)(2,1)}) %all-gather.20.cloned.1.call-update) | async-done | bytes 8716304 | tf_op jit(solution)/shard_map/all_gather | solution.py:65
  620.6 13.3 multiply_convert_fusion.2
  633.9 19.4 multiply_reduce_fusion.1
  658.8 194.4 %while.35 = (s32[]{:T(128)}, f32[14,384,64]{1,2,0:T(8,128)}, f32[14,1536,64]{1,2,0:T(8,128)}, f32[14,1536,64]{1,2,0:T(8,128)}, s32[14]{0:T(128)S(1)}, /*index=5*...) while((s32[]{:T(128)}, f32[14,384,64]{1,2,0:T(8,128)}, ...), condition=%wide.region_9.10_spmd.clone.clone, body=%wide.region_7.9_spmd.clone.sunk.clone | while | flops 384687744 | bytes 20083032 | solution.py:165
  867.7 19.5 reduce-scatter.18.cloned.1.call-done
  893.8 11.1 fusion.83
  905.0 19.4 fusion.48
  924.5 42.5 %reduce-scatter.22.cloned.1.call-done = f32[112,896]{1,0:T(8,128)} async-done(((f32[896,896]{1,0:T(8,128)}), f32[112,896]{1,0:T(8,128)}) %reduce-scatter.22.cloned.1.call-update) | async-done | bytes 401424 | tf_op jit(solution)/shard_map/reduce_scatter | solution.py:80
  969.0 88.1 %reduce-scatter.20.cloned.1.call-done = f32[896,144]{0,1:T(8,128)} async-done(((f32[896,1152]{0,1:T(8,128)}), f32[896,144]{0,1:T(8,128)}) %reduce-scatter.20.cloned.1.call-update) | async-done | bytes 516112 | tf_op jit(solution)/shard_map/reduce_scatter | solution.py:79
  1059.5 295.2 %reduce-scatter.26.cloned.1.call-done = f32[608,896]{1,0:T(8,128)} async-done(((f32[4864,896]{1,0:T(8,128)}), f32[608,896]{1,0:T(8,128)}) %reduce-scatter.26.cloned.1.call-update) | async-done | bytes 2179088 | tf_op jit(solution)/shard_map/reduce_scatter | solution.py:82
  1358.1 565.0 %reduce-scatter.24.cloned.1.call-done = f32[896,1216]{0,1:T(8,128)} async-done(((f32[896,9728]{0,1:T(8,128)}), f32[896,1216]{0,1:T(8,128)}) %reduce-scatter.24.cloned.1.call-update) | async-done | bytes 4358160 | tf_op jit(solution)/shard_map/reduce_scatter | solution.py:81
  1930.7 10.0 add_convert_fusion
  1940.9 7.0 psum.22
  1952.0 35.7 %all-reduce.7 = (f32[896]{0:T(1024)S(1)}, f32[1024]{0:T(1024)S(1)}, f32[128]{0:T(128)S(1)}, f32[896]{0:T(1024)S(1)}) all-reduce(f32[896]{0:T(1024)S(1)} %get-tuple-element.437, f32[1024]{0:T(1024)S(1)} %slice.95, f32[128]{0:T(128)S(1)} %slice.96, f32[896]{0:T(1024)S(1)} %copy-done.23), channel_id=3, replica_groups=mesh['seq'=4,'fsdp'=8] {'fsdp'}, use_global_device_ids=true, to_apply=%region_16.17.clone | all-reduce | flops 2944 | bytes 23552
  2001.5 7.1 reduce-scatter.34.cloned.1.call-done
  2008.6 50.0 %reduce-scatter.32.cloned.1.call-done = f32[224,1216]{1,0:T(8,128)} async-done(((f32[896,1216]{1,0:T(8,128)}), f32[224,1216]{1,0:T(8,128)}) %reduce-scatter.32.cloned.1.call-update) | async-done | bytes 1089552
  (403 shorter events, 308.0 us)
Async XLA Ops:
  7.2 10.3 copy-start.17
  7.2 29.1 %all-gather.14.cloned.1.call-start = ((), (), s32[]{:S(2)}) async-start(), calls=%async_computation.11 | async-start | bytes 2867200 | tf_op jit(solution)/shard_map/all_gather | solution.py:58
  7.9 71.0 %all-gather.18.cloned.1.call-start = ((), (), s32[]{:S(2)}) async-start(), calls=%async_computation.13 | async-start | bytes 1433600 | tf_op jit(solution)/shard_map/all_gather | solution.py:59
  8.7 99.5 %all-gather.10.cloned.1.call-start = ((), (), s32[]{:S(2)}) async-start(), calls=%async_computation.9 | async-start | bytes 2322432 | tf_op jit(solution)/shard_map/all_gather | solution.py:62
  17.4 229.8 %all-gather.12.cloned.1.call-start = ((), (), s32[]{:S(2)}) async-start(), calls=%async_computation.10 | async-start | bytes 1806336 | tf_op jit(solution)/shard_map/all_gather | solution.py:63
  24.7 464.0 %all-gather.16.cloned.1.call-start = ((), (), s32[]{:S(2)}) async-start(), calls=%async_computation.12 | async-start | bytes 19611648 | tf_op jit(solution)/shard_map/all_gather | solution.py:64
  40.5 25.7 %copy-start.25 = (s32[384]{0:T(512)S(1)}, s32[384]{0:T(512)}, u32[]{:S(2)}) copy-start(s32[384]{0:T(512)} %param.16) | copy-start | bytes 4612
  40.5 38.2 %copy-start = (bf16[384,896]{1,0:T(8,128)(2,1)S(1)}, bf16[384,896]{1,0:T(8,128)(2,1)}, u32[]{:S(2)}) copy-start(bf16[384,896]{1,0:T(8,128)(2,1)} %param.15) | copy-start | bytes 2064388
  40.5 580.0 %all-gather.20.cloned.1.call-start = ((), (), s32[]{:S(2)}) async-start(), calls=%async_computation.14 | async-start | bytes 9805824 | tf_op jit(solution)/shard_map/all_gather | solution.py:65
  81.3 805.9 %reduce-scatter.18.cloned.1.call-start = ((), (), s32[]{:S(2)}) async-start(), calls=%async_computation.15 | async-start | bytes 1966080 | tf_op jit(solution)/shard_map/reduce_scatter | solution.py:274
  126.0 121.3 %copy-start.1 = (bf16[384,896]{1,0:T(8,128)(2,1)S(1)}, bf16[384,896]{1,0:T(8,128)(2,1)}, u32[]{:S(2)}) copy-start(bf16[384,896]{1,0:T(8,128)(2,1)} %param.15) | copy-start | bytes 2064388
  503.7 130.1 %copy-start.5 = (f32[384,896]{1,0:T(8,128)S(1)}, f32[384,896]{1,0:T(8,128)}, u32[]{:S(2)}) copy-start(f32[384,896]{1,0:T(8,128)} %get-tuple-element.520) | copy-start | bytes 4128772
  633.9 19.4 copy-start.7
  633.9 19.4 copy-start.6
  633.9 19.4 copy-start.8
  860.7 106.3 %reduce-scatter.22.cloned.1.call-start = ((), (), s32[]{:S(2)}) async-start(), calls=%async_computation.17 | async-start | bytes 3612672 | tf_op jit(solution)/shard_map/reduce_scatter | solution.py:80
  864.6 192.6 %reduce-scatter.20.cloned.1.call-start = ((), (), s32[]{:S(2)}) async-start(), calls=%async_computation.16 | async-start | bytes 4644864 | tf_op jit(solution)/shard_map/reduce_scatter | solution.py:79
  867.7 21.6 %copy-start.2 = (bf16[384,896]{1,0:T(8,128)(2,1)S(1)}, bf16[384,896]{1,0:T(8,128)(2,1)}, u32[]{:S(2)}) copy-start(bf16[384,896]{1,0:T(8,128)(2,1)} %param.15) | copy-start | bytes 2064388
  892.8 462.0 %reduce-scatter.26.cloned.1.call-start = ((), (), s32[]{:S(2)}) async-start(), calls=%async_computation.19 | async-start | bytes 19611648 | tf_op jit(solution)/shard_map/reduce_scatter | solution.py:82
  904.9 1018.2 %reduce-scatter.24.cloned.1.call-start = ((), (), s32[]{:S(2)}) async-start(), calls=%async_computation.18 | async-start | bytes 39223296 | tf_op jit(solution)/shard_map/reduce_scatter | solution.py:81
  924.4 1073.8 %reduce-scatter.30.cloned.1.call-start = ((), (), s32[]{:S(2)}) async-start(), calls=%async_computation.21 | async-start | bytes 573440
  969.0 1030.9 %reduce-scatter.28.cloned.1.call-start = ((), (), s32[]{:S(2)}) async-start(), calls=%async_computation.20 | async-start | bytes 1146880
  1059.5 949.2 %reduce-scatter.34.cloned.1.call-start = ((), (), s32[]{:S(2)}) async-start(), calls=%async_computation.23 | async-start | bytes 2867200
  1357.9 700.8 %reduce-scatter.32.cloned.1.call-start = ((), (), s32[]{:S(2)}) async-start(), calls=%async_computation.22 | async-start | bytes 5734400
  (23 other events, 62.0 us)
Sparse Core Ops, SparseCore 0:
  9.6 26.6 all-gather.13
  37.8 18.2 all-gather.17
  58.9 49.1 all-gather.9
  110.2 42.8 all-gather.11
  154.4 334.2 all-gather.15
  491.3 129.2 all-gather.19
  860.8 26.3 reduce-scatter.17
  891.2 75.6 reduce-scatter.21
  970.5 86.5 reduce-scatter.19
  1061.4 293.2 reduce-scatter.25
  1359.2 563.9 reduce-scatter.23
  1925.5 20.3 reduce-scatter.29
  1948.5 24.2 reduce-scatter.27
  1976.0 32.6 reduce-scatter.33
  2011.6 46.9 reduce-scatter.31
where the time goes:
time: 2080 us; the launch traced here: 2070 us
  waiting for transfers between devices  1460 us (70%)
  matrix products  257 us (12%)
  loops' own time  110 us (5%)
  blocking collectives  104 us (5%)
  local copies, waits for them, and re-layouts  88.8 us (4%)
  other arithmetic  25 us (1%)
    reduce_scatter x1, waiting for transfers between devices, reduce_grads(): lax.psum_scatter(gate_up_term, 'fsdp', scatter_dimension=1, tiled=True)  565 us
    reduce_scatter x1, waiting for transfers between devices, reduce_grads(): lax.psum_scatter(down_term, 'fsdp', scatter_dimension=0, tiled=True)  295 us
    all_gather x1, waiting for transfers between devices, collect(): lax.all_gather(section_one[2], 'fsdp', axis=1, tiled=True)  238 us
    all_gather x1, waiting for transfers between devices, collect(): lax.all_gather(section_one[3], 'fsdp', axis=0, tiled=True)  117 us
    reduce_scatter x1, waiting for transfers between devices, reduce_grads(): lax.psum_scatter(qkv_term, 'fsdp', scatter_dimension=1, tiled=True)  88.1 us
    unnamed x19, waiting for transfers between devices  58.7 us
    unnamed x2, blocking collectives  57.6 us
    another operation x1, loops' own time, attend(): return lax.map(one_head, jnp.arange(HEADS))  55 us
  transfers between devices with their start and end apart: 15, of which 11 were waited for; matrix products, arithmetic and copies ran while one was open for 9% of the time, Pallas kernels for 0%

commit v1 on v0

v1 whole, which is shorter than its diff:
```python
import functools

import jax
import jax.numpy as jnp
from jax import lax
from jax.experimental import pallas as pl
from jax.experimental.pallas import tpu as pltpu
from jax.sharding import PartitionSpec as P

HEADS = 14
KV_HEADS = 2
HEAD = 64
FF = 4864
QW = 896
KVW = 128
PAIR = 2 * HEAD
PAIRS = HEADS // 2
OUTER = 4

EPSILON = 1e-06
ROPE_BASE = 1000000.0
MASKED = -1e30
VMEM_LIMIT = 50 * 1024 * 1024

F32 = jnp.float32
BF16 = jnp.bfloat16


def dot(left, right, left_dim, right_dim):
    return lax.dot_general(
        left, right, (((left_dim,), (right_dim,)), ((), ())), preferred_element_type=F32
    )


def swap(block, axis, size, bits):
    return lax.ppermute(block, axis, [(i, i ^ bits) for i in range(size)])


def seq_gather(block, size):
    blocks = {0: block}
    bit = size // 2
    while bit:
        blocks.update({o ^ bit: swap(b, "seq", size, bit) for o, b in blocks.items()})
        bit //= 2
    return blocks


def seq_scatter(stack, size, me):
    bit = 1
    while bit < size:
        cut = stack.reshape((size // (2 * bit), 2) + stack.shape[1:])
        digit = (me // bit) % 2
        given = lax.dynamic_index_in_dim(cut, 1 - digit, 1, keepdims=False)
        kept = lax.dynamic_index_in_dim(cut, digit, 1, keepdims=False)
        stack = kept.astype(F32) + swap(given.astype(BF16), "seq", size, bit).astype(F32)
        bit *= 2
    return stack[0]


def kv_sum(stack, size):
    parts = [stack[o] for o in range(size)]
    bit = 1
    while bit < size:
        for o in range(0, size, 2 * bit):
            got = swap(parts[o + bit].astype(BF16), "seq", size, bit)
            parts[o] = parts[o].astype(F32) + got.astype(F32)
        bit *= 2
    return parts[0]


def fsdp_gather(block, size):
    blocks = {0: block}
    inner = size // OUTER
    for k in range(1, OUTER):
        blocks[k * inner] = swap(block, "fsdp", size, k * inner)
    for m in range(1, inner):
        for k in range(OUTER):
            blocks[k * inner + m] = swap(blocks[k * inner], "fsdp", size, m)
    return blocks


def fsdp_gather_small(block, size):
    inner = size // OUTER
    column = jnp.stack([block] + [swap(block, "fsdp", size, k * inner) for k in range(1, OUTER)])
    columns = [column] + [swap(column, "fsdp", size, m) for m in range(1, inner)]
    return jnp.stack(columns, axis=1).reshape((size,) + block.shape)


def fsdp_scatter(stack, size, me):
    inner = size // OUTER
    my_outer, my_inner = me // inner, me % inner
    cut = stack.reshape((OUTER, inner) + stack.shape[1:])

    def column(index):
        return lax.dynamic_index_in_dim(cut, index, 1, keepdims=False)

    total = column(my_inner).astype(F32)
    for m in range(1, inner):
        got = swap(column(my_inner ^ m).astype(BF16), "fsdp", size, m)
        total = total + got.astype(F32)
    low = total.astype(BF16)
    mine = lax.dynamic_index_in_dim(total, my_outer, 0, keepdims=False)
    for k in range(1, OUTER):
        given = lax.dynamic_index_in_dim(low, my_outer ^ k, 0, keepdims=False)
        mine = mine + swap(given, "fsdp", size, k * inner).astype(F32)
    return mine


def on_device(body, name, out_shapes, scratch, me, arrays):
    vmem = pl.BlockSpec(memory_space=pltpu.VMEM)
    return pl.pallas_call(
        body,
        in_specs=[pl.BlockSpec(memory_space=pltpu.SMEM)] + [vmem] * len(arrays),
        out_specs=[vmem] * len(out_shapes),
        out_shape=out_shapes,
        scratch_shapes=scratch,
        compiler_params=pltpu.CompilerParams(vmem_limit_bytes=VMEM_LIMIT),
        name=name,
    )(me, *arrays)


def padded(rows):
    return -(-rows // 16) * 16


def cut_ff(me, gate_up_weight, down_weight, size):
    width = gate_up_weight.shape[0]
    half = down_weight.shape[0]
    strip = half // size
    tall = padded(strip)

    def body(me_ref, gu_ref, d_ref, *refs):
        outs, held = refs[:size], refs[size]
        turned = gu_ref[...].astype(F32).T
        down = d_ref[...].astype(F32)
        blank = jnp.zeros((tall - strip, width), F32)
        for q in range(size):
            one = turned[q * strip : (q + 1) * strip]
            two = turned[half + q * strip : half + (q + 1) * strip]
            three = down[q * strip : (q + 1) * strip]
            parts = [one, blank, two, blank, three, blank]
            held[q] = jnp.concatenate(parts, axis=0).astype(BF16)
        for o in range(size):
            outs[o][...] = held[me_ref[0] ^ o]

    shape = jax.ShapeDtypeStruct((3 * tall, width), BF16)
    scratch = [pltpu.VMEM((size, 3 * tall, width), BF16)]
    return on_device(body, "cut_ff", [shape] * size, scratch, me, (gate_up_weight, down_weight))


def join_lanes(me, blocks):
    size = len(blocks)
    rows, width = blocks[0].shape

    def body(me_ref, *refs):
        ins, out, held = refs[:size], refs[size], refs[size + 1]
        for o in range(size):
            held[me_ref[0] ^ o] = ins[o][...]
        out[...] = jnp.concatenate([held[q].astype(F32) for q in range(size)], 1).astype(BF16)

    return on_device(
        body,
        "join_lanes",
        [jax.ShapeDtypeStruct((rows, size * width), BF16)],
        [pltpu.VMEM((size, rows, width), BF16)],
        me,
        blocks,
    )[0]


def join_qkv(me, blocks, rows):
    size = len(blocks)
    count, tall, width = blocks[0].shape

    def body(me_ref, *refs):
        ins, out, vectors, held = refs[:size], refs[size], refs[size + 1], refs[size + 2]
        for o in range(size):
            held[me_ref[0] ^ o] = ins[o][...]
        for f in range(count):
            parts = [held[q, f, :rows].astype(F32) for q in range(size)]
            out[me_ref[1] ^ f] = jnp.concatenate(parts, axis=1).astype(BF16)
            vectors[me_ref[1] ^ f] = ins[0][f, rows:]

    return on_device(
        body,
        "join_qkv",
        [
            jax.ShapeDtypeStruct((count, rows, size * width), BF16),
            jax.ShapeDtypeStruct((count, tall - rows, width), BF16),
        ],
        [pltpu.VMEM((size, count, tall, width), BF16)],
        me,
        blocks,
    )


def cut_lanes(me, sums, size):
    rows = sum(s.shape[0] for s in sums)
    width = sums[0].shape[1] // size

    def body(me_ref, *refs):
        ins, outs, held = refs[: len(sums)], refs[len(sums) : -1], refs[-1]
        whole = jnp.concatenate([r[...] for r in ins], axis=0)
        for q in range(size):
            held[q] = whole[:, q * width : (q + 1) * width].astype(BF16)
        for o in range(size):
            outs[o][...] = held[me_ref[0] ^ o]

    shape = jax.ShapeDtypeStruct((rows, width), BF16)
    scratch = [pltpu.VMEM((size, rows, width), BF16)]
    return on_device(body, "cut_lanes", [shape] * size, scratch, me, sums)


def join_ff(me, blocks, strip):
    size = len(blocks)
    rows, width = blocks[0].shape
    tall = rows // 3

    def body(me_ref, *refs):
        ins, gu, down, held = refs[:size], refs[size], refs[size + 1], refs[size + 2]
        for o in range(size):
            held[me_ref[0] ^ o] = ins[o][...].astype(F32)
        cut = [
            [held[q, i * tall : i * tall + strip] for q in range(size)] for i in range(3)
        ]
        gu[...] = jnp.concatenate(cut[0] + cut[1], axis=0).T
        down[...] = jnp.concatenate(cut[2], axis=0)

    return on_device(
        body,
        "join_ff",
        [
            jax.ShapeDtypeStruct((width, 2 * size * strip), F32),
            jax.ShapeDtypeStruct((size * strip, width), F32),
        ],
        [pltpu.VMEM((size, rows, width), F32)],
        me,
        blocks,
    )


def feed_forward(me, weight_blocks, row_blocks, cot_all):
    count, size = len(weight_blocks), len(row_blocks)
    rows, width = row_blocks[0].shape
    tall = weight_blocks[0].shape[0] // 3
    units = count * tall
    step_units = 256

    def body(me_ref, *refs):
        blocks, xs = refs[:count], refs[count : count + size]
        g_ref = refs[count + size]
        hid, gg, gu, gn, part, x_out = refs[count + size + 1 : count + size + 7]
        gu_w, d_w, x_all, sems = refs[count + size + 7 :]
        step = pl.program_id(0)

        @pl.when(step == 0)
        def _():
            copies = []
            for o in range(count):
                f = me_ref[1] ^ o
                copies.append((blocks[o].at[pl.ds(0, 2 * tall)], gu_w.at[f]))
                copies.append((blocks[o].at[pl.ds(2 * tall, tall)], d_w.at[f]))
            for o in range(size):
                copies.append((xs[o], x_all.at[me_ref[0] ^ o]))
            started = [
                pltpu.make_async_copy(src, dst, sems.at[i]) for i, (src, dst) in enumerate(copies)
            ]
            for copy in started:
                copy.start()
            for copy in started:
                copy.wait()

        x = x_all[step]
        g = g_ref[...]
        x_out[...] = x
        gate_w = gu_w[: count // 2].reshape(units, width)
        up_w = gu_w[count // 2 :].reshape(units, width)
        down_w = d_w[...].reshape(units, width)
        for begin in range(0, units, step_units):
            at = slice(begin, begin + step_units)
            gate = dot(x, gate_w[at], 1, 1)
            up = dot(x, up_w[at], 1, 1)
            grad_hidden = dot(g, down_w[at], 1, 1)
            sigmoid = 0.5 * jnp.tanh(0.5 * gate) + 0.5
            silu = gate * sigmoid
            hid[:, at] = (silu * up).astype(BF16)
            gg[:, at] = (grad_hidden * up * (sigmoid + silu * (1.0 - sigmoid))).astype(BF16)
            gu[:, at] = (grad_hidden * silu).astype(BF16)
        gn[...] = (dot(gg[...], gate_w, 1, 0) + dot(gu[...], up_w, 1, 0)).astype(BF16)
        part[...] = dot(hid[...], down_w, 1, 0).astype(BF16)

    hbm = pl.BlockSpec(memory_space=pl.ANY)
    by_rows = lambda n: pl.BlockSpec((rows, n), lambda i: (i, 0))
    like = lambda n: jax.ShapeDtypeStruct((size * rows, n), BF16)
    return pl.pallas_call(
        body,
        grid=(size,),
        in_specs=[pl.BlockSpec(memory_space=pltpu.SMEM)]
        + [hbm] * (count + size)
        + [by_rows(width)],
        out_specs=[by_rows(units)] * 3 + [by_rows(width)] * 3,
        out_shape=[like(units)] * 3 + [like(width)] * 3,
        scratch_shapes=[
            pltpu.VMEM((count, 2 * tall, width), BF16),
            pltpu.VMEM((count, tall, width), BF16),
            pltpu.VMEM((size, rows, width), BF16),
            pltpu.SemaphoreType.DMA((2 * count + size,)),
        ],
        compiler_params=pltpu.CompilerParams(vmem_limit_bytes=VMEM_LIMIT),
        cost_estimate=pl.CostEstimate(
            flops=12 * size * rows * units * width,
            bytes_accessed=2 * (3 * units * width + size * rows * (3 * units + 5 * width)),
            transcendentals=size * rows * units,
        ),
        name="feed_forward",
    )(me, *weight_blocks, *row_blocks, cot_all)


def both_heads(pair):
    lane = lax.broadcasted_iota(jnp.int32, pair.shape, 1)
    zero = jnp.zeros_like(pair)
    return jnp.concatenate(
        [jnp.where(lane < HEAD, pair, zero), jnp.where(lane < HEAD, zero, pair)], axis=0
    )


def fill_bias(low_ref, high_ref, place_ref, bias_ref):
    place = place_ref[...]
    allowed = (place >= low_ref[...]) & (place <= high_ref[...])
    bias = jnp.where(allowed, 0.0, MASKED).astype(F32)
    rows = bias.shape[1]
    bias_ref[:, :rows] = bias
    bias_ref[:, rows:] = bias


def own_rows(wide, rows):
    return jnp.concatenate([wide[:HEAD, :rows], wide[HEAD:, rows:]], axis=0)


def attend_kernel(low_ref, high_ref, place_ref, q_ref, k_ref, vt_ref, o_ref, lse_ref, bias_ref):
    @pl.when(pl.program_id(0) == 0)
    def _():
        fill_bias(low_ref, high_ref, place_ref, bias_ref)

    rows = q_ref.shape[0]
    queries = both_heads(q_ref[...])
    keys = k_ref[0]
    values_t = vt_ref[0]
    outs, totals = [], []
    for begin in range(0, 2 * rows, 256):
        scores = dot(keys, queries[begin : begin + 256], 1, 1) + bias_ref[:, begin : begin + 256]
        top = jnp.max(scores, axis=0, keepdims=True)
        probs = jnp.exp(scores - top)
        total = jnp.sum(probs, axis=0, keepdims=True)
        outs.append(dot(values_t, probs.astype(BF16), 1, 0) / total)
        totals.append(top + jnp.log(total))
    wide = jnp.concatenate(outs, axis=1)
    o_ref[...] = own_rows(wide, rows).T.astype(BF16)
    lse_ref[0] = jnp.concatenate(totals, axis=1)


def attend_back_kernel(
    low_ref, high_ref, place_ref, q_ref, g_ref, o_ref, lse_ref, k_ref, kt_ref, v_ref,
    dq_ref, dk_ref, dv_ref, bias_ref,
):
    step = pl.program_id(0)

    @pl.when(step == 0)
    def _():
        fill_bias(low_ref, high_ref, place_ref, bias_ref)

    @pl.when((step == 0) | (step == PAIRS // 2) | (step == PAIRS // 2 + 1))
    def _():
        dk_ref[...] = jnp.zeros_like(dk_ref)
        dv_ref[...] = jnp.zeros_like(dv_ref)

    rows = q_ref.shape[0]
    queries = both_heads(q_ref[...])
    grads = both_heads(g_ref[...])
    keys = k_ref[0]
    keys_t = kt_ref[0]
    values = v_ref[0]
    product = (g_ref[...].astype(F32) * o_ref[...].astype(F32)).T
    delta = jnp.concatenate(
        [
            jnp.sum(product[:HEAD], axis=0, keepdims=True),
            jnp.sum(product[HEAD:], axis=0, keepdims=True),
        ],
        axis=1,
    )
    lse = lse_ref[0]
    outs = []
    for begin in range(0, 2 * rows, 256):
        part = slice(begin, begin + 256)
        scores = dot(keys, queries[part], 1, 1) + bias_ref[:, part]
        probs = jnp.exp(scores - lse[:, part])
        grad_probs = dot(values, grads[part], 1, 1)
        grad_scores = (probs * (grad_probs - delta[:, part])).astype(BF16)
        outs.append(dot(keys_t, grad_scores, 1, 0))
        dk_ref[0] += dot(grad_scores, queries[part], 1, 0)
        dv_ref[0] += dot(probs.astype(BF16), grads[part], 1, 0)
    wide = jnp.concatenate(outs, axis=1)
    dq_ref[...] = own_rows(wide, rows).T * 0.125


def variant(step):
    half = PAIRS // 2
    return jnp.where(step < half, 0, jnp.where(step == half, 1, 2))


def attend(low, high, place, queries, pair_keys, pair_values_t):
    rows, count = queries.shape[0], pair_keys.shape[1]
    whole = lambda shape: pl.BlockSpec(shape, lambda i: (0,) * len(shape))
    pair = pl.BlockSpec((rows, PAIR), lambda i: (0, i))
    return pl.pallas_call(
        attend_kernel,
        grid=(PAIRS,),
        in_specs=[
            whole((1, rows)),
            whole((1, rows)),
            whole((count, 1)),
            pair,
            pl.BlockSpec((1, count, PAIR), lambda i: (variant(i), 0, 0)),
            pl.BlockSpec((1, PAIR, count), lambda i: (variant(i), 0, 0)),
        ],
        out_specs=[pair, pl.BlockSpec((1, 1, 2 * rows), lambda i: (i, 0, 0))],
        out_shape=[
            jax.ShapeDtypeStruct((rows, QW), BF16),
            jax.ShapeDtypeStruct((PAIRS, 1, 2 * rows), F32),
        ],
        scratch_shapes=[pltpu.VMEM((count, 2 * rows), F32)],
        compiler_params=pltpu.CompilerParams(vmem_limit_bytes=VMEM_LIMIT),
        cost_estimate=pl.CostEstimate(
            flops=4 * HEADS * rows * count * PAIR,
            bytes_accessed=4 * rows * QW + 1024 * count,
            transcendentals=HEADS * rows * count,
        ),
        name="attend",
    )(low, high, place, queries, pair_keys, pair_values_t)


def attend_back(low, high, place, queries, grads, outs, lse, pair_keys, pair_keys_t, pair_values):
    rows, count = queries.shape[0], pair_keys.shape[1]
    whole = lambda shape: pl.BlockSpec(shape, lambda i: (0,) * len(shape))
    pair = pl.BlockSpec((rows, PAIR), lambda i: (0, i))
    tall = pl.BlockSpec((1, count, PAIR), lambda i: (variant(i), 0, 0))
    return pl.pallas_call(
        attend_back_kernel,
        grid=(PAIRS,),
        in_specs=[
            whole((1, rows)),
            whole((1, rows)),
            whole((count, 1)),
            pair,
            pair,
            pair,
            pl.BlockSpec((1, 1, 2 * rows), lambda i: (i, 0, 0)),
            tall,
            pl.BlockSpec((1, PAIR, count), lambda i: (variant(i), 0, 0)),
            tall,
        ],
        out_specs=[pair, tall, tall],
        out_shape=[
            jax.ShapeDtypeStruct((rows, QW), F32),
            jax.ShapeDtypeStruct((3, count, PAIR), F32),
            jax.ShapeDtypeStruct((3, count, PAIR), F32),
        ],
        scratch_shapes=[pltpu.VMEM((count, 2 * rows), F32)],
        compiler_params=pltpu.CompilerParams(vmem_limit_bytes=VMEM_LIMIT),
        cost_estimate=pl.CostEstimate(
            flops=10 * HEADS * rows * count * PAIR,
            bytes_accessed=8 * rows * QW + 4096 * count,
            transcendentals=HEADS * rows * count,
        ),
        name="attend_back",
    )(low, high, place, queries, grads, outs, lse, pair_keys, pair_keys_t, pair_values)


def pair_up(heads):
    one, two = heads[:, :HEAD], heads[:, HEAD:]
    return jnp.stack(
        [jnp.concatenate([one, one], 1), heads, jnp.concatenate([two, two], 1)]
    )


def unpair(sums):
    one = sums[0, :, :HEAD] + sums[0, :, HEAD:] + sums[1, :, :HEAD]
    two = sums[2, :, :HEAD] + sums[2, :, HEAD:] + sums[1, :, HEAD:]
    return jnp.concatenate([one, two], axis=1)


def rms_scale(values_in):
    return lax.rsqrt(jnp.mean(values_in * values_in, axis=-1, keepdims=True) + EPSILON)


def angle_tables(places):
    exponent = jnp.arange(HEAD // 2, dtype=F32) * 2.0 / HEAD
    frequency = ROPE_BASE ** (-exponent)
    turn = places.astype(F32)[:, None] * frequency[None, :]
    cosine, sine = lax.optimization_barrier((jnp.cos(turn), jnp.sin(turn)))
    return jnp.concatenate([cosine] * 4, axis=1), jnp.concatenate([sine] * 4, axis=1)


def widen(table, width):
    return jnp.concatenate([table] * (width // PAIR), axis=1)


def first_halves(shape):
    return lax.broadcasted_iota(jnp.int32, shape, 1) % HEAD < HEAD // 2


def rotate(tensor, cosine, sine):
    half = HEAD // 2
    ahead, behind = jnp.roll(tensor, -half, axis=1), jnp.roll(tensor, half, axis=1)
    turned = jnp.where(first_halves(tensor.shape), -ahead, behind)
    width = tensor.shape[1]
    return tensor * widen(cosine, width) + turned * widen(sine, width)


def rotate_back(grad_in, cosine, sine):
    half = HEAD // 2
    width = grad_in.shape[1]
    scaled = grad_in * widen(sine, width)
    ahead, behind = jnp.roll(scaled, -half, axis=1), jnp.roll(scaled, half, axis=1)
    return grad_in * widen(cosine, width) + jnp.where(
        first_halves(grad_in.shape), ahead, -behind
    )


def norm_back(grad_in, row_data, scale_in, gain_in):
    gain_term = jnp.sum(grad_in * row_data * scale_in, axis=0)
    grad_normed = grad_in * gain_in
    inner_mean = jnp.mean(grad_normed * row_data, axis=-1, keepdims=True)
    return (
        scale_in * grad_normed - row_data * scale_in * scale_in * scale_in * inner_mean,
        gain_term,
    )


def pad_row(vector, width):
    return jnp.pad(vector, (0, width - vector.shape[0]))[None, :]


def lanes_from_stack(stack):
    count, rows, width = stack.shape
    return jnp.transpose(stack, (1, 0, 2)).reshape(rows, count * width)


def stack_from_lanes(array, count):
    rows, width = array.shape
    return jnp.transpose(array.reshape(rows, count, width // count), (1, 0, 2))


def per_device(
    seq_size, fsdp_size, tokens, segment_ids, positions, norm_one, qkv_weight, qkv_bias,
    out_weight, norm_two, gate_up_weight, down_weight, cotangent,
):
    my_seq, my_fsdp = lax.axis_index("seq"), lax.axis_index("fsdp")
    me = jnp.stack([my_seq, my_fsdp]).astype(jnp.int32)
    offsets = range(seq_size)
    row_count = tokens.shape[0]
    width = qkv_weight.shape[0]
    qkv_rows = qkv_weight.shape[1]
    strip = down_weight.shape[0] // seq_size
    tall = padded(strip)

    ff_cut = cut_ff(me, gate_up_weight, down_weight, seq_size)
    ff_share = [ff_cut[0]] + [swap(ff_cut[o], "seq", seq_size, o) for o in offsets if o]
    ff_blocks = fsdp_gather(join_lanes(me, ff_share), fsdp_size)
    ff_blocks = [ff_blocks[o] for o in range(fsdp_size)]

    qkv_tall = padded(qkv_rows)
    packed = jnp.concatenate(
        [
            jnp.pad(qkv_weight.T, ((0, qkv_tall - qkv_rows), (0, 0))),
            pad_row(norm_one, width),
            pad_row(qkv_bias, width),
            pad_row(norm_two, width),
            jnp.zeros((13, width), BF16),
        ],
        axis=0,
    )
    packed_blocks = seq_gather(fsdp_gather_small(packed, fsdp_size), seq_size)
    qkv_t, vectors = join_qkv(me, [packed_blocks[o] for o in offsets], qkv_tall)
    qkv_t = qkv_t[:, :qkv_rows].reshape(fsdp_size * qkv_rows, -1)
    gain_one = vectors[:, 0, : norm_one.shape[0]].reshape(-1).astype(F32)
    bias_full = vectors[:, 1, : qkv_bias.shape[0]].reshape(-1).astype(F32)
    gain_two = vectors[:, 2, : norm_two.shape[0]].reshape(-1).astype(F32)

    out_part = lax.all_gather(out_weight, "fsdp", axis=0, tiled=True)
    out_full = lanes_from_stack(lax.all_gather(out_part, "seq", axis=0, tiled=False))
    cot_all = lax.all_gather(cotangent, "seq", axis=0, tiled=True)

    inputs = tokens.astype(F32)
    scale_one = rms_scale(inputs)
    normed_one = (inputs * scale_one * gain_one).astype(BF16)
    joined = dot(normed_one, qkv_t, 1, 1) + bias_full
    cosine, sine = angle_tables(positions)
    turned = rotate(joined[:, : QW + KVW], cosine, sine).astype(BF16)
    queries = turned[:, :QW] * jnp.asarray(0.125, BF16)
    kv_local = jnp.concatenate([turned[:, QW:], joined[:, QW + KVW :].astype(BF16)], axis=1)
    kv_blocks = seq_gather(kv_local, seq_size)
    kv_all = jnp.concatenate([kv_blocks[o] for o in offsets], axis=0)
    row_place = jnp.arange(row_count, dtype=jnp.int32)
    high = my_seq * row_count + row_place
    low = high - positions
    place = jnp.concatenate([(my_seq ^ o) * row_count + row_place for o in offsets])[:, None]
    low, high = low[None, :], high[None, :]
    pair_keys = pair_up(kv_all[:, :KVW])
    pair_values = pair_up(kv_all[:, KVW:])
    pair_keys_t = jnp.transpose(pair_keys, (0, 2, 1))
    pair_values_t = jnp.transpose(pair_values, (0, 2, 1))
    attn_flat, lse = attend(low, high, place, queries, pair_keys, pair_values_t)

    residual = inputs + dot(attn_flat, out_full, 1, 0)
    scale_two = rms_scale(residual)
    normed_two = (residual * scale_two * gain_two).astype(BF16)
    normed_blocks = seq_gather(normed_two, seq_size)
    hidden, grad_gate, grad_up, grad_normed, layer_part, normed_all = feed_forward(
        me, ff_blocks, [normed_blocks[o] for o in offsets], cot_all
    )
    by_seq = lambda rows: rows.reshape(seq_size, row_count, -1)
    grad_normed_two = seq_scatter(by_seq(grad_normed), seq_size, my_seq)
    down_term = dot(hidden, cot_all, 0, 0).astype(BF16).reshape(fsdp_size, tall, -1)
    gate_term = dot(grad_gate, normed_all, 0, 0).astype(BF16).reshape(fsdp_size // 2, 2, tall, -1)
    up_term = dot(grad_up, normed_all, 0, 0).astype(BF16).reshape(fsdp_size // 2, 2, tall, -1)
    chunks = [down_term] + [
        jnp.concatenate([gate_term[:, i], up_term[:, i]], axis=0) for i in range(2)
    ]
    down_sum, one_sum, two_sum = [fsdp_scatter(c, fsdp_size, my_fsdp) for c in chunks]
    layer_out = residual + seq_scatter(by_seq(layer_part), seq_size, my_seq)

    ff_back = cut_lanes(me, (one_sum, two_sum, down_sum), seq_size)
    ff_got = [ff_back[0]] + [swap(ff_back[o], "seq", seq_size, o) for o in offsets if o]
    grad_gate_up, grad_down = join_ff(me, ff_got, strip)

    grad_path, norm_two_term = norm_back(grad_normed_two, residual, scale_two, gain_two)
    grad_residual = cotangent.astype(F32) + grad_path
    grad_branch = grad_residual.astype(BF16)
    grad_attn = dot(grad_branch, out_full, 1, 1).astype(BF16)
    out_term = stack_from_lanes(dot(attn_flat, grad_branch, 0, 0).astype(BF16), seq_size)
    out_mine = seq_scatter(out_term, seq_size, my_seq).reshape(fsdp_size, -1, width)
    grad_queries, key_sums, value_sums = attend_back(
        low, high, place, queries, grad_attn, attn_flat, lse, pair_keys, pair_keys_t, pair_values
    )
    kv_terms = jnp.concatenate([unpair(key_sums), unpair(value_sums)], axis=1)
    kv_mine = kv_sum(by_seq(kv_terms), seq_size)
    turned_back = rotate_back(
        jnp.concatenate([grad_queries, kv_mine[:, :KVW]], axis=1), cosine, sine
    )
    grad_joined = jnp.concatenate([turned_back, kv_mine[:, KVW:]], axis=1).astype(BF16)
    grad_normed_one = dot(grad_joined, qkv_t, 1, 0)
    grad_path_one, norm_one_term = norm_back(grad_normed_one, inputs, scale_one, gain_one)
    grad_tokens = grad_residual + grad_path_one
    bias_term = jnp.sum(grad_joined.astype(F32), axis=0)

    def vector_rows(vector):
        rows = vector.reshape(fsdp_size, 1, -1)
        return jnp.pad(rows, ((0, 0), (0, 0), (0, width - rows.shape[2])))

    vector_terms = [norm_one_term, bias_term[: QW + KVW], bias_term[QW + KVW :], norm_two_term]
    small = jnp.concatenate([vector_rows(v) for v in vector_terms], axis=1).astype(BF16)
    small = jnp.pad(small, ((0, 0), (0, 16 - len(vector_terms)), (0, 0)))
    qkv_term = stack_from_lanes(dot(grad_joined, normed_one, 0, 0).astype(BF16), seq_size)
    qkv_term = qkv_term.reshape(seq_size, fsdp_size, qkv_rows, width)
    tail = jnp.concatenate(
        [qkv_term, jnp.broadcast_to(small[None], (seq_size,) + small.shape)], axis=2
    )
    tail_mine = seq_scatter(tail, seq_size, my_seq)
    tail_sum = fsdp_scatter(
        jnp.concatenate([tail_mine, out_mine], axis=1), fsdp_size, my_fsdp
    )
    pieces = [
        tail_sum[qkv_rows + i, : v.shape[0] // fsdp_size] for i, v in enumerate(vector_terms)
    ]
    return (
        layer_out.astype(BF16),
        grad_tokens,
        pieces[0],
        tail_sum[:qkv_rows].T,
        pieces[1],
        pieces[2],
        tail_sum[qkv_rows + 16 :],
        pieces[3],
        grad_gate_up,
        grad_down,
    )


def solution(mesh):
    rows, both = P(("fsdp", "seq"), None), P(("fsdp", "seq"))
    return jax.shard_map(
        functools.partial(per_device, mesh.shape["seq"], mesh.shape["fsdp"]),
        mesh=mesh,
        in_specs=(
            rows, both, both, P("fsdp"), P("seq", "fsdp"), P("fsdp"), P("fsdp", "seq"),
            P("fsdp"), P("seq", "fsdp"), P("fsdp", "seq"), rows,
        ),
        out_specs=(
            rows, rows, P("fsdp"), P("seq", "fsdp"), P("fsdp"), P("fsdp"), P("fsdp", "seq"),
            P("fsdp"), P("seq", "fsdp"), P("fsdp", "seq"),
        ),
        check_vma=False,
    )
```

time: 2080 us -> 491 us (0.24)
  waiting for transfers between devices: 1460 us -> 164 us
  matrix products: 257 us -> 29.1 us
  loops' own time: 110 us -> 0 us
  Pallas kernels: 0 us -> 89.7 us
  blocking collectives: 104 us -> 35.5 us
  starting transfers between devices: 1.19 us -> 60.5 us
  local copies, waits for them, and re-layouts: 88.8 us -> 47.9 us
    reduce_scatter x5 -> x0, waiting for transfers between devices: 1010 us -> none  [the longest x1 565 us: reduce_grads(): lax.psum_scatter(gate_up_term, 'fsdp', scatter_dimension=1, tiled=True)]
    all_gather x6 -> x2, waiting for transfers between devices: 393 us -> 0.03 us  [the longest x1 0.02 us: per_device(): lax.all_gather(out_part, 'seq', axis=0, tiled=False)]
    dot_general x110 -> x9, matrix products: 257 us -> 29.1 us  [dot(): lax.dot_general(left, right, (((left_dim,), (right_dim,)), ((), ())), pre...]
    ppermute x0 -> x53, waiting for transfers between devices: none -> 164 us  [swap(): return lax.ppermute(block, axis, [(i, i ^ bits) for i in range(size)])]
    another operation x2 -> x0, loops' own time: 110 us -> none  [the longest x1 55 us: attend(): return lax.map(one_head, jnp.arange(HEADS))]
    pallas_call x0 -> x8, Pallas kernels: none -> 89.7 us  [the longest x1 31.9 us: feed_forward(): pl.pallas_call(body, grid=(size,), in_specs=[pl.BlockSpec(memory_space=pl...]
    ppermute x0 -> x53, starting transfers between devices: none -> 60.4 us  [swap(): return lax.ppermute(block, axis, [(i, i ^ bits) for i in range(size)])]
    unnamed x19 -> x2, waiting for transfers between devices: 58.7 us -> 0.03 us
  transfers between devices with their start and end apart: 15 -> 55, of which waited for: 11 -> 19; matrix products, arithmetic and copies ran while one was open for 9% -> 20% of each run, Pallas kernels for 0% -> 12%
where the time goes in v1:
time: 491 us; the launch traced here: 482 us
  waiting for transfers between devices  164 us (33%)
  Pallas kernels  89.7 us (18%)
  starting transfers between devices  60.5 us (12%)
  local copies, waits for them, and re-layouts  47.9 us (10%)
  other arithmetic  39.9 us (8%)
  blocking collectives  35.5 us (7%)
  matrix products  29.1 us (6%)
  between operations  15.7 us (3%)
    ppermute x53, waiting for transfers between devices, swap(): return lax.ppermute(block, axis, [(i, i ^ bits) for i in range(size)])  164 us
    ppermute x53, starting transfers between devices, swap(): return lax.ppermute(block, axis, [(i, i ^ bits) for i in range(size)])  60.4 us
    all_gather x1, blocking collectives, per_device(): out_part = lax.all_gather(out_weight, 'fsdp', axis=0, tiled=True)  35.5 us
    pallas_call x1, Pallas kernels, feed_forward(): pl.pallas_call(body, grid=(size,), in_specs=[pl.BlockSpec(memory_space=pl...  31.9 us
    dot_general x9, matrix products, dot(): lax.dot_general(left, right, (((left_dim,), (right_dim,)), ((), ())), pre...  29.1 us
    pallas_call x1, Pallas kernels, attend_back(): pl.pallas_call(attend_back_kernel, grid=(PAIRS,), in_specs=[whole((1, row...  26.3 us
    pallas_call x1, Pallas kernels, attend(): pl.pallas_call(attend_kernel, grid=(PAIRS,), in_specs=[whole((1, rows)),...  23.2 us
    unnamed x115, local copies, waits for them, and re-layouts  11 us
  transfers between devices with their start and end apart: 55, of which 19 were waited for; matrix products, arithmetic and copies ran while one was open for 20% of the time, Pallas kernels for 12%

profile of v1, /device:TPU:0, one launch (start us, length us, event | category | flops | bytes accessed | tf_op | source)
XLA Modules:
  0.0 482.5 jit_solution(15691332998786891334)
XLA Ops:
  7.2 35.5 %all_gather.12 = bf16[896,224]{1,0:T(8,128)(2,1)} all-gather(bf16[112,224]{1,0:T(8,128)(2,1)} %param.16), channel_id=1, replica_groups=mesh['seq'=4,'fsdp'=8] {'fsdp'}, dimensions={0}, use_global_device_ids=true | all-gather | bytes 451584 | tf_op jit(solution)/shard_map/all_gather | solution.py:590
  47.0 3.3 collective-permute-start.2
  53.8 3.9 collective-permute-start.3
  71.4 23.6 %collective-permute-done.5.refs_2_ = bf16[8,160,224]{2,1,0:T(8,128)(2,1)S(1)} collective-permute-done((bf16[8,160,224]{2,1,0:T(8,128)(2,1)S(1)}, bf16[8,160,224]{2,1,0:T(8,128)(2,1)S(1)}, u32[]{:S(2)}, u32[]{:S(2)}) %collective-permute-start.5) | collective-permute-done | bytes 573472 | tf_op jit(solution)/shard_map/ppermute | solution.py:36
  128.4 23.2 %attend.1 = (bf16[384,896]{1,0:T(8,128)(2,1)S(1)}, f32[7,1,768]{2,1,0:T(1,128)S(1)}) custom-call(s32[1,384]{1,0:T(1,128)S(1)} %broadcast_in_dim.14.low_ref, s32[1,384]{1,0:T(1,128)S(1)} %iota_add_fusion.4.high_ref, s32[1536,1]{1,0:T(8,128)S(1)} %broadcast_in_dim.21.place_ref, bf16[384,896]{1,0:T(8,128)(2,1)S(1)} %copy-done, ...), custom_call_target="tpu_custom_call" | custom-call | flops 4227858432 | bytes 2949120 | tf_op jit(solution)/shard_map/attend/pallas_call | solution.py:415
  151.6 4.1 copy.65
  161.8 11.6 %collective-permute-done.16.refs_4_ = bf16[480,896]{1,0:T(8,128)(2,1)} collective-permute-done((bf16[480,896]{1,0:T(8,128)(2,1)S(1)}, bf16[480,896]{1,0:T(8,128)(2,1)}, u32[]{:S(2)}, u32[]{:S(2)}) %collective-permute-start.16) | collective-permute-done | bytes 860192 | tf_op jit(solution)/shard_map/ppermute | solution.py:36
  180.0 3.6 collective-permute-done.15.refs_3_
  183.6 18.4 %collective-permute-done.17.refs_5_ = bf16[480,896]{1,0:T(8,128)(2,1)} collective-permute-done((bf16[480,896]{1,0:T(8,128)(2,1)}, bf16[480,896]{1,0:T(8,128)(2,1)}, u32[]{:S(2)}, u32[]{:S(2)}) %collective-permute-start.17) | collective-permute-done | bytes 860192 | tf_op jit(solution)/shard_map/ppermute | solution.py:36
  202.1 17.0 %collective-permute-done.19.refs_7_ = bf16[480,896]{1,0:T(8,128)(2,1)} collective-permute-done((bf16[480,896]{1,0:T(8,128)(2,1)}, bf16[480,896]{1,0:T(8,128)(2,1)}, u32[]{:S(2)}, u32[]{:S(2)}) %collective-permute-start.19) | collective-permute-done | bytes 860192 | tf_op jit(solution)/shard_map/ppermute | solution.py:36
  219.1 31.9 %feed_forward.1 = (bf16[1536,1280]{1,0:T(8,128)(2,1)}, bf16[1536,1280]{1,0:T(8,128)(2,1)}, bf16[1536,1280]{1,0:T(8,128)(2,1)}, bf16[1536,896]{1,0:T(8,128)(2,1)}...) custom-call(s32[2]{0:T(128)S(1)} %pad_add_fusion.1.me_ref, bf16[480,896]{1,0:T(8,128)(2,1)S(1)} %join_lanes.1.refs_0_, ...), custom_call_target="tpu_custom_call" | custom-call | flops 21139292160 | bytes 32440320 | tf_op jit(solution)/shard_map/feed_forward/pallas_call | solution.py:295
  251.0 7.4 %convolution_convert_fusion = bf16[1280,896]{1,0:T(8,128)(2,1)S(1)} fusion(bf16[1536,1280]{1,0:T(8,128)(2,1)} %get-tuple-element.53, bf16[1536,896]{1,0:T(8,128)(2,1)} %all-gather.4.cloned.1.call-done.refs_12_), kind=kOutput, calls=%fused_computation.2 | convolution fusion | flops 3524362240 | bytes 8978432 | tf_op jit(solution)/shard_map/dot_general | solution.py:30
  261.8 4.5 convolution_convert_fusion.2
  266.4 4.5 convolution_convert_fusion.1
  279.3 13.2 %collective-permute-done.26 = bf16[1,384,896]{2,1,0:T(8,128)(2,1)S(1)} collective-permute-done((bf16[1,384,896]{2,1,0:T(8,128)(2,1)S(1)}, bf16[1,384,896]{2,1,0:T(8,128)(2,1)S(1)}, u32[]{:S(2)}, u32[]{:S(2)}) %collective-permute-start.26) | collective-permute-done | bytes 688160 | tf_op jit(solution)/shard_map/ppermute | solution.py:36
  292.9 13.6 %collective-permute-done.24 = bf16[1,384,896]{2,1,0:T(8,128)(2,1)S(1)} collective-permute-done((bf16[1,384,896]{2,1,0:T(8,128)(2,1)S(1)}, bf16[1,384,896]{2,1,0:T(8,128)(2,1)S(1)}, u32[]{:S(2)}, u32[]{:S(2)}) %collective-permute-start.24) | collective-permute-done | bytes 688160 | tf_op jit(solution)/shard_map/ppermute | solution.py:36
  309.7 26.3 %attend_back.1 = (f32[384,896]{1,0:T(8,128)}, f32[3,1536,128]{2,1,0:T(8,128)}, f32[3,1536,128]{2,1,0:T(8,128)}) custom-call(s32[1,384]{1,0:T(1,128)S(1)} %broadcast_in_dim.14.low_ref, s32[1,384]{1,0:T(1,128)S(1)} %iota_add_fusion.4.high_ref, s32[1536,1]{1,0:T(8,128)S(1)} %broadcast_in_dim.21.place_ref, bf16[384,896]{1,0:T(8,128)(2,1)S(1)} %copy-done.1, ...), custom_call_target="tpu_custom_call" | custom-call | flops 10569646080 | bytes 9043968 | tf_op jit(solution)/shard_map/attend_back/pallas_call | solution.py:447
  358.2 3.9 fusion.16
  391.8 15.4 %collective-permute-done.44 = bf16[160,896]{1,0:T(8,128)(2,1)S(1)} collective-permute-done((bf16[160,896]{1,0:T(8,128)(2,1)S(1)}, bf16[160,896]{1,0:T(8,128)(2,1)S(1)}, u32[]{:S(2)}, u32[]{:S(2)}) %collective-permute-start.44) | collective-permute-done | bytes 286752 | tf_op jit(solution)/shard_map/ppermute | solution.py:36
  414.3 17.6 %collective-permute-done.40 = bf16[160,896]{1,0:T(8,128)(2,1)} collective-permute-done((bf16[160,896]{1,0:T(8,128)(2,1)}, bf16[160,896]{1,0:T(8,128)(2,1)}, u32[]{:S(2)}, u32[]{:S(2)}) %collective-permute-start.40) | collective-permute-done | bytes 286752 | tf_op jit(solution)/shard_map/ppermute | solution.py:36
  436.3 7.0 %collective-permute-done.51.refs_2_ = bf16[480,224]{1,0:T(8,128)(2,1)S(1)} collective-permute-done((bf16[480,224]{1,0:T(8,128)(2,1)S(1)}, bf16[480,224]{1,0:T(8,128)(2,1)S(1)}, u32[]{:S(2)}, u32[]{:S(2)}) %collective-permute-start.51) | collective-permute-done | bytes 215072 | tf_op jit(solution)/shard_map/ppermute | solution.py:36
  443.3 4.4 collective-permute-done.52.refs_3_
  452.2 6.6 %collective-permute-start.35 = (bf16[272,224]{1,0:T(8,128)(2,1)S(1)}, bf16[272,224]{1,0:T(8,128)(2,1)S(1)}, u32[]{:S(2)}, u32[]{:S(2)}) collective-permute-start(bf16[272,224]{1,0:T(8,128)(2,1)S(1)} %get-tuple-element.145), channel_id=1, source_target_pairs={{0,2},{1,3},{2,0},{3,1},{4,6},{5,7},{6,4},{7,5},{8,10},{9,11},{10,... | collective-permute-start | bytes 365576 | tf_op jit(solution)/shard_map/ppermute | solution.py:36
  465.2 7.0 %collective-permute-done.36 = bf16[272,224]{1,0:T(8,128)(2,1)S(1)} collective-permute-done((bf16[272,224]{1,0:T(8,128)(2,1)S(1)}, bf16[272,224]{1,0:T(8,128)(2,1)S(1)}, u32[]{:S(2)}, u32[]{:S(2)}) %collective-permute-start.36) | collective-permute-done | bytes 121888 | tf_op jit(solution)/shard_map/ppermute | solution.py:36
  (343 shorter events, 159.2 us)
Async XLA Ops:
  7.2 144.4 %all-gather.6.cloned.1.call-start = ((), (), s32[]{:S(2)}) async-start(), calls=%async_computation.1 | async-start | bytes 2293760 | tf_op jit(solution)/shard_map/all_gather | solution.py:591
  42.7 176.3 %all-gather.4.cloned.1.call-start = ((), (), s32[]{:S(2)}) async-start(), calls=%async_computation | async-start | bytes 3440640 | tf_op jit(solution)/shard_map/all_gather | solution.py:592
  59.5 49.2 %collective-permute-start.10 = (bf16[480,224]{1,0:T(8,128)(2,1)}, bf16[480,224]{1,0:T(8,128)(2,1)S(1)}, u32[]{:S(2)}, u32[]{:S(2)}) collective-permute-start(bf16[480,224]{1,0:T(8,128)(2,1)} %get-tuple-element.41), channel_id=1, source_target_pairs={{0,8},{8,0},{16,24},{24,16},{1,9},{9,1},{17,25},{25,17},{2,10},{10... | collective-permute-start | bytes 645128 | tf_op jit(solution)/shard_map/ppermute | solution.py:36
  59.5 49.2 %collective-permute-start.11 = (bf16[480,224]{1,0:T(8,128)(2,1)}, bf16[480,224]{1,0:T(8,128)(2,1)S(1)}, u32[]{:S(2)}, u32[]{:S(2)}) collective-permute-start(bf16[480,224]{1,0:T(8,128)(2,1)} %get-tuple-element.42), channel_id=1, source_target_pairs={{0,16},{8,24},{16,0},{24,8},{1,17},{9,25},{17,1},{25,9},{2,18},{10... | collective-permute-start | bytes 645128 | tf_op jit(solution)/shard_map/ppermute | solution.py:36
  61.0 48.4 %collective-permute-start.12 = (bf16[480,224]{1,0:T(8,128)(2,1)}, bf16[480,224]{1,0:T(8,128)(2,1)S(1)}, u32[]{:S(2)}, u32[]{:S(2)}) collective-permute-start(bf16[480,224]{1,0:T(8,128)(2,1)} %get-tuple-element.43), channel_id=1, source_target_pairs={{0,24},{8,16},{16,8},{24,0},{1,25},{9,17},{17,9},{25,1},{2,26},{10... | collective-permute-start | bytes 645128 | tf_op jit(solution)/shard_map/ppermute | solution.py:36
  63.0 32.0 %collective-permute-start.5 = (bf16[8,160,224]{2,1,0:T(8,128)(2,1)S(1)}, bf16[8,160,224]{2,1,0:T(8,128)(2,1)S(1)}, u32[]{:S(2)}, u32[]{:S(2)}) collective-permute-start(bf16[8,160,224]{2,1,0:T(8,128)(2,1)S(1)} %bitcast.213), channel_id=1, source_target_pairs={{0,16},{8,24},{16,0},{24,8},{1,17},{9,25},{17,1},{25,9},{2,18},{10... | collective-permute-start | bytes 1720328 | tf_op jit(solution)/shard_map/ppermute | solution.py:36
  112.9 48.3 %collective-permute-start.14 = (bf16[480,896]{1,0:T(8,128)(2,1)S(1)}, bf16[480,896]{1,0:T(8,128)(2,1)}, u32[]{:S(2)}, u32[]{:S(2)}) collective-permute-start(bf16[480,896]{1,0:T(8,128)(2,1)S(1)} %join_lanes.1.refs_0_), channel_id=1, source_target_pairs={{0,2},{1,3},{2,0},{3,1},{4,6},{5,7},{6,4},{7,5},{8,10},{9,11},{10,... | collective-permute-start | bytes 2580488 | tf_op jit(solution)/shard_map/ppermute | solution.py:36
  113.5 59.9 %collective-permute-start.16 = (bf16[480,896]{1,0:T(8,128)(2,1)S(1)}, bf16[480,896]{1,0:T(8,128)(2,1)}, u32[]{:S(2)}, u32[]{:S(2)}) collective-permute-start(bf16[480,896]{1,0:T(8,128)(2,1)S(1)} %join_lanes.1.refs_0_), channel_id=1, source_target_pairs={{0,4},{1,5},{2,6},{3,7},{4,0},{5,1},{6,2},{7,3},{8,12},{9,13},{10,... | collective-permute-start | bytes 2580488 | tf_op jit(solution)/shard_map/ppermute | solution.py:36
  115.9 59.0 %collective-permute-start.18 = (bf16[480,896]{1,0:T(8,128)(2,1)S(1)}, bf16[480,896]{1,0:T(8,128)(2,1)}, u32[]{:S(2)}, u32[]{:S(2)}) collective-permute-start(bf16[480,896]{1,0:T(8,128)(2,1)S(1)} %join_lanes.1.refs_0_), channel_id=1, source_target_pairs={{0,6},{1,7},{2,4},{3,5},{4,2},{5,3},{6,0},{7,1},{8,14},{9,15},{10,... | collective-permute-start | bytes 2580488 | tf_op jit(solution)/shard_map/ppermute | solution.py:36
  119.0 56.4 %collective-permute-start.13 = (bf16[480,896]{1,0:T(8,128)(2,1)S(1)}, bf16[480,896]{1,0:T(8,128)(2,1)}, u32[]{:S(2)}, u32[]{:S(2)}) collective-permute-start(bf16[480,896]{1,0:T(8,128)(2,1)S(1)} %join_lanes.1.refs_0_), channel_id=1, source_target_pairs={{0,1},{1,0},{2,3},{3,2},{4,5},{5,4},{6,7},{7,6},{8,9},{9,8},{10,11... | collective-permute-start | bytes 2580488 | tf_op jit(solution)/shard_map/ppermute | solution.py:36
  173.4 28.6 %collective-permute-start.17 = (bf16[480,896]{1,0:T(8,128)(2,1)}, bf16[480,896]{1,0:T(8,128)(2,1)}, u32[]{:S(2)}, u32[]{:S(2)}) collective-permute-start(bf16[480,896]{1,0:T(8,128)(2,1)} %collective-permute-done.16.refs_4_), channel_id=1, source_target_pairs={{0,1},{1,0},{2,3},{3,2},{4,5},{5,4},{6,7},{7,6},{8,9},{9,8},{10,11... | collective-permute-start | bytes 2580488 | tf_op jit(solution)/shard_map/ppermute | solution.py:36
  174.9 44.2 %collective-permute-start.19 = (bf16[480,896]{1,0:T(8,128)(2,1)}, bf16[480,896]{1,0:T(8,128)(2,1)}, u32[]{:S(2)}, u32[]{:S(2)}) collective-permute-start(bf16[480,896]{1,0:T(8,128)(2,1)} %collective-permute-done.18.refs_6_), channel_id=1, source_target_pairs={{0,1},{1,0},{2,3},{3,2},{4,5},{5,4},{6,7},{7,6},{8,9},{9,8},{10,11... | collective-permute-start | bytes 2580488 | tf_op jit(solution)/shard_map/ppermute | solution.py:36
  175.4 43.6 %collective-permute-start.20 = (bf16[384,896]{1,0:T(8,128)(2,1)}, bf16[384,896]{1,0:T(8,128)(2,1)}, u32[]{:S(2)}, u32[]{:S(2)}) collective-permute-start(bf16[384,896]{1,0:T(8,128)(2,1)} %multiply_convert_fusion.refs_8_), channel_id=1, source_target_pairs={{0,8},{8,0},{16,24},{24,16},{1,9},{9,1},{17,25},{25,17},{2,10},{10... | collective-permute-start | bytes 2064392 | tf_op jit(solution)/shard_map/ppermute | solution.py:36
  177.6 41.4 %collective-permute-start.22 = (bf16[384,896]{1,0:T(8,128)(2,1)}, bf16[384,896]{1,0:T(8,128)(2,1)}, u32[]{:S(2)}, u32[]{:S(2)}) collective-permute-start(bf16[384,896]{1,0:T(8,128)(2,1)} %collective-permute-done.21.refs_10_), channel_id=1, source_target_pairs={{0,8},{8,0},{16,24},{24,16},{1,9},{9,1},{17,25},{25,17},{2,10},{10... | collective-permute-start | bytes 2064392 | tf_op jit(solution)/shard_map/ppermute | solution.py:36
  259.6 81.1 %collective-permute-start.46 = (bf16[4,160,896]{2,1,0:T(8,128)(2,1)}, bf16[4,160,896]{2,1,0:T(8,128)(2,1)}, u32[]{:S(2)}, u32[]{:S(2)}) collective-permute-start(bf16[4,160,896]{2,1,0:T(8,128)(2,1)} %dynamic-slice_bitcast_fusion.2), channel_id=1, source_target_pairs={{0,1},{1,0},{2,3},{3,2},{4,5},{5,4},{6,7},{7,6},{8,9},{9,8},{10,11... | collective-permute-start | bytes 3440648 | tf_op jit(solution)/shard_map/ppermute | solution.py:36
  273.0 95.4 %collective-permute-start.42 = (bf16[4,160,896]{2,1,0:T(8,128)(2,1)}, bf16[4,160,896]{2,1,0:T(8,128)(2,1)}, u32[]{:S(2)}, u32[]{:S(2)}) collective-permute-start(bf16[4,160,896]{2,1,0:T(8,128)(2,1)} %dynamic-slice_bitcast_fusion.3), channel_id=1, source_target_pairs={{0,1},{1,0},{2,3},{3,2},{4,5},{5,4},{6,7},{7,6},{8,9},{9,8},{10,11... | collective-permute-start | bytes 3440648 | tf_op jit(solution)/shard_map/ppermute | solution.py:36
  275.9 30.7 %collective-permute-start.24 = (bf16[1,384,896]{2,1,0:T(8,128)(2,1)S(1)}, bf16[1,384,896]{2,1,0:T(8,128)(2,1)S(1)}, u32[]{:S(2)}, u32[]{:S(2)}) collective-permute-start(bf16[1,384,896]{2,1,0:T(8,128)(2,1)S(1)} %dynamic-slice_convert_fusion.1), channel_id=1, source_target_pairs={{0,16},{8,24},{16,0},{24,8},{1,17},{9,25},{17,1},{25,9},{2,18},{10... | collective-permute-start | bytes 2064392 | tf_op jit(solution)/shard_map/ppermute | solution.py:36
  278.0 93.5 %collective-permute-start.38 = (bf16[4,160,896]{2,1,0:T(8,128)(2,1)}, bf16[4,160,896]{2,1,0:T(8,128)(2,1)}, u32[]{:S(2)}, u32[]{:S(2)}) collective-permute-start(bf16[4,160,896]{2,1,0:T(8,128)(2,1)} %dynamic-slice_bitcast_fusion.4), channel_id=1, source_target_pairs={{0,1},{1,0},{2,3},{3,2},{4,5},{5,4},{6,7},{7,6},{8,9},{9,8},{10,11... | collective-permute-start | bytes 3440648 | tf_op jit(solution)/shard_map/ppermute | solution.py:36
  345.5 36.3 %collective-permute-start.47 = (bf16[160,896]{1,0:T(8,128)(2,1)}, bf16[160,896]{1,0:T(8,128)(2,1)}, u32[]{:S(2)}, u32[]{:S(2)}) collective-permute-start(bf16[160,896]{1,0:T(8,128)(2,1)} %get-tuple-element.128), channel_id=1, source_target_pairs={{0,2},{1,3},{2,0},{3,1},{4,6},{5,7},{6,4},{7,5},{8,10},{9,11},{10,... | collective-permute-start | bytes 860168 | tf_op jit(solution)/shard_map/ppermute | solution.py:36
  349.6 35.9 %collective-permute-start.48 = (bf16[160,896]{1,0:T(8,128)(2,1)}, bf16[160,896]{1,0:T(8,128)(2,1)}, u32[]{:S(2)}, u32[]{:S(2)}) collective-permute-start(bf16[160,896]{1,0:T(8,128)(2,1)} %get-tuple-element.130), channel_id=1, source_target_pairs={{0,4},{1,5},{2,6},{3,7},{4,0},{5,1},{6,2},{7,3},{8,12},{9,13},{10,... | collective-permute-start | bytes 860168 | tf_op jit(solution)/shard_map/ppermute | solution.py:36
  380.9 26.4 %collective-permute-start.44 = (bf16[160,896]{1,0:T(8,128)(2,1)S(1)}, bf16[160,896]{1,0:T(8,128)(2,1)S(1)}, u32[]{:S(2)}, u32[]{:S(2)}) collective-permute-start(bf16[160,896]{1,0:T(8,128)(2,1)S(1)} %get-tuple-element.133), channel_id=1, source_target_pairs={{0,4},{1,5},{2,6},{3,7},{4,0},{5,1},{6,2},{7,3},{8,12},{9,13},{10,... | collective-permute-start | bytes 860168 | tf_op jit(solution)/shard_map/ppermute | solution.py:36
  381.8 25.5 %collective-permute-start.45 = (bf16[160,896]{1,0:T(8,128)(2,1)S(1)}, bf16[160,896]{1,0:T(8,128)(2,1)S(1)}, u32[]{:S(2)}, u32[]{:S(2)}) collective-permute-start(bf16[160,896]{1,0:T(8,128)(2,1)S(1)} %get-tuple-element.132), channel_id=1, source_target_pairs={{0,6},{1,7},{2,4},{3,5},{4,2},{5,3},{6,0},{7,1},{8,14},{9,15},{10,... | collective-permute-start | bytes 860168 | tf_op jit(solution)/shard_map/ppermute | solution.py:36
  389.2 25.2 %collective-permute-start.39 = (bf16[160,896]{1,0:T(8,128)(2,1)}, bf16[160,896]{1,0:T(8,128)(2,1)}, u32[]{:S(2)}, u32[]{:S(2)}) collective-permute-start(bf16[160,896]{1,0:T(8,128)(2,1)} %get-tuple-element.134), channel_id=1, source_target_pairs={{0,2},{1,3},{2,0},{3,1},{4,6},{5,7},{6,4},{7,5},{8,10},{9,11},{10,... | collective-permute-start | bytes 860168 | tf_op jit(solution)/shard_map/ppermute | solution.py:36
  413.2 37.6 %collective-permute-start.34 = (bf16[4,272,224]{2,1,0:T(8,128)(2,1)}, bf16[4,272,224]{2,1,0:T(8,128)(2,1)}, u32[]{:S(2)}, u32[]{:S(2)}) collective-permute-start(bf16[4,272,224]{2,1,0:T(8,128)(2,1)} %fusion.36), channel_id=1, source_target_pairs={{0,1},{1,0},{2,3},{3,2},{4,5},{5,4},{6,7},{7,6},{8,9},{9,8},{10,11... | collective-permute-start | bytes 1462280 | tf_op jit(solution)/shard_map/ppermute | solution.py:36
  (87 other events, 871.1 us)
Sparse Core Ops, SparseCore 0:
  42.9 22.9 all-gather.5
  67.4 36.9 all-gather.3

commit v2 on v1

--- a/solution.py
+++ b/solution.py
@@ -36,6 +36,10 @@
     return lax.ppermute(block, axis, [(i, i ^ bits) for i in range(size)])
 
 
+def after(array, *others):
+    return lax.optimization_barrier((array,) + others)[0]
+
+
 def seq_gather(block, size):
     blocks = {0: block}
     bit = size // 2
@@ -45,65 +49,64 @@
     return blocks
 
 
+def fsdp_bits(size):
+    inner = size // OUTER
+    outer_bits, inner_bits = [], []
+    bit = 1
+    while bit < size:
+        (outer_bits if bit >= inner else inner_bits).append(bit)
+        bit *= 2
+    return outer_bits + inner_bits
+
+
+def fsdp_gather_small(block, size):
+    stack, offsets = block[None], [0]
+    for bit in fsdp_bits(size):
+        stack = jnp.concatenate([stack, swap(stack, "fsdp", size, bit)], axis=0)
+        offsets = offsets + [o ^ bit for o in offsets]
+    return stack, offsets
+
+
+def halve(stack, bit, me):
+    above = stack.shape[0] // (2 * bit)
+    cut = stack.reshape((above, 2, bit) + stack.shape[1:])
+    digit = (me // bit) % 2
+    kept = lax.dynamic_index_in_dim(cut, digit, 1, keepdims=False)
+    given = lax.dynamic_index_in_dim(cut, 1 - digit, 1, keepdims=False)
+    merge = lambda part: part.reshape((above * bit,) + stack.shape[1:])
+    return merge(kept), merge(given).astype(BF16)
+
+
+def add(kept, got):
+    return kept.astype(F32) + got.astype(F32)
+
+
 def seq_scatter(stack, size, me):
     bit = 1
     while bit < size:
-        cut = stack.reshape((size // (2 * bit), 2) + stack.shape[1:])
-        digit = (me // bit) % 2
-        given = lax.dynamic_index_in_dim(cut, 1 - digit, 1, keepdims=False)
-        kept = lax.dynamic_index_in_dim(cut, digit, 1, keepdims=False)
-        stack = kept.astype(F32) + swap(given.astype(BF16), "seq", size, bit).astype(F32)
+        kept, given = halve(stack, 1, me // bit)
+        stack = add(kept, swap(given, "seq", size, bit))
         bit *= 2
     return stack[0]
 
 
-def kv_sum(stack, size):
-    parts = [stack[o] for o in range(size)]
-    bit = 1
-    while bit < size:
-        for o in range(0, size, 2 * bit):
-            got = swap(parts[o + bit].astype(BF16), "seq", size, bit)
-            parts[o] = parts[o].astype(F32) + got.astype(F32)
-        bit *= 2
-    return parts[0]
-
-
-def fsdp_gather(block, size):
-    blocks = {0: block}
-    inner = size // OUTER
-    for k in range(1, OUTER):
-        blocks[k * inner] = swap(block, "fsdp", size, k * inner)
-    for m in range(1, inner):
-        for k in range(OUTER):
-            blocks[k * inner + m] = swap(blocks[k * inner], "fsdp", size, m)
-    return blocks
-
-
-def fsdp_gather_small(block, size):
-    inner = size // OUTER
-    column = jnp.stack([block] + [swap(block, "fsdp", size, k * inner) for k in range(1, OUTER)])
-    columns = [column] + [swap(column, "fsdp", size, m) for m in range(1, inner)]
-    return jnp.stack(columns, axis=1).reshape((size,) + block.shape)
+def fsdp_halve(stack, size, bit, me, resolved):
+    place = bit
+    digit = me // bit
+    for taken in resolved:
+        if taken < bit:
+            place //= 2
+    kept, given = halve(stack, place, digit * place)
+    return kept, given
 
 
 def fsdp_scatter(stack, size, me):
-    inner = size // OUTER
-    my_outer, my_inner = me // inner, me % inner
-    cut = stack.reshape((OUTER, inner) + stack.shape[1:])
-
-    def column(index):
-        return lax.dynamic_index_in_dim(cut, index, 1, keepdims=False)
-
-    total = column(my_inner).astype(F32)
-    for m in range(1, inner):
-        got = swap(column(my_inner ^ m).astype(BF16), "fsdp", size, m)
-        total = total + got.astype(F32)
-    low = total.astype(BF16)
-    mine = lax.dynamic_index_in_dim(total, my_outer, 0, keepdims=False)
-    for k in range(1, OUTER):
-        given = lax.dynamic_index_in_dim(low, my_outer ^ k, 0, keepdims=False)
-        mine = mine + swap(given, "fsdp", size, k * inner).astype(F32)
-    return mine
+    resolved = []
+    for bit in reversed(fsdp_bits(size)):
+        kept, given = fsdp_halve(stack, size, bit, me, resolved)
+        stack = add(kept, swap(given, "fsdp", size, bit))
+        resolved.append(bit)
+    return stack[0]
 
 
 def on_device(body, name, out_shapes, scratch, me, arrays):
@@ -168,29 +171,25 @@
     )[0]
 
 
-def join_qkv(me, blocks, rows):
+def join_both(me, blocks, offsets, rows):
     size = len(blocks)
     count, tall, width = blocks[0].shape
+    shapes = [jax.ShapeDtypeStruct((count, rows, size * width), BF16)]
+    if tall > rows:
+        shapes.append(jax.ShapeDtypeStruct((count, tall - rows, width), BF16))
 
     def body(me_ref, *refs):
-        ins, out, vectors, held = refs[:size], refs[size], refs[size + 1], refs[size + 2]
+        ins, out, held = refs[:size], refs[size], refs[-1]
         for o in range(size):
             held[me_ref[0] ^ o] = ins[o][...]
-        for f in range(count):
-            parts = [held[q, f, :rows].astype(F32) for q in range(size)]
+        for j, f in enumerate(offsets):
+            parts = [held[q, j, :rows].astype(F32) for q in range(size)]
             out[me_ref[1] ^ f] = jnp.concatenate(parts, axis=1).astype(BF16)
-            vectors[me_ref[1] ^ f] = ins[0][f, rows:]
+            if tall > rows:
+                refs[size + 1][me_ref[1] ^ f] = ins[0][j, rows:]
 
     return on_device(
-        body,
-        "join_qkv",
-        [
-            jax.ShapeDtypeStruct((count, rows, size * width), BF16),
-            jax.ShapeDtypeStruct((count, tall - rows, width), BF16),
-        ],
-        [pltpu.VMEM((size, count, tall, width), BF16)],
-        me,
-        blocks,
+        body, "join_both", shapes, [pltpu.VMEM((size, count, tall, width), BF16)], me, blocks
     )
 
 
@@ -239,7 +238,7 @@
     )
 
 
-def feed_forward(me, weight_blocks, row_blocks, cot_all):
+def feed_forward(me, weight_blocks, row_blocks, cot_blocks):
     count, size = len(weight_blocks), len(row_blocks)
     rows, width = row_blocks[0].shape
     tall = weight_blocks[0].shape[0] // 3
@@ -247,10 +246,10 @@
     step_units = 256
 
     def body(me_ref, *refs):
-        blocks, xs = refs[:count], refs[count : count + size]
-        g_ref = refs[count + size]
-        hid, gg, gu, gn, part, x_out = refs[count + size + 1 : count + size + 7]
-        gu_w, d_w, x_all, sems = refs[count + size + 7 :]
+        blocks = refs[:count]
+        xs, gs = refs[count : count + size], refs[count + size : count + 2 * size]
+        hid, gg, gu, gn, part, x_out, g_out = refs[count + 2 * size : count + 2 * size + 7]
+        gu_w, d_w, x_all, g_all, sems = refs[count + 2 * size + 7 :]
         step = pl.program_id(0)
 
         @pl.when(step == 0)
@@ -262,6 +261,7 @@
                 copies.append((blocks[o].at[pl.ds(2 * tall, tall)], d_w.at[f]))
             for o in range(size):
                 copies.append((xs[o], x_all.at[me_ref[0] ^ o]))
+                copies.append((gs[o], g_all.at[me_ref[0] ^ o]))
             started = [
                 pltpu.make_async_copy(src, dst, sems.at[i]) for i, (src, dst) in enumerate(copies)
             ]
@@ -271,8 +271,9 @@
                 copy.wait()
 
         x = x_all[step]
-        g = g_ref[...]
+        g = g_all[step]
         x_out[...] = x
+        g_out[...] = g
         gate_w = gu_w[: count // 2].reshape(units, width)
         up_w = gu_w[count // 2 :].reshape(units, width)
         down_w = d_w[...].reshape(units, width)
@@ -296,15 +297,15 @@
         body,
         grid=(size,),
         in_specs=[pl.BlockSpec(memory_space=pltpu.SMEM)]
-        + [hbm] * (count + size)
-        + [by_rows(width)],
-        out_specs=[by_rows(units)] * 3 + [by_rows(width)] * 3,
-        out_shape=[like(units)] * 3 + [like(width)] * 3,
+        + [hbm] * (count + 2 * size),
+        out_specs=[by_rows(units)] * 3 + [by_rows(width)] * 4,
+        out_shape=[like(units)] * 3 + [like(width)] * 4,
         scratch_shapes=[
             pltpu.VMEM((count, 2 * tall, width), BF16),
             pltpu.VMEM((count, tall, width), BF16),
             pltpu.VMEM((size, rows, width), BF16),
-            pltpu.SemaphoreType.DMA((2 * count + size,)),
+            pltpu.VMEM((size, rows, width), BF16),
+            pltpu.SemaphoreType.DMA((2 * count + 2 * size,)),
         ],
         compiler_params=pltpu.CompilerParams(vmem_limit_bytes=VMEM_LIMIT),
         cost_estimate=pl.CostEstimate(
@@ -313,7 +314,7 @@
             transcendentals=size * rows * units,
         ),
         name="feed_forward",
-    )(me, *weight_blocks, *row_blocks, cot_all)
+    )(me, *weight_blocks, *row_blocks, *cot_blocks)
 
 
 def both_heads(pair):
@@ -337,15 +338,35 @@
     return jnp.concatenate([wide[:HEAD, :rows], wide[HEAD:, rows:]], axis=0)
 
 
-def attend_kernel(low_ref, high_ref, place_ref, q_ref, k_ref, vt_ref, o_ref, lse_ref, bias_ref):
-    @pl.when(pl.program_id(0) == 0)
+def pairing(kv_refs, step, begin):
+    both = jnp.concatenate([r[:, begin : begin + PAIR] for r in kv_refs], axis=0).astype(F32)
+    crossed = pltpu.roll(both, HEAD, 1)
+    lane = lax.broadcasted_iota(jnp.int32, both.shape, 1)
+    first = jnp.where(step <= PAIRS // 2, both, crossed)
+    second = jnp.where(step < PAIRS // 2, crossed, both)
+    return jnp.where(lane < HEAD, first, second)
+
+
+def attend_kernel(
+    size, low_ref, high_ref, place_ref, q_ref, *refs,
+):
+    kv_refs = refs[:size]
+    o_ref, lse_ref, bias_ref, k_ref, vt_ref = refs[size:]
+    step = pl.program_id(0)
+
+    @pl.when(step == 0)
     def _():
         fill_bias(low_ref, high_ref, place_ref, bias_ref)
 
+    @pl.when((step == 0) | (step == PAIRS // 2) | (step == PAIRS // 2 + 1))
+    def _():
+        k_ref[...] = pairing(kv_refs, step, 0).astype(BF16)
+        vt_ref[...] = pairing(kv_refs, step, PAIR).T.astype(BF16)
+
     rows = q_ref.shape[0]
     queries = both_heads(q_ref[...])
-    keys = k_ref[0]
-    values_t = vt_ref[0]
+    keys = k_ref[...]
+    values_t = vt_ref[...]
     outs, totals = [], []
     for begin in range(0, 2 * rows, 256):
         scores = dot(keys, queries[begin : begin + 256], 1, 1) + bias_ref[:, begin : begin + 256]
@@ -360,26 +381,32 @@
 
 
 def attend_back_kernel(
-    low_ref, high_ref, place_ref, q_ref, g_ref, o_ref, lse_ref, k_ref, kt_ref, v_ref,
-    dq_ref, dk_ref, dv_ref, bias_ref,
+    size, low_ref, high_ref, place_ref, q_ref, g_ref, o_ref, lse_ref, *refs,
 ):
+    kv_refs = refs[:size]
+    dq_ref, dkv_ref, bias_ref, k_ref, kt_ref, v_ref, dk_ref, dv_ref = refs[size:]
     step = pl.program_id(0)
 
     @pl.when(step == 0)
     def _():
         fill_bias(low_ref, high_ref, place_ref, bias_ref)
+        dkv_ref[...] = jnp.zeros_like(dkv_ref)
 
     @pl.when((step == 0) | (step == PAIRS // 2) | (step == PAIRS // 2 + 1))
     def _():
+        keys_now = pairing(kv_refs, step, 0)
+        k_ref[...] = keys_now.astype(BF16)
+        kt_ref[...] = keys_now.T.astype(BF16)
+        v_ref[...] = pairing(kv_refs, step, PAIR).astype(BF16)
         dk_ref[...] = jnp.zeros_like(dk_ref)
         dv_ref[...] = jnp.zeros_like(dv_ref)
 
     rows = q_ref.shape[0]
     queries = both_heads(q_ref[...])
     grads = both_heads(g_ref[...])
-    keys = k_ref[0]
-    keys_t = kt_ref[0]
-    values = v_ref[0]
+    keys = k_ref[...]
+    keys_t = kt_ref[...]
+    values = v_ref[...]
     product = (g_ref[...].astype(F32) * o_ref[...].astype(F32)).T
     delta = jnp.concatenate(
         [
@@ -397,96 +424,95 @@
         grad_probs = dot(values, grads[part], 1, 1)
         grad_scores = (probs * (grad_probs - delta[:, part])).astype(BF16)
         outs.append(dot(keys_t, grad_scores, 1, 0))
-        dk_ref[0] += dot(grad_scores, queries[part], 1, 0)
-        dv_ref[0] += dot(probs.astype(BF16), grads[part], 1, 0)
+        dk_ref[...] += dot(grad_scores, queries[part], 1, 0)
+        dv_ref[...] += dot(probs.astype(BF16), grads[part], 1, 0)
     wide = jnp.concatenate(outs, axis=1)
     dq_ref[...] = own_rows(wide, rows).T * 0.125
 
-
-def variant(step):
-    half = PAIRS // 2
-    return jnp.where(step < half, 0, jnp.where(step == half, 1, 2))
-
-
-def attend(low, high, place, queries, pair_keys, pair_values_t):
-    rows, count = queries.shape[0], pair_keys.shape[1]
-    whole = lambda shape: pl.BlockSpec(shape, lambda i: (0,) * len(shape))
+    def fold(own_lanes):
+        for at, sums in ((0, dk_ref), (PAIR, dv_ref)):
+            sums_now = sums[...]
+            lane = lax.broadcasted_iota(jnp.int32, sums_now.shape, 1)
+            both = sums_now + pltpu.roll(sums_now, HEAD, 1)
+            kept = jnp.where((lane < HEAD) == own_lanes, both, 0.0)
+            dkv_ref[:, at : at + PAIR] += kept
+
+    @pl.when(step == PAIRS // 2 - 1)
+    def _():
+        fold(True)
+
+    @pl.when(step == PAIRS // 2)
+    def _():
+        dkv_ref[:, :PAIR] += dk_ref[...]
+        dkv_ref[:, PAIR:] += dv_ref[...]
+
+    @pl.when(step == PAIRS - 1)
+    def _():
+        fold(False)
+
+
+def whole(shape):
+    return pl.BlockSpec(shape, lambda i: (0,) * len(shape))
+
+
+def attend(low, high, place, queries, kv_blocks):
+    rows, count, size = queries.shape[0], place.shape[0], len(kv_blocks)
     pair = pl.BlockSpec((rows, PAIR), lambda i: (0, i))
     return pl.pallas_call(
-        attend_kernel,
+        functools.partial(attend_kernel, size),
         grid=(PAIRS,),
-        in_specs=[
-            whole((1, rows)),
-            whole((1, rows)),
-            whole((count, 1)),
-            pair,
-            pl.BlockSpec((1, count, PAIR), lambda i: (variant(i), 0, 0)),
-            pl.BlockSpec((1, PAIR, count), lambda i: (variant(i), 0, 0)),
-        ],
+        in_specs=[whole((1, rows)), whole((1, rows)), whole((count, 1)), pair]
+        + [whole((rows, 2 * KVW))] * size,
         out_specs=[pair, pl.BlockSpec((1, 1, 2 * rows), lambda i: (i, 0, 0))],
         out_shape=[
             jax.ShapeDtypeStruct((rows, QW), BF16),
             jax.ShapeDtypeStruct((PAIRS, 1, 2 * rows), F32),
         ],
-        scratch_shapes=[pltpu.VMEM((count, 2 * rows), F32)],
+        scratch_shapes=[
+            pltpu.VMEM((count, 2 * rows), F32),
+            pltpu.VMEM((count, PAIR), BF16),
+            pltpu.VMEM((PAIR, count), BF16),
+        ],
         compiler_params=pltpu.CompilerParams(vmem_limit_bytes=VMEM_LIMIT),
         cost_estimate=pl.CostEstimate(
-            flops=4 * HEADS * rows * count * PAIR,
+            flops=8 * HEADS * rows * count * PAIR,
             bytes_accessed=4 * rows * QW + 1024 * count,
             transcendentals=HEADS * rows * count,
         ),
         name="attend",
-    )(low, high, place, queries, pair_keys, pair_values_t)
-
-
-def attend_back(low, high, place, queries, grads, outs, lse, pair_keys, pair_keys_t, pair_values):
-    rows, count = queries.shape[0], pair_keys.shape[1]
-    whole = lambda shape: pl.BlockSpec(shape, lambda i: (0,) * len(shape))
+    )(low, high, place, queries, *kv_blocks)
+
+
+def attend_back(low, high, place, queries, grads, outs, lse, kv_blocks):
+    rows, count, size = queries.shape[0], place.shape[0], len(kv_blocks)
     pair = pl.BlockSpec((rows, PAIR), lambda i: (0, i))
-    tall = pl.BlockSpec((1, count, PAIR), lambda i: (variant(i), 0, 0))
     return pl.pallas_call(
-        attend_back_kernel,
+        functools.partial(attend_back_kernel, size),
         grid=(PAIRS,),
-        in_specs=[
-            whole((1, rows)),
-            whole((1, rows)),
-            whole((count, 1)),
-            pair,
-            pair,
-            pair,
-            pl.BlockSpec((1, 1, 2 * rows), lambda i: (i, 0, 0)),
-            tall,
-            pl.BlockSpec((1, PAIR, count), lambda i: (variant(i), 0, 0)),
-            tall,
-        ],
-        out_specs=[pair, tall, tall],
+        in_specs=[whole((1, rows)), whole((1, rows)), whole((count, 1)), pair, pair, pair]
+        + [pl.BlockSpec((1, 1, 2 * rows), lambda i: (i, 0, 0))]
+        + [whole((rows, 2 * KVW))] * size,
+        out_specs=[pair, whole((count, 2 * KVW))],
         out_shape=[
             jax.ShapeDtypeStruct((rows, QW), F32),
-            jax.ShapeDtypeStruct((3, count, PAIR), F32),
-            jax.ShapeDtypeStruct((3, count, PAIR), F32),
+            jax.ShapeDtypeStruct((count, 2 * KVW), F32),
         ],
-        scratch_shapes=[pltpu.VMEM((count, 2 * rows), F32)],
+        scratch_shapes=[
+            pltpu.VMEM((count, 2 * rows), F32),
+            pltpu.VMEM((count, PAIR), BF16),
+            pltpu.VMEM((PAIR, count), BF16),
+            pltpu.VMEM((count, PAIR), BF16),
+            pltpu.VMEM((count, PAIR), F32),
+            pltpu.VMEM((count, PAIR), F32),
+        ],
         compiler_params=pltpu.CompilerParams(vmem_limit_bytes=VMEM_LIMIT),
         cost_estimate=pl.CostEstimate(
-            flops=10 * HEADS * rows * count * PAIR,
+            flops=16 * HEADS * rows * count * PAIR,
             bytes_accessed=8 * rows * QW + 4096 * count,
             transcendentals=HEADS * rows * count,
         ),
         name="attend_back",
-    )(low, high, place, queries, grads, outs, lse, pair_keys, pair_keys_t, pair_values)
-
-
-def pair_up(heads):
-    one, two = heads[:, :HEAD], heads[:, HEAD:]
-    return jnp.stack(
-        [jnp.concatenate([one, one], 1), heads, jnp.concatenate([two, two], 1)]
-    )
-
-
-def unpair(sums):
-    one = sums[0, :, :HEAD] + sums[0, :, HEAD:] + sums[1, :, :HEAD]
-    two = sums[2, :, :HEAD] + sums[2, :, HEAD:] + sums[1, :, HEAD:]
-    return jnp.concatenate([one, two], axis=1)
+    )(low, high, place, queries, grads, outs, lse, *kv_blocks)
 
 
 def rms_scale(values_in):
@@ -539,11 +565,6 @@
 
 def pad_row(vector, width):
     return jnp.pad(vector, (0, width - vector.shape[0]))[None, :]
-
-
-def lanes_from_stack(stack):
-    count, rows, width = stack.shape
-    return jnp.transpose(stack, (1, 0, 2)).reshape(rows, count * width)
 
 
 def stack_from_lanes(array, count):
@@ -564,11 +585,6 @@
     strip = down_weight.shape[0] // seq_size
     tall = padded(strip)
 
-    ff_cut = cut_ff(me, gate_up_weight, down_weight, seq_size)
-    ff_share = [ff_cut[0]] + [swap(ff_cut[o], "seq", seq_size, o) for o in offsets if o]
-    ff_blocks = fsdp_gather(join_lanes(me, ff_share), fsdp_size)
-    ff_blocks = [ff_blocks[o] for o in range(fsdp_size)]
-
     qkv_tall = padded(qkv_rows)
     packed = jnp.concatenate(
         [
@@ -580,16 +596,30 @@
         ],
         axis=0,
     )
-    packed_blocks = seq_gather(fsdp_gather_small(packed, fsdp_size), seq_size)
-    qkv_t, vectors = join_qkv(me, [packed_blocks[o] for o in offsets], qkv_tall)
+    packed_stack, fsdp_order = fsdp_gather_small(packed, fsdp_size)
+    packed_blocks = seq_gather(packed_stack, seq_size)
+
+    ff_cut = cut_ff(me, gate_up_weight, down_weight, seq_size)
+    ff_share = [ff_cut[0]] + [swap(ff_cut[o], "seq", seq_size, o) for o in offsets if o]
+    ff_block = join_lanes(me, ff_share)
+    ff_blocks = {0: ff_block}
+    for bit in fsdp_bits(fsdp_size):
+        ff_blocks.update({o ^ bit: swap(b, "fsdp", fsdp_size, bit) for o, b in ff_blocks.items()})
+    inner = fsdp_size // OUTER
+
+    qkv_blocks = [packed_blocks[o] for o in offsets]
+    qkv_blocks[0] = after(qkv_blocks[0], ff_block)
+    qkv_t, vectors = join_both(me, qkv_blocks, fsdp_order, qkv_tall)
     qkv_t = qkv_t[:, :qkv_rows].reshape(fsdp_size * qkv_rows, -1)
     gain_one = vectors[:, 0, : norm_one.shape[0]].reshape(-1).astype(F32)
     bias_full = vectors[:, 1, : qkv_bias.shape[0]].reshape(-1).astype(F32)
     gain_two = vectors[:, 2, : norm_two.shape[0]].reshape(-1).astype(F32)
 
-    out_part = lax.all_gather(out_weight, "fsdp", axis=0, tiled=True)
-    out_full = lanes_from_stack(lax.all_gather(out_part, "seq", axis=0, tiled=False))
-    cot_all = lax.all_gather(cotangent, "seq", axis=0, tiled=True)
+    cot_blocks = seq_gather(after(cotangent, packed_blocks[seq_size // 2]), seq_size)
+    out_stack, out_order = fsdp_gather_small(after(out_weight, ff_block), fsdp_size)
+    out_blocks = seq_gather(out_stack, seq_size)
+    out_full = join_both(me, [out_blocks[o] for o in offsets], out_order, out_weight.shape[0])[0]
+    out_full = out_full.reshape(QW, -1)
 
     inputs = tokens.astype(F32)
     scale_one = rms_scale(inputs)
@@ -600,35 +630,67 @@
     queries = turned[:, :QW] * jnp.asarray(0.125, BF16)
     kv_local = jnp.concatenate([turned[:, QW:], joined[:, QW + KVW :].astype(BF16)], axis=1)
     kv_blocks = seq_gather(kv_local, seq_size)
-    kv_all = jnp.concatenate([kv_blocks[o] for o in offsets], axis=0)
+    kv_blocks = [kv_blocks[o] for o in offsets]
     row_place = jnp.arange(row_count, dtype=jnp.int32)
     high = my_seq * row_count + row_place
     low = high - positions
     place = jnp.concatenate([(my_seq ^ o) * row_count + row_place for o in offsets])[:, None]
     low, high = low[None, :], high[None, :]
-    pair_keys = pair_up(kv_all[:, :KVW])
-    pair_values = pair_up(kv_all[:, KVW:])
-    pair_keys_t = jnp.transpose(pair_keys, (0, 2, 1))
-    pair_values_t = jnp.transpose(pair_values, (0, 2, 1))
-    attn_flat, lse = attend(low, high, place, queries, pair_keys, pair_values_t)
+    queries_now = after(queries, ff_blocks[inner], ff_blocks[2 * inner])
+    attn_flat, lse = attend(low, high, place, queries_now, kv_blocks)
 
     residual = inputs + dot(attn_flat, out_full, 1, 0)
     scale_two = rms_scale(residual)
     normed_two = (residual * scale_two * gain_two).astype(BF16)
     normed_blocks = seq_gather(normed_two, seq_size)
-    hidden, grad_gate, grad_up, grad_normed, layer_part, normed_all = feed_forward(
-        me, ff_blocks, [normed_blocks[o] for o in offsets], cot_all
+    hidden, grad_gate, grad_up, grad_normed, layer_part, normed_all, cot_all = feed_forward(
+        me,
+        [ff_blocks[o] for o in range(fsdp_size)],
+        [normed_blocks[o] for o in offsets],
+        [cot_blocks[o] for o in offsets],
     )
     by_seq = lambda rows: rows.reshape(seq_size, row_count, -1)
-    grad_normed_two = seq_scatter(by_seq(grad_normed), seq_size, my_seq)
+
+    kept, given = halve(by_seq(grad_normed), 1, my_seq)
+    normed_sum = add(kept, swap(given, "seq", seq_size, 1))
+    bit = 2
+    while bit < seq_size:
+        kept, given = halve(normed_sum, 1, my_seq // bit)
+        normed_sum = add(kept, swap(given, "seq", seq_size, bit))
+        bit *= 2
+    grad_normed_two = normed_sum[0]
     down_term = dot(hidden, cot_all, 0, 0).astype(BF16).reshape(fsdp_size, tall, -1)
+    grad_gate, grad_up = after(grad_gate, given), after(grad_up, given)
     gate_term = dot(grad_gate, normed_all, 0, 0).astype(BF16).reshape(fsdp_size // 2, 2, tall, -1)
     up_term = dot(grad_up, normed_all, 0, 0).astype(BF16).reshape(fsdp_size // 2, 2, tall, -1)
+
     chunks = [down_term] + [
         jnp.concatenate([gate_term[:, i], up_term[:, i]], axis=0) for i in range(2)
     ]
-    down_sum, one_sum, two_sum = [fsdp_scatter(c, fsdp_size, my_fsdp) for c in chunks]
-    layer_out = residual + seq_scatter(by_seq(layer_part), seq_size, my_seq)
+    bits = list(reversed(fsdp_bits(fsdp_size)))
+    steps = []
+    for chunk in chunks:
+        kept, given = fsdp_halve(chunk, fsdp_size, bits[0], my_fsdp, [])
+        if steps:
+            given = after(given, steps[-1][0])
+        got = [swap(given, "fsdp", fsdp_size, bits[0])]
+        stack = add(kept, got[0])
+        for at in range(1, len(bits)):
+            kept, given = fsdp_halve(stack, fsdp_size, bits[at], my_fsdp, bits[:at])
+            got.append(swap(given, "fsdp", fsdp_size, bits[at]))
+            stack = add(kept, got[-1])
+        steps.append(got + [stack[0]])
+    down_sum, one_sum, two_sum = [s[-1] for s in steps]
+
+    kept, given = halve(by_seq(layer_part), 1, my_seq)
+    layer_sum = add(kept, swap(given, "seq", seq_size, 1))
+    bit = 2
+    while bit < seq_size:
+        kept, given = halve(layer_sum, 1, my_seq // bit)
+        given = after(given, grad_normed_two)
+        layer_sum = add(kept, swap(given, "seq", seq_size, bit))
+        bit *= 2
+    layer_out = residual + layer_sum[0]
 
     ff_back = cut_lanes(me, (one_sum, two_sum, down_sum), seq_size)
     ff_got = [ff_back[0]] + [swap(ff_back[o], "seq", seq_size, o) for o in offsets if o]
@@ -640,11 +702,18 @@
     grad_attn = dot(grad_branch, out_full, 1, 1).astype(BF16)
     out_term = stack_from_lanes(dot(attn_flat, grad_branch, 0, 0).astype(BF16), seq_size)
     out_mine = seq_scatter(out_term, seq_size, my_seq).reshape(fsdp_size, -1, width)
-    grad_queries, key_sums, value_sums = attend_back(
-        low, high, place, queries, grad_attn, attn_flat, lse, pair_keys, pair_keys_t, pair_values
-    )
-    kv_terms = jnp.concatenate([unpair(key_sums), unpair(value_sums)], axis=1)
-    kv_mine = kv_sum(by_seq(kv_terms), seq_size)
+    grad_attn = after(grad_attn, steps[0][0], gate_term, up_term)
+    grad_queries, kv_terms = attend_back(
+        low, high, place, queries, grad_attn, attn_flat, lse, kv_blocks
+    )
+    kv_terms = after(kv_terms, steps[1][0], steps[0][1])
+    kv_sum = by_seq(kv_terms)
+    bit = 1
+    while bit < seq_size:
+        cut = kv_sum.reshape((-1, 2) + kv_sum.shape[1:])
+        kv_sum = add(cut[:, 0], swap(cut[:, 1].astype(BF16), "seq", seq_size, bit))
+        bit *= 2
+    kv_mine = kv_sum[0]
     turned_back = rotate_back(
         jnp.concatenate([grad_queries, kv_mine[:, :KVW]], axis=1), cosine, sine
     )
@@ -666,7 +735,7 @@
     tail = jnp.concatenate(
         [qkv_term, jnp.broadcast_to(small[None], (seq_size,) + small.shape)], axis=2
     )
-    tail_mine = seq_scatter(tail, seq_size, my_seq)
+    tail_mine = seq_scatter(after(tail, steps[2][0], steps[1][1]), seq_size, my_seq)
     tail_sum = fsdp_scatter(
         jnp.concatenate([tail_mine, out_mine], axis=1), fsdp_size, my_fsdp
     )

time: 491 us -> 460 us (0.937)
  blocking collectives: 35.5 us -> 0 us
  between operations: 15.7 us -> 2.13 us
  local copies, waits for them, and re-layouts: 47.9 us -> 57.5 us
  starting transfers between devices: 60.5 us -> 67.4 us
  other arithmetic: 39.9 us -> 34.3 us
    all_gather x1 -> x0, blocking collectives: 35.5 us -> none  [per_device(): out_part = lax.all_gather(out_weight, 'fsdp', axis=0, tiled=True)]
    convert_element_type x6 -> x1, other arithmetic: 10.8 us -> 0.07 us  [halve(): return (merge(kept), merge(given).astype(BF16))]
    reshape x0 -> x7, local copies, waits for them, and re-layouts: none -> 8.64 us  [halve(): merge = lambda part: part.reshape((above * bit,) + stack.shape[1:])]
    ppermute x53 -> x56, starting transfers between devices: 60.4 us -> 67.4 us  [swap(): return lax.ppermute(block, axis, [(i, i ^ bits) for i in range(size)])]
    concatenate x2, local copies, waits for them, and re-layouts: 5.93 us -> 12.6 us  [widen(): return jnp.concatenate([table] * (width // PAIR), axis=1)]
    squeeze x10 -> x0, local copies, waits for them, and re-layouts: 6.56 us -> none  [the longest x3 3.43 us: column(): return lax.dynamic_index_in_dim(cut, index, 1, keepdims=False)]
    unnamed x115 -> x97, local copies, waits for them, and re-layouts: 11 us -> 17.5 us
    convert_element_type x4 -> x14, local copies, waits for them, and re-layouts: 1.12 us -> 7.03 us  [the longest x12 5.82 us: halve(): return (merge(kept), merge(given).astype(BF16))]
  transfers between devices with their start and end apart: 55 -> 56, of which waited for: 19 -> 22; matrix products, arithmetic and copies ran while one was open for 20% -> 21% of each run, Pallas kernels for 12% -> 14%
where the time goes in v2:
time: 460 us; the launch traced here: 452 us
  waiting for transfers between devices  168 us (37%)
  Pallas kernels  94 us (20%)
  starting transfers between devices  67.4 us (15%)
  local copies, waits for them, and re-layouts  57.5 us (12%)
  other arithmetic  34.3 us (7%)
  matrix products  28.8 us (6%)
    ppermute x56, waiting for transfers between devices, swap(): return lax.ppermute(block, axis, [(i, i ^ bits) for i in range(size)])  168 us
    ppermute x56, starting transfers between devices, swap(): return lax.ppermute(block, axis, [(i, i ^ bits) for i in range(size)])  67.4 us
    pallas_call x1, Pallas kernels, feed_forward(): pl.pallas_call(body, grid=(size,), in_specs=[pl.BlockSpec(memory_space=pl...  31.9 us
    dot_general x9, matrix products, dot(): lax.dot_general(left, right, (((left_dim,), (right_dim,)), ((), ())), pre...  28.8 us
    pallas_call x1, Pallas kernels, attend_back(): pl.pallas_call(functools.partial(attend_back_kernel, size), grid=(PAIRS,)...  28.2 us
    pallas_call x1, Pallas kernels, attend(): pl.pallas_call(functools.partial(attend_kernel, size), grid=(PAIRS,), in_...  23.4 us
    unnamed x97, local copies, waits for them, and re-layouts  17.5 us
    add x15, other arithmetic, add(): return kept.astype(F32) + got.astype(F32)  13.8 us
  transfers between devices with their start and end apart: 56, of which 22 were waited for; matrix products, arithmetic and copies ran while one was open for 21% of the time, Pallas kernels for 14%

profile of v2, /device:TPU:0, one launch (start us, length us, event | category | flops | bytes accessed | tf_op | source)
XLA Modules:
  0.0 452.0 jit_solution(5614412017825674351)
XLA Ops:
  16.9 7.4 %collective-permute-done.1 = bf16[2,160,224]{2,1,0:T(8,128)(2,1)S(1)} collective-permute-done((bf16[2,160,224]{2,1,0:T(8,128)(2,1)S(1)}, bf16[2,160,224]{2,1,0:T(8,128)(2,1)S(1)}, u32[]{:S(2)}, u32[]{:S(2)}) %collective-permute-start.1) | collective-permute-done | bytes 143392 | tf_op jit(solution)/shard_map/ppermute | solution.py:36
  28.5 4.5 collective-permute-done.2
  34.9 8.0 %collective-permute-done.15 = bf16[2,112,224]{2,1,0:T(8,128)(2,1)S(1)} collective-permute-done((bf16[2,112,224]{2,1,0:T(8,128)(2,1)S(1)}, bf16[2,112,224]{2,1,0:T(8,128)(2,1)S(1)}, u32[]{:S(2)}, u32[]{:S(2)}) %collective-permute-start.15) | collective-permute-done | bytes 100384 | tf_op jit(solution)/shard_map/ppermute | solution.py:36
  49.6 9.7 %concatenate.92 = f32[384,1024]{1,0:T(8,128)} concatenate(f32[384,32]{1,0:T(8,128)} %get-tuple-element.54, f32[384,32]{1,0:T(8,128)} %get-tuple-element.54, f32[384,32]{1,0:T(8,128)} %get-tuple-element.54, f32[384,32]{1,0:T(8,128)} %get-tuple-element.54, f32[384,32]{1,0:T(8,128)} %get-tuple-element.54, f32[384,32]{1,0:T(8,128)} %get-tuple-element.54, ...), dimensions={1} | concatenate | bytes 3145728 | tf_op jit(solution)/shard_map/concatenate | solution.py:531
  81.7 22.8 %collective-permute-done.9.refs_2_ = bf16[480,896]{1,0:T(8,128)(2,1)} collective-permute-done((bf16[480,896]{1,0:T(8,128)(2,1)}, bf16[480,896]{1,0:T(8,128)(2,1)}, u32[]{:S(2)}, u32[]{:S(2)}) %collective-permute-start.9) | collective-permute-done | bytes 860192 | tf_op jit(solution)/shard_map/ppermute | solution.py:36
  111.1 18.0 %collective-permute-start.29 = (bf16[384,896]{1,0:T(8,128)(2,1)}, bf16[384,896]{1,0:T(8,128)(2,1)}, u32[]{:S(2)}, u32[]{:S(2)}) collective-permute-start(bf16[384,896]{1,0:T(8,128)(2,1)} %refs_12_), channel_id=1, source_target_pairs={{0,16},{8,24},{16,0},{24,8},{1,17},{9,25},{17,1},{25,9},{2,18},{10... | collective-permute-start | bytes 2064392 | tf_op jit(solution)/shard_map/ppermute | solution.py:36
  132.8 23.4 %attend.1 = (bf16[384,896]{1,0:T(8,128)(2,1)S(1)}, f32[7,1,768]{2,1,0:T(1,128)S(1)}) custom-call(s32[1,384]{1,0:T(1,128)S(1)} %broadcast_in_dim.18.low_ref, s32[1,384]{1,0:T(1,128)S(1)} %iota_add_fusion.4.high_ref, s32[1536,1]{1,0:T(8,128)S(1)} %broadcast_in_dim.51.place_ref, bf16[384,896]{1,0:T(8,128)(2,1)S(1)} %copy-done, ...), custom_call_target="tpu_custom_call" | custom-call | flops 8455716864 | bytes 2949120 | tf_op jit(solution)/shard_map/attend/pallas_call | solution.py:461
  163.3 15.5 %collective-permute-done.26.refs_10_ = bf16[384,896]{1,0:T(8,128)(2,1)} collective-permute-done((bf16[384,896]{1,0:T(8,128)(2,1)}, bf16[384,896]{1,0:T(8,128)(2,1)}, u32[]{:S(2)}, u32[]{:S(2)}) %collective-permute-start.26) | collective-permute-done | bytes 688160 | tf_op jit(solution)/shard_map/ppermute | solution.py:36
  178.8 4.1 collective-permute-done.22.refs_5_
  183.0 18.0 %collective-permute-done.24.refs_7_ = bf16[480,896]{1,0:T(8,128)(2,1)} collective-permute-done((bf16[480,896]{1,0:T(8,128)(2,1)}, bf16[480,896]{1,0:T(8,128)(2,1)}, u32[]{:S(2)}, u32[]{:S(2)}) %collective-permute-start.24) | collective-permute-done | bytes 860192 | tf_op jit(solution)/shard_map/ppermute | solution.py:36
  202.1 31.9 %feed_forward.1 = (bf16[1536,1280]{1,0:T(8,128)(2,1)}, bf16[1536,1280]{1,0:T(8,128)(2,1)}, bf16[1536,1280]{1,0:T(8,128)(2,1)}, bf16[1536,896]{1,0:T(8,128)(2,1)}...) custom-call(s32[2]{0:T(128)S(1)} %pad_add_fusion.1.me_ref, ...), custom_call_target="tpu_custom_call" | custom-call | flops 21139292160 | bytes 32440320 | tf_op jit(solution)/shard_map/feed_forward/pallas_call | solution.py:296
  234.1 7.3 %convolution_convert_fusion.3 = bf16[1280,896]{1,0:T(8,128)(2,1)S(1)} fusion(bf16[1536,1280]{1,0:T(8,128)(2,1)} %get-tuple-element.63, bf16[1536,896]{1,0:T(8,128)(2,1)} %get-tuple-element.64), kind=kOutput, calls=%fused_computation.3 | convolution fusion | flops 3524362240 | bytes 8978432 | tf_op jit(solution)/shard_map/dot_general | solution.py:30
  249.1 21.9 %collective-permute-done.35 = bf16[4,160,896]{2,1,0:T(8,128)(2,1)} collective-permute-done((bf16[4,160,896]{2,1,0:T(8,128)(2,1)}, bf16[4,160,896]{2,1,0:T(8,128)(2,1)}, u32[]{:S(2)}, u32[]{:S(2)}) %collective-permute-start.35) | collective-permute-done | bytes 1146912 | tf_op jit(solution)/shard_map/ppermute | solution.py:36
  276.4 4.5 convolution_convert_fusion.1
  280.9 4.7 %convolution_convert_fusion.2 = bf16[1280,896]{1,0:T(8,128)(2,1)S(1)} fusion(bf16[1536,1280]{1,0:T(8,128)(2,1)S(1)} %copy-done.44, bf16[1536,896]{1,0:T(8,128)(2,1)S(1)} %copy-done.46), kind=kOutput, calls=%fused_computation.2 | convolution fusion | flops 3524362240 | bytes 8978432 | tf_op jit(solution)/shard_map/dot_general | solution.py:30
  302.1 11.5 %collective-permute-done.36 = bf16[4,160,896]{2,1,0:T(8,128)(2,1)} collective-permute-done((bf16[4,160,896]{2,1,0:T(8,128)(2,1)}, bf16[4,160,896]{2,1,0:T(8,128)(2,1)}, u32[]{:S(2)}, u32[]{:S(2)}) %collective-permute-start.36) | collective-permute-done | bytes 1146912 | tf_op jit(solution)/shard_map/ppermute | solution.py:36
  314.1 4.0 subtract_add_fusion
  319.8 28.2 %attend_back.1 = (f32[384,896]{1,0:T(8,128)}, f32[1536,256]{1,0:T(8,128)}) custom-call(s32[1,384]{1,0:T(1,128)S(1)} %broadcast_in_dim.18.low_ref, s32[1,384]{1,0:T(1,128)S(1)} %iota_add_fusion.4.high_ref, s32[1536,1]{1,0:T(8,128)S(1)} %broadcast_in_dim.51.place_ref, bf16[384,896]{1,0:T(8,128)(2,1)S(1)} %copy-done.1, ...), custom_call_target="tpu_custom_call" | custom-call | flops 16911433728 | bytes 9043968 | tf_op jit(solution)/shard_map/attend_back/pallas_call | solution.py:489
  357.0 3.9 collective-permute-done.39
  373.3 7.5 %collective-permute-done.41 = bf16[2,160,896]{2,1,0:T(8,128)(2,1)} collective-permute-done((bf16[2,160,896]{2,1,0:T(8,128)(2,1)}, bf16[2,160,896]{2,1,0:T(8,128)(2,1)}, u32[]{:S(2)}, u32[]{:S(2)}) %collective-permute-start.41) | collective-permute-done | bytes 573472 | tf_op jit(solution)/shard_map/ppermute | solution.py:36
  400.6 10.8 %collective-permute-done.43 = bf16[1,8,160,224]{3,2,1,0:T(8,128)(2,1)} collective-permute-done((bf16[1,8,160,224]{3,2,1,0:T(8,128)(2,1)}, bf16[1,8,160,224]{3,2,1,0:T(8,128)(2,1)}, u32[]{:S(2)}, u32[]{:S(2)}) %collective-permute-start.43) | collective-permute-done | bytes 573472 | tf_op jit(solution)/shard_map/ppermute | solution.py:36
  415.7 4.8 %collective-permute-done.50 = bf16[2,160,896]{2,1,0:T(8,128)(2,1)} collective-permute-done((bf16[2,160,896]{2,1,0:T(8,128)(2,1)}, bf16[2,160,896]{2,1,0:T(8,128)(2,1)}, u32[]{:S(2)}, u32[]{:S(2)}) %collective-permute-start.50) | collective-permute-done | bytes 573472 | tf_op jit(solution)/shard_map/ppermute | solution.py:36
  421.9 5.0 %collective-permute-done.46 = bf16[4,272,224]{2,1,0:T(8,128)(2,1)S(1)} collective-permute-done((bf16[4,272,224]{2,1,0:T(8,128)(2,1)S(1)}, bf16[4,272,224]{2,1,0:T(8,128)(2,1)S(1)}, u32[]{:S(2)}, u32[]{:S(2)}) %collective-permute-start.46) | collective-permute-done | bytes 487456 | tf_op jit(solution)/shard_map/ppermute | solution.py:36
  434.3 6.5 %collective-permute-done.47 = bf16[2,272,224]{2,1,0:T(8,128)(2,1)S(1)} collective-permute-done((bf16[2,272,224]{2,1,0:T(8,128)(2,1)S(1)}, bf16[2,272,224]{2,1,0:T(8,128)(2,1)S(1)}, u32[]{:S(2)}, u32[]{:S(2)}) %collective-permute-start.47) | collective-permute-done | bytes 243744 | tf_op jit(solution)/shard_map/ppermute | solution.py:36
  (322 shorter events, 165.9 us)
Async XLA Ops:
  45.9 24.0 %collective-permute-start.6 = (bf16[8,160,224]{2,1,0:T(8,128)(2,1)S(1)}, bf16[8,160,224]{2,1,0:T(8,128)(2,1)S(1)}, u32[]{:S(2)}, u32[]{:S(2)}) collective-permute-start(bf16[8,160,224]{2,1,0:T(8,128)(2,1)S(1)} %pad_maximum_fusion.5.refs_0_), channel_id=1, source_target_pairs={{0,8},{8,0},{16,24},{24,16},{1,9},{9,1},{17,25},{25,17},{2,10},{10... | collective-permute-start | bytes 1720328 | tf_op jit(solution)/shard_map/ppermute | solution.py:36
  47.8 22.6 %collective-permute-start.8 = (bf16[8,160,224]{2,1,0:T(8,128)(2,1)S(1)}, bf16[8,160,224]{2,1,0:T(8,128)(2,1)S(1)}, u32[]{:S(2)}, u32[]{:S(2)}) collective-permute-start(bf16[8,160,224]{2,1,0:T(8,128)(2,1)S(1)} %collective-permute-done.7.refs_2_), channel_id=1, source_target_pairs={{0,8},{8,0},{16,24},{24,16},{1,9},{9,1},{17,25},{25,17},{2,10},{10... | collective-permute-start | bytes 1720328 | tf_op jit(solution)/shard_map/ppermute | solution.py:36
  63.6 40.9 %collective-permute-start.9 = (bf16[480,896]{1,0:T(8,128)(2,1)}, bf16[480,896]{1,0:T(8,128)(2,1)}, u32[]{:S(2)}, u32[]{:S(2)}) collective-permute-start(bf16[480,896]{1,0:T(8,128)(2,1)} %join_lanes.1.refs_0_), channel_id=1, source_target_pairs={{0,2},{1,3},{2,0},{3,1},{4,6},{5,7},{6,4},{7,5},{8,10},{9,11},{10,... | collective-permute-start | bytes 2580488 | tf_op jit(solution)/shard_map/ppermute | solution.py:36
  66.5 42.4 %collective-permute-start.10 = (bf16[480,896]{1,0:T(8,128)(2,1)}, bf16[480,896]{1,0:T(8,128)(2,1)}, u32[]{:S(2)}, u32[]{:S(2)}) collective-permute-start(bf16[480,896]{1,0:T(8,128)(2,1)} %join_lanes.1.refs_0_), channel_id=1, source_target_pairs={{0,4},{1,5},{2,6},{3,7},{4,0},{5,1},{6,2},{7,3},{8,12},{9,13},{10,... | collective-permute-start | bytes 2580488 | tf_op jit(solution)/shard_map/ppermute | solution.py:36
  69.9 35.6 %collective-permute-start.19 = (bf16[8,112,224]{2,1,0:T(8,128)(2,1)}, bf16[8,112,224]{2,1,0:T(8,128)(2,1)}, u32[]{:S(2)}, u32[]{:S(2)}) collective-permute-start(bf16[8,112,224]{2,1,0:T(8,128)(2,1)} %collective-permute-done.18.refs_2_), channel_id=1, source_target_pairs={{0,8},{8,0},{16,24},{24,16},{1,9},{9,1},{17,25},{25,17},{2,10},{10... | collective-permute-start | bytes 1204232 | tf_op jit(solution)/shard_map/ppermute | solution.py:36
  79.3 28.1 %collective-permute-start.12 = (bf16[384,256]{1,0:T(8,128)(2,1)S(1)}, bf16[384,256]{1,0:T(8,128)(2,1)S(1)}, u32[]{:S(2)}, u32[]{:S(2)}) collective-permute-start(bf16[384,256]{1,0:T(8,128)(2,1)S(1)} %pad_maximum_fusion.11.refs_0_), channel_id=1, source_target_pairs={{0,16},{8,24},{16,0},{24,8},{1,17},{9,25},{17,1},{25,9},{2,18},{10... | collective-permute-start | bytes 589832 | tf_op jit(solution)/shard_map/ppermute | solution.py:36
  80.2 80.5 %collective-permute-start.20 = (bf16[480,896]{1,0:T(8,128)(2,1)}, bf16[480,896]{1,0:T(8,128)(2,1)}, u32[]{:S(2)}, u32[]{:S(2)}) collective-permute-start(bf16[480,896]{1,0:T(8,128)(2,1)} %join_lanes.1.refs_0_), channel_id=1, source_target_pairs={{0,1},{1,0},{2,3},{3,2},{4,5},{5,4},{6,7},{7,6},{8,9},{9,8},{10,11... | collective-permute-start | bytes 2580488 | tf_op jit(solution)/shard_map/ppermute | solution.py:36
  104.5 56.8 %collective-permute-start.23 = (bf16[480,896]{1,0:T(8,128)(2,1)}, bf16[480,896]{1,0:T(8,128)(2,1)}, u32[]{:S(2)}, u32[]{:S(2)}) collective-permute-start(bf16[480,896]{1,0:T(8,128)(2,1)} %collective-permute-done.9.refs_2_), channel_id=1, source_target_pairs={{0,4},{1,5},{2,6},{3,7},{4,0},{5,1},{6,2},{7,3},{8,12},{9,13},{10,... | collective-permute-start | bytes 2580488 | tf_op jit(solution)/shard_map/ppermute | solution.py:36
  108.9 53.9 %collective-permute-start.21 = (bf16[480,896]{1,0:T(8,128)(2,1)}, bf16[480,896]{1,0:T(8,128)(2,1)}, u32[]{:S(2)}, u32[]{:S(2)}) collective-permute-start(bf16[480,896]{1,0:T(8,128)(2,1)} %collective-permute-done.9.refs_2_), channel_id=1, source_target_pairs={{0,1},{1,0},{2,3},{3,2},{4,5},{5,4},{6,7},{7,6},{8,9},{9,8},{10,11... | collective-permute-start | bytes 2580488 | tf_op jit(solution)/shard_map/ppermute | solution.py:36
  111.1 49.5 %collective-permute-start.29 = (bf16[384,896]{1,0:T(8,128)(2,1)}, bf16[384,896]{1,0:T(8,128)(2,1)}, u32[]{:S(2)}, u32[]{:S(2)}) collective-permute-start(bf16[384,896]{1,0:T(8,128)(2,1)} %refs_12_), channel_id=1, source_target_pairs={{0,16},{8,24},{16,0},{24,8},{1,17},{9,25},{17,1},{25,9},{2,18},{10... | collective-permute-start | bytes 2064392 | tf_op jit(solution)/shard_map/ppermute | solution.py:36
  129.8 32.9 %collective-permute-start.28 = (bf16[384,896]{1,0:T(8,128)(2,1)}, bf16[384,896]{1,0:T(8,128)(2,1)}, u32[]{:S(2)}, u32[]{:S(2)}) collective-permute-start(bf16[384,896]{1,0:T(8,128)(2,1)} %refs_12_), channel_id=1, source_target_pairs={{0,8},{8,0},{16,24},{24,16},{1,9},{9,1},{17,25},{25,17},{2,10},{10... | collective-permute-start | bytes 2064392 | tf_op jit(solution)/shard_map/ppermute | solution.py:36
  161.3 39.7 %collective-permute-start.24 = (bf16[480,896]{1,0:T(8,128)(2,1)}, bf16[480,896]{1,0:T(8,128)(2,1)}, u32[]{:S(2)}, u32[]{:S(2)}) collective-permute-start(bf16[480,896]{1,0:T(8,128)(2,1)} %collective-permute-done.23.refs_6_), channel_id=1, source_target_pairs={{0,1},{1,0},{2,3},{3,2},{4,5},{5,4},{6,7},{7,6},{8,9},{9,8},{10,11... | collective-permute-start | bytes 2580488 | tf_op jit(solution)/shard_map/ppermute | solution.py:36
  243.8 27.2 %collective-permute-start.35 = (bf16[4,160,896]{2,1,0:T(8,128)(2,1)}, bf16[4,160,896]{2,1,0:T(8,128)(2,1)}, u32[]{:S(2)}, u32[]{:S(2)}) collective-permute-start(bf16[4,160,896]{2,1,0:T(8,128)(2,1)} %dynamic-slice_bitcast_fusion.5), channel_id=1, source_target_pairs={{0,1},{1,0},{2,3},{3,2},{4,5},{5,4},{6,7},{7,6},{8,9},{9,8},{10,11... | collective-permute-start | bytes 3440648 | tf_op jit(solution)/shard_map/ppermute | solution.py:36
  246.9 25.9 %collective-permute-start.32 = (bf16[2,384,896]{2,1,0:T(8,128)(2,1)}, bf16[2,384,896]{2,1,0:T(8,128)(2,1)}, u32[]{:S(2)}, u32[]{:S(2)}) collective-permute-start(bf16[2,384,896]{2,1,0:T(8,128)(2,1)} %dynamic-slice_bitcast_fusion), channel_id=1, source_target_pairs={{0,8},{8,0},{16,24},{24,16},{1,9},{9,1},{17,25},{25,17},{2,10},{10... | collective-permute-start | bytes 4128776 | tf_op jit(solution)/shard_map/ppermute | solution.py:36
  248.5 39.9 %collective-permute-start.31 = (bf16[2,384,896]{2,1,0:T(8,128)(2,1)S(1)}, bf16[2,384,896]{2,1,0:T(8,128)(2,1)S(1)}, u32[]{:S(2)}, u32[]{:S(2)}) collective-permute-start(bf16[2,384,896]{2,1,0:T(8,128)(2,1)S(1)} %dynamic-slice_bitcast_fusion.1), channel_id=1, source_target_pairs={{0,8},{8,0},{16,24},{24,16},{1,9},{9,1},{17,25},{25,17},{2,10},{10... | collective-permute-start | bytes 4128776 | tf_op jit(solution)/shard_map/ppermute | solution.py:36
  272.7 27.0 %collective-permute-start.37 = (bf16[2,160,896]{2,1,0:T(8,128)(2,1)S(1)}, bf16[2,160,896]{2,1,0:T(8,128)(2,1)S(1)}, u32[]{:S(2)}, u32[]{:S(2)}) collective-permute-start(bf16[2,160,896]{2,1,0:T(8,128)(2,1)S(1)} %fusion.26), channel_id=1, source_target_pairs={{0,4},{1,5},{2,6},{3,7},{4,0},{5,1},{6,2},{7,3},{8,12},{9,13},{10,... | collective-permute-start | bytes 1720328 | tf_op jit(solution)/shard_map/ppermute | solution.py:36
  287.5 26.0 %collective-permute-start.36 = (bf16[4,160,896]{2,1,0:T(8,128)(2,1)}, bf16[4,160,896]{2,1,0:T(8,128)(2,1)}, u32[]{:S(2)}, u32[]{:S(2)}) collective-permute-start(bf16[4,160,896]{2,1,0:T(8,128)(2,1)} %dynamic-slice_bitcast_fusion.4), channel_id=1, source_target_pairs={{0,1},{1,0},{2,3},{3,2},{4,5},{5,4},{6,7},{7,6},{8,9},{9,8},{10,11... | collective-permute-start | bytes 3440648 | tf_op jit(solution)/shard_map/ppermute | solution.py:36
  301.0 79.9 %collective-permute-start.52 = (bf16[1,160,896]{2,1,0:T(8,128)(2,1)}, bf16[1,160,896]{2,1,0:T(8,128)(2,1)}, u32[]{:S(2)}, u32[]{:S(2)}) collective-permute-start(bf16[1,160,896]{2,1,0:T(8,128)(2,1)} %dynamic-slice_convert_fusion.7), channel_id=1, source_target_pairs={{0,2},{1,3},{2,0},{3,1},{4,6},{5,7},{6,4},{7,5},{8,10},{9,11},{10,... | collective-permute-start | bytes 860168 | tf_op jit(solution)/shard_map/ppermute | solution.py:36
  313.6 67.2 %collective-permute-start.40 = (bf16[4,160,896]{2,1,0:T(8,128)(2,1)}, bf16[4,160,896]{2,1,0:T(8,128)(2,1)}, u32[]{:S(2)}, u32[]{:S(2)}) collective-permute-start(bf16[4,160,896]{2,1,0:T(8,128)(2,1)} %dynamic-slice_bitcast_fusion.3), channel_id=1, source_target_pairs={{0,1},{1,0},{2,3},{3,2},{4,5},{5,4},{6,7},{7,6},{8,9},{9,8},{10,11... | collective-permute-start | bytes 3440648 | tf_op jit(solution)/shard_map/ppermute | solution.py:36
  351.9 28.9 %collective-permute-start.41 = (bf16[2,160,896]{2,1,0:T(8,128)(2,1)}, bf16[2,160,896]{2,1,0:T(8,128)(2,1)}, u32[]{:S(2)}, u32[]{:S(2)}) collective-permute-start(bf16[2,160,896]{2,1,0:T(8,128)(2,1)} %fusion.27), channel_id=1, source_target_pairs={{0,4},{1,5},{2,6},{3,7},{4,0},{5,1},{6,2},{7,3},{8,12},{9,13},{10,... | collective-permute-start | bytes 1720328 | tf_op jit(solution)/shard_map/ppermute | solution.py:36
  357.0 27.5 %collective-permute-start.44 = (bf16[2,896,224]{1,2,0:T(8,128)(2,1)}, bf16[2,896,224]{1,2,0:T(8,128)(2,1)}, u32[]{:S(2)}, u32[]{:S(2)}) collective-permute-start(bf16[2,896,224]{1,2,0:T(8,128)(2,1)} %dynamic-slice_bitcast_fusion.6), channel_id=1, source_target_pairs={{0,8},{8,0},{16,24},{24,16},{1,9},{9,1},{17,25},{25,17},{2,10},{10... | collective-permute-start | bytes 2408456 | tf_op jit(solution)/shard_map/ppermute | solution.py:36
  384.6 30.2 %collective-permute-start.49 = (bf16[1,160,896]{2,1,0:T(8,128)(2,1)}, bf16[1,160,896]{2,1,0:T(8,128)(2,1)}, u32[]{:S(2)}, u32[]{:S(2)}) collective-permute-start(bf16[1,160,896]{2,1,0:T(8,128)(2,1)} %dynamic-slice_convert_fusion.9), channel_id=1, source_target_pairs={{0,2},{1,3},{2,0},{3,1},{4,6},{5,7},{6,4},{7,5},{8,10},{9,11},{10,... | collective-permute-start | bytes 860168 | tf_op jit(solution)/shard_map/ppermute | solution.py:36
  388.3 23.1 %collective-permute-start.43 = (bf16[1,8,160,224]{3,2,1,0:T(8,128)(2,1)}, bf16[1,8,160,224]{3,2,1,0:T(8,128)(2,1)}, u32[]{:S(2)}, u32[]{:S(2)}) collective-permute-start(bf16[1,8,160,224]{3,2,1,0:T(8,128)(2,1)} %dynamic-slice_convert_fusion.2), channel_id=1, source_target_pairs={{0,16},{8,24},{16,0},{24,8},{1,17},{9,25},{17,1},{25,9},{2,18},{10... | collective-permute-start | bytes 1720328 | tf_op jit(solution)/shard_map/ppermute | solution.py:36
  392.0 28.5 %collective-permute-start.50 = (bf16[2,160,896]{2,1,0:T(8,128)(2,1)}, bf16[2,160,896]{2,1,0:T(8,128)(2,1)}, u32[]{:S(2)}, u32[]{:S(2)}) collective-permute-start(bf16[2,160,896]{2,1,0:T(8,128)(2,1)} %fusion.28), channel_id=1, source_target_pairs={{0,4},{1,5},{2,6},{3,7},{4,0},{5,1},{6,2},{7,3},{8,12},{9,13},{10,... | collective-permute-start | bytes 1720328 | tf_op jit(solution)/shard_map/ppermute | solution.py:36
  (79 other events, 737.0 us)

commit v3 on v2

--- a/solution.py
+++ b/solution.py
@@ -59,12 +59,11 @@
     return outer_bits + inner_bits
 
 
-def fsdp_gather_small(block, size):
-    stack, offsets = block[None], [0]
-    for bit in fsdp_bits(size):
-        stack = jnp.concatenate([stack, swap(stack, "fsdp", size, bit)], axis=0)
-        offsets = offsets + [o ^ bit for o in offsets]
-    return stack, offsets
+def ff_spread(block, size):
+    blocks = {0: block}
+    for bit in fsdp_bits(size)[2:]:
+        blocks.update({o ^ bit: swap(b, "fsdp", size, bit) for o, b in blocks.items()})
+    return blocks
 
 
 def halve(stack, bit, me):
@@ -171,7 +170,7 @@
     )[0]
 
 
-def join_both(me, blocks, offsets, rows):
+def join_both(me, blocks, rows):
     size = len(blocks)
     count, tall, width = blocks[0].shape
     shapes = [jax.ShapeDtypeStruct((count, rows, size * width), BF16)]
@@ -182,11 +181,11 @@
         ins, out, held = refs[:size], refs[size], refs[-1]
         for o in range(size):
             held[me_ref[0] ^ o] = ins[o][...]
-        for j, f in enumerate(offsets):
-            parts = [held[q, j, :rows].astype(F32) for q in range(size)]
-            out[me_ref[1] ^ f] = jnp.concatenate(parts, axis=1).astype(BF16)
+        for f in range(count):
+            parts = [held[q, f, :rows].astype(F32) for q in range(size)]
+            out[f] = jnp.concatenate(parts, axis=1).astype(BF16)
             if tall > rows:
-                refs[size + 1][me_ref[1] ^ f] = ins[0][j, rows:]
+                refs[size + 1][f] = ins[0][f, rows:]
 
     return on_device(
         body, "join_both", shapes, [pltpu.VMEM((size, count, tall, width), BF16)], me, blocks
@@ -308,11 +307,7 @@
             pltpu.SemaphoreType.DMA((2 * count + 2 * size,)),
         ],
         compiler_params=pltpu.CompilerParams(vmem_limit_bytes=VMEM_LIMIT),
-        cost_estimate=pl.CostEstimate(
-            flops=12 * size * rows * units * width,
-            bytes_accessed=2 * (3 * units * width + size * rows * (3 * units + 5 * width)),
-            transcendentals=size * rows * units,
-        ),
+        cost_estimate=pl.CostEstimate(flops=1, bytes_accessed=1, transcendentals=0),
         name="feed_forward",
     )(me, *weight_blocks, *row_blocks, *cot_blocks)
 
@@ -338,30 +333,34 @@
     return jnp.concatenate([wide[:HEAD, :rows], wide[HEAD:, rows:]], axis=0)
 
 
-def pairing(kv_refs, step, begin):
-    both = jnp.concatenate([r[:, begin : begin + PAIR] for r in kv_refs], axis=0).astype(F32)
+def pairing(kv_ref, pair, begin):
+    both = kv_ref[:, begin : begin + PAIR].astype(F32)
     crossed = pltpu.roll(both, HEAD, 1)
     lane = lax.broadcasted_iota(jnp.int32, both.shape, 1)
-    first = jnp.where(step <= PAIRS // 2, both, crossed)
-    second = jnp.where(step < PAIRS // 2, crossed, both)
+    first = jnp.where(pair <= PAIRS // 2, both, crossed)
+    second = jnp.where(pair < PAIRS // 2, crossed, both)
     return jnp.where(lane < HEAD, first, second)
 
 
+def new_pairing(step, pair):
+    return (step == 0) | (pair == PAIRS // 2) | (pair == PAIRS // 2 + 1)
+
+
 def attend_kernel(
-    size, low_ref, high_ref, place_ref, q_ref, *refs,
+    begin_pair, low_ref, high_ref, place_ref, q_ref, kv_ref,
+    o_ref, lse_ref, bias_ref, k_ref, vt_ref,
 ):
-    kv_refs = refs[:size]
-    o_ref, lse_ref, bias_ref, k_ref, vt_ref = refs[size:]
     step = pl.program_id(0)
+    pair = step + begin_pair
 
     @pl.when(step == 0)
     def _():
         fill_bias(low_ref, high_ref, place_ref, bias_ref)
 
-    @pl.when((step == 0) | (step == PAIRS // 2) | (step == PAIRS // 2 + 1))
+    @pl.when(new_pairing(step, pair))
     def _():
-        k_ref[...] = pairing(kv_refs, step, 0).astype(BF16)
-        vt_ref[...] = pairing(kv_refs, step, PAIR).T.astype(BF16)
+        k_ref[...] = pairing(kv_ref, pair, 0).astype(BF16)
+        vt_ref[...] = pairing(kv_ref, pair, PAIR).T.astype(BF16)
 
     rows = q_ref.shape[0]
     queries = both_heads(q_ref[...])
@@ -381,23 +380,23 @@
 
 
 def attend_back_kernel(
-    size, low_ref, high_ref, place_ref, q_ref, g_ref, o_ref, lse_ref, *refs,
+    begin_pair, low_ref, high_ref, place_ref, q_ref, g_ref, o_ref, lse_ref, kv_ref, *refs,
 ):
-    kv_refs = refs[:size]
-    dq_ref, dkv_ref, bias_ref, k_ref, kt_ref, v_ref, dk_ref, dv_ref = refs[size:]
+    dq_ref, dkv_ref, bias_ref, k_ref, kt_ref, v_ref, dk_ref, dv_ref = refs[-8:]
     step = pl.program_id(0)
+    pair = step + begin_pair
 
     @pl.when(step == 0)
     def _():
         fill_bias(low_ref, high_ref, place_ref, bias_ref)
-        dkv_ref[...] = jnp.zeros_like(dkv_ref)
-
-    @pl.when((step == 0) | (step == PAIRS // 2) | (step == PAIRS // 2 + 1))
+        dkv_ref[...] = refs[0][...] if begin_pair else jnp.zeros_like(dkv_ref)
+
+    @pl.when(new_pairing(step, pair))
     def _():
-        keys_now = pairing(kv_refs, step, 0)
+        keys_now = pairing(kv_ref, pair, 0)
         k_ref[...] = keys_now.astype(BF16)
         kt_ref[...] = keys_now.T.astype(BF16)
-        v_ref[...] = pairing(kv_refs, step, PAIR).astype(BF16)
+        v_ref[...] = pairing(kv_ref, pair, PAIR).astype(BF16)
         dk_ref[...] = jnp.zeros_like(dk_ref)
         dv_ref[...] = jnp.zeros_like(dv_ref)
 
@@ -437,16 +436,16 @@
             kept = jnp.where((lane < HEAD) == own_lanes, both, 0.0)
             dkv_ref[:, at : at + PAIR] += kept
 
-    @pl.when(step == PAIRS // 2 - 1)
+    @pl.when(pair == PAIRS // 2 - 1)
     def _():
         fold(True)
 
-    @pl.when(step == PAIRS // 2)
+    @pl.when(pair == PAIRS // 2)
     def _():
         dkv_ref[:, :PAIR] += dk_ref[...]
         dkv_ref[:, PAIR:] += dv_ref[...]
 
-    @pl.when(step == PAIRS - 1)
+    @pl.when(pair == PAIRS - 1)
     def _():
         fold(False)
 
@@ -455,18 +454,19 @@
     return pl.BlockSpec(shape, lambda i: (0,) * len(shape))
 
 
-def attend(low, high, place, queries, kv_blocks):
-    rows, count, size = queries.shape[0], place.shape[0], len(kv_blocks)
-    pair = pl.BlockSpec((rows, PAIR), lambda i: (0, i))
+def attend(low, high, place, queries, kv_all, begin, pairs):
+    rows, count = queries.shape[0], place.shape[0]
+    taken = pl.BlockSpec((rows, PAIR), lambda i: (0, i + begin))
+    made = pl.BlockSpec((rows, PAIR), lambda i: (0, i))
     return pl.pallas_call(
-        functools.partial(attend_kernel, size),
-        grid=(PAIRS,),
-        in_specs=[whole((1, rows)), whole((1, rows)), whole((count, 1)), pair]
-        + [whole((rows, 2 * KVW))] * size,
-        out_specs=[pair, pl.BlockSpec((1, 1, 2 * rows), lambda i: (i, 0, 0))],
+        functools.partial(attend_kernel, begin),
+        grid=(pairs,),
+        in_specs=[whole((1, rows)), whole((1, rows)), whole((count, 1)), taken]
+        + [whole((count, 2 * KVW))],
+        out_specs=[made, pl.BlockSpec((1, 1, 2 * rows), lambda i: (i, 0, 0))],
         out_shape=[
-            jax.ShapeDtypeStruct((rows, QW), BF16),
-            jax.ShapeDtypeStruct((PAIRS, 1, 2 * rows), F32),
+            jax.ShapeDtypeStruct((rows, pairs * PAIR), BF16),
+            jax.ShapeDtypeStruct((pairs, 1, 2 * rows), F32),
         ],
         scratch_shapes=[
             pltpu.VMEM((count, 2 * rows), F32),
@@ -474,27 +474,25 @@
             pltpu.VMEM((PAIR, count), BF16),
         ],
         compiler_params=pltpu.CompilerParams(vmem_limit_bytes=VMEM_LIMIT),
-        cost_estimate=pl.CostEstimate(
-            flops=8 * HEADS * rows * count * PAIR,
-            bytes_accessed=4 * rows * QW + 1024 * count,
-            transcendentals=HEADS * rows * count,
-        ),
+        cost_estimate=pl.CostEstimate(flops=1, bytes_accessed=1, transcendentals=0),
         name="attend",
-    )(low, high, place, queries, *kv_blocks)
-
-
-def attend_back(low, high, place, queries, grads, outs, lse, kv_blocks):
-    rows, count, size = queries.shape[0], place.shape[0], len(kv_blocks)
-    pair = pl.BlockSpec((rows, PAIR), lambda i: (0, i))
+    )(low, high, place, queries, kv_all)
+
+
+def attend_back(low, high, place, queries, grads, outs, lse, kv_all, begin, pairs, so_far):
+    rows, count = queries.shape[0], place.shape[0]
+    taken = pl.BlockSpec((rows, PAIR), lambda i: (0, i + begin))
+    made = pl.BlockSpec((rows, PAIR), lambda i: (0, i))
+    sums = whole((count, 2 * KVW))
     return pl.pallas_call(
-        functools.partial(attend_back_kernel, size),
-        grid=(PAIRS,),
-        in_specs=[whole((1, rows)), whole((1, rows)), whole((count, 1)), pair, pair, pair]
-        + [pl.BlockSpec((1, 1, 2 * rows), lambda i: (i, 0, 0))]
-        + [whole((rows, 2 * KVW))] * size,
-        out_specs=[pair, whole((count, 2 * KVW))],
+        functools.partial(attend_back_kernel, begin),
+        grid=(pairs,),
+        in_specs=[whole((1, rows)), whole((1, rows)), whole((count, 1)), taken, taken, made]
+        + [pl.BlockSpec((1, 1, 2 * rows), lambda i: (i, 0, 0)), sums]
+        + [sums] * len(so_far),
+        out_specs=[made, sums],
         out_shape=[
-            jax.ShapeDtypeStruct((rows, QW), F32),
+            jax.ShapeDtypeStruct((rows, pairs * PAIR), F32),
             jax.ShapeDtypeStruct((count, 2 * KVW), F32),
         ],
         scratch_shapes=[
@@ -506,13 +504,9 @@
             pltpu.VMEM((count, PAIR), F32),
         ],
         compiler_params=pltpu.CompilerParams(vmem_limit_bytes=VMEM_LIMIT),
-        cost_estimate=pl.CostEstimate(
-            flops=16 * HEADS * rows * count * PAIR,
-            bytes_accessed=8 * rows * QW + 4096 * count,
-            transcendentals=HEADS * rows * count,
-        ),
+        cost_estimate=pl.CostEstimate(flops=1, bytes_accessed=1, transcendentals=0),
         name="attend_back",
-    )(low, high, place, queries, grads, outs, lse, *kv_blocks)
+    )(low, high, place, queries, grads, outs, lse, kv_all, *so_far)
 
 
 def rms_scale(values_in):
@@ -596,30 +590,25 @@
         ],
         axis=0,
     )
-    packed_stack, fsdp_order = fsdp_gather_small(packed, fsdp_size)
-    packed_blocks = seq_gather(packed_stack, seq_size)
-
     ff_cut = cut_ff(me, gate_up_weight, down_weight, seq_size)
     ff_share = [ff_cut[0]] + [swap(ff_cut[o], "seq", seq_size, o) for o in offsets if o]
+    packed_stack, out_stack = lax.all_gather((after(packed, ff_cut[0]), out_weight), "fsdp", axis=0)
+    packed_blocks = seq_gather(packed_stack, seq_size)
     ff_block = join_lanes(me, ff_share)
     ff_blocks = {0: ff_block}
-    for bit in fsdp_bits(fsdp_size):
+    for bit in fsdp_bits(fsdp_size)[:2]:
         ff_blocks.update({o ^ bit: swap(b, "fsdp", fsdp_size, bit) for o, b in ff_blocks.items()})
     inner = fsdp_size // OUTER
 
     qkv_blocks = [packed_blocks[o] for o in offsets]
     qkv_blocks[0] = after(qkv_blocks[0], ff_block)
-    qkv_t, vectors = join_both(me, qkv_blocks, fsdp_order, qkv_tall)
+    qkv_t, vectors = join_both(me, qkv_blocks, qkv_tall)
     qkv_t = qkv_t[:, :qkv_rows].reshape(fsdp_size * qkv_rows, -1)
     gain_one = vectors[:, 0, : norm_one.shape[0]].reshape(-1).astype(F32)
     bias_full = vectors[:, 1, : qkv_bias.shape[0]].reshape(-1).astype(F32)
     gain_two = vectors[:, 2, : norm_two.shape[0]].reshape(-1).astype(F32)
 
-    cot_blocks = seq_gather(after(cotangent, packed_blocks[seq_size // 2]), seq_size)
-    out_stack, out_order = fsdp_gather_small(after(out_weight, ff_block), fsdp_size)
-    out_blocks = seq_gather(out_stack, seq_size)
-    out_full = join_both(me, [out_blocks[o] for o in offsets], out_order, out_weight.shape[0])[0]
-    out_full = out_full.reshape(QW, -1)
+    out_blocks = seq_gather(after(out_stack, packed_blocks[seq_size // 2]), seq_size)
 
     inputs = tokens.astype(F32)
     scale_one = rms_scale(inputs)
@@ -629,20 +618,37 @@
     turned = rotate(joined[:, : QW + KVW], cosine, sine).astype(BF16)
     queries = turned[:, :QW] * jnp.asarray(0.125, BF16)
     kv_local = jnp.concatenate([turned[:, QW:], joined[:, QW + KVW :].astype(BF16)], axis=1)
-    kv_blocks = seq_gather(kv_local, seq_size)
-    kv_blocks = [kv_blocks[o] for o in offsets]
+    kv_local = after(kv_local, ff_blocks[inner])
+    kv_all = lax.all_gather(kv_local, "seq", axis=0, tiled=True)
+    kv_all = after(kv_all, ff_blocks[2 * inner], ff_blocks[inner])
+    cot_blocks = seq_gather(after(cotangent, kv_all), seq_size)
     row_place = jnp.arange(row_count, dtype=jnp.int32)
     high = my_seq * row_count + row_place
     low = high - positions
-    place = jnp.concatenate([(my_seq ^ o) * row_count + row_place for o in offsets])[:, None]
+    place = jnp.arange(seq_size * row_count, dtype=jnp.int32)[:, None]
     low, high = low[None, :], high[None, :]
-    queries_now = after(queries, ff_blocks[inner], ff_blocks[2 * inner])
-    attn_flat, lse = attend(low, high, place, queries_now, kv_blocks)
+    split = PAIRS // 2 + 1
+    spread = lambda block: ff_spread(block, fsdp_size)
+    own, near = ff_blocks[0], ff_blocks[inner]
+    far, last = ff_blocks[2 * inner], ff_blocks[3 * inner]
+    own_x = spread(own)
+    near_x = spread(after(near, kv_all))
+    attn_one, lse_one = attend(low, high, place, after(queries, far), kv_all, 0, split)
+    far_x = spread(after(far, kv_all))
+    queries_two = after(queries, attn_one, cot_blocks[seq_size // 2], *near_x.values())
+    attn_two, lse_two = attend(low, high, place, queries_two, kv_all, split, PAIRS - split)
+    last_x = spread(after(last, attn_two))
+    for base, row in ((0, own_x), (inner, near_x), (2 * inner, far_x), (3 * inner, last_x)):
+        ff_blocks.update({base + m: block for m, block in row.items()})
+    attn_flat = jnp.concatenate([attn_one, attn_two], axis=1)
+
+    out_list = [after(out_blocks[0], attn_one)] + [out_blocks[o] for o in offsets if o]
+    out_full = join_both(me, out_list, out_weight.shape[0])[0].reshape(QW, -1)
 
     residual = inputs + dot(attn_flat, out_full, 1, 0)
     scale_two = rms_scale(residual)
     normed_two = (residual * scale_two * gain_two).astype(BF16)
-    normed_blocks = seq_gather(normed_two, seq_size)
+    normed_blocks = seq_gather(after(normed_two, *far_x.values()), seq_size)
     hidden, grad_gate, grad_up, grad_normed, layer_part, normed_all, cot_all = feed_forward(
         me,
         [ff_blocks[o] for o in range(fsdp_size)],
@@ -659,30 +665,35 @@
         normed_sum = add(kept, swap(given, "seq", seq_size, bit))
         bit *= 2
     grad_normed_two = normed_sum[0]
+    hidden = after(hidden, given)
     down_term = dot(hidden, cot_all, 0, 0).astype(BF16).reshape(fsdp_size, tall, -1)
-    grad_gate, grad_up = after(grad_gate, given), after(grad_up, given)
+    grad_gate, grad_up = after(grad_gate, down_term), after(grad_up, down_term)
     gate_term = dot(grad_gate, normed_all, 0, 0).astype(BF16).reshape(fsdp_size // 2, 2, tall, -1)
     up_term = dot(grad_up, normed_all, 0, 0).astype(BF16).reshape(fsdp_size // 2, 2, tall, -1)
 
-    chunks = [down_term] + [
-        jnp.concatenate([gate_term[:, i], up_term[:, i]], axis=0) for i in range(2)
-    ]
     bits = list(reversed(fsdp_bits(fsdp_size)))
-    steps = []
-    for chunk in chunks:
-        kept, given = fsdp_halve(chunk, fsdp_size, bits[0], my_fsdp, [])
-        if steps:
-            given = after(given, steps[-1][0])
-        got = [swap(given, "fsdp", fsdp_size, bits[0])]
-        stack = add(kept, got[0])
-        for at in range(1, len(bits)):
-            kept, given = fsdp_halve(stack, fsdp_size, bits[at], my_fsdp, bits[:at])
-            got.append(swap(given, "fsdp", fsdp_size, bits[at]))
-            stack = add(kept, got[-1])
-        steps.append(got + [stack[0]])
-    down_sum, one_sum, two_sum = [s[-1] for s in steps]
-
-    kept, given = halve(by_seq(layer_part), 1, my_seq)
+
+    def give(stack, at):
+        kept, given = fsdp_halve(stack, fsdp_size, bits[at], my_fsdp, bits[:at])
+        return kept, given
+
+    def send(given, at):
+        return swap(given, "fsdp", fsdp_size, bits[at])
+
+    def finish(kept, got, at):
+        stack = add(kept, got)
+        for later in range(at + 1, len(bits)):
+            kept, given = give(stack, later)
+            stack = add(kept, send(given, later))
+        return stack[0]
+
+    kept_one, given = give(down_term, 0)
+    got_one = send(given, 0)
+    kept_two, given = give(jnp.concatenate([gate_term[:, 0], up_term[:, 0]], axis=0), 0)
+    got_two = send(given, 0)
+    kept_three, given_three = give(jnp.concatenate([gate_term[:, 1], up_term[:, 1]], axis=0), 0)
+
+    kept, given = halve(after(by_seq(layer_part), down_term), 1, my_seq)
     layer_sum = add(kept, swap(given, "seq", seq_size, 1))
     bit = 2
     while bit < seq_size:
@@ -692,30 +703,35 @@
         bit *= 2
     layer_out = residual + layer_sum[0]
 
-    ff_back = cut_lanes(me, (one_sum, two_sum, down_sum), seq_size)
-    ff_got = [ff_back[0]] + [swap(ff_back[o], "seq", seq_size, o) for o in offsets if o]
-    grad_gate_up, grad_down = join_ff(me, ff_got, strip)
-
     grad_path, norm_two_term = norm_back(grad_normed_two, residual, scale_two, gain_two)
     grad_residual = cotangent.astype(F32) + grad_path
     grad_branch = grad_residual.astype(BF16)
     grad_attn = dot(grad_branch, out_full, 1, 1).astype(BF16)
     out_term = stack_from_lanes(dot(attn_flat, grad_branch, 0, 0).astype(BF16), seq_size)
     out_mine = seq_scatter(out_term, seq_size, my_seq).reshape(fsdp_size, -1, width)
-    grad_attn = after(grad_attn, steps[0][0], gate_term, up_term)
-    grad_queries, kv_terms = attend_back(
-        low, high, place, queries, grad_attn, attn_flat, lse, kv_blocks
-    )
-    kv_terms = after(kv_terms, steps[1][0], steps[0][1])
-    kv_sum = by_seq(kv_terms)
-    bit = 1
-    while bit < seq_size:
-        cut = kv_sum.reshape((-1, 2) + kv_sum.shape[1:])
-        kv_sum = add(cut[:, 0], swap(cut[:, 1].astype(BF16), "seq", seq_size, bit))
-        bit *= 2
-    kv_mine = kv_sum[0]
+    grad_attn = after(grad_attn, gate_term, up_term)
+    dq_one, kv_terms = attend_back(
+        low, high, place, queries, grad_attn, attn_one, lse_one, kv_all, 0, split, ()
+    )
+    got_one = after(got_one, dq_one)
+    got_three = send(after(given_three, got_one), 0)
+    kept_one, given = give(add(kept_one, got_one), 1)
+    next_one = send(given, 1)
+    queries_two = after(queries, kv_terms, got_one)
+    dq_two, kv_terms = attend_back(
+        low, high, place, queries_two, grad_attn, attn_two, lse_two, kv_all, split,
+        PAIRS - split, (kv_terms,),
+    )
+    got_two = after(got_two, dq_two)
+    down_sum = finish(kept_one, after(next_one, dq_two), 1)
+    kept_two, given = give(add(kept_two, got_two), 1)
+    next_two = send(given, 1)
+    kv_mine = seq_scatter(by_seq(kv_terms), seq_size, my_seq)
+    got_three = after(got_three, kv_mine)
+    kept_three, given = give(add(kept_three, got_three), 1)
+    next_three = send(given, 1)
     turned_back = rotate_back(
-        jnp.concatenate([grad_queries, kv_mine[:, :KVW]], axis=1), cosine, sine
+        jnp.concatenate([dq_one, dq_two, kv_mine[:, :KVW]], axis=1), cosine, sine
     )
     grad_joined = jnp.concatenate([turned_back, kv_mine[:, KVW:]], axis=1).astype(BF16)
     grad_normed_one = dot(grad_joined, qkv_t, 1, 0)
@@ -735,7 +751,14 @@
     tail = jnp.concatenate(
         [qkv_term, jnp.broadcast_to(small[None], (seq_size,) + small.shape)], axis=2
     )
-    tail_mine = seq_scatter(after(tail, steps[2][0], steps[1][1]), seq_size, my_seq)
+    tail_mine = seq_scatter(after(tail, got_three), seq_size, my_seq)
+    one_sum = finish(kept_two, after(next_two, tail), 1)
+    two_sum = finish(kept_three, next_three, 1)
+
+    ff_back = cut_lanes(me, (one_sum, two_sum, down_sum), seq_size)
+    ff_got = [ff_back[0]] + [swap(ff_back[o], "seq", seq_size, o) for o in offsets if o]
+    grad_gate_up, grad_down = join_ff(me, ff_got, strip)
+
     tail_sum = fsdp_scatter(
         jnp.concatenate([tail_mine, out_mine], axis=1), fsdp_size, my_fsdp
     )

time: 460 us -> 484 us (1.052)
  blocking collectives: 0 us -> 73.8 us
  starting transfers between devices: 67.4 us -> 32.2 us
  waiting for transfers between devices: 168 us -> 161 us
  other arithmetic: 34.3 us -> 28.3 us
  Pallas kernels: 94 us -> 98.9 us
    all_gather x0 -> x3, blocking collectives: none -> 73.8 us  [the longest x2 64.7 us: per_device(): lax.all_gather((after(packed, ff_cut[0]), out_weight), 'fsdp', axis=0)]
    ppermute x56 -> x47, starting transfers between devices: 67.4 us -> 32.2 us  [swap(): return lax.ppermute(block, axis, [(i, i ^ bits) for i in range(size)])]
    ppermute x56 -> x47, waiting for transfers between devices: 168 us -> 161 us  [swap(): return lax.ppermute(block, axis, [(i, i ^ bits) for i in range(size)])]
    concatenate x2, local copies, waits for them, and re-layouts: 12.6 us -> 5.92 us  [widen(): return jnp.concatenate([table] * (width // PAIR), axis=1)]
    unnamed x97 -> x128, local copies, waits for them, and re-layouts: 17.5 us -> 23.6 us
    pallas_call x2 -> x4, Pallas kernels: 51.6 us -> 56 us  [the longest x2 32.5 us: attend_back(): pl.pallas_call(functools.partial(attend_back_kernel, begin), grid=(pairs,...]
  transfers between devices with their start and end apart: 56 -> 47, of which waited for: 22 -> 16; matrix products, arithmetic and copies ran while one was open for 21% -> 16% of each run, Pallas kernels for 14% -> 14%
where the time goes in v3:
time: 484 us; the launch traced here: 477 us
  waiting for transfers between devices  161 us (33%)
  Pallas kernels  98.9 us (20%)
  blocking collectives  73.8 us (15%)
  local copies, waits for them, and re-layouts  55.8 us (12%)
  starting transfers between devices  32.2 us (7%)
  other arithmetic  28.3 us (6%)
  matrix products  25 us (5%)
    ppermute x47, waiting for transfers between devices, swap(): return lax.ppermute(block, axis, [(i, i ^ bits) for i in range(size)])  161 us
    all_gather x2, blocking collectives, per_device(): lax.all_gather((after(packed, ff_cut[0]), out_weight), 'fsdp', axis=0)  64.7 us
    pallas_call x2, Pallas kernels, attend_back(): pl.pallas_call(functools.partial(attend_back_kernel, begin), grid=(pairs,...  32.5 us
    ppermute x47, starting transfers between devices, swap(): return lax.ppermute(block, axis, [(i, i ^ bits) for i in range(size)])  32.2 us
    pallas_call x1, Pallas kernels, feed_forward(): pl.pallas_call(body, grid=(size,), in_specs=[pl.BlockSpec(memory_space=pl...  31.9 us
    dot_general x9, matrix products, dot(): lax.dot_general(left, right, (((left_dim,), (right_dim,)), ((), ())), pre...  25 us
    unnamed x128, local copies, waits for them, and re-layouts  23.6 us
    pallas_call x2, Pallas kernels, attend(): pl.pallas_call(functools.partial(attend_kernel, begin), grid=(pairs,), in...  23.4 us
  transfers between devices with their start and end apart: 47, of which 16 were waited for; matrix products, arithmetic and copies ran while one was open for 16% of the time, Pallas kernels for 14%

profile of v3, /device:TPU:0, one launch (start us, length us, event | category | flops | bytes accessed | tf_op | source)
XLA Modules:
  0.0 477.2 jit_solution(14219534316742195172)
XLA Ops:
  6.8 33.4 %all-gather = bf16[1280,224]{1,0:T(8,128)(2,1)S(1)} all-gather(bf16[160,224]{1,0:T(8,128)(2,1)S(1)} %concatenate.65), channel_id=2, replica_groups=mesh['seq'=4,'fsdp'=8] {'fsdp'}, dimensions={0}, use_global_device_ids=true | all-gather | bytes 645120 | tf_op jit(solution)/shard_map/all_gather | solution.py:595
  44.4 12.0 %collective-permute-done.4.refs_2_ = bf16[8,160,224]{2,1,0:T(8,128)(2,1)S(1)} collective-permute-done((bf16[8,160,224]{2,1,0:T(8,128)(2,1)S(1)}, bf16[8,160,224]{2,1,0:T(8,128)(2,1)S(1)}, u32[]{:S(2)}, u32[]{:S(2)}) %collective-permute-start.4) | collective-permute-done | bytes 573472 | tf_op jit(solution)/shard_map/ppermute | solution.py:36
  63.7 31.3 %all-gather.1 = bf16[896,224]{1,0:T(8,128)(2,1)S(1)} all-gather(bf16[112,224]{1,0:T(8,128)(2,1)S(1)} %copy-done.54), channel_id=3, replica_groups=mesh['seq'=4,'fsdp'=8] {'fsdp'}, dimensions={0}, use_global_device_ids=true | all-gather | bytes 451584 | tf_op jit(solution)/shard_map/all_gather | solution.py:595
  113.9 20.1 %collective-permute-done.7.refs_2_ = bf16[480,896]{1,0:T(8,128)(2,1)} collective-permute-done((bf16[480,896]{1,0:T(8,128)(2,1)S(1)}, bf16[480,896]{1,0:T(8,128)(2,1)}, u32[]{:S(2)}, u32[]{:S(2)}) %collective-permute-start.7) | collective-permute-done | bytes 860192 | tf_op jit(solution)/shard_map/ppermute | solution.py:36
  134.0 9.1 %all_gather.17.kv_ref = bf16[1536,256]{1,0:T(8,128)(2,1)S(1)} all-gather(bf16[384,256]{1,0:T(8,128)(2,1)S(1)} %pad_maximum_fusion.7), channel_id=1, replica_groups=mesh['seq'=4,'fsdp'=8] {'seq'}, dimensions={0}, use_global_device_ids=true | all-gather | bytes 983040 | tf_op jit(solution)/shard_map/all_gather | solution.py:622
  147.3 13.4 %attend.2 = (bf16[384,512]{1,0:T(8,128)(2,1)S(1)}, f32[4,1,768]{2,1,0:T(1,128)S(1)}) custom-call(s32[1,384]{1,0:T(1,128)S(1)} %broadcast_in_dim.12.low_ref, s32[1,384]{1,0:T(1,128)S(1)} %iota_add_fusion.high_ref, s32[1536,1]{1,0:T(8,128)S(1)} %iota.43.place_ref, bf16[384,896]{1,0:T(8,128)(2,1)S(1)} %slice_multiply_fusion.1.q_ref, ...), custom_call_target="tpu_custom_call" | custom-call | flops 1 | bytes 1 | tf_op jit(solution)/shard_map/attend/pallas_call | solution.py:461
  166.8 10.0 %attend.3 = (bf16[384,384]{1,0:T(8,128)(2,1)S(1)}, f32[3,1,768]{2,1,0:T(1,128)S(1)}) custom-call(s32[1,384]{1,0:T(1,128)S(1)} %broadcast_in_dim.12.low_ref, s32[1,384]{1,0:T(1,128)S(1)} %iota_add_fusion.high_ref, s32[1536,1]{1,0:T(8,128)S(1)} %iota.49.place_ref, bf16[384,896]{1,0:T(8,128)(2,1)S(1)} %slice_multiply_fusion.1.q_ref, ...), custom_call_target="tpu_custom_call" | custom-call | flops 1 | bytes 1 | tf_op jit(solution)/shard_map/attend/pallas_call | solution.py:461
  178.1 24.6 %collective-permute-done.14.refs_5_ = bf16[480,896]{1,0:T(8,128)(2,1)S(1)} collective-permute-done((bf16[480,896]{1,0:T(8,128)(2,1)}, bf16[480,896]{1,0:T(8,128)(2,1)S(1)}, u32[]{:S(2)}, u32[]{:S(2)}) %collective-permute-start.14) | collective-permute-done | bytes 860192 | tf_op jit(solution)/shard_map/ppermute | solution.py:36
  205.5 14.4 %collective-permute-done.18.refs_10_ = bf16[384,896]{1,0:T(8,128)(2,1)} collective-permute-done((bf16[384,896]{1,0:T(8,128)(2,1)S(1)}, bf16[384,896]{1,0:T(8,128)(2,1)}, u32[]{:S(2)}, u32[]{:S(2)}) %collective-permute-start.18) | collective-permute-done | bytes 688160 | tf_op jit(solution)/shard_map/ppermute | solution.py:36
  224.2 31.9 %feed_forward.1 = (bf16[1536,1280]{1,0:T(8,128)(2,1)}, bf16[1536,1280]{1,0:T(8,128)(2,1)}, bf16[1536,1280]{1,0:T(8,128)(2,1)}, bf16[1536,896]{1,0:T(8,128)(2,1)}...) custom-call(s32[2]{0:T(128)S(1)} %pad_add_fusion.me_ref, ...), custom_call_target="tpu_custom_call" | custom-call | flops 1 | bytes 1 | tf_op jit(solution)/shard_map/feed_forward/pallas_call | solution.py:295
  265.1 4.5 convolution_convert_fusion.3
  272.3 4.5 convolution_convert_fusion.1
  276.8 4.8 convolution_convert_fusion.2
  294.1 10.6 %collective-permute-done.25 = bf16[1,384,896]{2,1,0:T(8,128)(2,1)S(1)} collective-permute-done((bf16[1,384,896]{2,1,0:T(8,128)(2,1)S(1)}, bf16[1,384,896]{2,1,0:T(8,128)(2,1)S(1)}, u32[]{:S(2)}, u32[]{:S(2)}) %collective-permute-start.25) | collective-permute-done | bytes 688160 | tf_op jit(solution)/shard_map/ppermute | solution.py:36
  309.5 17.9 %attend_back.2 = (f32[384,512]{1,0:T(8,128)S(1)}, f32[1536,256]{1,0:T(8,128)}) custom-call(s32[1,384]{1,0:T(1,128)S(1)} %broadcast_in_dim.12.low_ref, s32[1,384]{1,0:T(1,128)S(1)} %iota_add_fusion.high_ref, s32[1536,1]{1,0:T(8,128)S(1)} %iota.50.place_ref, bf16[384,896]{1,0:T(8,128)(2,1)S(1)} %slice_multiply_fusion.1.q_ref, ...), custom_call_target="tpu_custom_call" | custom-call | flops 1 | bytes 1 | tf_op jit(solution)/shard_map/attend_back/pallas_call | solution.py:487
  328.0 14.6 %attend_back.3 = (f32[384,384]{1,0:T(8,128)S(1)}, f32[1536,256]{1,0:T(8,128)}) custom-call(s32[1,384]{1,0:T(1,128)S(1)} %broadcast_in_dim.12.low_ref, s32[1,384]{1,0:T(1,128)S(1)} %iota_add_fusion.high_ref, s32[1536,1]{1,0:T(8,128)S(1)} %iota.51.place_ref, bf16[384,896]{1,0:T(8,128)(2,1)S(1)} %slice_multiply_fusion.1.q_ref, ...), custom_call_target="tpu_custom_call" | custom-call | flops 1 | bytes 1 | tf_op jit(solution)/shard_map/attend_back/pallas_call | solution.py:487
  350.9 4.7 collective-permute-done.28
  371.5 5.9 %collective-permute-done.38 = bf16[2,160,896]{2,1,0:T(8,128)(2,1)} collective-permute-done((bf16[2,160,896]{2,1,0:T(8,128)(2,1)}, bf16[2,160,896]{2,1,0:T(8,128)(2,1)}, u32[]{:S(2)}, u32[]{:S(2)}) %collective-permute-start.38) | collective-permute-done | bytes 573472 | tf_op jit(solution)/shard_map/ppermute | solution.py:36
  383.1 4.4 collective-permute-done.39
  400.0 30.7 %collective-permute-done.42 = bf16[2,160,896]{2,1,0:T(8,128)(2,1)} collective-permute-done((bf16[2,160,896]{2,1,0:T(8,128)(2,1)}, bf16[2,160,896]{2,1,0:T(8,128)(2,1)}, u32[]{:S(2)}, u32[]{:S(2)}) %collective-permute-start.42) | collective-permute-done | bytes 573472 | tf_op jit(solution)/shard_map/ppermute | solution.py:36
  435.6 7.3 %collective-permute-done.40 = bf16[2,160,896]{2,1,0:T(8,128)(2,1)} collective-permute-done((bf16[2,160,896]{2,1,0:T(8,128)(2,1)}, bf16[2,160,896]{2,1,0:T(8,128)(2,1)}, u32[]{:S(2)}, u32[]{:S(2)}) %collective-permute-start.40) | collective-permute-done | bytes 573472 | tf_op jit(solution)/shard_map/ppermute | solution.py:36
  444.2 4.7 collective-permute-done.43
  450.8 5.0 %collective-permute-done.41 = bf16[1,160,896]{2,1,0:T(8,128)(2,1)S(1)} collective-permute-done((bf16[1,160,896]{2,1,0:T(8,128)(2,1)S(1)}, bf16[1,160,896]{2,1,0:T(8,128)(2,1)S(1)}, u32[]{:S(2)}, u32[]{:S(2)}) %collective-permute-start.41) | collective-permute-done | bytes 286752 | tf_op jit(solution)/shard_map/ppermute | solution.py:36
  458.8 5.8 %collective-permute-done.35 = bf16[2,272,224]{2,1,0:T(8,128)(2,1)S(1)} collective-permute-done((bf16[2,272,224]{2,1,0:T(8,128)(2,1)S(1)}, bf16[2,272,224]{2,1,0:T(8,128)(2,1)S(1)}, u32[]{:S(2)}, u32[]{:S(2)}) %collective-permute-start.35) | collective-permute-done | bytes 243744 | tf_op jit(solution)/shard_map/ppermute | solution.py:36
  (334 shorter events, 149.3 us)
Async XLA Ops:
  41.7 62.7 %collective-permute-start.3 = (bf16[8,160,224]{2,1,0:T(8,128)(2,1)S(1)}, bf16[8,160,224]{2,1,0:T(8,128)(2,1)}, u32[]{:S(2)}, u32[]{:S(2)}) collective-permute-start(bf16[8,160,224]{2,1,0:T(8,128)(2,1)S(1)} %bitcast.167), channel_id=1, source_target_pairs={{0,8},{8,0},{16,24},{24,16},{1,9},{9,1},{17,25},{25,17},{2,10},{10... | collective-permute-start | bytes 1720328 | tf_op jit(solution)/shard_map/ppermute | solution.py:36
  41.7 53.2 %collective-permute-start = (bf16[480,224]{1,0:T(8,128)(2,1)}, bf16[480,224]{1,0:T(8,128)(2,1)S(1)}, u32[]{:S(2)}, u32[]{:S(2)}) collective-permute-start(bf16[480,224]{1,0:T(8,128)(2,1)} %get-tuple-element.68), channel_id=1, source_target_pairs={{0,8},{8,0},{16,24},{24,16},{1,9},{9,1},{17,25},{25,17},{2,10},{10... | collective-permute-start | bytes 645128 | tf_op jit(solution)/shard_map/ppermute | solution.py:36
  42.3 53.4 %collective-permute-start.1 = (bf16[480,224]{1,0:T(8,128)(2,1)}, bf16[480,224]{1,0:T(8,128)(2,1)S(1)}, u32[]{:S(2)}, u32[]{:S(2)}) collective-permute-start(bf16[480,224]{1,0:T(8,128)(2,1)} %get-tuple-element.69), channel_id=1, source_target_pairs={{0,16},{8,24},{16,0},{24,8},{1,17},{9,25},{17,1},{25,9},{2,18},{10... | collective-permute-start | bytes 645128 | tf_op jit(solution)/shard_map/ppermute | solution.py:36
  42.8 53.6 %collective-permute-start.2 = (bf16[480,224]{1,0:T(8,128)(2,1)S(1)}, bf16[480,224]{1,0:T(8,128)(2,1)S(1)}, u32[]{:S(2)}, u32[]{:S(2)}) collective-permute-start(bf16[480,224]{1,0:T(8,128)(2,1)S(1)} %get-tuple-element.70), channel_id=1, source_target_pairs={{0,24},{8,16},{16,8},{24,0},{1,25},{9,17},{17,9},{25,1},{2,26},{10... | collective-permute-start | bytes 645128 | tf_op jit(solution)/shard_map/ppermute | solution.py:36
  56.4 48.0 %collective-permute-start.5 = (bf16[8,160,224]{2,1,0:T(8,128)(2,1)S(1)}, bf16[8,160,224]{2,1,0:T(8,128)(2,1)}, u32[]{:S(2)}, u32[]{:S(2)}) collective-permute-start(bf16[8,160,224]{2,1,0:T(8,128)(2,1)S(1)} %collective-permute-done.4.refs_2_), channel_id=1, source_target_pairs={{0,8},{8,0},{16,24},{24,16},{1,9},{9,1},{17,25},{25,17},{2,10},{10... | collective-permute-start | bytes 1720328 | tf_op jit(solution)/shard_map/ppermute | solution.py:36
  101.8 32.2 %collective-permute-start.7 = (bf16[480,896]{1,0:T(8,128)(2,1)S(1)}, bf16[480,896]{1,0:T(8,128)(2,1)}, u32[]{:S(2)}, u32[]{:S(2)}) collective-permute-start(bf16[480,896]{1,0:T(8,128)(2,1)S(1)} %join_lanes.1.refs_0_), channel_id=1, source_target_pairs={{0,2},{1,3},{2,0},{3,1},{4,6},{5,7},{6,4},{7,5},{8,10},{9,11},{10,... | collective-permute-start | bytes 2580488 | tf_op jit(solution)/shard_map/ppermute | solution.py:36
  101.8 41.3 %collective-permute-start.6 = (bf16[480,896]{1,0:T(8,128)(2,1)S(1)}, bf16[480,896]{1,0:T(8,128)(2,1)}, u32[]{:S(2)}, u32[]{:S(2)}) collective-permute-start(bf16[480,896]{1,0:T(8,128)(2,1)S(1)} %join_lanes.1.refs_0_), channel_id=1, source_target_pairs={{0,4},{1,5},{2,6},{3,7},{4,0},{5,1},{6,2},{7,3},{8,12},{9,13},{10,... | collective-permute-start | bytes 2580488 | tf_op jit(solution)/shard_map/ppermute | solution.py:36
  102.9 43.6 %collective-permute-start.11 = (bf16[8,112,224]{2,1,0:T(8,128)(2,1)S(1)}, bf16[8,112,224]{2,1,0:T(8,128)(2,1)}, u32[]{:S(2)}, u32[]{:S(2)}) collective-permute-start(bf16[8,112,224]{2,1,0:T(8,128)(2,1)S(1)} %bitcast.169), channel_id=1, source_target_pairs={{0,16},{8,24},{16,0},{24,8},{1,17},{9,25},{17,1},{25,9},{2,18},{10... | collective-permute-start | bytes 1204232 | tf_op jit(solution)/shard_map/ppermute | solution.py:36
  143.1 23.5 %collective-permute-start.9 = (bf16[480,896]{1,0:T(8,128)(2,1)}, bf16[480,896]{1,0:T(8,128)(2,1)}, u32[]{:S(2)}, u32[]{:S(2)}) collective-permute-start(bf16[480,896]{1,0:T(8,128)(2,1)} %collective-permute-done.7.refs_2_), channel_id=1, source_target_pairs={{0,1},{1,0},{2,3},{3,2},{4,5},{5,4},{6,7},{7,6},{8,9},{9,8},{10,11... | collective-permute-start | bytes 2580488 | tf_op jit(solution)/shard_map/ppermute | solution.py:36
  146.0 20.7 %collective-permute-start.8 = (bf16[384,896]{1,0:T(8,128)(2,1)S(1)}, bf16[384,896]{1,0:T(8,128)(2,1)}, u32[]{:S(2)}, u32[]{:S(2)}) collective-permute-start(bf16[384,896]{1,0:T(8,128)(2,1)S(1)} %copy-done.3), channel_id=1, source_target_pairs={{0,16},{8,24},{16,0},{24,8},{1,17},{9,25},{17,1},{25,9},{2,18},{10... | collective-permute-start | bytes 2064392 | tf_op jit(solution)/shard_map/ppermute | solution.py:36
  147.0 58.4 %collective-permute-start.13 = (bf16[480,896]{1,0:T(8,128)(2,1)S(1)}, bf16[480,896]{1,0:T(8,128)(2,1)}, u32[]{:S(2)}, u32[]{:S(2)}) collective-permute-start(bf16[480,896]{1,0:T(8,128)(2,1)S(1)} %join_lanes.1.refs_0_), channel_id=1, source_target_pairs={{0,1},{1,0},{2,3},{3,2},{4,5},{5,4},{6,7},{7,6},{8,9},{9,8},{10,11... | collective-permute-start | bytes 2580488 | tf_op jit(solution)/shard_map/ppermute | solution.py:36
  162.6 40.6 %collective-permute-start.15 = (bf16[480,896]{1,0:T(8,128)(2,1)}, bf16[480,896]{1,0:T(8,128)(2,1)}, u32[]{:S(2)}, u32[]{:S(2)}) collective-permute-start(bf16[480,896]{1,0:T(8,128)(2,1)} %collective-permute-done.7.refs_2_), channel_id=1, source_target_pairs={{0,4},{1,5},{2,6},{3,7},{4,0},{5,1},{6,2},{7,3},{8,12},{9,13},{10,... | collective-permute-start | bytes 2580488 | tf_op jit(solution)/shard_map/ppermute | solution.py:36
  162.7 40.0 %collective-permute-start.14 = (bf16[480,896]{1,0:T(8,128)(2,1)}, bf16[480,896]{1,0:T(8,128)(2,1)S(1)}, u32[]{:S(2)}, u32[]{:S(2)}) collective-permute-start(bf16[480,896]{1,0:T(8,128)(2,1)} %collective-permute-done.6.refs_4_), channel_id=1, source_target_pairs={{0,1},{1,0},{2,3},{3,2},{4,5},{5,4},{6,7},{7,6},{8,9},{9,8},{10,11... | collective-permute-start | bytes 2580488 | tf_op jit(solution)/shard_map/ppermute | solution.py:36
  203.2 20.9 %collective-permute-start.16 = (bf16[480,896]{1,0:T(8,128)(2,1)}, bf16[480,896]{1,0:T(8,128)(2,1)}, u32[]{:S(2)}, u32[]{:S(2)}) collective-permute-start(bf16[480,896]{1,0:T(8,128)(2,1)} %collective-permute-done.15.refs_6_), channel_id=1, source_target_pairs={{0,1},{1,0},{2,3},{3,2},{4,5},{5,4},{6,7},{7,6},{8,9},{9,8},{10,11... | collective-permute-start | bytes 2580488 | tf_op jit(solution)/shard_map/ppermute | solution.py:36
  263.6 21.0 %collective-permute-start.24 = (bf16[1,384,896]{2,1,0:T(8,128)(2,1)S(1)}, bf16[1,384,896]{2,1,0:T(8,128)(2,1)S(1)}, u32[]{:S(2)}, u32[]{:S(2)}) collective-permute-start(bf16[1,384,896]{2,1,0:T(8,128)(2,1)S(1)} %dynamic-slice_convert_fusion.1), channel_id=1, source_target_pairs={{0,16},{8,24},{16,0},{24,8},{1,17},{9,25},{17,1},{25,9},{2,18},{10... | collective-permute-start | bytes 2064392 | tf_op jit(solution)/shard_map/ppermute | solution.py:36
  269.8 17.5 %collective-permute-start.23 = (bf16[2,384,896]{2,1,0:T(8,128)(2,1)S(1)}, bf16[2,384,896]{2,1,0:T(8,128)(2,1)S(1)}, u32[]{:S(2)}, u32[]{:S(2)}) collective-permute-start(bf16[2,384,896]{2,1,0:T(8,128)(2,1)S(1)} %dynamic-slice_bitcast_fusion), channel_id=1, source_target_pairs={{0,8},{8,0},{16,24},{24,16},{1,9},{9,1},{17,25},{25,17},{2,10},{10... | collective-permute-start | bytes 4128776 | tf_op jit(solution)/shard_map/ppermute | solution.py:36
  282.7 44.7 %collective-permute-start.26 = (bf16[4,160,896]{2,1,0:T(8,128)(2,1)}, bf16[4,160,896]{2,1,0:T(8,128)(2,1)}, u32[]{:S(2)}, u32[]{:S(2)}) collective-permute-start(bf16[4,160,896]{2,1,0:T(8,128)(2,1)} %dynamic-slice_bitcast_fusion.5), channel_id=1, source_target_pairs={{0,1},{1,0},{2,3},{3,2},{4,5},{5,4},{6,7},{7,6},{8,9},{9,8},{10,11... | collective-permute-start | bytes 3440648 | tf_op jit(solution)/shard_map/ppermute | solution.py:36
  290.6 53.2 %collective-permute-start.37 = (bf16[4,160,896]{2,1,0:T(8,128)(2,1)}, bf16[4,160,896]{2,1,0:T(8,128)(2,1)}, u32[]{:S(2)}, u32[]{:S(2)}) collective-permute-start(bf16[4,160,896]{2,1,0:T(8,128)(2,1)} %dynamic-slice_bitcast_fusion.3), channel_id=1, source_target_pairs={{0,1},{1,0},{2,3},{3,2},{4,5},{5,4},{6,7},{7,6},{8,9},{9,8},{10,11... | collective-permute-start | bytes 3440648 | tf_op jit(solution)/shard_map/ppermute | solution.py:36
  327.4 51.4 %collective-permute-start.29 = (bf16[4,160,896]{2,1,0:T(8,128)(2,1)}, bf16[4,160,896]{2,1,0:T(8,128)(2,1)}, u32[]{:S(2)}, u32[]{:S(2)}) collective-permute-start(bf16[4,160,896]{2,1,0:T(8,128)(2,1)} %dynamic-slice_bitcast_fusion.4), channel_id=1, source_target_pairs={{0,1},{1,0},{2,3},{3,2},{4,5},{5,4},{6,7},{7,6},{8,9},{9,8},{10,11... | collective-permute-start | bytes 3440648 | tf_op jit(solution)/shard_map/ppermute | solution.py:36
  349.8 27.6 %collective-permute-start.38 = (bf16[2,160,896]{2,1,0:T(8,128)(2,1)}, bf16[2,160,896]{2,1,0:T(8,128)(2,1)}, u32[]{:S(2)}, u32[]{:S(2)}) collective-permute-start(bf16[2,160,896]{2,1,0:T(8,128)(2,1)} %fusion.24), channel_id=1, source_target_pairs={{0,4},{1,5},{2,6},{3,7},{4,0},{5,1},{6,2},{7,3},{8,12},{9,13},{10,... | collective-permute-start | bytes 1720328 | tf_op jit(solution)/shard_map/ppermute | solution.py:36
  350.7 28.2 %collective-permute-start.32 = (bf16[2,896,224]{1,2,0:T(8,128)(2,1)}, bf16[2,896,224]{1,2,0:T(8,128)(2,1)}, u32[]{:S(2)}, u32[]{:S(2)}) collective-permute-start(bf16[2,896,224]{1,2,0:T(8,128)(2,1)} %dynamic-slice_bitcast_fusion.6), channel_id=1, source_target_pairs={{0,8},{8,0},{16,24},{24,16},{1,9},{9,1},{17,25},{25,17},{2,10},{10... | collective-permute-start | bytes 2408456 | tf_op jit(solution)/shard_map/ppermute | solution.py:36
  390.7 40.0 %collective-permute-start.42 = (bf16[2,160,896]{2,1,0:T(8,128)(2,1)}, bf16[2,160,896]{2,1,0:T(8,128)(2,1)}, u32[]{:S(2)}, u32[]{:S(2)}) collective-permute-start(bf16[2,160,896]{2,1,0:T(8,128)(2,1)} %fusion.26), channel_id=1, source_target_pairs={{0,4},{1,5},{2,6},{3,7},{4,0},{5,1},{6,2},{7,3},{8,12},{9,13},{10,... | collective-permute-start | bytes 1720328 | tf_op jit(solution)/shard_map/ppermute | solution.py:36
  392.5 50.4 %collective-permute-start.40 = (bf16[2,160,896]{2,1,0:T(8,128)(2,1)}, bf16[2,160,896]{2,1,0:T(8,128)(2,1)}, u32[]{:S(2)}, u32[]{:S(2)}) collective-permute-start(bf16[2,160,896]{2,1,0:T(8,128)(2,1)} %fusion.25), channel_id=1, source_target_pairs={{0,4},{1,5},{2,6},{3,7},{4,0},{5,1},{6,2},{7,3},{8,12},{9,13},{10,... | collective-permute-start | bytes 1720328 | tf_op jit(solution)/shard_map/ppermute | solution.py:36
  397.2 35.2 %collective-permute-start.31 = (bf16[1,8,160,224]{3,2,1,0:T(8,128)(2,1)}, bf16[1,8,160,224]{3,2,1,0:T(8,128)(2,1)}, u32[]{:S(2)}, u32[]{:S(2)}) collective-permute-start(bf16[1,8,160,224]{3,2,1,0:T(8,128)(2,1)} %dynamic-slice_convert_fusion.2), channel_id=1, source_target_pairs={{0,16},{8,24},{16,0},{24,8},{1,17},{9,25},{17,1},{25,9},{2,18},{10... | collective-permute-start | bytes 1720328 | tf_op jit(solution)/shard_map/ppermute | solution.py:36
  (85 other events, 825.9 us)

commit v4 on v3

--- a/solution.py
+++ b/solution.py
@@ -57,6 +57,11 @@
         (outer_bits if bit >= inner else inner_bits).append(bit)
         bit *= 2
     return outer_bits + inner_bits
+
+
+def column_gather(block, size):
+    inner = size // OUTER
+    return jnp.stack([block] + [swap(block, "fsdp", size, k * inner) for k in range(1, OUTER)])
 
 
 def ff_spread(block, size):
@@ -170,25 +175,38 @@
     )[0]
 
 
-def join_both(me, blocks, rows):
-    size = len(blocks)
-    count, tall, width = blocks[0].shape
+def join_both(me, pieces, rows):
+    size, parts_each = len(pieces), len(pieces[0])
+    _, tall, width = pieces[0][0].shape
+    count = sum(part.shape[0] for part in pieces[0])
+    inner = count // OUTER
+    order = [k * inner + m for m in range(inner) for k in range(OUTER)]
     shapes = [jax.ShapeDtypeStruct((count, rows, size * width), BF16)]
     if tall > rows:
         shapes.append(jax.ShapeDtypeStruct((count, tall - rows, width), BF16))
 
     def body(me_ref, *refs):
-        ins, out, held = refs[:size], refs[size], refs[-1]
+        ins, out, held = refs[: size * parts_each], refs[size * parts_each], refs[-1]
         for o in range(size):
-            held[me_ref[0] ^ o] = ins[o][...]
+            at = 0
+            for part in ins[o * parts_each : (o + 1) * parts_each]:
+                for j in range(part.shape[0]):
+                    place = me_ref[1] ^ order[at]
+                    held[me_ref[0] ^ o, place] = part[j]
+                    if tall > rows and o == 0:
+                        refs[size * parts_each + 1][place] = part[j, rows:]
+                    at += 1
         for f in range(count):
             parts = [held[q, f, :rows].astype(F32) for q in range(size)]
             out[f] = jnp.concatenate(parts, axis=1).astype(BF16)
-            if tall > rows:
-                refs[size + 1][f] = ins[0][f, rows:]
 
     return on_device(
-        body, "join_both", shapes, [pltpu.VMEM((size, count, tall, width), BF16)], me, blocks
+        body,
+        "join_both",
+        shapes,
+        [pltpu.VMEM((size, count, tall, width), BF16)],
+        me,
+        [block for row in pieces for block in row],
     )
 
 
@@ -587,23 +605,26 @@
             pad_row(qkv_bias, width),
             pad_row(norm_two, width),
             jnp.zeros((13, width), BF16),
+            out_weight,
         ],
         axis=0,
     )
     ff_cut = cut_ff(me, gate_up_weight, down_weight, seq_size)
     ff_share = [ff_cut[0]] + [swap(ff_cut[o], "seq", seq_size, o) for o in offsets if o]
-    packed_stack, out_stack = lax.all_gather((after(packed, ff_cut[0]), out_weight), "fsdp", axis=0)
-    packed_blocks = seq_gather(packed_stack, seq_size)
+    columns = ff_spread(after(column_gather(packed, fsdp_size), ff_cut[1]), fsdp_size)
     ff_block = join_lanes(me, ff_share)
+    wide = qkv_tall + 16
+    packed_stack = jnp.concatenate([columns[m][:, :wide] for m in sorted(columns)], axis=0)
+    out_stack = jnp.concatenate([columns[m][:, wide:] for m in sorted(columns)], axis=0)
+    packed_blocks = seq_gather(after(packed_stack, ff_block), seq_size)
     ff_blocks = {0: ff_block}
     for bit in fsdp_bits(fsdp_size)[:2]:
         ff_blocks.update({o ^ bit: swap(b, "fsdp", fsdp_size, bit) for o, b in ff_blocks.items()})
     inner = fsdp_size // OUTER
 
-    qkv_blocks = [packed_blocks[o] for o in offsets]
-    qkv_blocks[0] = after(qkv_blocks[0], ff_block)
-    qkv_t, vectors = join_both(me, qkv_blocks, qkv_tall)
-    qkv_t = qkv_t[:, :qkv_rows].reshape(fsdp_size * qkv_rows, -1)
+    qkv_pieces = [[packed_blocks[o]] for o in offsets]
+    qkv_t, vectors = join_both(me, qkv_pieces, qkv_tall)
+    qkv_t = after(qkv_t, ff_blocks[2 * inner], ff_blocks[inner])[:, :qkv_rows].reshape(fsdp_size * qkv_rows, -1)
     gain_one = vectors[:, 0, : norm_one.shape[0]].reshape(-1).astype(F32)
     bias_full = vectors[:, 1, : qkv_bias.shape[0]].reshape(-1).astype(F32)
     gain_two = vectors[:, 2, : norm_two.shape[0]].reshape(-1).astype(F32)
@@ -618,7 +639,6 @@
     turned = rotate(joined[:, : QW + KVW], cosine, sine).astype(BF16)
     queries = turned[:, :QW] * jnp.asarray(0.125, BF16)
     kv_local = jnp.concatenate([turned[:, QW:], joined[:, QW + KVW :].astype(BF16)], axis=1)
-    kv_local = after(kv_local, ff_blocks[inner])
     kv_all = lax.all_gather(kv_local, "seq", axis=0, tiled=True)
     kv_all = after(kv_all, ff_blocks[2 * inner], ff_blocks[inner])
     cot_blocks = seq_gather(after(cotangent, kv_all), seq_size)
@@ -635,20 +655,31 @@
     near_x = spread(after(near, kv_all))
     attn_one, lse_one = attend(low, high, place, after(queries, far), kv_all, 0, split)
     far_x = spread(after(far, kv_all))
-    queries_two = after(queries, attn_one, cot_blocks[seq_size // 2], *near_x.values())
+    queries_two = after(queries, attn_one, cot_blocks[seq_size // 2])
     attn_two, lse_two = attend(low, high, place, queries_two, kv_all, split, PAIRS - split)
-    last_x = spread(after(last, attn_two))
+    last_x = spread(last)
     for base, row in ((0, own_x), (inner, near_x), (2 * inner, far_x), (3 * inner, last_x)):
         ff_blocks.update({base + m: block for m, block in row.items()})
     attn_flat = jnp.concatenate([attn_one, attn_two], axis=1)
 
-    out_list = [after(out_blocks[0], attn_one)] + [out_blocks[o] for o in offsets if o]
+    out_list = [[out_blocks[o]] for o in offsets]
+    out_list[0][0] = after(out_list[0][0], attn_one)
     out_full = join_both(me, out_list, out_weight.shape[0])[0].reshape(QW, -1)
 
     residual = inputs + dot(attn_flat, out_full, 1, 0)
     scale_two = rms_scale(residual)
     normed_two = (residual * scale_two * gain_two).astype(BF16)
-    normed_blocks = seq_gather(after(normed_two, *far_x.values()), seq_size)
+    normed_two = after(normed_two, *near_x.values())
+    normed_blocks = {0: normed_two}
+    bit = seq_size // 2
+    while bit:
+        if bit == 1:
+            top = seq_size // 2
+            normed_blocks[top] = after(normed_blocks[top], last, *far_x.values())
+        normed_blocks.update(
+            {o ^ bit: swap(b, "seq", seq_size, bit) for o, b in normed_blocks.items()}
+        )
+        bit //= 2
     hidden, grad_gate, grad_up, grad_normed, layer_part, normed_all, cot_all = feed_forward(
         me,
         [ff_blocks[o] for o in range(fsdp_size)],
@@ -695,21 +726,16 @@
 
     kept, given = halve(after(by_seq(layer_part), down_term), 1, my_seq)
     layer_sum = add(kept, swap(given, "seq", seq_size, 1))
-    bit = 2
-    while bit < seq_size:
-        kept, given = halve(layer_sum, 1, my_seq // bit)
-        given = after(given, grad_normed_two)
-        layer_sum = add(kept, swap(given, "seq", seq_size, bit))
-        bit *= 2
-    layer_out = residual + layer_sum[0]
+    kept_layer, given_layer = halve(layer_sum, 1, my_seq // 2)
 
     grad_path, norm_two_term = norm_back(grad_normed_two, residual, scale_two, gain_two)
     grad_residual = cotangent.astype(F32) + grad_path
     grad_branch = grad_residual.astype(BF16)
     grad_attn = dot(grad_branch, out_full, 1, 1).astype(BF16)
     out_term = stack_from_lanes(dot(attn_flat, grad_branch, 0, 0).astype(BF16), seq_size)
-    out_mine = seq_scatter(out_term, seq_size, my_seq).reshape(fsdp_size, -1, width)
-    grad_attn = after(grad_attn, gate_term, up_term)
+    kept, given = halve(out_term, 1, my_seq)
+    out_sum = add(kept, swap(given, "seq", seq_size, 1))
+    grad_attn = after(grad_attn, gate_term, up_term, given_layer)
     dq_one, kv_terms = attend_back(
         low, high, place, queries, grad_attn, attn_one, lse_one, kv_all, 0, split, ()
     )
@@ -723,10 +749,24 @@
         PAIRS - split, (kv_terms,),
     )
     got_two = after(got_two, dq_two)
-    down_sum = finish(kept_one, after(next_one, dq_two), 1)
+    next_one = after(next_one, dq_two)
+    down_sum = finish(kept_one, next_one, 1)
     kept_two, given = give(add(kept_two, got_two), 1)
     next_two = send(given, 1)
-    kv_mine = seq_scatter(by_seq(kv_terms), seq_size, my_seq)
+    kept, given = halve(by_seq(kv_terms), 1, my_seq)
+    kv_sum = add(kept, swap(given, "seq", seq_size, 1))
+    bit = 2
+    while bit < seq_size:
+        kept, given = halve(kv_sum, 1, my_seq // bit)
+        kv_sum = add(kept, swap(after(given, got_two), "seq", seq_size, bit))
+        bit *= 2
+    kv_mine = kv_sum[0]
+    bit = 2
+    while bit < seq_size:
+        kept, given = halve(out_sum, 1, my_seq // bit)
+        out_sum = add(kept, swap(after(given, kv_mine), "seq", seq_size, bit))
+        bit *= 2
+    out_mine = out_sum[0].reshape(fsdp_size, -1, width)
     got_three = after(got_three, kv_mine)
     kept_three, given = give(add(kept_three, got_three), 1)
     next_three = send(given, 1)
@@ -751,8 +791,17 @@
     tail = jnp.concatenate(
         [qkv_term, jnp.broadcast_to(small[None], (seq_size,) + small.shape)], axis=2
     )
-    tail_mine = seq_scatter(after(tail, got_three), seq_size, my_seq)
-    one_sum = finish(kept_two, after(next_two, tail), 1)
+    tail = after(tail, next_two)
+    tail_mine = seq_scatter(tail, seq_size, my_seq)
+    got_layer = swap(after(given_layer, tail_mine), "seq", seq_size, 2)
+    layer_sum = add(kept_layer, got_layer)
+    bit = 4
+    while bit < seq_size:
+        kept, given = halve(layer_sum, 1, my_seq // bit)
+        layer_sum = add(kept, swap(given, "seq", seq_size, bit))
+        bit *= 2
+    layer_out = residual + layer_sum[0]
+    one_sum = finish(kept_two, next_two, 1)
     two_sum = finish(kept_three, next_three, 1)
 
     ff_back = cut_lanes(me, (one_sum, two_sum, down_sum), seq_size)
@@ -760,7 +809,7 @@
     grad_gate_up, grad_down = join_ff(me, ff_got, strip)
 
     tail_sum = fsdp_scatter(
-        jnp.concatenate([tail_mine, out_mine], axis=1), fsdp_size, my_fsdp
+        after(jnp.concatenate([tail_mine, out_mine], axis=1), next_three), fsdp_size, my_fsdp
     )
     pieces = [
         tail_sum[qkv_rows + i, : v.shape[0] // fsdp_size] for i, v in enumerate(vector_terms)

time: 484 us -> 417 us (0.86)
  blocking collectives: 73.8 us -> 8.27 us
  waiting for transfers between devices: 161 us -> 150 us
  starting transfers between devices: 32.2 us -> 40.2 us
    all_gather x2 -> x0, blocking collectives: 64.7 us -> none  [per_device(): lax.all_gather((after(packed, ff_cut[0]), out_weight), 'fsdp', axis=0)]
    ppermute x47 -> x51, waiting for transfers between devices: 161 us -> 150 us  [swap(): return lax.ppermute(block, axis, [(i, i ^ bits) for i in range(size)])]
    ppermute x47 -> x51, starting transfers between devices: 32.2 us -> 40.2 us  [swap(): return lax.ppermute(block, axis, [(i, i ^ bits) for i in range(size)])]
    unnamed x128 -> x130, local copies, waits for them, and re-layouts: 23.6 us -> 17.3 us
  transfers between devices with their start and end apart: 47 -> 51, of which waited for: 16 -> 19; matrix products, arithmetic and copies ran while one was open for 16% -> 21% of each run, Pallas kernels for 14% -> 16%
where the time goes in v4:
time: 417 us; the launch traced here: 410 us
  waiting for transfers between devices  150 us (36%)
  Pallas kernels  97.5 us (23%)
  local copies, waits for them, and re-layouts  55.7 us (13%)
  starting transfers between devices  40.2 us (10%)
  other arithmetic  29.8 us (7%)
  matrix products  26.5 us (6%)
  blocking collectives  8.27 us (2%)
    ppermute x51, waiting for transfers between devices, swap(): return lax.ppermute(block, axis, [(i, i ^ bits) for i in range(size)])  150 us
    ppermute x51, starting transfers between devices, swap(): return lax.ppermute(block, axis, [(i, i ^ bits) for i in range(size)])  40.2 us
    pallas_call x2, Pallas kernels, attend_back(): pl.pallas_call(functools.partial(attend_back_kernel, begin), grid=(pairs,...  32.6 us
    pallas_call x1, Pallas kernels, feed_forward(): pl.pallas_call(body, grid=(size,), in_specs=[pl.BlockSpec(memory_space=pl...  32 us
    dot_general x9, matrix products, dot(): lax.dot_general(left, right, (((left_dim,), (right_dim,)), ((), ())), pre...  26.5 us
    pallas_call x2, Pallas kernels, attend(): pl.pallas_call(functools.partial(attend_kernel, begin), grid=(pairs,), in...  23.4 us
    unnamed x130, local copies, waits for them, and re-layouts  17.3 us
    add x15, other arithmetic, add(): return kept.astype(F32) + got.astype(F32)  14.9 us
  transfers between devices with their start and end apart: 51, of which 19 were waited for; matrix products, arithmetic and copies ran while one was open for 21% of the time, Pallas kernels for 16%

profile of v4, /device:TPU:0, one launch (start us, length us, event | category | flops | bytes accessed | tf_op | source)
XLA Modules:
  0.0 409.8 jit_solution(14381332190936078733)
XLA Ops:
  13.3 7.7 %collective-permute-done.1 = bf16[272,224]{1,0:T(8,128)(2,1)S(1)} collective-permute-done((bf16[272,224]{1,0:T(8,128)(2,1)S(1)}, bf16[272,224]{1,0:T(8,128)(2,1)S(1)}, u32[]{:S(2)}, u32[]{:S(2)}) %collective-permute-start.1) | collective-permute-done | bytes 121888 | tf_op jit(solution)/shard_map/ppermute | solution.py:36
  24.6 6.9 %collective-permute-done.5.refs_2_ = bf16[480,224]{1,0:T(8,128)(2,1)S(1)} collective-permute-done((bf16[480,224]{1,0:T(8,128)(2,1)S(1)}, bf16[480,224]{1,0:T(8,128)(2,1)S(1)}, u32[]{:S(2)}, u32[]{:S(2)}) %collective-permute-start.5) | collective-permute-done | bytes 215072 | tf_op jit(solution)/shard_map/ppermute | solution.py:36
  31.4 4.5 %collective-permute-done.6.refs_3_ = bf16[480,224]{1,0:T(8,128)(2,1)S(1)} collective-permute-done((bf16[480,224]{1,0:T(8,128)(2,1)S(1)}, bf16[480,224]{1,0:T(8,128)(2,1)S(1)}, u32[]{:S(2)}, u32[]{:S(2)}) %collective-permute-start.6) | collective-permute-done | bytes 215072 | tf_op jit(solution)/shard_map/ppermute | solution.py:36
  49.2 5.4 %collective-permute-done.8.refs_2_ = bf16[8,160,224]{2,1,0:T(8,128)(2,1)S(1)} collective-permute-done((bf16[8,160,224]{2,1,0:T(8,128)(2,1)S(1)}, bf16[8,160,224]{2,1,0:T(8,128)(2,1)S(1)}, u32[]{:S(2)}, u32[]{:S(2)}) %collective-permute-start.8) | collective-permute-done | bytes 573472 | tf_op jit(solution)/shard_map/ppermute | solution.py:36
  60.3 20.8 %collective-permute-done.10.refs_4_ = bf16[480,896]{1,0:T(8,128)(2,1)} collective-permute-done((bf16[480,896]{1,0:T(8,128)(2,1)S(1)}, bf16[480,896]{1,0:T(8,128)(2,1)}, u32[]{:S(2)}, u32[]{:S(2)}) %collective-permute-start.10) | collective-permute-done | bytes 860192 | tf_op jit(solution)/shard_map/ppermute | solution.py:36
  87.1 8.3 %all_gather.3.kv_ref = bf16[1536,256]{1,0:T(8,128)(2,1)S(1)} all-gather(bf16[384,256]{1,0:T(8,128)(2,1)S(1)} %pad_maximum_fusion.11), channel_id=1, replica_groups=mesh['seq'=4,'fsdp'=8] {'seq'}, dimensions={0}, use_global_device_ids=true | all-gather | bytes 983040 | tf_op jit(solution)/shard_map/all_gather | solution.py:642
  99.5 13.4 %attend.2 = (bf16[384,512]{1,0:T(8,128)(2,1)S(1)}, f32[4,1,768]{2,1,0:T(1,128)S(1)}) custom-call(s32[1,384]{1,0:T(1,128)S(1)} %broadcast_in_dim.12.low_ref, s32[1,384]{1,0:T(1,128)S(1)} %iota_add_fusion.high_ref, s32[1536,1]{1,0:T(8,128)S(1)} %iota.43.place_ref, bf16[384,896]{1,0:T(8,128)(2,1)S(1)} %slice_multiply_fusion.1.q_ref, ...), custom_call_target="tpu_custom_call" | custom-call | flops 1 | bytes 1 | tf_op jit(solution)/shard_map/attend/pallas_call | solution.py:479
  118.9 10.0 %attend.3 = (bf16[384,384]{1,0:T(8,128)(2,1)S(1)}, f32[3,1,768]{2,1,0:T(1,128)S(1)}) custom-call(s32[1,384]{1,0:T(1,128)S(1)} %broadcast_in_dim.12.low_ref, s32[1,384]{1,0:T(1,128)S(1)} %iota_add_fusion.high_ref, s32[1536,1]{1,0:T(8,128)S(1)} %iota.49.place_ref, bf16[384,896]{1,0:T(8,128)(2,1)S(1)} %slice_multiply_fusion.1.q_ref, ...), custom_call_target="tpu_custom_call" | custom-call | flops 1 | bytes 1 | tf_op jit(solution)/shard_map/attend/pallas_call | solution.py:479
  130.3 7.6 %collective-permute-done.17.refs_3_ = bf16[480,896]{1,0:T(8,128)(2,1)S(1)} collective-permute-done((bf16[480,896]{1,0:T(8,128)(2,1)}, bf16[480,896]{1,0:T(8,128)(2,1)S(1)}, u32[]{:S(2)}, u32[]{:S(2)}) %collective-permute-start.17) | collective-permute-done | bytes 860192 | tf_op jit(solution)/shard_map/ppermute | solution.py:36
  139.9 16.4 %collective-permute-done.18.refs_5_ = bf16[480,896]{1,0:T(8,128)(2,1)S(1)} collective-permute-done((bf16[480,896]{1,0:T(8,128)(2,1)}, bf16[480,896]{1,0:T(8,128)(2,1)S(1)}, u32[]{:S(2)}, u32[]{:S(2)}) %collective-permute-start.18) | collective-permute-done | bytes 860192 | tf_op jit(solution)/shard_map/ppermute | solution.py:36
  157.2 16.7 %collective-permute-done.20.refs_7_ = bf16[480,896]{1,0:T(8,128)(2,1)} collective-permute-done((bf16[480,896]{1,0:T(8,128)(2,1)}, bf16[480,896]{1,0:T(8,128)(2,1)}, u32[]{:S(2)}, u32[]{:S(2)}) %collective-permute-start.20) | collective-permute-done | bytes 860192 | tf_op jit(solution)/shard_map/ppermute | solution.py:36
  175.9 32.0 %feed_forward.1 = (bf16[1536,1280]{1,0:T(8,128)(2,1)}, bf16[1536,1280]{1,0:T(8,128)(2,1)}, bf16[1536,1280]{1,0:T(8,128)(2,1)}, bf16[1536,896]{1,0:T(8,128)(2,1)}...) custom-call(s32[2]{0:T(128)S(1)} %pad_add_fusion.me_ref, ...), custom_call_target="tpu_custom_call" | custom-call | flops 1 | bytes 1 | tf_op jit(solution)/shard_map/feed_forward/pallas_call | solution.py:313
  216.1 4.5 %convolution_convert_fusion.3 = bf16[1280,896]{1,0:T(8,128)(2,1)S(1)} fusion(bf16[1536,1280]{1,0:T(8,128)(2,1)S(1)} %copy-done.59, bf16[1536,896]{1,0:T(8,128)(2,1)S(1)} %copy-done.61), kind=kOutput, calls=%fused_computation.3 | convolution fusion | flops 3524362240 | bytes 8978432 | tf_op jit(solution)/shard_map/dot_general | solution.py:30
  220.6 4.5 %convolution_convert_fusion.1 = bf16[1280,896]{1,0:T(8,128)(2,1)S(1)} fusion(bf16[1536,1280]{1,0:T(8,128)(2,1)S(1)} %copy-done.58, bf16[1536,896]{1,0:T(8,128)(2,1)S(1)} %copy-done.60), kind=kOutput, calls=%fused_computation.1 | convolution fusion | flops 3524362240 | bytes 8978432 | tf_op jit(solution)/shard_map/dot_general | solution.py:30
  225.2 4.8 %convolution_convert_fusion.2 = bf16[1280,896]{1,0:T(8,128)(2,1)S(1)} fusion(bf16[1536,1280]{1,0:T(8,128)(2,1)S(1)} %copy-done.57, bf16[1536,896]{1,0:T(8,128)(2,1)S(1)} %copy-done.60), kind=kOutput, calls=%fused_computation.2 | convolution fusion | flops 3524362240 | bytes 8978432 | tf_op jit(solution)/shard_map/dot_general | solution.py:30
  249.9 18.0 %attend_back.2 = (f32[384,512]{1,0:T(8,128)S(1)}, f32[1536,256]{1,0:T(8,128)}) custom-call(s32[1,384]{1,0:T(1,128)S(1)} %broadcast_in_dim.12.low_ref, s32[1,384]{1,0:T(1,128)S(1)} %iota_add_fusion.high_ref, s32[1536,1]{1,0:T(8,128)S(1)} %iota.50.place_ref, bf16[384,896]{1,0:T(8,128)(2,1)S(1)} %slice_multiply_fusion.1.q_ref, ...), custom_call_target="tpu_custom_call" | custom-call | flops 1 | bytes 1 | tf_op jit(solution)/shard_map/attend_back/pallas_call | solution.py:505
  271.7 14.6 %attend_back.3 = (f32[384,384]{1,0:T(8,128)S(1)}, f32[1536,256]{1,0:T(8,128)}) custom-call(s32[1,384]{1,0:T(1,128)S(1)} %broadcast_in_dim.12.low_ref, s32[1,384]{1,0:T(1,128)S(1)} %iota_add_fusion.high_ref, s32[1536,1]{1,0:T(8,128)S(1)} %iota.51.place_ref, bf16[384,896]{1,0:T(8,128)(2,1)S(1)} %slice_multiply_fusion.1.q_ref, ...), custom_call_target="tpu_custom_call" | custom-call | flops 1 | bytes 1 | tf_op jit(solution)/shard_map/attend_back/pallas_call | solution.py:505
  295.9 14.9 %collective-permute-done.46 = bf16[2,160,896]{2,1,0:T(8,128)(2,1)} collective-permute-done((bf16[2,160,896]{2,1,0:T(8,128)(2,1)S(1)}, bf16[2,160,896]{2,1,0:T(8,128)(2,1)}, u32[]{:S(2)}, u32[]{:S(2)}) %collective-permute-start.46) | collective-permute-done | bytes 573472 | tf_op jit(solution)/shard_map/ppermute | solution.py:36
  340.1 4.0 collective-permute-done.38
  347.4 17.0 %collective-permute-done.40 = bf16[2,160,896]{2,1,0:T(8,128)(2,1)} collective-permute-done((bf16[2,160,896]{2,1,0:T(8,128)(2,1)}, bf16[2,160,896]{2,1,0:T(8,128)(2,1)}, u32[]{:S(2)}, u32[]{:S(2)}) %collective-permute-start.40) | collective-permute-done | bytes 573472 | tf_op jit(solution)/shard_map/ppermute | solution.py:36
  369.8 4.7 %collective-permute-done.45 = bf16[1,160,896]{2,1,0:T(8,128)(2,1)S(1)} collective-permute-done((bf16[1,160,896]{2,1,0:T(8,128)(2,1)S(1)}, bf16[1,160,896]{2,1,0:T(8,128)(2,1)S(1)}, u32[]{:S(2)}, u32[]{:S(2)}) %collective-permute-start.45) | collective-permute-done | bytes 286752 | tf_op jit(solution)/shard_map/ppermute | solution.py:36
  377.8 4.2 %collective-permute-done.41 = bf16[4,272,224]{2,1,0:T(8,128)(2,1)S(1)} collective-permute-done((bf16[4,272,224]{2,1,0:T(8,128)(2,1)S(1)}, bf16[4,272,224]{2,1,0:T(8,128)(2,1)S(1)}, u32[]{:S(2)}, u32[]{:S(2)}) %collective-permute-start.41) | collective-permute-done | bytes 487456 | tf_op jit(solution)/shard_map/ppermute | solution.py:36
  391.9 5.3 %collective-permute-done.42 = bf16[2,272,224]{2,1,0:T(8,128)(2,1)S(1)} collective-permute-done((bf16[2,272,224]{2,1,0:T(8,128)(2,1)}, bf16[2,272,224]{2,1,0:T(8,128)(2,1)S(1)}, u32[]{:S(2)}, u32[]{:S(2)}) %collective-permute-start.42) | collective-permute-done | bytes 243744 | tf_op jit(solution)/shard_map/ppermute | solution.py:36
  397.4 6.7 %collective-permute-done.36 = bf16[1,384,896]{2,1,0:T(8,128)(2,1)} collective-permute-done((bf16[1,384,896]{2,1,0:T(8,128)(2,1)}, bf16[1,384,896]{2,1,0:T(8,128)(2,1)}, u32[]{:S(2)}, u32[]{:S(2)}) %collective-permute-start.36) | collective-permute-done | bytes 688160 | tf_op jit(solution)/shard_map/ppermute | solution.py:36
  (352 shorter events, 154.9 us)
Async XLA Ops:
  40.0 41.1 %collective-permute-start.10 = (bf16[480,896]{1,0:T(8,128)(2,1)S(1)}, bf16[480,896]{1,0:T(8,128)(2,1)}, u32[]{:S(2)}, u32[]{:S(2)}) collective-permute-start(bf16[480,896]{1,0:T(8,128)(2,1)S(1)} %join_lanes.1.refs_0_), channel_id=1, source_target_pairs={{0,4},{1,5},{2,6},{3,7},{4,0},{5,1},{6,2},{7,3},{8,12},{9,13},{10,... | collective-permute-start | bytes 2580488 | tf_op jit(solution)/shard_map/ppermute | solution.py:36
  43.2 38.0 %collective-permute-start.11 = (bf16[480,896]{1,0:T(8,128)(2,1)S(1)}, bf16[480,896]{1,0:T(8,128)(2,1)}, u32[]{:S(2)}, u32[]{:S(2)}) collective-permute-start(bf16[480,896]{1,0:T(8,128)(2,1)S(1)} %join_lanes.1.refs_0_), channel_id=1, source_target_pairs={{0,2},{1,3},{2,0},{3,1},{4,6},{5,7},{6,4},{7,5},{8,10},{9,11},{10,... | collective-permute-start | bytes 2580488 | tf_op jit(solution)/shard_map/ppermute | solution.py:36
  55.9 41.0 %collective-permute-start.14 = (bf16[8,112,224]{2,1,0:T(8,128)(2,1)S(1)}, bf16[8,112,224]{2,1,0:T(8,128)(2,1)}, u32[]{:S(2)}, u32[]{:S(2)}) collective-permute-start(bf16[8,112,224]{2,1,0:T(8,128)(2,1)S(1)} %pad_maximum_fusion.8.refs_0_), channel_id=1, source_target_pairs={{0,16},{8,24},{16,0},{24,8},{1,17},{9,25},{17,1},{25,9},{2,18},{10... | collective-permute-start | bytes 1204232 | tf_op jit(solution)/shard_map/ppermute | solution.py:36
  95.3 23.5 %collective-permute-start.12 = (bf16[384,896]{1,0:T(8,128)(2,1)S(1)}, bf16[384,896]{1,0:T(8,128)(2,1)}, u32[]{:S(2)}, u32[]{:S(2)}) collective-permute-start(bf16[384,896]{1,0:T(8,128)(2,1)S(1)} %copy-done.3), channel_id=1, source_target_pairs={{0,16},{8,24},{16,0},{24,8},{1,17},{9,25},{17,1},{25,9},{2,18},{10... | collective-permute-start | bytes 2064392 | tf_op jit(solution)/shard_map/ppermute | solution.py:36
  96.9 19.4 %collective-permute-start.15 = (bf16[8,112,224]{2,1,0:T(8,128)(2,1)}, bf16[8,112,224]{2,1,0:T(8,128)(2,1)}, u32[]{:S(2)}, u32[]{:S(2)}) collective-permute-start(bf16[8,112,224]{2,1,0:T(8,128)(2,1)} %collective-permute-done.14.refs_2_), channel_id=1, source_target_pairs={{0,8},{8,0},{16,24},{24,16},{1,9},{9,1},{17,25},{25,17},{2,10},{10... | collective-permute-start | bytes 1204232 | tf_op jit(solution)/shard_map/ppermute | solution.py:36
  97.4 59.4 %collective-permute-start.16 = (bf16[480,896]{1,0:T(8,128)(2,1)S(1)}, bf16[480,896]{1,0:T(8,128)(2,1)}, u32[]{:S(2)}, u32[]{:S(2)}) collective-permute-start(bf16[480,896]{1,0:T(8,128)(2,1)S(1)} %join_lanes.1.refs_0_), channel_id=1, source_target_pairs={{0,1},{1,0},{2,3},{3,2},{4,5},{5,4},{6,7},{7,6},{8,9},{9,8},{10,11... | collective-permute-start | bytes 2580488 | tf_op jit(solution)/shard_map/ppermute | solution.py:36
  98.0 40.5 %collective-permute-start.19 = (bf16[480,896]{1,0:T(8,128)(2,1)}, bf16[480,896]{1,0:T(8,128)(2,1)}, u32[]{:S(2)}, u32[]{:S(2)}) collective-permute-start(bf16[480,896]{1,0:T(8,128)(2,1)} %collective-permute-done.11.refs_2_), channel_id=1, source_target_pairs={{0,4},{1,5},{2,6},{3,7},{4,0},{5,1},{6,2},{7,3},{8,12},{9,13},{10,... | collective-permute-start | bytes 2580488 | tf_op jit(solution)/shard_map/ppermute | solution.py:36
  114.8 23.0 %collective-permute-start.17 = (bf16[480,896]{1,0:T(8,128)(2,1)}, bf16[480,896]{1,0:T(8,128)(2,1)S(1)}, u32[]{:S(2)}, u32[]{:S(2)}) collective-permute-start(bf16[480,896]{1,0:T(8,128)(2,1)} %collective-permute-done.11.refs_2_), channel_id=1, source_target_pairs={{0,1},{1,0},{2,3},{3,2},{4,5},{5,4},{6,7},{7,6},{8,9},{9,8},{10,11... | collective-permute-start | bytes 2580488 | tf_op jit(solution)/shard_map/ppermute | solution.py:36
  116.4 39.9 %collective-permute-start.18 = (bf16[480,896]{1,0:T(8,128)(2,1)}, bf16[480,896]{1,0:T(8,128)(2,1)S(1)}, u32[]{:S(2)}, u32[]{:S(2)}) collective-permute-start(bf16[480,896]{1,0:T(8,128)(2,1)} %collective-permute-done.10.refs_4_), channel_id=1, source_target_pairs={{0,1},{1,0},{2,3},{3,2},{4,5},{5,4},{6,7},{7,6},{8,9},{9,8},{10,11... | collective-permute-start | bytes 2580488 | tf_op jit(solution)/shard_map/ppermute | solution.py:36
  137.9 18.4 %collective-permute-start.22 = (bf16[384,896]{1,0:T(8,128)(2,1)S(1)}, bf16[384,896]{1,0:T(8,128)(2,1)}, u32[]{:S(2)}, u32[]{:S(2)}) collective-permute-start(bf16[384,896]{1,0:T(8,128)(2,1)S(1)} %multiply_convert_fusion.refs_8_), channel_id=1, source_target_pairs={{0,16},{8,24},{16,0},{24,8},{1,17},{9,25},{17,1},{25,9},{2,18},{10... | collective-permute-start | bytes 2064392 | tf_op jit(solution)/shard_map/ppermute | solution.py:36
  138.5 35.5 %collective-permute-start.20 = (bf16[480,896]{1,0:T(8,128)(2,1)}, bf16[480,896]{1,0:T(8,128)(2,1)}, u32[]{:S(2)}, u32[]{:S(2)}) collective-permute-start(bf16[480,896]{1,0:T(8,128)(2,1)} %collective-permute-done.19.refs_6_), channel_id=1, source_target_pairs={{0,1},{1,0},{2,3},{3,2},{4,5},{5,4},{6,7},{7,6},{8,9},{9,8},{10,11... | collective-permute-start | bytes 2580488 | tf_op jit(solution)/shard_map/ppermute | solution.py:36
  215.5 22.2 %collective-permute-start.28 = (bf16[1,384,896]{2,1,0:T(8,128)(2,1)S(1)}, bf16[1,384,896]{2,1,0:T(8,128)(2,1)S(1)}, u32[]{:S(2)}, u32[]{:S(2)}) collective-permute-start(bf16[1,384,896]{2,1,0:T(8,128)(2,1)S(1)} %dynamic-slice_convert_fusion.1), channel_id=1, source_target_pairs={{0,16},{8,24},{16,0},{24,8},{1,17},{9,25},{17,1},{25,9},{2,18},{10... | collective-permute-start | bytes 2064392 | tf_op jit(solution)/shard_map/ppermute | solution.py:36
  232.3 35.5 %collective-permute-start.29 = (bf16[4,160,896]{2,1,0:T(8,128)(2,1)}, bf16[4,160,896]{2,1,0:T(8,128)(2,1)}, u32[]{:S(2)}, u32[]{:S(2)}) collective-permute-start(bf16[4,160,896]{2,1,0:T(8,128)(2,1)} %dynamic-slice_bitcast_fusion.5), channel_id=1, source_target_pairs={{0,1},{1,0},{2,3},{3,2},{4,5},{5,4},{6,7},{7,6},{8,9},{9,8},{10,11... | collective-permute-start | bytes 3440648 | tf_op jit(solution)/shard_map/ppermute | solution.py:36
  234.7 51.6 %collective-permute-start.31 = (bf16[4,160,896]{2,1,0:T(8,128)(2,1)}, bf16[4,160,896]{2,1,0:T(8,128)(2,1)}, u32[]{:S(2)}, u32[]{:S(2)}) collective-permute-start(bf16[4,160,896]{2,1,0:T(8,128)(2,1)} %dynamic-slice_bitcast_fusion.4), channel_id=1, source_target_pairs={{0,1},{1,0},{2,3},{3,2},{4,5},{5,4},{6,7},{7,6},{8,9},{9,8},{10,11... | collective-permute-start | bytes 3440648 | tf_op jit(solution)/shard_map/ppermute | solution.py:36
  243.7 48.0 %collective-permute-start.37 = (bf16[2,896,224]{1,2,0:T(8,128)(2,1)}, bf16[2,896,224]{1,2,0:T(8,128)(2,1)}, u32[]{:S(2)}, u32[]{:S(2)}) collective-permute-start(bf16[2,896,224]{1,2,0:T(8,128)(2,1)} %dynamic-slice_bitcast_fusion.6), channel_id=1, source_target_pairs={{0,8},{8,0},{16,24},{24,16},{1,9},{9,1},{17,25},{25,17},{2,10},{10... | collective-permute-start | bytes 2408456 | tf_op jit(solution)/shard_map/ppermute | solution.py:36
  269.4 41.4 %collective-permute-start.46 = (bf16[2,160,896]{2,1,0:T(8,128)(2,1)S(1)}, bf16[2,160,896]{2,1,0:T(8,128)(2,1)}, u32[]{:S(2)}, u32[]{:S(2)}) collective-permute-start(bf16[2,160,896]{2,1,0:T(8,128)(2,1)S(1)} %fusion.23), channel_id=1, source_target_pairs={{0,4},{1,5},{2,6},{3,7},{4,0},{5,1},{6,2},{7,3},{8,12},{9,13},{10,... | collective-permute-start | bytes 1720328 | tf_op jit(solution)/shard_map/ppermute | solution.py:36
  270.9 64.2 %collective-permute-start.39 = (bf16[4,160,896]{2,1,0:T(8,128)(2,1)}, bf16[4,160,896]{2,1,0:T(8,128)(2,1)}, u32[]{:S(2)}, u32[]{:S(2)}) collective-permute-start(bf16[4,160,896]{2,1,0:T(8,128)(2,1)} %dynamic-slice_bitcast_fusion.3), channel_id=1, source_target_pairs={{0,1},{1,0},{2,3},{3,2},{4,5},{5,4},{6,7},{7,6},{8,9},{9,8},{10,11... | collective-permute-start | bytes 3440648 | tf_op jit(solution)/shard_map/ppermute | solution.py:36
  290.2 37.1 %collective-permute-start.33 = (bf16[2,160,896]{2,1,0:T(8,128)(2,1)}, bf16[2,160,896]{2,1,0:T(8,128)(2,1)}, u32[]{:S(2)}, u32[]{:S(2)}) collective-permute-start(bf16[2,160,896]{2,1,0:T(8,128)(2,1)} %fusion.21), channel_id=1, source_target_pairs={{0,4},{1,5},{2,6},{3,7},{4,0},{5,1},{6,2},{7,3},{8,12},{9,13},{10,... | collective-permute-start | bytes 1720328 | tf_op jit(solution)/shard_map/ppermute | solution.py:36
  294.4 18.4 %collective-permute-start.32 = (bf16[1,384,256]{2,1,0:T(8,128)(2,1)S(1)}, bf16[1,384,256]{2,1,0:T(8,128)(2,1)S(1)}, u32[]{:S(2)}, u32[]{:S(2)}) collective-permute-start(bf16[1,384,256]{2,1,0:T(8,128)(2,1)S(1)} %dynamic-slice_convert_fusion.12), channel_id=1, source_target_pairs={{0,16},{8,24},{16,0},{24,8},{1,17},{9,25},{17,1},{25,9},{2,18},{10... | collective-permute-start | bytes 589832 | tf_op jit(solution)/shard_map/ppermute | solution.py:36
  312.8 21.2 %collective-permute-start.47 = (bf16[1,160,896]{2,1,0:T(8,128)(2,1)}, bf16[1,160,896]{2,1,0:T(8,128)(2,1)}, u32[]{:S(2)}, u32[]{:S(2)}) collective-permute-start(bf16[1,160,896]{2,1,0:T(8,128)(2,1)} %dynamic-slice_convert_fusion.8), channel_id=1, source_target_pairs={{0,2},{1,3},{2,0},{3,1},{4,6},{5,7},{6,4},{7,5},{8,10},{9,11},{10,... | collective-permute-start | bytes 860168 | tf_op jit(solution)/shard_map/ppermute | solution.py:36
  331.1 37.5 %collective-permute-start.44 = (bf16[1,160,896]{2,1,0:T(8,128)(2,1)}, bf16[1,160,896]{2,1,0:T(8,128)(2,1)}, u32[]{:S(2)}, u32[]{:S(2)}) collective-permute-start(bf16[1,160,896]{2,1,0:T(8,128)(2,1)} %dynamic-slice_convert_fusion.10), channel_id=1, source_target_pairs={{0,2},{1,3},{2,0},{3,1},{4,6},{5,7},{6,4},{7,5},{8,10},{9,11},{10,... | collective-permute-start | bytes 860168 | tf_op jit(solution)/shard_map/ppermute | solution.py:36
  337.6 26.9 %collective-permute-start.40 = (bf16[2,160,896]{2,1,0:T(8,128)(2,1)}, bf16[2,160,896]{2,1,0:T(8,128)(2,1)}, u32[]{:S(2)}, u32[]{:S(2)}) collective-permute-start(bf16[2,160,896]{2,1,0:T(8,128)(2,1)} %fusion.22), channel_id=1, source_target_pairs={{0,4},{1,5},{2,6},{3,7},{4,0},{5,1},{6,2},{7,3},{8,12},{9,13},{10,... | collective-permute-start | bytes 1720328 | tf_op jit(solution)/shard_map/ppermute | solution.py:36
  339.5 26.6 %collective-permute-start.35 = (bf16[1,8,160,224]{3,2,1,0:T(8,128)(2,1)}, bf16[1,8,160,224]{3,2,1,0:T(8,128)(2,1)}, u32[]{:S(2)}, u32[]{:S(2)}) collective-permute-start(bf16[1,8,160,224]{3,2,1,0:T(8,128)(2,1)} %dynamic-slice_convert_fusion.2), channel_id=1, source_target_pairs={{0,16},{8,24},{16,0},{24,8},{1,17},{9,25},{17,1},{25,9},{2,18},{10... | collective-permute-start | bytes 1720328 | tf_op jit(solution)/shard_map/ppermute | solution.py:36
  377.5 26.6 %collective-permute-start.36 = (bf16[1,384,896]{2,1,0:T(8,128)(2,1)}, bf16[1,384,896]{2,1,0:T(8,128)(2,1)}, u32[]{:S(2)}, u32[]{:S(2)}) collective-permute-start(bf16[1,384,896]{2,1,0:T(8,128)(2,1)} %dynamic-slice_convert_fusion), channel_id=1, source_target_pairs={{0,16},{8,24},{16,0},{24,8},{1,17},{9,25},{17,1},{25,9},{2,18},{10... | collective-permute-start | bytes 2064392 | tf_op jit(solution)/shard_map/ppermute | solution.py:36
  (91 other events, 708.5 us)

commit v5 on v4

--- a/solution.py
+++ b/solution.py
@@ -611,7 +611,9 @@
     )
     ff_cut = cut_ff(me, gate_up_weight, down_weight, seq_size)
     ff_share = [ff_cut[0]] + [swap(ff_cut[o], "seq", seq_size, o) for o in offsets if o]
-    columns = ff_spread(after(column_gather(packed, fsdp_size), ff_cut[1]), fsdp_size)
+    columns = ff_spread(
+        after(column_gather(packed, fsdp_size), *ff_share[1:]), fsdp_size
+    )
     ff_block = join_lanes(me, ff_share)
     wide = qkv_tall + 16
     packed_stack = jnp.concatenate([columns[m][:, :wide] for m in sorted(columns)], axis=0)
@@ -624,7 +626,8 @@
 
     qkv_pieces = [[packed_blocks[o]] for o in offsets]
     qkv_t, vectors = join_both(me, qkv_pieces, qkv_tall)
-    qkv_t = after(qkv_t, ff_blocks[2 * inner], ff_blocks[inner])[:, :qkv_rows].reshape(fsdp_size * qkv_rows, -1)
+    own_x = ff_spread(ff_block, fsdp_size)
+    qkv_t = after(qkv_t, ff_blocks[2 * inner], ff_blocks[inner], *own_x.values())[:, :qkv_rows].reshape(fsdp_size * qkv_rows, -1)
     gain_one = vectors[:, 0, : norm_one.shape[0]].reshape(-1).astype(F32)
     bias_full = vectors[:, 1, : qkv_bias.shape[0]].reshape(-1).astype(F32)
     gain_two = vectors[:, 2, : norm_two.shape[0]].reshape(-1).astype(F32)
@@ -649,13 +652,14 @@
     low, high = low[None, :], high[None, :]
     split = PAIRS // 2 + 1
     spread = lambda block: ff_spread(block, fsdp_size)
-    own, near = ff_blocks[0], ff_blocks[inner]
+    near = ff_blocks[inner]
     far, last = ff_blocks[2 * inner], ff_blocks[3 * inner]
-    own_x = spread(own)
     near_x = spread(after(near, kv_all))
-    attn_one, lse_one = attend(low, high, place, after(queries, far), kv_all, 0, split)
+    attn_one, lse_one = attend(
+        low, high, place, after(queries, far), kv_all, 0, split
+    )
     far_x = spread(after(far, kv_all))
-    queries_two = after(queries, attn_one, cot_blocks[seq_size // 2])
+    queries_two = after(queries, attn_one, cot_blocks[seq_size // 2], *near_x.values())
     attn_two, lse_two = attend(low, high, place, queries_two, kv_all, split, PAIRS - split)
     last_x = spread(last)
     for base, row in ((0, own_x), (inner, near_x), (2 * inner, far_x), (3 * inner, last_x)):
@@ -669,13 +673,13 @@
     residual = inputs + dot(attn_flat, out_full, 1, 0)
     scale_two = rms_scale(residual)
     normed_two = (residual * scale_two * gain_two).astype(BF16)
-    normed_two = after(normed_two, *near_x.values())
+    normed_two = after(normed_two, *far_x.values())
     normed_blocks = {0: normed_two}
     bit = seq_size // 2
     while bit:
         if bit == 1:
             top = seq_size // 2
-            normed_blocks[top] = after(normed_blocks[top], last, *far_x.values())
+            normed_blocks[top] = after(normed_blocks[top], last)
         normed_blocks.update(
             {o ^ bit: swap(b, "seq", seq_size, bit) for o, b in normed_blocks.items()}
         )
@@ -721,36 +725,27 @@
     kept_one, given = give(down_term, 0)
     got_one = send(given, 0)
     kept_two, given = give(jnp.concatenate([gate_term[:, 0], up_term[:, 0]], axis=0), 0)
-    got_two = send(given, 0)
+    got_two = send(after(given, grad_normed_two), 0)
     kept_three, given_three = give(jnp.concatenate([gate_term[:, 1], up_term[:, 1]], axis=0), 0)
-
-    kept, given = halve(after(by_seq(layer_part), down_term), 1, my_seq)
-    layer_sum = add(kept, swap(given, "seq", seq_size, 1))
-    kept_layer, given_layer = halve(layer_sum, 1, my_seq // 2)
 
     grad_path, norm_two_term = norm_back(grad_normed_two, residual, scale_two, gain_two)
     grad_residual = cotangent.astype(F32) + grad_path
     grad_branch = grad_residual.astype(BF16)
     grad_attn = dot(grad_branch, out_full, 1, 1).astype(BF16)
-    out_term = stack_from_lanes(dot(attn_flat, grad_branch, 0, 0).astype(BF16), seq_size)
-    kept, given = halve(out_term, 1, my_seq)
-    out_sum = add(kept, swap(given, "seq", seq_size, 1))
-    grad_attn = after(grad_attn, gate_term, up_term, given_layer)
+    grad_attn = after(grad_attn, gate_term, up_term)
     dq_one, kv_terms = attend_back(
         low, high, place, queries, grad_attn, attn_one, lse_one, kv_all, 0, split, ()
     )
     got_one = after(got_one, dq_one)
     got_three = send(after(given_three, got_one), 0)
-    kept_one, given = give(add(kept_one, got_one), 1)
-    next_one = send(given, 1)
-    queries_two = after(queries, kv_terms, got_one)
+    kept_one, given_one = give(add(kept_one, got_one), 1)
+    next_one = send(given_one, 1)
+    queries_two = after(queries, kv_terms, given_one)
     dq_two, kv_terms = attend_back(
         low, high, place, queries_two, grad_attn, attn_two, lse_two, kv_all, split,
         PAIRS - split, (kv_terms,),
     )
     got_two = after(got_two, dq_two)
-    next_one = after(next_one, dq_two)
-    down_sum = finish(kept_one, next_one, 1)
     kept_two, given = give(add(kept_two, got_two), 1)
     next_two = send(given, 1)
     kept, given = halve(by_seq(kv_terms), 1, my_seq)
@@ -761,6 +756,16 @@
         kv_sum = add(kept, swap(after(given, got_two), "seq", seq_size, bit))
         bit *= 2
     kv_mine = kv_sum[0]
+    next_one, next_two = after(next_one, kv_mine), after(next_two, kv_mine)
+    down_sum = finish(kept_one, next_one, 1)
+
+    attn_late = after(attn_flat, dq_two)
+    out_term = stack_from_lanes(dot(attn_late, grad_branch, 0, 0).astype(BF16), seq_size)
+    kept, given = halve(out_term, 1, my_seq)
+    out_sum = add(kept, swap(given, "seq", seq_size, 1))
+    kept, given = halve(after(by_seq(layer_part), dq_two), 1, my_seq)
+    layer_sum = add(kept, swap(given, "seq", seq_size, 1))
+    kept_layer, given_layer = halve(layer_sum, 1, my_seq // 2)
     bit = 2
     while bit < seq_size:
         kept, given = halve(out_sum, 1, my_seq // bit)

time: 417 us -> 391 us (0.938)
  waiting for transfers between devices: 150 us -> 122 us
  starting transfers between devices: 40.2 us -> 44.6 us
    ppermute x51, waiting for transfers between devices: 150 us -> 122 us  [swap(): return lax.ppermute(block, axis, [(i, i ^ bits) for i in range(size)])]
    ppermute x51, starting transfers between devices: 40.2 us -> 44.6 us  [swap(): return lax.ppermute(block, axis, [(i, i ^ bits) for i in range(size)])]
    unnamed x130 -> x114, local copies, waits for them, and re-layouts: 17.3 us -> 16.4 us
  transfers between devices with their start and end apart: 51 -> 51, of which waited for: 19 -> 23; matrix products, arithmetic and copies ran while one was open for 21% -> 22% of each run, Pallas kernels for 16% -> 17%
where the time goes in v5:
time: 391 us; the launch traced here: 384 us
  waiting for transfers between devices  122 us (31%)
  Pallas kernels  97.4 us (25%)
  local copies, waits for them, and re-layouts  55.5 us (14%)
  starting transfers between devices  44.6 us (11%)
  other arithmetic  29.8 us (8%)
  matrix products  25.1 us (6%)
  blocking collectives  8.05 us (2%)
    ppermute x51, waiting for transfers between devices, swap(): return lax.ppermute(block, axis, [(i, i ^ bits) for i in range(size)])  122 us
    ppermute x51, starting transfers between devices, swap(): return lax.ppermute(block, axis, [(i, i ^ bits) for i in range(size)])  44.6 us
    pallas_call x2, Pallas kernels, attend_back(): pl.pallas_call(functools.partial(attend_back_kernel, begin), grid=(pairs,...  32.7 us
    pallas_call x1, Pallas kernels, feed_forward(): pl.pallas_call(body, grid=(size,), in_specs=[pl.BlockSpec(memory_space=pl...  31.9 us
    dot_general x9, matrix products, dot(): lax.dot_general(left, right, (((left_dim,), (right_dim,)), ((), ())), pre...  25.1 us
    pallas_call x2, Pallas kernels, attend(): pl.pallas_call(functools.partial(attend_kernel, begin), grid=(pairs,), in...  23.4 us
    add x15, other arithmetic, add(): return kept.astype(F32) + got.astype(F32)  16.7 us
    unnamed x114, local copies, waits for them, and re-layouts  16.4 us
  transfers between devices with their start and end apart: 51, of which 23 were waited for; matrix products, arithmetic and copies ran while one was open for 22% of the time, Pallas kernels for 17%

profile of v5, /device:TPU:0, one launch (start us, length us, event | category | flops | bytes accessed | tf_op | source)
XLA Modules:
  0.0 384.2 jit_solution(12776743327720322588)
XLA Ops:
  15.2 5.8 %collective-permute-done.1 = bf16[272,224]{1,0:T(8,128)(2,1)S(1)} collective-permute-done((bf16[272,224]{1,0:T(8,128)(2,1)S(1)}, bf16[272,224]{1,0:T(8,128)(2,1)S(1)}, u32[]{:S(2)}, u32[]{:S(2)}) %collective-permute-start.1) | collective-permute-done | bytes 121888 | tf_op jit(solution)/shard_map/ppermute | solution.py:36
  22.2 4.4 %collective-permute-done.5.refs_3_ = bf16[480,224]{1,0:T(8,128)(2,1)S(1)} collective-permute-done((bf16[480,224]{1,0:T(8,128)(2,1)S(1)}, bf16[480,224]{1,0:T(8,128)(2,1)S(1)}, u32[]{:S(2)}, u32[]{:S(2)}) %collective-permute-start.5) | collective-permute-done | bytes 215072 | tf_op jit(solution)/shard_map/ppermute | solution.py:36
  29.2 12.1 %collective-permute-done.6 = bf16[4,272,224]{2,1,0:T(8,128)(2,1)S(1)} collective-permute-done((bf16[4,272,224]{2,1,0:T(8,128)(2,1)S(1)}, bf16[4,272,224]{2,1,0:T(8,128)(2,1)S(1)}, u32[]{:S(2)}, u32[]{:S(2)}) %collective-permute-start.6) | collective-permute-done | bytes 487456 | tf_op jit(solution)/shard_map/ppermute | solution.py:36
  65.2 19.3 %collective-permute-done.10.refs_4_ = bf16[480,896]{1,0:T(8,128)(2,1)} collective-permute-done((bf16[480,896]{1,0:T(8,128)(2,1)S(1)}, bf16[480,896]{1,0:T(8,128)(2,1)}, u32[]{:S(2)}, u32[]{:S(2)}) %collective-permute-start.10) | collective-permute-done | bytes 860192 | tf_op jit(solution)/shard_map/ppermute | solution.py:36
  90.6 8.0 %all_gather.3.kv_ref = bf16[1536,256]{1,0:T(8,128)(2,1)S(1)} all-gather(bf16[384,256]{1,0:T(8,128)(2,1)S(1)} %pad_maximum_fusion.11), channel_id=1, replica_groups=mesh['seq'=4,'fsdp'=8] {'seq'}, dimensions={0}, use_global_device_ids=true | all-gather | bytes 983040 | tf_op jit(solution)/shard_map/all_gather | solution.py:645
  103.9 13.4 %attend.2 = (bf16[384,512]{1,0:T(8,128)(2,1)S(1)}, f32[4,1,768]{2,1,0:T(1,128)S(1)}) custom-call(s32[1,384]{1,0:T(1,128)S(1)} %broadcast_in_dim.12.low_ref, s32[1,384]{1,0:T(1,128)S(1)} %iota_add_fusion.high_ref, s32[1536,1]{1,0:T(8,128)S(1)} %iota.43.place_ref, bf16[384,896]{1,0:T(8,128)(2,1)S(1)} %slice_multiply_fusion.1.q_ref, ...), custom_call_target="tpu_custom_call" | custom-call | flops 1 | bytes 1 | tf_op jit(solution)/shard_map/attend/pallas_call | solution.py:479
  120.4 10.0 %attend.3 = (bf16[384,384]{1,0:T(8,128)(2,1)S(1)}, f32[3,1,768]{2,1,0:T(1,128)S(1)}) custom-call(s32[1,384]{1,0:T(1,128)S(1)} %broadcast_in_dim.12.low_ref, s32[1,384]{1,0:T(1,128)S(1)} %iota_add_fusion.high_ref, s32[1536,1]{1,0:T(8,128)S(1)} %iota.49.place_ref, bf16[384,896]{1,0:T(8,128)(2,1)S(1)} %slice_multiply_fusion.1.q_ref, ...), custom_call_target="tpu_custom_call" | custom-call | flops 1 | bytes 1 | tf_op jit(solution)/shard_map/attend/pallas_call | solution.py:479
  131.7 6.9 %collective-permute-done.18.refs_5_ = bf16[480,896]{1,0:T(8,128)(2,1)S(1)} collective-permute-done((bf16[480,896]{1,0:T(8,128)(2,1)}, bf16[480,896]{1,0:T(8,128)(2,1)S(1)}, u32[]{:S(2)}, u32[]{:S(2)}) %collective-permute-start.18) | collective-permute-done | bytes 860192 | tf_op jit(solution)/shard_map/ppermute | solution.py:36
  144.2 11.6 %collective-permute-done.22.refs_10_ = bf16[384,896]{1,0:T(8,128)(2,1)} collective-permute-done((bf16[384,896]{1,0:T(8,128)(2,1)S(1)}, bf16[384,896]{1,0:T(8,128)(2,1)}, u32[]{:S(2)}, u32[]{:S(2)}) %collective-permute-start.22) | collective-permute-done | bytes 688160 | tf_op jit(solution)/shard_map/ppermute | solution.py:36
  155.8 8.6 %collective-permute-done.20.refs_7_ = bf16[480,896]{1,0:T(8,128)(2,1)} collective-permute-done((bf16[480,896]{1,0:T(8,128)(2,1)}, bf16[480,896]{1,0:T(8,128)(2,1)}, u32[]{:S(2)}, u32[]{:S(2)}) %collective-permute-start.20) | collective-permute-done | bytes 860192 | tf_op jit(solution)/shard_map/ppermute | solution.py:36
  164.4 31.9 %feed_forward.1 = (bf16[1536,1280]{1,0:T(8,128)(2,1)}, bf16[1536,1280]{1,0:T(8,128)(2,1)}, bf16[1536,1280]{1,0:T(8,128)(2,1)}, bf16[1536,896]{1,0:T(8,128)(2,1)}...) custom-call(s32[2]{0:T(128)S(1)} %pad_add_fusion.me_ref, ...), custom_call_target="tpu_custom_call" | custom-call | flops 1 | bytes 1 | tf_op jit(solution)/shard_map/feed_forward/pallas_call | solution.py:313
  198.8 3.5 collective-permute-done.26
  204.5 4.5 %convolution_convert_fusion.3 = bf16[1280,896]{1,0:T(8,128)(2,1)S(1)} fusion(bf16[1536,1280]{1,0:T(8,128)(2,1)S(1)} %copy-done.51, bf16[1536,896]{1,0:T(8,128)(2,1)S(1)} %copy-done.53), kind=kOutput, calls=%fused_computation.3 | convolution fusion | flops 3524362240 | bytes 8978432 | tf_op jit(solution)/shard_map/dot_general | solution.py:30
  209.1 4.5 %convolution_convert_fusion.1 = bf16[1280,896]{1,0:T(8,128)(2,1)S(1)} fusion(bf16[1536,1280]{1,0:T(8,128)(2,1)S(1)} %copy-done.50, bf16[1536,896]{1,0:T(8,128)(2,1)S(1)} %copy-done.52), kind=kOutput, calls=%fused_computation.1 | convolution fusion | flops 3524362240 | bytes 8978432 | tf_op jit(solution)/shard_map/dot_general | solution.py:30
  215.7 4.7 %convolution_convert_fusion.2 = bf16[1280,896]{1,0:T(8,128)(2,1)S(1)} fusion(bf16[1536,1280]{1,0:T(8,128)(2,1)S(1)} %copy-done.49, bf16[1536,896]{1,0:T(8,128)(2,1)S(1)} %copy-done.52), kind=kOutput, calls=%fused_computation.2 | convolution fusion | flops 3524362240 | bytes 8978432 | tf_op jit(solution)/shard_map/dot_general | solution.py:30
  231.5 17.8 %attend_back.2 = (f32[384,512]{1,0:T(8,128)S(1)}, f32[1536,256]{1,0:T(8,128)}) custom-call(s32[1,384]{1,0:T(1,128)S(1)} %broadcast_in_dim.12.low_ref, s32[1,384]{1,0:T(1,128)S(1)} %iota_add_fusion.high_ref, s32[1536,1]{1,0:T(8,128)S(1)} %iota.51.place_ref, bf16[384,896]{1,0:T(8,128)(2,1)S(1)} %slice_multiply_fusion.1.q_ref, ...), custom_call_target="tpu_custom_call" | custom-call | flops 1 | bytes 1 | tf_op jit(solution)/shard_map/attend_back/pallas_call | solution.py:505
  253.4 14.9 %attend_back.3 = (f32[384,384]{1,0:T(8,128)S(1)}, f32[1536,256]{1,0:T(8,128)}) custom-call(s32[1,384]{1,0:T(1,128)S(1)} %broadcast_in_dim.12.low_ref, s32[1,384]{1,0:T(1,128)S(1)} %iota_add_fusion.high_ref, s32[1536,1]{1,0:T(8,128)S(1)} %iota.50.place_ref, bf16[384,896]{1,0:T(8,128)(2,1)S(1)} %slice_multiply_fusion.1.q_ref, ...), custom_call_target="tpu_custom_call" | custom-call | flops 1 | bytes 1 | tf_op jit(solution)/shard_map/attend_back/pallas_call | solution.py:505
  295.1 4.3 %copy.62 = bf16[1152,4,224]{2,0,1:T(8,128)(2,1)} copy(bf16[1152,4,224]{0,2,1:T(8,128)(2,1)} %bitcast.198) | data formatting | bytes 4128768 | tf_op jit(solution)/shard_map/reshape | solution.py:584
  301.9 4.7 %collective-permute-done.33 = bf16[2,160,896]{2,1,0:T(8,128)(2,1)} collective-permute-done((bf16[2,160,896]{2,1,0:T(8,128)(2,1)}, bf16[2,160,896]{2,1,0:T(8,128)(2,1)}, u32[]{:S(2)}, u32[]{:S(2)}) %collective-permute-start.33) | collective-permute-done | bytes 573472 | tf_op jit(solution)/shard_map/ppermute | solution.py:36
  327.6 11.3 %collective-permute-done.40 = bf16[2,160,896]{2,1,0:T(8,128)(2,1)} collective-permute-done((bf16[2,160,896]{2,1,0:T(8,128)(2,1)}, bf16[2,160,896]{2,1,0:T(8,128)(2,1)}, u32[]{:S(2)}, u32[]{:S(2)}) %collective-permute-start.40) | collective-permute-done | bytes 573472 | tf_op jit(solution)/shard_map/ppermute | solution.py:36
  343.1 5.8 %collective-permute-done.45 = bf16[1,160,896]{2,1,0:T(8,128)(2,1)S(1)} collective-permute-done((bf16[1,160,896]{2,1,0:T(8,128)(2,1)S(1)}, bf16[1,160,896]{2,1,0:T(8,128)(2,1)S(1)}, u32[]{:S(2)}, u32[]{:S(2)}) %collective-permute-start.45) | collective-permute-done | bytes 286752 | tf_op jit(solution)/shard_map/ppermute | solution.py:36
  359.5 3.8 collective-permute-done.50.refs_3_
  366.4 5.5 %collective-permute-done.42 = bf16[2,272,224]{2,1,0:T(8,128)(2,1)S(1)} collective-permute-done((bf16[2,272,224]{2,1,0:T(8,128)(2,1)}, bf16[2,272,224]{2,1,0:T(8,128)(2,1)S(1)}, u32[]{:S(2)}, u32[]{:S(2)}) %collective-permute-start.42) | collective-permute-done | bytes 243744 | tf_op jit(solution)/shard_map/ppermute | solution.py:36
  372.1 6.5 %collective-permute-done.36 = bf16[1,384,896]{2,1,0:T(8,128)(2,1)} collective-permute-done((bf16[1,384,896]{2,1,0:T(8,128)(2,1)}, bf16[1,384,896]{2,1,0:T(8,128)(2,1)}, u32[]{:S(2)}, u32[]{:S(2)}) %collective-permute-start.36) | collective-permute-done | bytes 688160 | tf_op jit(solution)/shard_map/ppermute | solution.py:36
  (336 shorter events, 158.6 us)
Async XLA Ops:
  44.7 39.8 %collective-permute-start.10 = (bf16[480,896]{1,0:T(8,128)(2,1)S(1)}, bf16[480,896]{1,0:T(8,128)(2,1)}, u32[]{:S(2)}, u32[]{:S(2)}) collective-permute-start(bf16[480,896]{1,0:T(8,128)(2,1)S(1)} %join_lanes.1.refs_0_), channel_id=1, source_target_pairs={{0,4},{1,5},{2,6},{3,7},{4,0},{5,1},{6,2},{7,3},{8,12},{9,13},{10,... | collective-permute-start | bytes 2580488 | tf_op jit(solution)/shard_map/ppermute | solution.py:36
  46.4 38.1 %collective-permute-start.11 = (bf16[480,896]{1,0:T(8,128)(2,1)S(1)}, bf16[480,896]{1,0:T(8,128)(2,1)}, u32[]{:S(2)}, u32[]{:S(2)}) collective-permute-start(bf16[480,896]{1,0:T(8,128)(2,1)S(1)} %join_lanes.1.refs_0_), channel_id=1, source_target_pairs={{0,2},{1,3},{2,0},{3,1},{4,6},{5,7},{6,4},{7,5},{8,10},{9,11},{10,... | collective-permute-start | bytes 2580488 | tf_op jit(solution)/shard_map/ppermute | solution.py:36
  48.9 35.7 %collective-permute-start.12 = (bf16[480,896]{1,0:T(8,128)(2,1)S(1)}, bf16[480,896]{1,0:T(8,128)(2,1)}, u32[]{:S(2)}, u32[]{:S(2)}) collective-permute-start(bf16[480,896]{1,0:T(8,128)(2,1)S(1)} %join_lanes.1.refs_0_), channel_id=1, source_target_pairs={{0,1},{1,0},{2,3},{3,2},{4,5},{5,4},{6,7},{7,6},{8,9},{9,8},{10,11... | collective-permute-start | bytes 2580488 | tf_op jit(solution)/shard_map/ppermute | solution.py:36
  60.6 41.2 %collective-permute-start.16 = (bf16[8,112,224]{2,1,0:T(8,128)(2,1)S(1)}, bf16[8,112,224]{2,1,0:T(8,128)(2,1)}, u32[]{:S(2)}, u32[]{:S(2)}) collective-permute-start(bf16[8,112,224]{2,1,0:T(8,128)(2,1)S(1)} %pad_maximum_fusion.8.refs_0_), channel_id=1, source_target_pairs={{0,16},{8,24},{16,0},{24,8},{1,17},{9,25},{17,1},{25,9},{2,18},{10... | collective-permute-start | bytes 1204232 | tf_op jit(solution)/shard_map/ppermute | solution.py:36
  98.6 21.7 %collective-permute-start.14 = (bf16[480,896]{1,0:T(8,128)(2,1)}, bf16[480,896]{1,0:T(8,128)(2,1)}, u32[]{:S(2)}, u32[]{:S(2)}) collective-permute-start(bf16[480,896]{1,0:T(8,128)(2,1)} %collective-permute-done.11.refs_2_), channel_id=1, source_target_pairs={{0,1},{1,0},{2,3},{3,2},{4,5},{5,4},{6,7},{7,6},{8,9},{9,8},{10,11... | collective-permute-start | bytes 2580488 | tf_op jit(solution)/shard_map/ppermute | solution.py:36
  100.3 19.6 %collective-permute-start.13 = (bf16[384,896]{1,0:T(8,128)(2,1)S(1)}, bf16[384,896]{1,0:T(8,128)(2,1)}, u32[]{:S(2)}, u32[]{:S(2)}) collective-permute-start(bf16[384,896]{1,0:T(8,128)(2,1)S(1)} %copy-done.3), channel_id=1, source_target_pairs={{0,16},{8,24},{16,0},{24,8},{1,17},{9,25},{17,1},{25,9},{2,18},{10... | collective-permute-start | bytes 2064392 | tf_op jit(solution)/shard_map/ppermute | solution.py:36
  102.4 40.8 %collective-permute-start.19 = (bf16[480,896]{1,0:T(8,128)(2,1)}, bf16[480,896]{1,0:T(8,128)(2,1)}, u32[]{:S(2)}, u32[]{:S(2)}) collective-permute-start(bf16[480,896]{1,0:T(8,128)(2,1)} %collective-permute-done.11.refs_2_), channel_id=1, source_target_pairs={{0,4},{1,5},{2,6},{3,7},{4,0},{5,1},{6,2},{7,3},{8,12},{9,13},{10,... | collective-permute-start | bytes 2580488 | tf_op jit(solution)/shard_map/ppermute | solution.py:36
  117.5 21.2 %collective-permute-start.18 = (bf16[480,896]{1,0:T(8,128)(2,1)}, bf16[480,896]{1,0:T(8,128)(2,1)S(1)}, u32[]{:S(2)}, u32[]{:S(2)}) collective-permute-start(bf16[480,896]{1,0:T(8,128)(2,1)} %collective-permute-done.10.refs_4_), channel_id=1, source_target_pairs={{0,1},{1,0},{2,3},{3,2},{4,5},{5,4},{6,7},{7,6},{8,9},{9,8},{10,11... | collective-permute-start | bytes 2580488 | tf_op jit(solution)/shard_map/ppermute | solution.py:36
  143.1 21.3 %collective-permute-start.20 = (bf16[480,896]{1,0:T(8,128)(2,1)}, bf16[480,896]{1,0:T(8,128)(2,1)}, u32[]{:S(2)}, u32[]{:S(2)}) collective-permute-start(bf16[480,896]{1,0:T(8,128)(2,1)} %collective-permute-done.19.refs_6_), channel_id=1, source_target_pairs={{0,1},{1,0},{2,3},{3,2},{4,5},{5,4},{6,7},{7,6},{8,9},{9,8},{10,11... | collective-permute-start | bytes 2580488 | tf_op jit(solution)/shard_map/ppermute | solution.py:36
  143.7 20.7 %collective-permute-start.25 = (bf16[384,896]{1,0:T(8,128)(2,1)}, bf16[384,896]{1,0:T(8,128)(2,1)}, u32[]{:S(2)}, u32[]{:S(2)}) collective-permute-start(bf16[384,896]{1,0:T(8,128)(2,1)} %collective-permute-done.13.refs_14_), channel_id=1, source_target_pairs={{0,8},{8,0},{16,24},{24,16},{1,9},{9,1},{17,25},{25,17},{2,10},{10... | collective-permute-start | bytes 2064392 | tf_op jit(solution)/shard_map/ppermute | solution.py:36
  144.2 20.2 %collective-permute-start.21 = (bf16[384,896]{1,0:T(8,128)(2,1)S(1)}, bf16[384,896]{1,0:T(8,128)(2,1)}, u32[]{:S(2)}, u32[]{:S(2)}) collective-permute-start(bf16[384,896]{1,0:T(8,128)(2,1)S(1)} %multiply_convert_fusion.refs_8_), channel_id=1, source_target_pairs={{0,8},{8,0},{16,24},{24,16},{1,9},{9,1},{17,25},{25,17},{2,10},{10... | collective-permute-start | bytes 2064392 | tf_op jit(solution)/shard_map/ppermute | solution.py:36
  204.4 21.2 %collective-permute-start.27 = (bf16[1,384,896]{2,1,0:T(8,128)(2,1)S(1)}, bf16[1,384,896]{2,1,0:T(8,128)(2,1)S(1)}, u32[]{:S(2)}, u32[]{:S(2)}) collective-permute-start(bf16[1,384,896]{2,1,0:T(8,128)(2,1)S(1)} %dynamic-slice_convert_fusion.1), channel_id=1, source_target_pairs={{0,16},{8,24},{16,0},{24,8},{1,17},{9,25},{17,1},{25,9},{2,18},{10... | collective-permute-start | bytes 2064392 | tf_op jit(solution)/shard_map/ppermute | solution.py:36
  221.8 28.4 %collective-permute-start.28 = (bf16[4,160,896]{2,1,0:T(8,128)(2,1)}, bf16[4,160,896]{2,1,0:T(8,128)(2,1)}, u32[]{:S(2)}, u32[]{:S(2)}) collective-permute-start(bf16[4,160,896]{2,1,0:T(8,128)(2,1)} %dynamic-slice_bitcast_fusion.5), channel_id=1, source_target_pairs={{0,1},{1,0},{2,3},{3,2},{4,5},{5,4},{6,7},{7,6},{8,9},{9,8},{10,11... | collective-permute-start | bytes 3440648 | tf_op jit(solution)/shard_map/ppermute | solution.py:36
  227.4 47.4 %collective-permute-start.31 = (bf16[4,160,896]{2,1,0:T(8,128)(2,1)}, bf16[4,160,896]{2,1,0:T(8,128)(2,1)}, u32[]{:S(2)}, u32[]{:S(2)}) collective-permute-start(bf16[4,160,896]{2,1,0:T(8,128)(2,1)} %dynamic-slice_bitcast_fusion.4), channel_id=1, source_target_pairs={{0,1},{1,0},{2,3},{3,2},{4,5},{5,4},{6,7},{7,6},{8,9},{9,8},{10,11... | collective-permute-start | bytes 3440648 | tf_op jit(solution)/shard_map/ppermute | solution.py:36
  252.9 35.6 %collective-permute-start.46 = (bf16[2,160,896]{2,1,0:T(8,128)(2,1)}, bf16[2,160,896]{2,1,0:T(8,128)(2,1)}, u32[]{:S(2)}, u32[]{:S(2)}) collective-permute-start(bf16[2,160,896]{2,1,0:T(8,128)(2,1)} %fusion.19), channel_id=1, source_target_pairs={{0,4},{1,5},{2,6},{3,7},{4,0},{5,1},{6,2},{7,3},{8,12},{9,13},{10,... | collective-permute-start | bytes 1720328 | tf_op jit(solution)/shard_map/ppermute | solution.py:36
  269.5 32.3 %collective-permute-start.39 = (bf16[4,160,896]{2,1,0:T(8,128)(2,1)}, bf16[4,160,896]{2,1,0:T(8,128)(2,1)}, u32[]{:S(2)}, u32[]{:S(2)}) collective-permute-start(bf16[4,160,896]{2,1,0:T(8,128)(2,1)} %dynamic-slice_bitcast_fusion.3), channel_id=1, source_target_pairs={{0,1},{1,0},{2,3},{3,2},{4,5},{5,4},{6,7},{7,6},{8,9},{9,8},{10,11... | collective-permute-start | bytes 3440648 | tf_op jit(solution)/shard_map/ppermute | solution.py:36
  273.1 50.3 %collective-permute-start.29 = (bf16[2,384,896]{2,1,0:T(8,128)(2,1)}, bf16[2,384,896]{2,1,0:T(8,128)(2,1)}, u32[]{:S(2)}, u32[]{:S(2)}) collective-permute-start(bf16[2,384,896]{2,1,0:T(8,128)(2,1)} %dynamic-slice_bitcast_fusion), channel_id=1, source_target_pairs={{0,8},{8,0},{16,24},{24,16},{1,9},{9,1},{17,25},{25,17},{2,10},{10... | collective-permute-start | bytes 4128776 | tf_op jit(solution)/shard_map/ppermute | solution.py:36
  278.9 27.7 %collective-permute-start.33 = (bf16[2,160,896]{2,1,0:T(8,128)(2,1)}, bf16[2,160,896]{2,1,0:T(8,128)(2,1)}, u32[]{:S(2)}, u32[]{:S(2)}) collective-permute-start(bf16[2,160,896]{2,1,0:T(8,128)(2,1)} %fusion.20), channel_id=1, source_target_pairs={{0,4},{1,5},{2,6},{3,7},{4,0},{5,1},{6,2},{7,3},{8,12},{9,13},{10,... | collective-permute-start | bytes 1720328 | tf_op jit(solution)/shard_map/ppermute | solution.py:36
  292.6 18.7 %collective-permute-start.47 = (bf16[1,160,896]{2,1,0:T(8,128)(2,1)S(1)}, bf16[1,160,896]{2,1,0:T(8,128)(2,1)S(1)}, u32[]{:S(2)}, u32[]{:S(2)}) collective-permute-start(bf16[1,160,896]{2,1,0:T(8,128)(2,1)S(1)} %dynamic-slice_convert_fusion.8), channel_id=1, source_target_pairs={{0,2},{1,3},{2,0},{3,1},{4,6},{5,7},{6,4},{7,5},{8,10},{9,11},{10,... | collective-permute-start | bytes 860168 | tf_op jit(solution)/shard_map/ppermute | solution.py:36
  293.9 21.9 %collective-permute-start.38 = (bf16[1,896,224]{1,2,0:T(8,128)(2,1)}, bf16[1,896,224]{1,2,0:T(8,128)(2,1)}, u32[]{:S(2)}, u32[]{:S(2)}) collective-permute-start(bf16[1,896,224]{1,2,0:T(8,128)(2,1)} %dynamic-slice_convert_fusion.7), channel_id=1, source_target_pairs={{0,16},{8,24},{16,0},{24,8},{1,17},{9,25},{17,1},{25,9},{2,18},{10... | collective-permute-start | bytes 1204232 | tf_op jit(solution)/shard_map/ppermute | solution.py:36
  310.3 28.5 %collective-permute-start.40 = (bf16[2,160,896]{2,1,0:T(8,128)(2,1)}, bf16[2,160,896]{2,1,0:T(8,128)(2,1)}, u32[]{:S(2)}, u32[]{:S(2)}) collective-permute-start(bf16[2,160,896]{2,1,0:T(8,128)(2,1)} %fusion.21), channel_id=1, source_target_pairs={{0,4},{1,5},{2,6},{3,7},{4,0},{5,1},{6,2},{7,3},{8,12},{9,13},{10,... | collective-permute-start | bytes 1720328 | tf_op jit(solution)/shard_map/ppermute | solution.py:36
  314.5 28.6 %collective-permute-start.44 = (bf16[1,160,896]{2,1,0:T(8,128)(2,1)}, bf16[1,160,896]{2,1,0:T(8,128)(2,1)S(1)}, u32[]{:S(2)}, u32[]{:S(2)}) collective-permute-start(bf16[1,160,896]{2,1,0:T(8,128)(2,1)} %dynamic-slice_convert_fusion.10), channel_id=1, source_target_pairs={{0,2},{1,3},{2,0},{3,1},{4,6},{5,7},{6,4},{7,5},{8,10},{9,11},{10,... | collective-permute-start | bytes 860168 | tf_op jit(solution)/shard_map/ppermute | solution.py:36
  322.0 18.2 %collective-permute-start.35 = (bf16[1,8,160,224]{3,2,1,0:T(8,128)(2,1)S(1)}, bf16[1,8,160,224]{3,2,1,0:T(8,128)(2,1)S(1)}, u32[]{:S(2)}, u32[]{:S(2)}) collective-permute-start(bf16[1,8,160,224]{3,2,1,0:T(8,128)(2,1)S(1)} %dynamic-slice_convert_fusion.2), channel_id=1, source_target_pairs={{0,16},{8,24},{16,0},{24,8},{1,17},{9,25},{17,1},{25,9},{2,18},{10... | collective-permute-start | bytes 1720328 | tf_op jit(solution)/shard_map/ppermute | solution.py:36
  352.0 26.6 %collective-permute-start.36 = (bf16[1,384,896]{2,1,0:T(8,128)(2,1)}, bf16[1,384,896]{2,1,0:T(8,128)(2,1)}, u32[]{:S(2)}, u32[]{:S(2)}) collective-permute-start(bf16[1,384,896]{2,1,0:T(8,128)(2,1)} %dynamic-slice_convert_fusion), channel_id=1, source_target_pairs={{0,16},{8,24},{16,0},{24,8},{1,17},{9,25},{17,1},{25,9},{2,18},{10... | collective-permute-start | bytes 2064392 | tf_op jit(solution)/shard_map/ppermute | solution.py:36
  (83 other events, 641.4 us)

commit v6 on v5

--- a/solution.py
+++ b/solution.py
@@ -104,13 +104,20 @@
     return kept, given
 
 
-def fsdp_scatter(stack, size, me):
+def fsdp_scatter(stack, size, me, earlier):
+    inner = size // OUTER
     resolved = []
-    for bit in reversed(fsdp_bits(size)):
+    for bit in reversed(fsdp_bits(size)[2:]):
         kept, given = fsdp_halve(stack, size, bit, me, resolved)
         stack = add(kept, swap(given, "fsdp", size, bit))
         resolved.append(bit)
-    return stack[0]
+    place = me // inner
+    low = after(stack.astype(BF16), earlier)
+    total = lax.dynamic_index_in_dim(stack, place, 0, keepdims=False)
+    for k in range(1, OUTER):
+        given = lax.dynamic_index_in_dim(low, place ^ k, 0, keepdims=False)
+        total = add(total, swap(given, "fsdp", size, k * inner))
+    return total
 
 
 def on_device(body, name, out_shapes, scratch, me, arrays):
@@ -265,9 +272,15 @@
     def body(me_ref, *refs):
         blocks = refs[:count]
         xs, gs = refs[count : count + size], refs[count + size : count + 2 * size]
-        hid, gg, gu, gn, part, x_out, g_out = refs[count + 2 * size : count + 2 * size + 7]
-        gu_w, d_w, x_all, g_all, sems = refs[count + 2 * size + 7 :]
+        outs = refs[count + 2 * size : count + 2 * size + 9]
+        hid, gg, gu, gn_kept, gn_given, part_kept, part_given, x_out, g_out = outs
+        gu_w, d_w, x_all, g_all, held, sems = refs[count + 2 * size + 9 :]
         step = pl.program_id(0)
+        core = me_ref[0] % 2
+        handed = [
+            pltpu.make_async_copy(src, dst, sems.at[2 * count + 2 * size + i])
+            for i, (src, dst) in enumerate(((x_all, x_out), (g_all, g_out)))
+        ]
 
         @pl.when(step == 0)
         def _():
@@ -286,11 +299,11 @@
                 copy.start()
             for copy in started:
                 copy.wait()
-
-        x = x_all[step]
-        g = g_all[step]
-        x_out[...] = x
-        g_out[...] = g
+            for copy in handed:
+                copy.start()
+
+        x = x_all[pl.ds(2 * step, 2)].reshape(2 * rows, width)
+        g = g_all[pl.ds(2 * step, 2)].reshape(2 * rows, width)
         gate_w = gu_w[: count // 2].reshape(units, width)
         up_w = gu_w[count // 2 :].reshape(units, width)
         down_w = d_w[...].reshape(units, width)
@@ -304,25 +317,40 @@
             hid[:, at] = (silu * up).astype(BF16)
             gg[:, at] = (grad_hidden * up * (sigmoid + silu * (1.0 - sigmoid))).astype(BF16)
             gu[:, at] = (grad_hidden * silu).astype(BF16)
-        gn[...] = (dot(gg[...], gate_w, 1, 0) + dot(gu[...], up_w, 1, 0)).astype(BF16)
-        part[...] = dot(hid[...], down_w, 1, 0).astype(BF16)
+
+        def hand_out(value, kept, given):
+            held[...] = value.astype(BF16).reshape(2, rows, width)
+            kept[0] = held[core]
+            given[0] = held[1 - core]
+
+        hand_out(dot(gg[...], gate_w, 1, 0) + dot(gu[...], up_w, 1, 0), gn_kept, gn_given)
+        hand_out(dot(hid[...], down_w, 1, 0), part_kept, part_given)
+
+        @pl.when(step == size // 2 - 1)
+        def _():
+            for copy in handed:
+                copy.wait()
 
     hbm = pl.BlockSpec(memory_space=pl.ANY)
-    by_rows = lambda n: pl.BlockSpec((rows, n), lambda i: (i, 0))
-    like = lambda n: jax.ShapeDtypeStruct((size * rows, n), BF16)
+    by_rows = pl.BlockSpec((2 * rows, units), lambda i: (i, 0))
+    by_pair = pl.BlockSpec((1, rows, width), lambda i: (i, 0, 0))
+    like = jax.ShapeDtypeStruct
     return pl.pallas_call(
         body,
-        grid=(size,),
+        grid=(size // 2,),
         in_specs=[pl.BlockSpec(memory_space=pltpu.SMEM)]
         + [hbm] * (count + 2 * size),
-        out_specs=[by_rows(units)] * 3 + [by_rows(width)] * 4,
-        out_shape=[like(units)] * 3 + [like(width)] * 4,
+        out_specs=[by_rows] * 3 + [by_pair] * 4 + [hbm] * 2,
+        out_shape=[like((size * rows, units), BF16)] * 3
+        + [like((size // 2, rows, width), BF16)] * 4
+        + [like((size, rows, width), BF16)] * 2,
         scratch_shapes=[
             pltpu.VMEM((count, 2 * tall, width), BF16),
             pltpu.VMEM((count, tall, width), BF16),
             pltpu.VMEM((size, rows, width), BF16),
             pltpu.VMEM((size, rows, width), BF16),
-            pltpu.SemaphoreType.DMA((2 * count + 2 * size,)),
+            pltpu.VMEM((2, rows, width), BF16),
+            pltpu.SemaphoreType.DMA((2 * count + 2 * size + 2,)),
         ],
         compiler_params=pltpu.CompilerParams(vmem_limit_bytes=VMEM_LIMIT),
         cost_estimate=pl.CostEstimate(flops=1, bytes_accessed=1, transcendentals=0),
@@ -597,6 +625,8 @@
     strip = down_weight.shape[0] // seq_size
     tall = padded(strip)
 
+    ff_cut = cut_ff(me, gate_up_weight, down_weight, seq_size)
+    ff_share = [ff_cut[0]] + [swap(ff_cut[o], "seq", seq_size, o) for o in offsets if o]
     qkv_tall = padded(qkv_rows)
     packed = jnp.concatenate(
         [
@@ -609,22 +639,21 @@
         ],
         axis=0,
     )
-    ff_cut = cut_ff(me, gate_up_weight, down_weight, seq_size)
-    ff_share = [ff_cut[0]] + [swap(ff_cut[o], "seq", seq_size, o) for o in offsets if o]
+    packed = after(packed, ff_cut[0])
+    ff_block = join_lanes(me, ff_share)
     columns = ff_spread(
-        after(column_gather(packed, fsdp_size), *ff_share[1:]), fsdp_size
-    )
-    ff_block = join_lanes(me, ff_share)
+        after(column_gather(packed, fsdp_size), ff_block), fsdp_size
+    )
     wide = qkv_tall + 16
-    packed_stack = jnp.concatenate([columns[m][:, :wide] for m in sorted(columns)], axis=0)
     out_stack = jnp.concatenate([columns[m][:, wide:] for m in sorted(columns)], axis=0)
-    packed_blocks = seq_gather(after(packed_stack, ff_block), seq_size)
+    columns[0] = after(columns[0], ff_block)
+    packed_pieces = [seq_gather(columns[m][:, :wide], seq_size) for m in sorted(columns)]
     ff_blocks = {0: ff_block}
     for bit in fsdp_bits(fsdp_size)[:2]:
         ff_blocks.update({o ^ bit: swap(b, "fsdp", fsdp_size, bit) for o, b in ff_blocks.items()})
     inner = fsdp_size // OUTER
 
-    qkv_pieces = [[packed_blocks[o]] for o in offsets]
+    qkv_pieces = [[piece[o] for piece in packed_pieces] for o in offsets]
     qkv_t, vectors = join_both(me, qkv_pieces, qkv_tall)
     own_x = ff_spread(ff_block, fsdp_size)
     qkv_t = after(qkv_t, ff_blocks[2 * inner], ff_blocks[inner], *own_x.values())[:, :qkv_rows].reshape(fsdp_size * qkv_rows, -1)
@@ -632,7 +661,7 @@
     bias_full = vectors[:, 1, : qkv_bias.shape[0]].reshape(-1).astype(F32)
     gain_two = vectors[:, 2, : norm_two.shape[0]].reshape(-1).astype(F32)
 
-    out_blocks = seq_gather(after(out_stack, packed_blocks[seq_size // 2]), seq_size)
+    out_blocks = seq_gather(after(out_stack, packed_pieces[-1][seq_size // 2]), seq_size)
 
     inputs = tokens.astype(F32)
     scale_one = rms_scale(inputs)
@@ -643,7 +672,7 @@
     queries = turned[:, :QW] * jnp.asarray(0.125, BF16)
     kv_local = jnp.concatenate([turned[:, QW:], joined[:, QW + KVW :].astype(BF16)], axis=1)
     kv_all = lax.all_gather(kv_local, "seq", axis=0, tiled=True)
-    kv_all = after(kv_all, ff_blocks[2 * inner], ff_blocks[inner])
+    kv_all = after(kv_all, ff_blocks[2 * inner])
     cot_blocks = seq_gather(after(cotangent, kv_all), seq_size)
     row_place = jnp.arange(row_count, dtype=jnp.int32)
     high = my_seq * row_count + row_place
@@ -684,15 +713,18 @@
             {o ^ bit: swap(b, "seq", seq_size, bit) for o, b in normed_blocks.items()}
         )
         bit //= 2
-    hidden, grad_gate, grad_up, grad_normed, layer_part, normed_all, cot_all = feed_forward(
+    (
+        hidden, grad_gate, grad_up, kept, given, kept_layer, given_layer, normed_all, cot_all,
+    ) = feed_forward(
         me,
         [ff_blocks[o] for o in range(fsdp_size)],
         [normed_blocks[o] for o in offsets],
         [cot_blocks[o] for o in offsets],
     )
+    normed_all = normed_all.reshape(seq_size * row_count, -1)
+    cot_all = cot_all.reshape(seq_size * row_count, -1)
     by_seq = lambda rows: rows.reshape(seq_size, row_count, -1)
 
-    kept, given = halve(by_seq(grad_normed), 1, my_seq)
     normed_sum = add(kept, swap(given, "seq", seq_size, 1))
     bit = 2
     while bit < seq_size:
@@ -763,8 +795,7 @@
     out_term = stack_from_lanes(dot(attn_late, grad_branch, 0, 0).astype(BF16), seq_size)
     kept, given = halve(out_term, 1, my_seq)
     out_sum = add(kept, swap(given, "seq", seq_size, 1))
-    kept, given = halve(after(by_seq(layer_part), dq_two), 1, my_seq)
-    layer_sum = add(kept, swap(given, "seq", seq_size, 1))
+    layer_sum = add(kept_layer, swap(after(given_layer, dq_two), "seq", seq_size, 1))
     kept_layer, given_layer = halve(layer_sum, 1, my_seq // 2)
     bit = 2
     while bit < seq_size:
@@ -798,7 +829,7 @@
     )
     tail = after(tail, next_two)
     tail_mine = seq_scatter(tail, seq_size, my_seq)
-    got_layer = swap(after(given_layer, tail_mine), "seq", seq_size, 2)
+    got_layer = swap(after(given_layer, kv_mine), "seq", seq_size, 2)
     layer_sum = add(kept_layer, got_layer)
     bit = 4
     while bit < seq_size:
@@ -814,7 +845,7 @@
     grad_gate_up, grad_down = join_ff(me, ff_got, strip)
 
     tail_sum = fsdp_scatter(
-        after(jnp.concatenate([tail_mine, out_mine], axis=1), next_three), fsdp_size, my_fsdp
+        jnp.concatenate([tail_mine, out_mine], axis=1), fsdp_size, my_fsdp, next_three
     )
     pieces = [
         tail_sum[qkv_rows + i, : v.shape[0] // fsdp_size] for i, v in enumerate(vector_terms)

time: 391 us -> 369 us (0.944)
  waiting for transfers between devices: 122 us -> 90.7 us
  starting transfers between devices: 44.6 us -> 50.8 us
    ppermute x51 -> x55, waiting for transfers between devices: 122 us -> 90.7 us  [swap(): return lax.ppermute(block, axis, [(i, i ^ bits) for i in range(size)])]
    ppermute x51 -> x55, starting transfers between devices: 44.6 us -> 50.8 us  [swap(): return lax.ppermute(block, axis, [(i, i ^ bits) for i in range(size)])]
    reshape x7 -> x5, local copies, waits for them, and re-layouts: 8.49 us -> 4.81 us  [halve(): merge = lambda part: part.reshape((above * bit,) + stack.shape[1:])]
    unnamed x114 -> x112, local copies, waits for them, and re-layouts: 16.4 us -> 16.3 us
    add x15 -> x14, other arithmetic: 16.7 us -> 16.7 us  [add(): return kept.astype(F32) + got.astype(F32)]
  transfers between devices with their start and end apart: 51 -> 55, of which waited for: 23 -> 23; matrix products, arithmetic and copies ran while one was open for 22% -> 24% of each run, Pallas kernels for 17% -> 18%
where the time goes in v6:
time: 369 us; the launch traced here: 362 us
  Pallas kernels  99.5 us (27%)
  waiting for transfers between devices  90.7 us (25%)
  local copies, waits for them, and re-layouts  52.9 us (14%)
  starting transfers between devices  50.8 us (14%)
  other arithmetic  32.1 us (9%)
  matrix products  25.1 us (7%)
  blocking collectives  8.31 us (2%)
    ppermute x55, waiting for transfers between devices, swap(): return lax.ppermute(block, axis, [(i, i ^ bits) for i in range(size)])  90.7 us
    ppermute x55, starting transfers between devices, swap(): return lax.ppermute(block, axis, [(i, i ^ bits) for i in range(size)])  50.8 us
    pallas_call x1, Pallas kernels, feed_forward(): pl.pallas_call(body, grid=(size // 2,), in_specs=[pl.BlockSpec(memory_spa...  33.8 us
    pallas_call x2, Pallas kernels, attend_back(): pl.pallas_call(functools.partial(attend_back_kernel, begin), grid=(pairs,...  32.4 us
    dot_general x9, matrix products, dot(): lax.dot_general(left, right, (((left_dim,), (right_dim,)), ((), ())), pre...  25.1 us
    pallas_call x2, Pallas kernels, attend(): pl.pallas_call(functools.partial(attend_kernel, begin), grid=(pairs,), in...  23.4 us
    add x14, other arithmetic, add(): return kept.astype(F32) + got.astype(F32)  16.7 us
    unnamed x112, local copies, waits for them, and re-layouts  16.3 us
  transfers between devices with their start and end apart: 55, of which 23 were waited for; matrix products, arithmetic and copies ran while one was open for 24% of the time, Pallas kernels for 18%

profile of v6, /device:TPU:0, one launch (start us, length us, event | category | flops | bytes accessed | tf_op | source)
XLA Modules:
  0.0 361.8 jit_solution(12122111566499037759)
XLA Ops:
  15.4 8.0 %collective-permute-done.1 = bf16[272,224]{1,0:T(8,128)(2,1)S(1)} collective-permute-done((bf16[272,224]{1,0:T(8,128)(2,1)S(1)}, bf16[272,224]{1,0:T(8,128)(2,1)S(1)}, u32[]{:S(2)}, u32[]{:S(2)}) %collective-permute-start.1) | collective-permute-done | bytes 121888 | tf_op jit(solution)/shard_map/ppermute | solution.py:36
  35.5 3.8 %collective-permute-done.9.refs_4_ = bf16[4,160,224]{2,1,0:T(8,128)(2,1)S(1)} collective-permute-done((bf16[4,160,224]{2,1,0:T(8,128)(2,1)S(1)}, bf16[4,160,224]{2,1,0:T(8,128)(2,1)S(1)}, u32[]{:S(2)}, u32[]{:S(2)}) %collective-permute-start.9) | collective-permute-done | bytes 286752 | tf_op jit(solution)/shard_map/ppermute | solution.py:36
  46.4 7.3 %collective-permute-done.10.refs_5_ = bf16[4,160,224]{2,1,0:T(8,128)(2,1)S(1)} collective-permute-done((bf16[4,160,224]{2,1,0:T(8,128)(2,1)S(1)}, bf16[4,160,224]{2,1,0:T(8,128)(2,1)S(1)}, u32[]{:S(2)}, u32[]{:S(2)}) %collective-permute-start.10) | collective-permute-done | bytes 286752 | tf_op jit(solution)/shard_map/ppermute | solution.py:36
  63.5 3.2 join_both.2
  66.7 5.7 %collective-permute-done.13.refs_4_ = bf16[480,896]{1,0:T(8,128)(2,1)} collective-permute-done((bf16[480,896]{1,0:T(8,128)(2,1)S(1)}, bf16[480,896]{1,0:T(8,128)(2,1)}, u32[]{:S(2)}, u32[]{:S(2)}) %collective-permute-start.13) | collective-permute-done | bytes 860192 | tf_op jit(solution)/shard_map/ppermute | solution.py:36
  72.7 3.1 convolution_add_fusion
  78.5 8.3 %all_gather.3.kv_ref = bf16[1536,256]{1,0:T(8,128)(2,1)S(1)} all-gather(bf16[384,256]{1,0:T(8,128)(2,1)S(1)} %pad_maximum_fusion.9), channel_id=1, replica_groups=mesh['seq'=4,'fsdp'=8] {'seq'}, dimensions={0}, use_global_device_ids=true | all-gather | bytes 983040 | tf_op jit(solution)/shard_map/all_gather | solution.py:674
  90.6 13.4 %attend.2 = (bf16[384,512]{1,0:T(8,128)(2,1)S(1)}, f32[4,1,768]{2,1,0:T(1,128)S(1)}) custom-call(s32[1,384]{1,0:T(1,128)S(1)} %broadcast_in_dim.12.low_ref, s32[1,384]{1,0:T(1,128)S(1)} %iota_add_fusion.high_ref, s32[1536,1]{1,0:T(8,128)S(1)} %iota.43.place_ref, bf16[384,896]{1,0:T(8,128)(2,1)S(1)} %slice_multiply_fusion.1.q_ref, ...), custom_call_target="tpu_custom_call" | custom-call | flops 1 | bytes 1 | tf_op jit(solution)/shard_map/attend/pallas_call | solution.py:507
  109.2 10.0 %attend.3 = (bf16[384,384]{1,0:T(8,128)(2,1)S(1)}, f32[3,1,768]{2,1,0:T(1,128)S(1)}) custom-call(s32[1,384]{1,0:T(1,128)S(1)} %broadcast_in_dim.12.low_ref, s32[1,384]{1,0:T(1,128)S(1)} %iota_add_fusion.high_ref, s32[1536,1]{1,0:T(8,128)S(1)} %iota.49.place_ref, bf16[384,896]{1,0:T(8,128)(2,1)S(1)} %slice_multiply_fusion.1.q_ref, ...), custom_call_target="tpu_custom_call" | custom-call | flops 1 | bytes 1 | tf_op jit(solution)/shard_map/attend/pallas_call | solution.py:507
  120.5 6.3 %collective-permute-done.21.refs_5_ = bf16[480,896]{1,0:T(8,128)(2,1)S(1)} collective-permute-done((bf16[480,896]{1,0:T(8,128)(2,1)}, bf16[480,896]{1,0:T(8,128)(2,1)S(1)}, u32[]{:S(2)}, u32[]{:S(2)}) %collective-permute-start.21) | collective-permute-done | bytes 860192 | tf_op jit(solution)/shard_map/ppermute | solution.py:36
  131.8 12.0 %collective-permute-done.25.refs_10_ = bf16[384,896]{1,0:T(8,128)(2,1)S(1)} collective-permute-done((bf16[384,896]{1,0:T(8,128)(2,1)S(1)}, bf16[384,896]{1,0:T(8,128)(2,1)S(1)}, u32[]{:S(2)}, u32[]{:S(2)}) %collective-permute-start.25) | collective-permute-done | bytes 688160 | tf_op jit(solution)/shard_map/ppermute | solution.py:36
  143.9 7.1 %collective-permute-done.23.refs_7_ = bf16[480,896]{1,0:T(8,128)(2,1)S(1)} collective-permute-done((bf16[480,896]{1,0:T(8,128)(2,1)}, bf16[480,896]{1,0:T(8,128)(2,1)S(1)}, u32[]{:S(2)}, u32[]{:S(2)}) %collective-permute-start.23) | collective-permute-done | bytes 860192 | tf_op jit(solution)/shard_map/ppermute | solution.py:36
  151.9 33.8 %feed_forward.1 = (bf16[1536,1280]{1,0:T(8,128)(2,1)}, bf16[1536,1280]{1,0:T(8,128)(2,1)}, bf16[1536,1280]{1,0:T(8,128)(2,1)}, bf16[2,384,896]{2,1,0:T(8,128)(2,...) custom-call(s32[2]{0:T(128)S(1)} %pad_add_fusion.me_ref, ...), custom_call_target="tpu_custom_call" | custom-call | flops 1 | bytes 1 | tf_op jit(solution)/shard_map/feed_forward/pallas_call | solution.py:338
  185.9 3.3 collective-permute-done.29
  193.0 4.5 %convolution_convert_fusion.3 = bf16[1280,896]{1,0:T(8,128)(2,1)S(1)} fusion(bf16[1536,1280]{1,0:T(8,128)(2,1)S(1)} %copy-done.50, bf16[1536,896]{1,0:T(8,128)(2,1)S(1)} %bitcast.191), kind=kOutput, calls=%fused_computation.3 | convolution fusion | flops 3524362240 | bytes 8978432 | tf_op jit(solution)/shard_map/dot_general | solution.py:30
  197.6 4.7 %convolution_convert_fusion.1 = bf16[1280,896]{1,0:T(8,128)(2,1)S(1)} fusion(bf16[1536,1280]{1,0:T(8,128)(2,1)S(1)} %copy-done.49, bf16[1536,896]{1,0:T(8,128)(2,1)S(1)} %bitcast.189), kind=kOutput, calls=%fused_computation.1 | convolution fusion | flops 3524362240 | bytes 8978432 | tf_op jit(solution)/shard_map/dot_general | solution.py:30
  204.4 4.5 %convolution_convert_fusion.2 = bf16[1280,896]{1,0:T(8,128)(2,1)S(1)} fusion(bf16[1536,1280]{1,0:T(8,128)(2,1)S(1)} %copy-done.48, bf16[1536,896]{1,0:T(8,128)(2,1)S(1)} %bitcast.190), kind=kOutput, calls=%fused_computation.2 | convolution fusion | flops 3524362240 | bytes 8978432 | tf_op jit(solution)/shard_map/dot_general | solution.py:30
  219.9 18.0 %attend_back.2 = (f32[384,512]{1,0:T(8,128)S(1)}, f32[1536,256]{1,0:T(8,128)}) custom-call(s32[1,384]{1,0:T(1,128)S(1)} %broadcast_in_dim.12.low_ref, s32[1,384]{1,0:T(1,128)S(1)} %iota_add_fusion.high_ref, s32[1536,1]{1,0:T(8,128)S(1)} %iota.51.place_ref, bf16[384,896]{1,0:T(8,128)(2,1)S(1)} %slice_multiply_fusion.1.q_ref, ...), custom_call_target="tpu_custom_call" | custom-call | flops 1 | bytes 1 | tf_op jit(solution)/shard_map/attend_back/pallas_call | solution.py:533
  241.8 14.4 %attend_back.3 = (f32[384,384]{1,0:T(8,128)S(1)}, f32[1536,256]{1,0:T(8,128)}) custom-call(s32[1,384]{1,0:T(1,128)S(1)} %broadcast_in_dim.12.low_ref, s32[1,384]{1,0:T(1,128)S(1)} %iota_add_fusion.high_ref, s32[1536,1]{1,0:T(8,128)S(1)} %iota.50.place_ref, bf16[384,896]{1,0:T(8,128)(2,1)S(1)} %slice_multiply_fusion.1.q_ref, ...), custom_call_target="tpu_custom_call" | custom-call | flops 1 | bytes 1 | tf_op jit(solution)/shard_map/attend_back/pallas_call | solution.py:533
  282.4 4.4 %copy.43 = bf16[1152,4,224]{2,0,1:T(8,128)(2,1)} copy(bf16[1152,4,224]{0,2,1:T(8,128)(2,1)} %bitcast.181) | data formatting | bytes 4128768 | tf_op jit(solution)/shard_map/reshape | solution.py:612
  314.0 12.0 %collective-permute-done.44 = bf16[2,160,896]{2,1,0:T(8,128)(2,1)} collective-permute-done((bf16[2,160,896]{2,1,0:T(8,128)(2,1)}, bf16[2,160,896]{2,1,0:T(8,128)(2,1)}, u32[]{:S(2)}, u32[]{:S(2)}) %collective-permute-start.44) | collective-permute-done | bytes 573472 | tf_op jit(solution)/shard_map/ppermute | solution.py:36
  330.9 5.1 %collective-permute-done.49 = bf16[1,160,896]{2,1,0:T(8,128)(2,1)S(1)} collective-permute-done((bf16[1,160,896]{2,1,0:T(8,128)(2,1)S(1)}, bf16[1,160,896]{2,1,0:T(8,128)(2,1)S(1)}, u32[]{:S(2)}, u32[]{:S(2)}) %collective-permute-start.49) | collective-permute-done | bytes 286752 | tf_op jit(solution)/shard_map/ppermute | solution.py:36
  338.9 4.0 %collective-permute-done.42 = bf16[4,272,224]{2,1,0:T(8,128)(2,1)S(1)} collective-permute-done((bf16[4,272,224]{2,1,0:T(8,128)(2,1)S(1)}, bf16[4,272,224]{2,1,0:T(8,128)(2,1)S(1)}, u32[]{:S(2)}, u32[]{:S(2)}) %collective-permute-start.42) | collective-permute-done | bytes 487456 | tf_op jit(solution)/shard_map/ppermute | solution.py:36
  353.9 3.5 collective-permute-done.46
  (335 shorter events, 159.0 us)
Async XLA Ops:
  31.3 41.1 %collective-permute-start.13 = (bf16[480,896]{1,0:T(8,128)(2,1)S(1)}, bf16[480,896]{1,0:T(8,128)(2,1)}, u32[]{:S(2)}, u32[]{:S(2)}) collective-permute-start(bf16[480,896]{1,0:T(8,128)(2,1)S(1)} %join_lanes.1.refs_0_), channel_id=1, source_target_pairs={{0,4},{1,5},{2,6},{3,7},{4,0},{5,1},{6,2},{7,3},{8,12},{9,13},{10,... | collective-permute-start | bytes 2580488 | tf_op jit(solution)/shard_map/ppermute | solution.py:36
  33.0 39.5 %collective-permute-start.14 = (bf16[480,896]{1,0:T(8,128)(2,1)S(1)}, bf16[480,896]{1,0:T(8,128)(2,1)}, u32[]{:S(2)}, u32[]{:S(2)}) collective-permute-start(bf16[480,896]{1,0:T(8,128)(2,1)S(1)} %join_lanes.1.refs_0_), channel_id=1, source_target_pairs={{0,2},{1,3},{2,0},{3,1},{4,6},{5,7},{6,4},{7,5},{8,10},{9,11},{10,... | collective-permute-start | bytes 2580488 | tf_op jit(solution)/shard_map/ppermute | solution.py:36
  39.3 33.2 %collective-permute-start.15 = (bf16[480,896]{1,0:T(8,128)(2,1)S(1)}, bf16[480,896]{1,0:T(8,128)(2,1)}, u32[]{:S(2)}, u32[]{:S(2)}) collective-permute-start(bf16[480,896]{1,0:T(8,128)(2,1)S(1)} %join_lanes.1.refs_0_), channel_id=1, source_target_pairs={{0,1},{1,0},{2,3},{3,2},{4,5},{5,4},{6,7},{7,6},{8,9},{9,8},{10,11... | collective-permute-start | bytes 2580488 | tf_op jit(solution)/shard_map/ppermute | solution.py:36
  61.7 26.9 %collective-permute-start.19 = (bf16[8,112,224]{2,1,0:T(8,128)(2,1)S(1)}, bf16[8,112,224]{2,1,0:T(8,128)(2,1)}, u32[]{:S(2)}, u32[]{:S(2)}) collective-permute-start(bf16[8,112,224]{2,1,0:T(8,128)(2,1)S(1)} %pad_maximum_fusion.6.refs_0_), channel_id=1, source_target_pairs={{0,16},{8,24},{16,0},{24,8},{1,17},{9,25},{17,1},{25,9},{2,18},{10... | collective-permute-start | bytes 1204232 | tf_op jit(solution)/shard_map/ppermute | solution.py:36
  86.8 22.3 %collective-permute-start.17 = (bf16[480,896]{1,0:T(8,128)(2,1)}, bf16[480,896]{1,0:T(8,128)(2,1)}, u32[]{:S(2)}, u32[]{:S(2)}) collective-permute-start(bf16[480,896]{1,0:T(8,128)(2,1)} %collective-permute-done.14.refs_2_), channel_id=1, source_target_pairs={{0,1},{1,0},{2,3},{3,2},{4,5},{5,4},{6,7},{7,6},{8,9},{9,8},{10,11... | collective-permute-start | bytes 2580488 | tf_op jit(solution)/shard_map/ppermute | solution.py:36
  87.4 20.3 %collective-permute-start.16 = (bf16[384,896]{1,0:T(8,128)(2,1)S(1)}, bf16[384,896]{1,0:T(8,128)(2,1)}, u32[]{:S(2)}, u32[]{:S(2)}) collective-permute-start(bf16[384,896]{1,0:T(8,128)(2,1)S(1)} %copy-done.3), channel_id=1, source_target_pairs={{0,16},{8,24},{16,0},{24,8},{1,17},{9,25},{17,1},{25,9},{2,18},{10... | collective-permute-start | bytes 2064392 | tf_op jit(solution)/shard_map/ppermute | solution.py:36
  88.5 17.2 %collective-permute-start.20 = (bf16[8,112,224]{2,1,0:T(8,128)(2,1)}, bf16[8,112,224]{2,1,0:T(8,128)(2,1)}, u32[]{:S(2)}, u32[]{:S(2)}) collective-permute-start(bf16[8,112,224]{2,1,0:T(8,128)(2,1)} %collective-permute-done.19.refs_2_), channel_id=1, source_target_pairs={{0,8},{8,0},{16,24},{24,16},{1,9},{9,1},{17,25},{25,17},{2,10},{10... | collective-permute-start | bytes 1204232 | tf_op jit(solution)/shard_map/ppermute | solution.py:36
  89.0 40.8 %collective-permute-start.22 = (bf16[480,896]{1,0:T(8,128)(2,1)}, bf16[480,896]{1,0:T(8,128)(2,1)}, u32[]{:S(2)}, u32[]{:S(2)}) collective-permute-start(bf16[480,896]{1,0:T(8,128)(2,1)} %collective-permute-done.14.refs_2_), channel_id=1, source_target_pairs={{0,4},{1,5},{2,6},{3,7},{4,0},{5,1},{6,2},{7,3},{8,12},{9,13},{10,... | collective-permute-start | bytes 2580488 | tf_op jit(solution)/shard_map/ppermute | solution.py:36
  104.1 22.7 %collective-permute-start.21 = (bf16[480,896]{1,0:T(8,128)(2,1)}, bf16[480,896]{1,0:T(8,128)(2,1)S(1)}, u32[]{:S(2)}, u32[]{:S(2)}) collective-permute-start(bf16[480,896]{1,0:T(8,128)(2,1)} %collective-permute-done.13.refs_4_), channel_id=1, source_target_pairs={{0,1},{1,0},{2,3},{3,2},{4,5},{5,4},{6,7},{7,6},{8,9},{9,8},{10,11... | collective-permute-start | bytes 2580488 | tf_op jit(solution)/shard_map/ppermute | solution.py:36
  126.8 17.0 %collective-permute-start.25 = (bf16[384,896]{1,0:T(8,128)(2,1)S(1)}, bf16[384,896]{1,0:T(8,128)(2,1)S(1)}, u32[]{:S(2)}, u32[]{:S(2)}) collective-permute-start(bf16[384,896]{1,0:T(8,128)(2,1)S(1)} %multiply_convert_fusion.refs_8_), channel_id=1, source_target_pairs={{0,16},{8,24},{16,0},{24,8},{1,17},{9,25},{17,1},{25,9},{2,18},{10... | collective-permute-start | bytes 2064392 | tf_op jit(solution)/shard_map/ppermute | solution.py:36
  129.8 21.2 %collective-permute-start.23 = (bf16[480,896]{1,0:T(8,128)(2,1)}, bf16[480,896]{1,0:T(8,128)(2,1)S(1)}, u32[]{:S(2)}, u32[]{:S(2)}) collective-permute-start(bf16[480,896]{1,0:T(8,128)(2,1)} %collective-permute-done.22.refs_6_), channel_id=1, source_target_pairs={{0,1},{1,0},{2,3},{3,2},{4,5},{5,4},{6,7},{7,6},{8,9},{9,8},{10,11... | collective-permute-start | bytes 2580488 | tf_op jit(solution)/shard_map/ppermute | solution.py:36
  131.8 19.2 %collective-permute-start.24 = (bf16[384,896]{1,0:T(8,128)(2,1)S(1)}, bf16[384,896]{1,0:T(8,128)(2,1)S(1)}, u32[]{:S(2)}, u32[]{:S(2)}) collective-permute-start(bf16[384,896]{1,0:T(8,128)(2,1)S(1)} %multiply_convert_fusion.refs_8_), channel_id=1, source_target_pairs={{0,8},{8,0},{16,24},{24,16},{1,9},{9,1},{17,25},{25,17},{2,10},{10... | collective-permute-start | bytes 2064392 | tf_op jit(solution)/shard_map/ppermute | solution.py:36
  191.5 23.6 %collective-permute-start.30 = (bf16[1,384,896]{2,1,0:T(8,128)(2,1)S(1)}, bf16[1,384,896]{2,1,0:T(8,128)(2,1)S(1)}, u32[]{:S(2)}, u32[]{:S(2)}) collective-permute-start(bf16[1,384,896]{2,1,0:T(8,128)(2,1)S(1)} %dynamic-slice_convert_fusion.1), channel_id=1, source_target_pairs={{0,16},{8,24},{16,0},{24,8},{1,17},{9,25},{17,1},{25,9},{2,18},{10... | collective-permute-start | bytes 2064392 | tf_op jit(solution)/shard_map/ppermute | solution.py:36
  210.2 28.4 %collective-permute-start.31 = (bf16[4,160,896]{2,1,0:T(8,128)(2,1)}, bf16[4,160,896]{2,1,0:T(8,128)(2,1)}, u32[]{:S(2)}, u32[]{:S(2)}) collective-permute-start(bf16[4,160,896]{2,1,0:T(8,128)(2,1)} %dynamic-slice_bitcast_fusion.3), channel_id=1, source_target_pairs={{0,1},{1,0},{2,3},{3,2},{4,5},{5,4},{6,7},{7,6},{8,9},{9,8},{10,11... | collective-permute-start | bytes 3440648 | tf_op jit(solution)/shard_map/ppermute | solution.py:36
  216.8 46.4 %collective-permute-start.34 = (bf16[4,160,896]{2,1,0:T(8,128)(2,1)}, bf16[4,160,896]{2,1,0:T(8,128)(2,1)}, u32[]{:S(2)}, u32[]{:S(2)}) collective-permute-start(bf16[4,160,896]{2,1,0:T(8,128)(2,1)} %dynamic-slice_bitcast_fusion.2), channel_id=1, source_target_pairs={{0,1},{1,0},{2,3},{3,2},{4,5},{5,4},{6,7},{7,6},{8,9},{9,8},{10,11... | collective-permute-start | bytes 3440648 | tf_op jit(solution)/shard_map/ppermute | solution.py:36
  241.4 36.3 %collective-permute-start.50 = (bf16[2,160,896]{2,1,0:T(8,128)(2,1)}, bf16[2,160,896]{2,1,0:T(8,128)(2,1)}, u32[]{:S(2)}, u32[]{:S(2)}) collective-permute-start(bf16[2,160,896]{2,1,0:T(8,128)(2,1)} %fusion.24), channel_id=1, source_target_pairs={{0,4},{1,5},{2,6},{3,7},{4,0},{5,1},{6,2},{7,3},{8,12},{9,13},{10,... | collective-permute-start | bytes 1720328 | tf_op jit(solution)/shard_map/ppermute | solution.py:36
  257.5 34.9 %collective-permute-start.43 = (bf16[4,160,896]{2,1,0:T(8,128)(2,1)}, bf16[4,160,896]{2,1,0:T(8,128)(2,1)}, u32[]{:S(2)}, u32[]{:S(2)}) collective-permute-start(bf16[4,160,896]{2,1,0:T(8,128)(2,1)} %dynamic-slice_bitcast_fusion.1), channel_id=1, source_target_pairs={{0,1},{1,0},{2,3},{3,2},{4,5},{5,4},{6,7},{7,6},{8,9},{9,8},{10,11... | collective-permute-start | bytes 3440648 | tf_op jit(solution)/shard_map/ppermute | solution.py:36
  260.5 49.6 %collective-permute-start.32 = (bf16[2,384,896]{2,1,0:T(8,128)(2,1)}, bf16[2,384,896]{2,1,0:T(8,128)(2,1)}, u32[]{:S(2)}, u32[]{:S(2)}) collective-permute-start(bf16[2,384,896]{2,1,0:T(8,128)(2,1)} %get-tuple-element.118), channel_id=1, source_target_pairs={{0,8},{8,0},{16,24},{24,16},{1,9},{9,1},{17,25},{25,17},{2,10},{10... | collective-permute-start | bytes 4128776 | tf_op jit(solution)/shard_map/ppermute | solution.py:36
  266.3 27.1 %collective-permute-start.37 = (bf16[2,160,896]{2,1,0:T(8,128)(2,1)}, bf16[2,160,896]{2,1,0:T(8,128)(2,1)}, u32[]{:S(2)}, u32[]{:S(2)}) collective-permute-start(bf16[2,160,896]{2,1,0:T(8,128)(2,1)} %fusion.25), channel_id=1, source_target_pairs={{0,4},{1,5},{2,6},{3,7},{4,0},{5,1},{6,2},{7,3},{8,12},{9,13},{10,... | collective-permute-start | bytes 1720328 | tf_op jit(solution)/shard_map/ppermute | solution.py:36
  279.9 18.4 %collective-permute-start.51 = (bf16[1,160,896]{2,1,0:T(8,128)(2,1)S(1)}, bf16[1,160,896]{2,1,0:T(8,128)(2,1)}, u32[]{:S(2)}, u32[]{:S(2)}) collective-permute-start(bf16[1,160,896]{2,1,0:T(8,128)(2,1)S(1)} %dynamic-slice_convert_fusion.7), channel_id=1, source_target_pairs={{0,2},{1,3},{2,0},{3,1},{4,6},{5,7},{6,4},{7,5},{8,10},{9,11},{10,... | collective-permute-start | bytes 860168 | tf_op jit(solution)/shard_map/ppermute | solution.py:36
  297.2 28.8 %collective-permute-start.44 = (bf16[2,160,896]{2,1,0:T(8,128)(2,1)}, bf16[2,160,896]{2,1,0:T(8,128)(2,1)}, u32[]{:S(2)}, u32[]{:S(2)}) collective-permute-start(bf16[2,160,896]{2,1,0:T(8,128)(2,1)} %fusion.26), channel_id=1, source_target_pairs={{0,4},{1,5},{2,6},{3,7},{4,0},{5,1},{6,2},{7,3},{8,12},{9,13},{10,... | collective-permute-start | bytes 1720328 | tf_op jit(solution)/shard_map/ppermute | solution.py:36
  301.8 28.0 %collective-permute-start.48 = (bf16[1,160,896]{2,1,0:T(8,128)(2,1)}, bf16[1,160,896]{2,1,0:T(8,128)(2,1)}, u32[]{:S(2)}, u32[]{:S(2)}) collective-permute-start(bf16[1,160,896]{2,1,0:T(8,128)(2,1)} %dynamic-slice_convert_fusion.9), channel_id=1, source_target_pairs={{0,2},{1,3},{2,0},{3,1},{4,6},{5,7},{6,4},{7,5},{8,10},{9,11},{10,... | collective-permute-start | bytes 860168 | tf_op jit(solution)/shard_map/ppermute | solution.py:36
  309.2 18.1 %collective-permute-start.39 = (bf16[1,8,160,224]{3,2,1,0:T(8,128)(2,1)S(1)}, bf16[1,8,160,224]{3,2,1,0:T(8,128)(2,1)S(1)}, u32[]{:S(2)}, u32[]{:S(2)}) collective-permute-start(bf16[1,8,160,224]{3,2,1,0:T(8,128)(2,1)S(1)} %dynamic-slice_convert_fusion.2), channel_id=1, source_target_pairs={{0,16},{8,24},{16,0},{24,8},{1,17},{9,25},{17,1},{25,9},{2,18},{10... | collective-permute-start | bytes 1720328 | tf_op jit(solution)/shard_map/ppermute | solution.py:36
  312.8 32.3 %collective-permute-start.36 = (bf16[1,384,896]{2,1,0:T(8,128)(2,1)}, bf16[1,384,896]{2,1,0:T(8,128)(2,1)}, u32[]{:S(2)}, u32[]{:S(2)}) collective-permute-start(bf16[1,384,896]{2,1,0:T(8,128)(2,1)} %dynamic-slice_convert_fusion), channel_id=1, source_target_pairs={{0,16},{8,24},{16,0},{24,8},{1,17},{9,25},{17,1},{25,9},{2,18},{10... | collective-permute-start | bytes 2064392 | tf_op jit(solution)/shard_map/ppermute | solution.py:36
  (85 other events, 710.1 us)

commit v7 on v6

--- a/solution.py
+++ b/solution.py
@@ -274,7 +274,7 @@
         xs, gs = refs[count : count + size], refs[count + size : count + 2 * size]
         outs = refs[count + 2 * size : count + 2 * size + 9]
         hid, gg, gu, gn_kept, gn_given, part_kept, part_given, x_out, g_out = outs
-        gu_w, d_w, x_all, g_all, held, sems = refs[count + 2 * size + 9 :]
+        gu_w, d_w, x_all, g_all, sems = refs[count + 2 * size + 9 :]
         step = pl.program_id(0)
         core = me_ref[0] % 2
         handed = [
@@ -302,8 +302,8 @@
             for copy in handed:
                 copy.start()
 
-        x = x_all[pl.ds(2 * step, 2)].reshape(2 * rows, width)
-        g = g_all[pl.ds(2 * step, 2)].reshape(2 * rows, width)
+        x = x_all[step]
+        g = g_all[step]
         gate_w = gu_w[: count // 2].reshape(units, width)
         up_w = gu_w[count // 2 :].reshape(units, width)
         down_w = d_w[...].reshape(units, width)
@@ -318,26 +318,34 @@
             gg[:, at] = (grad_hidden * up * (sigmoid + silu * (1.0 - sigmoid))).astype(BF16)
             gu[:, at] = (grad_hidden * silu).astype(BF16)
 
+        mine = step % 2 == core
+
         def hand_out(value, kept, given):
-            held[...] = value.astype(BF16).reshape(2, rows, width)
-            kept[0] = held[core]
-            given[0] = held[1 - core]
+            low = value.astype(BF16)
+
+            @pl.when(mine)
+            def _():
+                kept[0] = low
+
+            @pl.when(jnp.logical_not(mine))
+            def _():
+                given[0] = low
 
         hand_out(dot(gg[...], gate_w, 1, 0) + dot(gu[...], up_w, 1, 0), gn_kept, gn_given)
         hand_out(dot(hid[...], down_w, 1, 0), part_kept, part_given)
 
-        @pl.when(step == size // 2 - 1)
+        @pl.when(step == size - 1)
         def _():
             for copy in handed:
                 copy.wait()
 
     hbm = pl.BlockSpec(memory_space=pl.ANY)
-    by_rows = pl.BlockSpec((2 * rows, units), lambda i: (i, 0))
-    by_pair = pl.BlockSpec((1, rows, width), lambda i: (i, 0, 0))
+    by_rows = pl.BlockSpec((rows, units), lambda i: (i, 0))
+    by_pair = pl.BlockSpec((1, rows, width), lambda i: (i // 2, 0, 0))
     like = jax.ShapeDtypeStruct
     return pl.pallas_call(
         body,
-        grid=(size // 2,),
+        grid=(size,),
         in_specs=[pl.BlockSpec(memory_space=pltpu.SMEM)]
         + [hbm] * (count + 2 * size),
         out_specs=[by_rows] * 3 + [by_pair] * 4 + [hbm] * 2,
@@ -349,7 +357,6 @@
             pltpu.VMEM((count, tall, width), BF16),
             pltpu.VMEM((size, rows, width), BF16),
             pltpu.VMEM((size, rows, width), BF16),
-            pltpu.VMEM((2, rows, width), BF16),
             pltpu.SemaphoreType.DMA((2 * count + 2 * size + 2,)),
         ],
         compiler_params=pltpu.CompilerParams(vmem_limit_bytes=VMEM_LIMIT),
@@ -583,24 +590,94 @@
     return tensor * widen(cosine, width) + turned * widen(sine, width)
 
 
-def rotate_back(grad_in, cosine, sine):
-    half = HEAD // 2
-    width = grad_in.shape[1]
-    scaled = grad_in * widen(sine, width)
-    ahead, behind = jnp.roll(scaled, -half, axis=1), jnp.roll(scaled, half, axis=1)
-    return grad_in * widen(cosine, width) + jnp.where(
-        first_halves(grad_in.shape), ahead, -behind
-    )
-
-
-def norm_back(grad_in, row_data, scale_in, gain_in):
-    gain_term = jnp.sum(grad_in * row_data * scale_in, axis=0)
+def norm_back_rows(grad_in, row_data, scale_in, gain_in):
+    gain_term = jnp.sum(grad_in * row_data * scale_in, axis=0, keepdims=True)
     grad_normed = grad_in * gain_in
     inner_mean = jnp.mean(grad_normed * row_data, axis=-1, keepdims=True)
     return (
         scale_in * grad_normed - row_data * scale_in * scale_in * scale_in * inner_mean,
         gain_term,
     )
+
+
+def residual_back(me, kept, got, residual, scale_two, gain_two, cotangent, out_full):
+    rows, width = residual.shape
+
+    def body(me_ref, kept_ref, got_ref, res_ref, scale_ref, gain_ref, cot_ref, out_ref,
+             grad_ref, branch_ref, attn_ref, term_ref):
+        grad = kept_ref[...] + got_ref[...].astype(F32)
+        path, term_ref[...] = norm_back_rows(grad, res_ref[...], scale_ref[...], gain_ref[...])
+        full = cot_ref[...].astype(F32) + path
+        grad_ref[...] = full
+        branch_ref[...] = full.astype(BF16)
+        attn_ref[...] = dot(full.astype(BF16), out_ref[...], 1, 1).astype(BF16)
+
+    shapes = [
+        jax.ShapeDtypeStruct((rows, width), F32),
+        jax.ShapeDtypeStruct((rows, width), BF16),
+        jax.ShapeDtypeStruct((rows, QW), BF16),
+        jax.ShapeDtypeStruct((1, width), F32),
+    ]
+    arrays = (kept, got, residual, scale_two, gain_two[None, :], cotangent, out_full)
+    return on_device(body, "residual_back", shapes, [], me, arrays)
+
+
+def joined_back(
+    me, dq_one, dq_two, kept, got, cosine, sine, qkv_t, tokens, scale_one, gain_one,
+    grad_residual, normed_one, norm_two_term, seq_size, fsdp_size,
+):
+    rows, width = tokens.shape
+    total = qkv_t.shape[0]
+    each, lanes = total // fsdp_size, width // seq_size
+    tall = padded(each)
+
+    def body(me_ref, dq1_ref, dq2_ref, kept_ref, got_ref, cos_ref, sin_ref, w_ref, x_ref,
+             scale_ref, gain_ref, res_ref, n1_ref, term_ref,
+             tokens_ref, mine_ref, other_ref, held):
+        kv = kept_ref[...] + got_ref[...].astype(F32)
+        turned = jnp.concatenate([dq1_ref[...], dq2_ref[...], kv[:, :KVW]], axis=1)
+        across = turned.shape[1]
+        scaled = turned * widen(sin_ref[...], across)
+        ahead = pltpu.roll(scaled, across - HEAD // 2, 1)
+        behind = pltpu.roll(scaled, HEAD // 2, 1)
+        turned = turned * widen(cos_ref[...], across) + jnp.where(
+            first_halves(turned.shape), ahead, -behind
+        )
+        joined = jnp.concatenate([turned, kv[:, KVW:]], axis=1).astype(BF16)
+        wide = joined.astype(F32)
+        grad_normed = dot(joined, w_ref[...], 1, 0)
+        path, one_term = norm_back_rows(
+            grad_normed, x_ref[...].astype(F32), scale_ref[...], gain_ref[...]
+        )
+        tokens_ref[...] = res_ref[...] + path
+        bias = jnp.sum(wide, axis=0, keepdims=True)
+        weight = dot(wide.T.astype(BF16), n1_ref[...], 1, 0)
+        vectors = [one_term, bias[:, : QW + KVW], bias[:, QW + KVW :], term_ref[...]]
+        for f in range(fsdp_size):
+            lines = []
+            for vector in vectors:
+                n = vector.shape[1] // fsdp_size
+                piece = vector[:, f * n : (f + 1) * n]
+                lines.append(jnp.concatenate([piece, jnp.zeros((1, lanes - n), F32)], axis=1))
+            blank = jnp.zeros((tall - each, lanes), F32)
+            below = [blank] * (tall > each) + lines + [jnp.zeros((12, lanes), F32)]
+            for s in range(seq_size):
+                part = weight[f * each : (f + 1) * each, s * lanes : (s + 1) * lanes]
+                held[s, f] = jnp.concatenate([part] + below, axis=0).astype(BF16)
+        core = me_ref[0] % 2
+        for y in range(seq_size // 2):
+            mine_ref[y] = held[2 * y + core]
+            other_ref[y] = held[2 * y + 1 - core]
+
+    block = (fsdp_size, tall + 16, lanes)
+    half = jax.ShapeDtypeStruct((seq_size // 2,) + block, BF16)
+    shapes = [jax.ShapeDtypeStruct((rows, width), F32), half, half]
+    arrays = (
+        dq_one, dq_two, kept, got, cosine, sine, qkv_t, tokens, scale_one, gain_one[None, :],
+        grad_residual, normed_one, norm_two_term,
+    )
+    scratch = [pltpu.VMEM((seq_size,) + block, BF16)]
+    return on_device(body, "joined_back", shapes, scratch, me, arrays)
 
 
 def pad_row(vector, width):
@@ -645,23 +722,25 @@
         after(column_gather(packed, fsdp_size), ff_block), fsdp_size
     )
     wide = qkv_tall + 16
-    out_stack = jnp.concatenate([columns[m][:, wide:] for m in sorted(columns)], axis=0)
     columns[0] = after(columns[0], ff_block)
     packed_pieces = [seq_gather(columns[m][:, :wide], seq_size) for m in sorted(columns)]
     ff_blocks = {0: ff_block}
-    for bit in fsdp_bits(fsdp_size)[:2]:
-        ff_blocks.update({o ^ bit: swap(b, "fsdp", fsdp_size, bit) for o, b in ff_blocks.items()})
     inner = fsdp_size // OUTER
+    near = swap(ff_block, "fsdp", fsdp_size, inner)
+    far = swap(ff_block, "fsdp", fsdp_size, 2 * inner)
 
     qkv_pieces = [[piece[o] for piece in packed_pieces] for o in offsets]
     qkv_t, vectors = join_both(me, qkv_pieces, qkv_tall)
+    out_stack = jnp.concatenate([columns[m][:, wide:] for m in sorted(columns)], axis=0)
+    out_stack = after(out_stack, packed_pieces[-1][seq_size // 2])
+    out_blocks = seq_gather(out_stack, seq_size)
+
     own_x = ff_spread(ff_block, fsdp_size)
-    qkv_t = after(qkv_t, ff_blocks[2 * inner], ff_blocks[inner], *own_x.values())[:, :qkv_rows].reshape(fsdp_size * qkv_rows, -1)
+    last = swap(after(near, qkv_t), "fsdp", fsdp_size, 2 * inner)
+    qkv_t = after(qkv_t, far, near, *own_x.values())[:, :qkv_rows].reshape(fsdp_size * qkv_rows, -1)
     gain_one = vectors[:, 0, : norm_one.shape[0]].reshape(-1).astype(F32)
     bias_full = vectors[:, 1, : qkv_bias.shape[0]].reshape(-1).astype(F32)
     gain_two = vectors[:, 2, : norm_two.shape[0]].reshape(-1).astype(F32)
-
-    out_blocks = seq_gather(after(out_stack, packed_pieces[-1][seq_size // 2]), seq_size)
 
     inputs = tokens.astype(F32)
     scale_one = rms_scale(inputs)
@@ -672,7 +751,6 @@
     queries = turned[:, :QW] * jnp.asarray(0.125, BF16)
     kv_local = jnp.concatenate([turned[:, QW:], joined[:, QW + KVW :].astype(BF16)], axis=1)
     kv_all = lax.all_gather(kv_local, "seq", axis=0, tiled=True)
-    kv_all = after(kv_all, ff_blocks[2 * inner])
     cot_blocks = seq_gather(after(cotangent, kv_all), seq_size)
     row_place = jnp.arange(row_count, dtype=jnp.int32)
     high = my_seq * row_count + row_place
@@ -681,14 +759,12 @@
     low, high = low[None, :], high[None, :]
     split = PAIRS // 2 + 1
     spread = lambda block: ff_spread(block, fsdp_size)
-    near = ff_blocks[inner]
-    far, last = ff_blocks[2 * inner], ff_blocks[3 * inner]
     near_x = spread(after(near, kv_all))
     attn_one, lse_one = attend(
         low, high, place, after(queries, far), kv_all, 0, split
     )
     far_x = spread(after(far, kv_all))
-    queries_two = after(queries, attn_one, cot_blocks[seq_size // 2], *near_x.values())
+    queries_two = after(queries, attn_one, last, cot_blocks[seq_size // 2], *near_x.values())
     attn_two, lse_two = attend(low, high, place, queries_two, kv_all, split, PAIRS - split)
     last_x = spread(last)
     for base, row in ((0, own_x), (inner, near_x), (2 * inner, far_x), (3 * inner, last_x)):
@@ -702,13 +778,12 @@
     residual = inputs + dot(attn_flat, out_full, 1, 0)
     scale_two = rms_scale(residual)
     normed_two = (residual * scale_two * gain_two).astype(BF16)
-    normed_two = after(normed_two, *far_x.values())
     normed_blocks = {0: normed_two}
     bit = seq_size // 2
     while bit:
         if bit == 1:
             top = seq_size // 2
-            normed_blocks[top] = after(normed_blocks[top], last)
+            normed_blocks[top] = after(normed_blocks[top], *far_x.values())
         normed_blocks.update(
             {o ^ bit: swap(b, "seq", seq_size, bit) for o, b in normed_blocks.items()}
         )
@@ -729,9 +804,10 @@
     bit = 2
     while bit < seq_size:
         kept, given = halve(normed_sum, 1, my_seq // bit)
-        normed_sum = add(kept, swap(given, "seq", seq_size, bit))
+        got = swap(given, "seq", seq_size, bit)
+        normed_sum = add(kept, got)
         bit *= 2
-    grad_normed_two = normed_sum[0]
+    normed_kept, normed_got = kept[0], got[0]
     hidden = after(hidden, given)
     down_term = dot(hidden, cot_all, 0, 0).astype(BF16).reshape(fsdp_size, tall, -1)
     grad_gate, grad_up = after(grad_gate, down_term), after(grad_up, down_term)
@@ -757,13 +833,12 @@
     kept_one, given = give(down_term, 0)
     got_one = send(given, 0)
     kept_two, given = give(jnp.concatenate([gate_term[:, 0], up_term[:, 0]], axis=0), 0)
-    got_two = send(after(given, grad_normed_two), 0)
+    got_two = send(after(given, normed_got), 0)
     kept_three, given_three = give(jnp.concatenate([gate_term[:, 1], up_term[:, 1]], axis=0), 0)
 
-    grad_path, norm_two_term = norm_back(grad_normed_two, residual, scale_two, gain_two)
-    grad_residual = cotangent.astype(F32) + grad_path
-    grad_branch = grad_residual.astype(BF16)
-    grad_attn = dot(grad_branch, out_full, 1, 1).astype(BF16)
+    grad_residual, grad_branch, grad_attn, norm_two_term = residual_back(
+        me, normed_kept, normed_got, residual, scale_two, gain_two, cotangent, out_full
+    )
     grad_attn = after(grad_attn, gate_term, up_term)
     dq_one, kv_terms = attend_back(
         low, high, place, queries, grad_attn, attn_one, lse_one, kv_all, 0, split, ()
@@ -784,12 +859,11 @@
     kv_sum = add(kept, swap(given, "seq", seq_size, 1))
     bit = 2
     while bit < seq_size:
-        kept, given = halve(kv_sum, 1, my_seq // bit)
-        kv_sum = add(kept, swap(after(given, got_two), "seq", seq_size, bit))
+        kv_kept, given = halve(kv_sum, 1, my_seq // bit)
+        kv_got = swap(after(given, got_two), "seq", seq_size, bit)
+        kv_sum = add(kv_kept, kv_got)
         bit *= 2
-    kv_mine = kv_sum[0]
-    next_one, next_two = after(next_one, kv_mine), after(next_two, kv_mine)
-    down_sum = finish(kept_one, next_one, 1)
+    kv_mine = kv_got
 
     attn_late = after(attn_flat, dq_two)
     out_term = stack_from_lanes(dot(attn_late, grad_branch, 0, 0).astype(BF16), seq_size)
@@ -806,29 +880,21 @@
     got_three = after(got_three, kv_mine)
     kept_three, given = give(add(kept_three, got_three), 1)
     next_three = send(given, 1)
-    turned_back = rotate_back(
-        jnp.concatenate([dq_one, dq_two, kv_mine[:, :KVW]], axis=1), cosine, sine
-    )
-    grad_joined = jnp.concatenate([turned_back, kv_mine[:, KVW:]], axis=1).astype(BF16)
-    grad_normed_one = dot(grad_joined, qkv_t, 1, 0)
-    grad_path_one, norm_one_term = norm_back(grad_normed_one, inputs, scale_one, gain_one)
-    grad_tokens = grad_residual + grad_path_one
-    bias_term = jnp.sum(grad_joined.astype(F32), axis=0)
-
-    def vector_rows(vector):
-        rows = vector.reshape(fsdp_size, 1, -1)
-        return jnp.pad(rows, ((0, 0), (0, 0), (0, width - rows.shape[2])))
-
-    vector_terms = [norm_one_term, bias_term[: QW + KVW], bias_term[QW + KVW :], norm_two_term]
-    small = jnp.concatenate([vector_rows(v) for v in vector_terms], axis=1).astype(BF16)
-    small = jnp.pad(small, ((0, 0), (0, 16 - len(vector_terms)), (0, 0)))
-    qkv_term = stack_from_lanes(dot(grad_joined, normed_one, 0, 0).astype(BF16), seq_size)
-    qkv_term = qkv_term.reshape(seq_size, fsdp_size, qkv_rows, width)
-    tail = jnp.concatenate(
-        [qkv_term, jnp.broadcast_to(small[None], (seq_size,) + small.shape)], axis=2
-    )
-    tail = after(tail, next_two)
-    tail_mine = seq_scatter(tail, seq_size, my_seq)
+    grad_tokens, kept, given = joined_back(
+        me, dq_one, dq_two, kv_kept[0], kv_got[0], cosine, sine, qkv_t, tokens, scale_one,
+        gain_one, grad_residual, normed_one, norm_two_term, seq_size, fsdp_size,
+    )
+
+    next_one, next_two = after(next_one, grad_tokens), after(next_two, grad_tokens)
+    down_sum = finish(kept_one, next_one, 1)
+
+    tail_sum = add(kept, swap(given, "seq", seq_size, 1))
+    bit = 2
+    while bit < seq_size:
+        kept, given = halve(tail_sum, 1, my_seq // bit)
+        tail_sum = add(kept, swap(given, "seq", seq_size, bit))
+        bit *= 2
+    tail_mine = tail_sum[0]
     got_layer = swap(after(given_layer, kv_mine), "seq", seq_size, 2)
     layer_sum = add(kept_layer, got_layer)
     bit = 4
@@ -845,11 +911,14 @@
     grad_gate_up, grad_down = join_ff(me, ff_got, strip)
 
     tail_sum = fsdp_scatter(
-        jnp.concatenate([tail_mine, out_mine], axis=1), fsdp_size, my_fsdp, next_three
-    )
-    pieces = [
-        tail_sum[qkv_rows + i, : v.shape[0] // fsdp_size] for i, v in enumerate(vector_terms)
-    ]
+        after(jnp.concatenate([tail_mine, out_mine], axis=1), next_two),
+        fsdp_size,
+        my_fsdp,
+        next_three,
+
+    )
+    lengths = [width * seq_size, QW + KVW, KVW, width * seq_size]
+    pieces = [tail_sum[qkv_tall + i, : n // fsdp_size] for i, n in enumerate(lengths)]
     return (
         layer_out.astype(BF16),
         grad_tokens,
@@ -857,7 +926,7 @@
         tail_sum[:qkv_rows].T,
         pieces[1],
         pieces[2],
-        tail_sum[qkv_rows + 16 :],
+        tail_sum[qkv_tall + 16 :],
         pieces[3],
         grad_gate_up,
         grad_down,

time: 369 us -> 380 us (1.030)
  waiting for transfers between devices: 90.7 us -> 120 us
  local copies, waits for them, and re-layouts: 52.9 us -> 38.1 us
  Pallas kernels: 99.5 us -> 114 us
  other arithmetic: 32.1 us -> 20 us
  matrix products: 25.1 us -> 20.2 us
    ppermute x55, waiting for transfers between devices: 90.7 us -> 120 us  [swap(): return lax.ppermute(block, axis, [(i, i ^ bits) for i in range(size)])]
    pallas_call x6 -> x8, Pallas kernels: 9.92 us -> 23.8 us  [on_device(): pl.pallas_call(body, in_specs=[pl.BlockSpec(memory_space=pltpu.SMEM)] + [...]
    unnamed x112 -> x115, local copies, waits for them, and re-layouts: 16.3 us -> 11.1 us
    dot_general x9 -> x6, matrix products: 25.1 us -> 20.2 us  [dot(): lax.dot_general(left, right, (((left_dim,), (right_dim,)), ((), ())), pre...]
    reshape x4 -> x0, local copies, waits for them, and re-layouts: 4.66 us -> none  [the longest x1 4.4 us: stack_from_lanes(): return jnp.transpose(array.reshape(rows, count, width // count), (1, 0, 2))]
    add x14 -> x13, other arithmetic: 16.7 us -> 13.1 us  [add(): return kept.astype(F32) + got.astype(F32)]
  transfers between devices with their start and end apart: 55 -> 55, of which waited for: 23 -> 23; matrix products, arithmetic and copies ran while one was open for 24% -> 16% of each run, Pallas kernels for 18% -> 21%
where the time goes in v7:
time: 380 us; the launch traced here: 373 us
  waiting for transfers between devices  120 us (32%)
  Pallas kernels  114 us (30%)
  starting transfers between devices  50.2 us (13%)
  local copies, waits for them, and re-layouts  38.1 us (10%)
  matrix products  20.2 us (5%)
  other arithmetic  20 us (5%)
  blocking collectives  8.43 us (2%)
    ppermute x55, waiting for transfers between devices, swap(): return lax.ppermute(block, axis, [(i, i ^ bits) for i in range(size)])  120 us
    ppermute x55, starting transfers between devices, swap(): return lax.ppermute(block, axis, [(i, i ^ bits) for i in range(size)])  50.2 us
    pallas_call x1, Pallas kernels, feed_forward(): pl.pallas_call(body, grid=(size,), in_specs=[pl.BlockSpec(memory_space=pl...  34.8 us
    pallas_call x2, Pallas kernels, attend_back(): pl.pallas_call(functools.partial(attend_back_kernel, begin), grid=(pairs,...  32.1 us
    pallas_call x8, Pallas kernels, on_device(): pl.pallas_call(body, in_specs=[pl.BlockSpec(memory_space=pltpu.SMEM)] + [...  23.8 us
    pallas_call x2, Pallas kernels, attend(): pl.pallas_call(functools.partial(attend_kernel, begin), grid=(pairs,), in...  23.4 us
    dot_general x6, matrix products, dot(): lax.dot_general(left, right, (((left_dim,), (right_dim,)), ((), ())), pre...  20.2 us
    add x13, other arithmetic, add(): return kept.astype(F32) + got.astype(F32)  13.1 us
  transfers between devices with their start and end apart: 55, of which 23 were waited for; matrix products, arithmetic and copies ran while one was open for 16% of the time, Pallas kernels for 21%

profile of v7, /device:TPU:0, one launch (start us, length us, event | category | flops | bytes accessed | tf_op | source)
XLA Modules:
  0.0 372.8 jit_solution(217146019968575112)
XLA Ops:
  15.4 8.0 %collective-permute-done.1 = bf16[272,224]{1,0:T(8,128)(2,1)S(1)} collective-permute-done((bf16[272,224]{1,0:T(8,128)(2,1)S(1)}, bf16[272,224]{1,0:T(8,128)(2,1)S(1)}, u32[]{:S(2)}, u32[]{:S(2)}) %collective-permute-start.1) | collective-permute-done | bytes 121888 | tf_op jit(solution)/shard_map/ppermute | solution.py:36
  35.5 3.8 %collective-permute-done.9.refs_4_ = bf16[4,160,224]{2,1,0:T(8,128)(2,1)S(1)} collective-permute-done((bf16[4,160,224]{2,1,0:T(8,128)(2,1)S(1)}, bf16[4,160,224]{2,1,0:T(8,128)(2,1)S(1)}, u32[]{:S(2)}, u32[]{:S(2)}) %collective-permute-start.9) | collective-permute-done | bytes 286752 | tf_op jit(solution)/shard_map/ppermute | solution.py:36
  46.1 6.7 %collective-permute-done.10.refs_5_ = bf16[4,160,224]{2,1,0:T(8,128)(2,1)} collective-permute-done((bf16[4,160,224]{2,1,0:T(8,128)(2,1)S(1)}, bf16[4,160,224]{2,1,0:T(8,128)(2,1)}, u32[]{:S(2)}, u32[]{:S(2)}) %collective-permute-start.10) | collective-permute-done | bytes 286752 | tf_op jit(solution)/shard_map/ppermute | solution.py:36
  62.6 3.3 join_both.2
  66.0 6.5 %collective-permute-done.13.refs_4_ = bf16[480,896]{1,0:T(8,128)(2,1)} collective-permute-done((bf16[480,896]{1,0:T(8,128)(2,1)S(1)}, bf16[480,896]{1,0:T(8,128)(2,1)}, u32[]{:S(2)}, u32[]{:S(2)}) %collective-permute-start.13) | collective-permute-done | bytes 860192 | tf_op jit(solution)/shard_map/ppermute | solution.py:36
  79.4 8.4 %all_gather.3.kv_ref = bf16[1536,256]{1,0:T(8,128)(2,1)S(1)} all-gather(bf16[384,256]{1,0:T(8,128)(2,1)S(1)} %pad_maximum_fusion.5), channel_id=1, replica_groups=mesh['seq'=4,'fsdp'=8] {'seq'}, dimensions={0}, use_global_device_ids=true | all-gather | bytes 983040 | tf_op jit(solution)/shard_map/all_gather | solution.py:753
  91.6 13.4 %attend.2 = (bf16[384,512]{1,0:T(8,128)(2,1)S(1)}, f32[4,1,768]{2,1,0:T(1,128)S(1)}) custom-call(s32[1,384]{1,0:T(1,128)S(1)} %broadcast_in_dim.10.low_ref, s32[1,384]{1,0:T(1,128)S(1)} %iota_add_fusion.high_ref, s32[1536,1]{1,0:T(8,128)S(1)} %iota.33.place_ref, bf16[384,896]{1,0:T(8,128)(2,1)S(1)} %slice_multiply_fusion.1.q_ref, ...), custom_call_target="tpu_custom_call" | custom-call | flops 1 | bytes 1 | tf_op jit(solution)/shard_map/attend/pallas_call | solution.py:514
  110.1 19.0 %collective-permute-done.16.refs_6_ = bf16[480,896]{1,0:T(8,128)(2,1)} collective-permute-done((bf16[480,896]{1,0:T(8,128)(2,1)}, bf16[480,896]{1,0:T(8,128)(2,1)}, u32[]{:S(2)}, u32[]{:S(2)}) %collective-permute-start.16) | collective-permute-done | bytes 860192 | tf_op jit(solution)/shard_map/ppermute | solution.py:36
  129.2 10.0 %attend.3 = (bf16[384,384]{1,0:T(8,128)(2,1)S(1)}, f32[3,1,768]{2,1,0:T(1,128)S(1)}) custom-call(s32[1,384]{1,0:T(1,128)S(1)} %broadcast_in_dim.10.low_ref, s32[1,384]{1,0:T(1,128)S(1)} %iota_add_fusion.high_ref, s32[1536,1]{1,0:T(8,128)S(1)} %iota.39.place_ref, bf16[384,896]{1,0:T(8,128)(2,1)S(1)} %slice_multiply_fusion.1.q_ref, ...), custom_call_target="tpu_custom_call" | custom-call | flops 1 | bytes 1 | tf_op jit(solution)/shard_map/attend/pallas_call | solution.py:514
  143.9 13.8 %collective-permute-done.25.refs_10_ = bf16[384,896]{1,0:T(8,128)(2,1)S(1)} collective-permute-done((bf16[384,896]{1,0:T(8,128)(2,1)S(1)}, bf16[384,896]{1,0:T(8,128)(2,1)S(1)}, u32[]{:S(2)}, u32[]{:S(2)}) %collective-permute-start.25) | collective-permute-done | bytes 688160 | tf_op jit(solution)/shard_map/ppermute | solution.py:36
  157.7 5.0 %collective-permute-done.23.refs_7_ = bf16[480,896]{1,0:T(8,128)(2,1)S(1)} collective-permute-done((bf16[480,896]{1,0:T(8,128)(2,1)}, bf16[480,896]{1,0:T(8,128)(2,1)S(1)}, u32[]{:S(2)}, u32[]{:S(2)}) %collective-permute-start.23) | collective-permute-done | bytes 860192 | tf_op jit(solution)/shard_map/ppermute | solution.py:36
  163.6 34.8 %feed_forward.1 = (bf16[1536,1280]{1,0:T(8,128)(2,1)}, bf16[1536,1280]{1,0:T(8,128)(2,1)}, bf16[1536,1280]{1,0:T(8,128)(2,1)}, bf16[2,384,896]{2,1,0:T(8,128)(2,...) custom-call(s32[2]{0:T(128)S(1)} %pad_add_fusion.me_ref, ...), custom_call_target="tpu_custom_call" | custom-call | flops 1 | bytes 1 | tf_op jit(solution)/shard_map/feed_forward/pallas_call | solution.py:346
  205.4 4.5 %convolution_convert_fusion.2 = bf16[1280,896]{1,0:T(8,128)(2,1)S(1)} fusion(bf16[1536,1280]{1,0:T(8,128)(2,1)S(1)} %copy-done.53, bf16[1536,896]{1,0:T(8,128)(2,1)S(1)} %bitcast.181), kind=kOutput, calls=%fused_computation.2 | convolution fusion | flops 3524362240 | bytes 8978432 | tf_op jit(solution)/shard_map/dot_general | solution.py:30
  209.9 4.5 %convolution_convert_fusion = bf16[1280,896]{1,0:T(8,128)(2,1)S(1)} fusion(bf16[1536,1280]{1,0:T(8,128)(2,1)S(1)} %copy-done.52, bf16[1536,896]{1,0:T(8,128)(2,1)S(1)} %bitcast.179), kind=kOutput, calls=%fused_computation | convolution fusion | flops 3524362240 | bytes 8978432 | tf_op jit(solution)/shard_map/dot_general | solution.py:30
  214.4 4.9 %convolution_convert_fusion.1 = bf16[1280,896]{1,0:T(8,128)(2,1)S(1)} fusion(bf16[1536,1280]{1,0:T(8,128)(2,1)S(1)} %copy-done.51, bf16[1536,896]{1,0:T(8,128)(2,1)S(1)} %bitcast.180), kind=kOutput, calls=%fused_computation.1 | convolution fusion | flops 3524362240 | bytes 8978432 | tf_op jit(solution)/shard_map/dot_general | solution.py:30
  225.8 4.7 %residual_back.1 = (f32[384,896]{1,0:T(8,128)}, bf16[384,896]{1,0:T(8,128)(2,1)S(1)}, bf16[384,896]{1,0:T(8,128)(2,1)S(1)}, f32[1,896]{1,0:T(1,128)S(1)}) custom-call(s32[2]{0:T(128)S(1)} %pad_add_fusion.me_ref, f32[384,896]{1,0:T(8,128)} %dynamic-slice_bitcast_fusion.kept_ref, bf16[384,896]{1,0:T(8,128)(2,1)S(1)} %bitcast.147, f32[384,896]{1,0:T(8,128)} %copy-done.25, ...), custom_call_target="tpu_custom_call" | custom-call | tf_op jit(solution)/shard_map/residual_back/pallas_call | solution.py:125
  230.5 17.9 %attend_back.2 = (f32[384,512]{1,0:T(8,128)S(1)}, f32[1536,256]{1,0:T(8,128)}) custom-call(s32[1,384]{1,0:T(1,128)S(1)} %broadcast_in_dim.10.low_ref, s32[1,384]{1,0:T(1,128)S(1)} %iota_add_fusion.high_ref, s32[1536,1]{1,0:T(8,128)S(1)} %iota.41.place_ref, bf16[384,896]{1,0:T(8,128)(2,1)S(1)} %slice_multiply_fusion.1.q_ref, ...), custom_call_target="tpu_custom_call" | custom-call | flops 1 | bytes 1 | tf_op jit(solution)/shard_map/attend_back/pallas_call | solution.py:540
  252.5 14.2 %attend_back.3 = (f32[384,384]{1,0:T(8,128)S(1)}, f32[1536,256]{1,0:T(8,128)}) custom-call(s32[1,384]{1,0:T(1,128)S(1)} %broadcast_in_dim.10.low_ref, s32[1,384]{1,0:T(1,128)S(1)} %iota_add_fusion.high_ref, s32[1536,1]{1,0:T(8,128)S(1)} %iota.40.place_ref, bf16[384,896]{1,0:T(8,128)(2,1)S(1)} %slice_multiply_fusion.1.q_ref, ...), custom_call_target="tpu_custom_call" | custom-call | flops 1 | bytes 1 | tf_op jit(solution)/shard_map/attend_back/pallas_call | solution.py:540
  281.3 9.3 %joined_back.1 = (f32[384,896]{1,0:T(8,128)}, bf16[2,8,160,224]{3,2,1,0:T(8,128)(2,1)}, bf16[2,8,160,224]{3,2,1,0:T(8,128)(2,1)}) custom-call(s32[2]{0:T(128)S(1)} %pad_add_fusion.me_ref, f32[384,512]{1,0:T(8,128)S(1)} %get-tuple-element.119.dq1_ref, f32[384,384]{1,0:T(8,128)S(1)} %get-tuple-element.123.dq2_ref, ...), custom_call_target="tpu_custom_call" | custom-call | tf_op jit(solution)/shard_map/joined_back/pallas_call | solution.py:125
  300.4 10.0 %collective-permute-done.51 = bf16[1,160,896]{2,1,0:T(8,128)(2,1)S(1)} collective-permute-done((bf16[1,160,896]{2,1,0:T(8,128)(2,1)S(1)}, bf16[1,160,896]{2,1,0:T(8,128)(2,1)S(1)}, u32[]{:S(2)}, u32[]{:S(2)}) %collective-permute-start.51) | collective-permute-done | bytes 286752 | tf_op jit(solution)/shard_map/ppermute | solution.py:36
  322.2 16.6 %collective-permute-done.44 = bf16[2,160,896]{2,1,0:T(8,128)(2,1)} collective-permute-done((bf16[2,160,896]{2,1,0:T(8,128)(2,1)}, bf16[2,160,896]{2,1,0:T(8,128)(2,1)}, u32[]{:S(2)}, u32[]{:S(2)}) %collective-permute-start.44) | collective-permute-done | bytes 573472 | tf_op jit(solution)/shard_map/ppermute | solution.py:36
  342.6 6.3 %collective-permute-done.49 = bf16[1,160,896]{2,1,0:T(8,128)(2,1)S(1)} collective-permute-done((bf16[1,160,896]{2,1,0:T(8,128)(2,1)S(1)}, bf16[1,160,896]{2,1,0:T(8,128)(2,1)S(1)}, u32[]{:S(2)}, u32[]{:S(2)}) %collective-permute-start.49) | collective-permute-done | bytes 286752 | tf_op jit(solution)/shard_map/ppermute | solution.py:36
  351.9 4.2 %collective-permute-done.42 = bf16[4,272,224]{2,1,0:T(8,128)(2,1)S(1)} collective-permute-done((bf16[4,272,224]{2,1,0:T(8,128)(2,1)S(1)}, bf16[4,272,224]{2,1,0:T(8,128)(2,1)S(1)}, u32[]{:S(2)}, u32[]{:S(2)}) %collective-permute-start.42) | collective-permute-done | bytes 487456 | tf_op jit(solution)/shard_map/ppermute | solution.py:36
  366.3 3.4 collective-permute-done.46
  (323 shorter events, 137.5 us)
Async XLA Ops:
  31.3 41.1 %collective-permute-start.13 = (bf16[480,896]{1,0:T(8,128)(2,1)S(1)}, bf16[480,896]{1,0:T(8,128)(2,1)}, u32[]{:S(2)}, u32[]{:S(2)}) collective-permute-start(bf16[480,896]{1,0:T(8,128)(2,1)S(1)} %join_lanes.1.refs_0_), channel_id=1, source_target_pairs={{0,4},{1,5},{2,6},{3,7},{4,0},{5,1},{6,2},{7,3},{8,12},{9,13},{10,... | collective-permute-start | bytes 2580488 | tf_op jit(solution)/shard_map/ppermute | solution.py:36
  33.0 39.5 %collective-permute-start.14 = (bf16[480,896]{1,0:T(8,128)(2,1)S(1)}, bf16[480,896]{1,0:T(8,128)(2,1)}, u32[]{:S(2)}, u32[]{:S(2)}) collective-permute-start(bf16[480,896]{1,0:T(8,128)(2,1)S(1)} %join_lanes.1.refs_0_), channel_id=1, source_target_pairs={{0,2},{1,3},{2,0},{3,1},{4,6},{5,7},{6,4},{7,5},{8,10},{9,11},{10,... | collective-permute-start | bytes 2580488 | tf_op jit(solution)/shard_map/ppermute | solution.py:36
  39.3 33.2 %collective-permute-start.15 = (bf16[480,896]{1,0:T(8,128)(2,1)S(1)}, bf16[480,896]{1,0:T(8,128)(2,1)}, u32[]{:S(2)}, u32[]{:S(2)}) collective-permute-start(bf16[480,896]{1,0:T(8,128)(2,1)S(1)} %join_lanes.1.refs_0_), channel_id=1, source_target_pairs={{0,1},{1,0},{2,3},{3,2},{4,5},{5,4},{6,7},{7,6},{8,9},{9,8},{10,11... | collective-permute-start | bytes 2580488 | tf_op jit(solution)/shard_map/ppermute | solution.py:36
  60.8 30.2 %collective-permute-start.20 = (bf16[8,112,224]{2,1,0:T(8,128)(2,1)S(1)}, bf16[8,112,224]{2,1,0:T(8,128)(2,1)S(1)}, u32[]{:S(2)}, u32[]{:S(2)}) collective-permute-start(bf16[8,112,224]{2,1,0:T(8,128)(2,1)S(1)} %pad_maximum_fusion.4.refs_0_), channel_id=1, source_target_pairs={{0,16},{8,24},{16,0},{24,8},{1,17},{9,25},{17,1},{25,9},{2,18},{10... | collective-permute-start | bytes 1204232 | tf_op jit(solution)/shard_map/ppermute | solution.py:36
  87.8 22.3 %collective-permute-start.18 = (bf16[480,896]{1,0:T(8,128)(2,1)}, bf16[480,896]{1,0:T(8,128)(2,1)}, u32[]{:S(2)}, u32[]{:S(2)}) collective-permute-start(bf16[480,896]{1,0:T(8,128)(2,1)} %collective-permute-done.14.refs_2_), channel_id=1, source_target_pairs={{0,1},{1,0},{2,3},{3,2},{4,5},{5,4},{6,7},{7,6},{8,9},{9,8},{10,11... | collective-permute-start | bytes 2580488 | tf_op jit(solution)/shard_map/ppermute | solution.py:36
  88.4 40.7 %collective-permute-start.16 = (bf16[480,896]{1,0:T(8,128)(2,1)}, bf16[480,896]{1,0:T(8,128)(2,1)}, u32[]{:S(2)}, u32[]{:S(2)}) collective-permute-start(bf16[480,896]{1,0:T(8,128)(2,1)} %collective-permute-done.14.refs_2_), channel_id=1, source_target_pairs={{0,4},{1,5},{2,6},{3,7},{4,0},{5,1},{6,2},{7,3},{8,12},{9,13},{10,... | collective-permute-start | bytes 2580488 | tf_op jit(solution)/shard_map/ppermute | solution.py:36
  90.1 19.5 %collective-permute-start.17 = (bf16[384,896]{1,0:T(8,128)(2,1)}, bf16[384,896]{1,0:T(8,128)(2,1)S(1)}, u32[]{:S(2)}, u32[]{:S(2)}) collective-permute-start(bf16[384,896]{1,0:T(8,128)(2,1)} %cot_ref.1), channel_id=1, source_target_pairs={{0,16},{8,24},{16,0},{24,8},{1,17},{9,25},{17,1},{25,9},{2,18},{10... | collective-permute-start | bytes 2064392 | tf_op jit(solution)/shard_map/ppermute | solution.py:36
  105.2 38.6 %collective-permute-start.22 = (bf16[480,896]{1,0:T(8,128)(2,1)}, bf16[480,896]{1,0:T(8,128)(2,1)S(1)}, u32[]{:S(2)}, u32[]{:S(2)}) collective-permute-start(bf16[480,896]{1,0:T(8,128)(2,1)} %collective-permute-done.13.refs_4_), channel_id=1, source_target_pairs={{0,1},{1,0},{2,3},{3,2},{4,5},{5,4},{6,7},{7,6},{8,9},{9,8},{10,11... | collective-permute-start | bytes 2580488 | tf_op jit(solution)/shard_map/ppermute | solution.py:36
  140.6 17.1 %collective-permute-start.25 = (bf16[384,896]{1,0:T(8,128)(2,1)S(1)}, bf16[384,896]{1,0:T(8,128)(2,1)S(1)}, u32[]{:S(2)}, u32[]{:S(2)}) collective-permute-start(bf16[384,896]{1,0:T(8,128)(2,1)S(1)} %multiply_convert_fusion.refs_8_), channel_id=1, source_target_pairs={{0,16},{8,24},{16,0},{24,8},{1,17},{9,25},{17,1},{25,9},{2,18},{10... | collective-permute-start | bytes 2064392 | tf_op jit(solution)/shard_map/ppermute | solution.py:36
  141.8 20.9 %collective-permute-start.23 = (bf16[480,896]{1,0:T(8,128)(2,1)}, bf16[480,896]{1,0:T(8,128)(2,1)S(1)}, u32[]{:S(2)}, u32[]{:S(2)}) collective-permute-start(bf16[480,896]{1,0:T(8,128)(2,1)} %collective-permute-done.16.refs_6_), channel_id=1, source_target_pairs={{0,1},{1,0},{2,3},{3,2},{4,5},{5,4},{6,7},{7,6},{8,9},{9,8},{10,11... | collective-permute-start | bytes 2580488 | tf_op jit(solution)/shard_map/ppermute | solution.py:36
  203.8 21.4 %collective-permute-start.30 = (bf16[1,384,896]{2,1,0:T(8,128)(2,1)S(1)}, bf16[1,384,896]{2,1,0:T(8,128)(2,1)S(1)}, u32[]{:S(2)}, u32[]{:S(2)}) collective-permute-start(bf16[1,384,896]{2,1,0:T(8,128)(2,1)S(1)} %dynamic-slice_convert_fusion.1), channel_id=1, source_target_pairs={{0,16},{8,24},{16,0},{24,8},{1,17},{9,25},{17,1},{25,9},{2,18},{10... | collective-permute-start | bytes 2064392 | tf_op jit(solution)/shard_map/ppermute | solution.py:36
  220.5 28.4 %collective-permute-start.31 = (bf16[4,160,896]{2,1,0:T(8,128)(2,1)}, bf16[4,160,896]{2,1,0:T(8,128)(2,1)}, u32[]{:S(2)}, u32[]{:S(2)}) collective-permute-start(bf16[4,160,896]{2,1,0:T(8,128)(2,1)} %dynamic-slice_bitcast_fusion.3), channel_id=1, source_target_pairs={{0,1},{1,0},{2,3},{3,2},{4,5},{5,4},{6,7},{7,6},{8,9},{9,8},{10,11... | collective-permute-start | bytes 3440648 | tf_op jit(solution)/shard_map/ppermute | solution.py:36
  225.2 48.3 %collective-permute-start.34 = (bf16[4,160,896]{2,1,0:T(8,128)(2,1)S(1)}, bf16[4,160,896]{2,1,0:T(8,128)(2,1)}, u32[]{:S(2)}, u32[]{:S(2)}) collective-permute-start(bf16[4,160,896]{2,1,0:T(8,128)(2,1)S(1)} %dynamic-slice_bitcast_fusion.2), channel_id=1, source_target_pairs={{0,1},{1,0},{2,3},{3,2},{4,5},{5,4},{6,7},{7,6},{8,9},{9,8},{10,11... | collective-permute-start | bytes 3440648 | tf_op jit(solution)/shard_map/ppermute | solution.py:36
  251.7 39.0 %collective-permute-start.50 = (bf16[2,160,896]{2,1,0:T(8,128)(2,1)}, bf16[2,160,896]{2,1,0:T(8,128)(2,1)}, u32[]{:S(2)}, u32[]{:S(2)}) collective-permute-start(bf16[2,160,896]{2,1,0:T(8,128)(2,1)} %fusion.8), channel_id=1, source_target_pairs={{0,4},{1,5},{2,6},{3,7},{4,0},{5,1},{6,2},{7,3},{8,12},{9,13},{10,... | collective-permute-start | bytes 1720328 | tf_op jit(solution)/shard_map/ppermute | solution.py:36
  268.0 29.3 %collective-permute-start.43 = (bf16[4,160,896]{2,1,0:T(8,128)(2,1)}, bf16[4,160,896]{2,1,0:T(8,128)(2,1)}, u32[]{:S(2)}, u32[]{:S(2)}) collective-permute-start(bf16[4,160,896]{2,1,0:T(8,128)(2,1)} %dynamic-slice_bitcast_fusion.1), channel_id=1, source_target_pairs={{0,1},{1,0},{2,3},{3,2},{4,5},{5,4},{6,7},{7,6},{8,9},{9,8},{10,11... | collective-permute-start | bytes 3440648 | tf_op jit(solution)/shard_map/ppermute | solution.py:36
  272.2 48.5 %collective-permute-start.32 = (bf16[2,384,896]{2,1,0:T(8,128)(2,1)}, bf16[2,384,896]{2,1,0:T(8,128)(2,1)S(1)}, u32[]{:S(2)}, u32[]{:S(2)}) collective-permute-start(bf16[2,384,896]{2,1,0:T(8,128)(2,1)} %get-tuple-element.124), channel_id=1, source_target_pairs={{0,8},{8,0},{16,24},{24,16},{1,9},{9,1},{17,25},{25,17},{2,10},{10... | collective-permute-start | bytes 4128776 | tf_op jit(solution)/shard_map/ppermute | solution.py:36
  276.7 34.5 %collective-permute-start.41 = (bf16[2,160,896]{2,1,0:T(8,128)(2,1)}, bf16[2,160,896]{2,1,0:T(8,128)(2,1)}, u32[]{:S(2)}, u32[]{:S(2)}) collective-permute-start(bf16[2,160,896]{2,1,0:T(8,128)(2,1)} %fusion.9), channel_id=1, source_target_pairs={{0,4},{1,5},{2,6},{3,7},{4,0},{5,1},{6,2},{7,3},{8,12},{9,13},{10,... | collective-permute-start | bytes 1720328 | tf_op jit(solution)/shard_map/ppermute | solution.py:36
  291.9 18.6 %collective-permute-start.51 = (bf16[1,160,896]{2,1,0:T(8,128)(2,1)S(1)}, bf16[1,160,896]{2,1,0:T(8,128)(2,1)S(1)}, u32[]{:S(2)}, u32[]{:S(2)}) collective-permute-start(bf16[1,160,896]{2,1,0:T(8,128)(2,1)S(1)} %dynamic-slice_convert_fusion.8), channel_id=1, source_target_pairs={{0,2},{1,3},{2,0},{3,1},{4,6},{5,7},{6,4},{7,5},{8,10},{9,11},{10,... | collective-permute-start | bytes 860168 | tf_op jit(solution)/shard_map/ppermute | solution.py:36
  294.2 23.3 %collective-permute-start.37 = (bf16[2,8,160,224]{3,2,1,0:T(8,128)(2,1)}, bf16[2,8,160,224]{3,2,1,0:T(8,128)(2,1)}, u32[]{:S(2)}, u32[]{:S(2)}) collective-permute-start(bf16[2,8,160,224]{3,2,1,0:T(8,128)(2,1)} %get-tuple-element.134), channel_id=1, source_target_pairs={{0,8},{8,0},{16,24},{24,16},{1,9},{9,1},{17,25},{25,17},{2,10},{10... | collective-permute-start | bytes 3440648 | tf_op jit(solution)/shard_map/ppermute | solution.py:36
  297.3 18.8 %collective-permute-start.40 = (bf16[1,896,224]{1,2,0:T(8,128)(2,1)S(1)}, bf16[1,896,224]{1,2,0:T(8,128)(2,1)S(1)}, u32[]{:S(2)}, u32[]{:S(2)}) collective-permute-start(bf16[1,896,224]{1,2,0:T(8,128)(2,1)S(1)} %dynamic-slice_convert_fusion.7), channel_id=1, source_target_pairs={{0,16},{8,24},{16,0},{24,8},{1,17},{9,25},{17,1},{25,9},{2,18},{10... | collective-permute-start | bytes 1204232 | tf_op jit(solution)/shard_map/ppermute | solution.py:36
  310.4 28.4 %collective-permute-start.44 = (bf16[2,160,896]{2,1,0:T(8,128)(2,1)}, bf16[2,160,896]{2,1,0:T(8,128)(2,1)}, u32[]{:S(2)}, u32[]{:S(2)}) collective-permute-start(bf16[2,160,896]{2,1,0:T(8,128)(2,1)} %fusion.10), channel_id=1, source_target_pairs={{0,4},{1,5},{2,6},{3,7},{4,0},{5,1},{6,2},{7,3},{8,12},{9,13},{10,... | collective-permute-start | bytes 1720328 | tf_op jit(solution)/shard_map/ppermute | solution.py:36
  313.6 28.6 %collective-permute-start.48 = (bf16[1,160,896]{2,1,0:T(8,128)(2,1)}, bf16[1,160,896]{2,1,0:T(8,128)(2,1)S(1)}, u32[]{:S(2)}, u32[]{:S(2)}) collective-permute-start(bf16[1,160,896]{2,1,0:T(8,128)(2,1)} %dynamic-slice_convert_fusion.10), channel_id=1, source_target_pairs={{0,2},{1,3},{2,0},{3,1},{4,6},{5,7},{6,4},{7,5},{8,10},{9,11},{10,... | collective-permute-start | bytes 860168 | tf_op jit(solution)/shard_map/ppermute | solution.py:36
  319.7 20.5 %collective-permute-start.38 = (bf16[1,8,160,224]{3,2,1,0:T(8,128)(2,1)S(1)}, bf16[1,8,160,224]{3,2,1,0:T(8,128)(2,1)S(1)}, u32[]{:S(2)}, u32[]{:S(2)}) collective-permute-start(bf16[1,8,160,224]{3,2,1,0:T(8,128)(2,1)S(1)} %dynamic-slice_convert_fusion.2), channel_id=1, source_target_pairs={{0,16},{8,24},{16,0},{24,8},{1,17},{9,25},{17,1},{25,9},{2,18},{10... | collective-permute-start | bytes 1720328 | tf_op jit(solution)/shard_map/ppermute | solution.py:36
  321.0 36.2 %collective-permute-start.36 = (bf16[1,384,896]{2,1,0:T(8,128)(2,1)S(1)}, bf16[1,384,896]{2,1,0:T(8,128)(2,1)S(1)}, u32[]{:S(2)}, u32[]{:S(2)}) collective-permute-start(bf16[1,384,896]{2,1,0:T(8,128)(2,1)S(1)} %dynamic-slice_convert_fusion), channel_id=1, source_target_pairs={{0,16},{8,24},{16,0},{24,8},{1,17},{9,25},{17,1},{25,9},{2,18},{10... | collective-permute-start | bytes 2064392 | tf_op jit(solution)/shard_map/ppermute | solution.py:36
  (87 other events, 872.1 us)

commit v8 on v7

--- a/solution.py
+++ b/solution.py
@@ -264,17 +264,19 @@
 
 def feed_forward(me, weight_blocks, row_blocks, cot_blocks):
     count, size = len(weight_blocks), len(row_blocks)
+    whole_blocks = [not isinstance(b, tuple) for b in weight_blocks]
+    flat = [part for b in weight_blocks for part in (b if isinstance(b, tuple) else (b,))]
+    given = len(flat)
     rows, width = row_blocks[0].shape
-    tall = weight_blocks[0].shape[0] // 3
+    tall = flat[0].shape[0] // 3
     units = count * tall
     step_units = 256
 
     def body(me_ref, *refs):
-        blocks = refs[:count]
-        xs, gs = refs[count : count + size], refs[count + size : count + 2 * size]
-        outs = refs[count + 2 * size : count + 2 * size + 9]
-        hid, gg, gu, gn_kept, gn_given, part_kept, part_given, x_out, g_out = outs
-        gu_w, d_w, x_all, g_all, sems = refs[count + 2 * size + 9 :]
+        blocks = list(refs[:given])
+        xs, gs = refs[given : given + size], refs[given + size : given + 2 * size]
+        hid, gg, gu, gn, part, x_out, g_out = refs[given + 2 * size : given + 2 * size + 7]
+        gu_w, d_w, x_all, g_all, sems = refs[given + 2 * size + 7 :]
         step = pl.program_id(0)
         core = me_ref[0] % 2
         handed = [
@@ -287,8 +289,13 @@
             copies = []
             for o in range(count):
                 f = me_ref[1] ^ o
-                copies.append((blocks[o].at[pl.ds(0, 2 * tall)], gu_w.at[f]))
-                copies.append((blocks[o].at[pl.ds(2 * tall, tall)], d_w.at[f]))
+                if whole_blocks[o]:
+                    block = blocks.pop(0)
+                    copies.append((block.at[pl.ds(0, 2 * tall)], gu_w.at[f]))
+                    copies.append((block.at[pl.ds(2 * tall, tall)], d_w.at[f]))
+                else:
+                    copies.append((blocks.pop(0), gu_w.at[f]))
+                    copies.append((blocks.pop(0), d_w.at[f]))
             for o in range(size):
                 copies.append((xs[o], x_all.at[me_ref[0] ^ o]))
                 copies.append((gs[o], g_all.at[me_ref[0] ^ o]))
@@ -318,21 +325,9 @@
             gg[:, at] = (grad_hidden * up * (sigmoid + silu * (1.0 - sigmoid))).astype(BF16)
             gu[:, at] = (grad_hidden * silu).astype(BF16)
 
-        mine = step % 2 == core
-
-        def hand_out(value, kept, given):
-            low = value.astype(BF16)
-
-            @pl.when(mine)
-            def _():
-                kept[0] = low
-
-            @pl.when(jnp.logical_not(mine))
-            def _():
-                given[0] = low
-
-        hand_out(dot(gg[...], gate_w, 1, 0) + dot(gu[...], up_w, 1, 0), gn_kept, gn_given)
-        hand_out(dot(hid[...], down_w, 1, 0), part_kept, part_given)
+        place = jnp.where(step % 2 == core, 0, 1)
+        gn[place, 0] = (dot(gg[...], gate_w, 1, 0) + dot(gu[...], up_w, 1, 0)).astype(BF16)
+        part[place, 0] = dot(hid[...], down_w, 1, 0).astype(BF16)
 
         @pl.when(step == size - 1)
         def _():
@@ -340,17 +335,17 @@
                 copy.wait()
 
     hbm = pl.BlockSpec(memory_space=pl.ANY)
-    by_rows = pl.BlockSpec((rows, units), lambda i: (i, 0))
-    by_pair = pl.BlockSpec((1, rows, width), lambda i: (i // 2, 0, 0))
+    by_rows = lambda n: pl.BlockSpec((rows, n), lambda i: (i, 0))
+    by_pair = pl.BlockSpec((2, 1, rows, width), lambda i: (0, i // 2, 0, 0))
     like = jax.ShapeDtypeStruct
     return pl.pallas_call(
         body,
         grid=(size,),
         in_specs=[pl.BlockSpec(memory_space=pltpu.SMEM)]
-        + [hbm] * (count + 2 * size),
-        out_specs=[by_rows] * 3 + [by_pair] * 4 + [hbm] * 2,
+        + [hbm] * (given + 2 * size),
+        out_specs=[by_rows(units)] * 3 + [by_pair] * 2 + [hbm] * 2,
         out_shape=[like((size * rows, units), BF16)] * 3
-        + [like((size // 2, rows, width), BF16)] * 4
+        + [like((2, size // 2, rows, width), BF16)] * 2
         + [like((size, rows, width), BF16)] * 2,
         scratch_shapes=[
             pltpu.VMEM((count, 2 * tall, width), BF16),
@@ -362,7 +357,7 @@
         compiler_params=pltpu.CompilerParams(vmem_limit_bytes=VMEM_LIMIT),
         cost_estimate=pl.CostEstimate(flops=1, bytes_accessed=1, transcendentals=0),
         name="feed_forward",
-    )(me, *weight_blocks, *row_blocks, *cot_blocks)
+    )(me, *flat, *row_blocks, *cot_blocks)
 
 
 def both_heads(pair):
@@ -764,7 +759,7 @@
         low, high, place, after(queries, far), kv_all, 0, split
     )
     far_x = spread(after(far, kv_all))
-    queries_two = after(queries, attn_one, last, cot_blocks[seq_size // 2], *near_x.values())
+    queries_two = after(queries, attn_one, cot_blocks[seq_size // 2], *near_x.values())
     attn_two, lse_two = attend(low, high, place, queries_two, kv_all, split, PAIRS - split)
     last_x = spread(last)
     for base, row in ((0, own_x), (inner, near_x), (2 * inner, far_x), (3 * inner, last_x)):
@@ -783,19 +778,19 @@
     while bit:
         if bit == 1:
             top = seq_size // 2
-            normed_blocks[top] = after(normed_blocks[top], *far_x.values())
+            normed_blocks[top] = after(normed_blocks[top], last, *far_x.values())
         normed_blocks.update(
             {o ^ bit: swap(b, "seq", seq_size, bit) for o, b in normed_blocks.items()}
         )
         bit //= 2
-    (
-        hidden, grad_gate, grad_up, kept, given, kept_layer, given_layer, normed_all, cot_all,
-    ) = feed_forward(
+    hidden, grad_gate, grad_up, grad_normed, layer_part, normed_all, cot_all = feed_forward(
         me,
         [ff_blocks[o] for o in range(fsdp_size)],
         [normed_blocks[o] for o in offsets],
         [cot_blocks[o] for o in offsets],
     )
+    kept, given = grad_normed[0], grad_normed[1]
+    kept_layer, given_layer = layer_part[0], layer_part[1]
     normed_all = normed_all.reshape(seq_size * row_count, -1)
     cot_all = cot_all.reshape(seq_size * row_count, -1)
     by_seq = lambda rows: rows.reshape(seq_size, row_count, -1)
@@ -830,6 +825,14 @@
             stack = add(kept, send(given, later))
         return stack[0]
 
+    def finish_pair(stacks, at):
+        for later in range(at, len(bits)):
+            halves = [give(stack, later) for stack in stacks]
+            got = send(jnp.concatenate([given for _, given in halves], axis=0), later)
+            n = halves[0][1].shape[0]
+            stacks = [add(halves[0][0], got[:n]), add(halves[1][0], got[n:])]
+        return stacks[0][0], stacks[1][0]
+
     kept_one, given = give(down_term, 0)
     got_one = send(given, 0)
     kept_two, given = give(jnp.concatenate([gate_term[:, 0], up_term[:, 0]], axis=0), 0)
@@ -839,15 +842,14 @@
     grad_residual, grad_branch, grad_attn, norm_two_term = residual_back(
         me, normed_kept, normed_got, residual, scale_two, gain_two, cotangent, out_full
     )
-    grad_attn = after(grad_attn, gate_term, up_term)
+    kept_one, given_one = give(add(kept_one, got_one), 1)
+    next_one = send(given_one, 1)
+    grad_attn = after(grad_attn, gate_term, up_term, given_one)
     dq_one, kv_terms = attend_back(
         low, high, place, queries, grad_attn, attn_one, lse_one, kv_all, 0, split, ()
     )
-    got_one = after(got_one, dq_one)
-    got_three = send(after(given_three, got_one), 0)
-    kept_one, given_one = give(add(kept_one, got_one), 1)
-    next_one = send(given_one, 1)
-    queries_two = after(queries, kv_terms, given_one)
+    got_three = send(after(given_three, dq_one), 0)
+    queries_two = after(queries, kv_terms)
     dq_two, kv_terms = attend_back(
         low, high, place, queries_two, grad_attn, attn_two, lse_two, kv_all, split,
         PAIRS - split, (kv_terms,),
@@ -855,39 +857,42 @@
     got_two = after(got_two, dq_two)
     kept_two, given = give(add(kept_two, got_two), 1)
     next_two = send(given, 1)
-    kept, given = halve(by_seq(kv_terms), 1, my_seq)
+    kept, given = halve(after(by_seq(kv_terms), next_one), 1, my_seq)
     kv_sum = add(kept, swap(given, "seq", seq_size, 1))
     bit = 2
     while bit < seq_size:
-        kv_kept, given = halve(kv_sum, 1, my_seq // bit)
-        kv_got = swap(after(given, got_two), "seq", seq_size, bit)
+        kv_kept, given_kv = halve(kv_sum, 1, my_seq // bit)
+        kv_got = swap(given_kv, "seq", seq_size, bit)
         kv_sum = add(kv_kept, kv_got)
         bit *= 2
     kv_mine = kv_got
 
-    attn_late = after(attn_flat, dq_two)
+    attn_late = after(attn_flat, given_kv)
     out_term = stack_from_lanes(dot(attn_late, grad_branch, 0, 0).astype(BF16), seq_size)
     kept, given = halve(out_term, 1, my_seq)
-    out_sum = add(kept, swap(given, "seq", seq_size, 1))
-    layer_sum = add(kept_layer, swap(after(given_layer, dq_two), "seq", seq_size, 1))
+    out_got = swap(given, "seq", seq_size, 1)
+    out_sum = add(kept, out_got)
+    layer_got = swap(after(given_layer, given_kv), "seq", seq_size, 1)
+    layer_sum = add(kept_layer, layer_got)
     kept_layer, given_layer = halve(layer_sum, 1, my_seq // 2)
+    grad_tokens, kept, given = joined_back(
+        me, dq_one, dq_two, kv_kept[0], after(kv_got[0], layer_got), cosine, sine, qkv_t, tokens, scale_one,
+        gain_one, grad_residual, normed_one, norm_two_term, seq_size, fsdp_size,
+    )
+
+    got_three = after(got_three, grad_tokens)
+    kept_three, given_last = give(add(kept_three, got_three), 1)
+    next_three = send(given_last, 1)
+    next_one, next_two = after(next_one, grad_tokens), after(next_two, grad_tokens)
+    both = [add(kept_one, next_one), add(kept_two, next_two)]
+    down_sum, one_sum = finish_pair(both, 2)
+
     bit = 2
     while bit < seq_size:
-        kept, given = halve(out_sum, 1, my_seq // bit)
-        out_sum = add(kept, swap(after(given, kv_mine), "seq", seq_size, bit))
+        kept_out, given_out = halve(out_sum, 1, my_seq // bit)
+        out_sum = add(kept_out, swap(after(given_out, grad_tokens), "seq", seq_size, bit))
         bit *= 2
     out_mine = out_sum[0].reshape(fsdp_size, -1, width)
-    got_three = after(got_three, kv_mine)
-    kept_three, given = give(add(kept_three, got_three), 1)
-    next_three = send(given, 1)
-    grad_tokens, kept, given = joined_back(
-        me, dq_one, dq_two, kv_kept[0], kv_got[0], cosine, sine, qkv_t, tokens, scale_one,
-        gain_one, grad_residual, normed_one, norm_two_term, seq_size, fsdp_size,
-    )
-
-    next_one, next_two = after(next_one, grad_tokens), after(next_two, grad_tokens)
-    down_sum = finish(kept_one, next_one, 1)
-
     tail_sum = add(kept, swap(given, "seq", seq_size, 1))
     bit = 2
     while bit < seq_size:
@@ -903,7 +908,6 @@
         layer_sum = add(kept, swap(given, "seq", seq_size, bit))
         bit *= 2
     layer_out = residual + layer_sum[0]
-    one_sum = finish(kept_two, next_two, 1)
     two_sum = finish(kept_three, next_three, 1)
 
     ff_back = cut_lanes(me, (one_sum, two_sum, down_sum), seq_size)

time: 380 us -> 427 us (1.12)
  waiting for transfers between devices: 120 us -> 158 us
  local copies, waits for them, and re-layouts: 38.1 us -> 49.4 us
    ppermute x55 -> x54, waiting for transfers between devices: 120 us -> 158 us  [swap(): return lax.ppermute(block, axis, [(i, i ^ bits) for i in range(size)])]
    squeeze x0 -> x2, local copies, waits for them, and re-layouts: none -> 5.21 us  [the longest x1 2.68 us: per_device(): kept_layer, given_layer = (layer_part[0], layer_part[1])]
    unnamed x115 -> x137, local copies, waits for them, and re-layouts: 11.1 us -> 15.7 us
    ppermute x55 -> x54, starting transfers between devices: 50.2 us -> 46.9 us  [swap(): return lax.ppermute(block, axis, [(i, i ^ bits) for i in range(size)])]
  transfers between devices with their start and end apart: 55 -> 54, of which waited for: 23 -> 23; matrix products, arithmetic and copies ran while one was open for 16% -> 16% of each run, Pallas kernels for 21% -> 18%
where the time goes in v8:
time: 427 us; the launch traced here: 420 us
  waiting for transfers between devices  158 us (37%)
  Pallas kernels  113 us (26%)
  local copies, waits for them, and re-layouts  49.4 us (12%)
  starting transfers between devices  46.9 us (11%)
  other arithmetic  23.5 us (6%)
  matrix products  18.9 us (4%)
  blocking collectives  8.43 us (2%)
    ppermute x54, waiting for transfers between devices, swap(): return lax.ppermute(block, axis, [(i, i ^ bits) for i in range(size)])  158 us
    ppermute x54, starting transfers between devices, swap(): return lax.ppermute(block, axis, [(i, i ^ bits) for i in range(size)])  46.9 us
    pallas_call x1, Pallas kernels, feed_forward(): pl.pallas_call(body, grid=(size,), in_specs=[pl.BlockSpec(memory_space=pl...  33.6 us
    pallas_call x2, Pallas kernels, attend_back(): pl.pallas_call(functools.partial(attend_back_kernel, begin), grid=(pairs,...  32.1 us
    pallas_call x8, Pallas kernels, on_device(): pl.pallas_call(body, in_specs=[pl.BlockSpec(memory_space=pltpu.SMEM)] + [...  24 us
    pallas_call x2, Pallas kernels, attend(): pl.pallas_call(functools.partial(attend_kernel, begin), grid=(pairs,), in...  23.4 us
    dot_general x6, matrix products, dot(): lax.dot_general(left, right, (((left_dim,), (right_dim,)), ((), ())), pre...  18.9 us
    unnamed x137, local copies, waits for them, and re-layouts  15.7 us
  transfers between devices with their start and end apart: 54, of which 23 were waited for; matrix products, arithmetic and copies ran while one was open for 16% of the time, Pallas kernels for 18%

profile of v8, /device:TPU:0, one launch (start us, length us, event | category | flops | bytes accessed | tf_op | source)
XLA Modules:
  0.0 420.1 jit_solution(15040567713924282506)
XLA Ops:
  15.4 8.0 %collective-permute-done.1 = bf16[272,224]{1,0:T(8,128)(2,1)S(1)} collective-permute-done((bf16[272,224]{1,0:T(8,128)(2,1)S(1)}, bf16[272,224]{1,0:T(8,128)(2,1)S(1)}, u32[]{:S(2)}, u32[]{:S(2)}) %collective-permute-start.1) | collective-permute-done | bytes 121888 | tf_op jit(solution)/shard_map/ppermute | solution.py:36
  35.5 3.8 collective-permute-done.9.refs_4_
  46.1 6.7 %collective-permute-done.10.refs_5_ = bf16[4,160,224]{2,1,0:T(8,128)(2,1)} collective-permute-done((bf16[4,160,224]{2,1,0:T(8,128)(2,1)S(1)}, bf16[4,160,224]{2,1,0:T(8,128)(2,1)}, u32[]{:S(2)}, u32[]{:S(2)}) %collective-permute-start.10) | collective-permute-done | bytes 286752 | tf_op jit(solution)/shard_map/ppermute | solution.py:36
  66.0 6.4 %collective-permute-done.13.refs_4_ = bf16[480,896]{1,0:T(8,128)(2,1)} collective-permute-done((bf16[480,896]{1,0:T(8,128)(2,1)S(1)}, bf16[480,896]{1,0:T(8,128)(2,1)}, u32[]{:S(2)}, u32[]{:S(2)}) %collective-permute-start.13) | collective-permute-done | bytes 860192 | tf_op jit(solution)/shard_map/ppermute | solution.py:36
  79.3 8.4 %all_gather.3.kv_ref = bf16[1536,256]{1,0:T(8,128)(2,1)S(1)} all-gather(bf16[384,256]{1,0:T(8,128)(2,1)S(1)} %pad_maximum_fusion.6), channel_id=1, replica_groups=mesh['seq'=4,'fsdp'=8] {'seq'}, dimensions={0}, use_global_device_ids=true | all-gather | bytes 983040 | tf_op jit(solution)/shard_map/all_gather | solution.py:748
  90.1 13.4 %attend.2 = (bf16[384,512]{1,0:T(8,128)(2,1)S(1)}, f32[4,1,768]{2,1,0:T(1,128)S(1)}) custom-call(s32[1,384]{1,0:T(1,128)S(1)} %broadcast_in_dim.10.low_ref, s32[1,384]{1,0:T(1,128)S(1)} %iota_add_fusion.high_ref, s32[1536,1]{1,0:T(8,128)S(1)} %iota.33.place_ref, bf16[384,896]{1,0:T(8,128)(2,1)S(1)} %slice_multiply_fusion.1.q_ref, ...), custom_call_target="tpu_custom_call" | custom-call | flops 1 | bytes 1 | tf_op jit(solution)/shard_map/attend/pallas_call | solution.py:509
  110.1 10.0 %attend.3 = (bf16[384,384]{1,0:T(8,128)(2,1)S(1)}, f32[3,1,768]{2,1,0:T(1,128)S(1)}) custom-call(s32[1,384]{1,0:T(1,128)S(1)} %broadcast_in_dim.10.low_ref, s32[1,384]{1,0:T(1,128)S(1)} %iota_add_fusion.high_ref, s32[1536,1]{1,0:T(8,128)S(1)} %iota.39.place_ref, bf16[384,896]{1,0:T(8,128)(2,1)S(1)} %slice_multiply_fusion.1.q_ref, ...), custom_call_target="tpu_custom_call" | custom-call | flops 1 | bytes 1 | tf_op jit(solution)/shard_map/attend/pallas_call | solution.py:509
  122.7 23.0 %collective-permute-done.22.refs_6_ = bf16[480,896]{1,0:T(8,128)(2,1)S(1)} collective-permute-done((bf16[480,896]{1,0:T(8,128)(2,1)}, bf16[480,896]{1,0:T(8,128)(2,1)S(1)}, u32[]{:S(2)}, u32[]{:S(2)}) %collective-permute-start.22) | collective-permute-done | bytes 860192 | tf_op jit(solution)/shard_map/ppermute | solution.py:36
  150.3 16.3 %collective-permute-done.23.refs_7_ = bf16[480,896]{1,0:T(8,128)(2,1)S(1)} collective-permute-done((bf16[480,896]{1,0:T(8,128)(2,1)S(1)}, bf16[480,896]{1,0:T(8,128)(2,1)S(1)}, u32[]{:S(2)}, u32[]{:S(2)}) %collective-permute-start.23) | collective-permute-done | bytes 860192 | tf_op jit(solution)/shard_map/ppermute | solution.py:36
  167.5 33.6 %feed_forward.1 = (bf16[1536,1280]{1,0:T(8,128)(2,1)}, bf16[1536,1280]{1,0:T(8,128)(2,1)}, bf16[1536,1280]{1,0:T(8,128)(2,1)}, bf16[2,2,384,896]{3,2,1,0:T(8,128...) custom-call(s32[2]{0:T(128)S(1)} %pad_add_fusion.me_ref, ...), custom_call_target="tpu_custom_call" | custom-call | flops 1 | bytes 1 | tf_op jit(solution)/shard_map/feed_forward/pallas_call | solution.py:341
  210.3 4.5 %convolution_convert_fusion.2 = bf16[1280,896]{1,0:T(8,128)(2,1)S(1)} fusion(bf16[1536,1280]{1,0:T(8,128)(2,1)S(1)} %copy-done.63, bf16[1536,896]{1,0:T(8,128)(2,1)S(1)} %bitcast.192), kind=kOutput, calls=%fused_computation.2 | convolution fusion | flops 3524362240 | bytes 8978432 | tf_op jit(solution)/shard_map/dot_general | solution.py:30
  215.6 4.5 %convolution_convert_fusion = bf16[1280,896]{1,0:T(8,128)(2,1)S(1)} fusion(bf16[1536,1280]{1,0:T(8,128)(2,1)S(1)} %copy-done.62, bf16[1536,896]{1,0:T(8,128)(2,1)S(1)} %bitcast.190), kind=kOutput, calls=%fused_computation | convolution fusion | flops 3524362240 | bytes 8978432 | tf_op jit(solution)/shard_map/dot_general | solution.py:30
  221.3 4.9 %convolution_convert_fusion.1 = bf16[1280,896]{1,0:T(8,128)(2,1)S(1)} fusion(bf16[1536,1280]{1,0:T(8,128)(2,1)S(1)} %copy-done.61, bf16[1536,896]{1,0:T(8,128)(2,1)S(1)} %bitcast.191), kind=kOutput, calls=%fused_computation.1 | convolution fusion | flops 3524362240 | bytes 8978432 | tf_op jit(solution)/shard_map/dot_general | solution.py:30
  226.3 16.4 %collective-permute-done.31 = bf16[4,160,896]{2,1,0:T(8,128)(2,1)S(1)} collective-permute-done((bf16[4,160,896]{2,1,0:T(8,128)(2,1)S(1)}, bf16[4,160,896]{2,1,0:T(8,128)(2,1)S(1)}, u32[]{:S(2)}, u32[]{:S(2)}) %collective-permute-start.31) | collective-permute-done | bytes 1146912 | tf_op jit(solution)/shard_map/ppermute | solution.py:36
  244.6 4.7 %residual_back.1 = (f32[384,896]{1,0:T(8,128)}, bf16[384,896]{1,0:T(8,128)(2,1)S(1)}, bf16[384,896]{1,0:T(8,128)(2,1)S(1)}, f32[1,896]{1,0:T(1,128)S(1)}) custom-call(s32[2]{0:T(128)S(1)} %pad_add_fusion.me_ref, f32[384,896]{1,0:T(8,128)} %dynamic-slice_bitcast_fusion.kept_ref, bf16[384,896]{1,0:T(8,128)(2,1)S(1)} %bitcast.158, f32[384,896]{1,0:T(8,128)} %copy-done.25, ...), custom_call_target="tpu_custom_call" | custom-call | tf_op jit(solution)/shard_map/residual_back/pallas_call | solution.py:125
  249.3 17.9 %attend_back.2 = (f32[384,512]{1,0:T(8,128)S(1)}, f32[1536,256]{1,0:T(8,128)}) custom-call(s32[1,384]{1,0:T(1,128)S(1)} %broadcast_in_dim.10.low_ref, s32[1,384]{1,0:T(1,128)S(1)} %iota_add_fusion.high_ref, s32[1536,1]{1,0:T(8,128)S(1)} %iota.41.place_ref, bf16[384,896]{1,0:T(8,128)(2,1)S(1)} %slice_multiply_fusion.1.q_ref, ...), custom_call_target="tpu_custom_call" | custom-call | flops 1 | bytes 1 | tf_op jit(solution)/shard_map/attend_back/pallas_call | solution.py:535
  267.3 14.2 %attend_back.3 = (f32[384,384]{1,0:T(8,128)S(1)}, f32[1536,256]{1,0:T(8,128)}) custom-call(s32[1,384]{1,0:T(1,128)S(1)} %broadcast_in_dim.10.low_ref, s32[1,384]{1,0:T(1,128)S(1)} %iota_add_fusion.high_ref, s32[1536,1]{1,0:T(8,128)S(1)} %iota.40.place_ref, bf16[384,896]{1,0:T(8,128)(2,1)S(1)} %slice_multiply_fusion.1.q_ref, ...), custom_call_target="tpu_custom_call" | custom-call | flops 1 | bytes 1 | tf_op jit(solution)/shard_map/attend_back/pallas_call | solution.py:535
  293.2 19.7 %collective-permute-done.41 = bf16[4,160,896]{2,1,0:T(8,128)(2,1)} collective-permute-done((bf16[4,160,896]{2,1,0:T(8,128)(2,1)}, bf16[4,160,896]{2,1,0:T(8,128)(2,1)}, u32[]{:S(2)}, u32[]{:S(2)}) %collective-permute-start.41) | collective-permute-done | bytes 1146912 | tf_op jit(solution)/shard_map/ppermute | solution.py:36
  322.6 9.3 %joined_back.1 = (f32[384,896]{1,0:T(8,128)}, bf16[2,8,160,224]{3,2,1,0:T(8,128)(2,1)}, bf16[2,8,160,224]{3,2,1,0:T(8,128)(2,1)}) custom-call(s32[2]{0:T(128)S(1)} %pad_add_fusion.me_ref, f32[384,512]{1,0:T(8,128)S(1)} %get-tuple-element.121.dq1_ref, f32[384,384]{1,0:T(8,128)S(1)} %get-tuple-element.122.dq2_ref, ...), custom_call_target="tpu_custom_call" | custom-call | tf_op jit(solution)/shard_map/joined_back/pallas_call | solution.py:125
  331.9 5.1 %collective-permute-done.44 = bf16[4,160,896]{2,1,0:T(8,128)(2,1)} collective-permute-done((bf16[4,160,896]{2,1,0:T(8,128)(2,1)}, bf16[4,160,896]{2,1,0:T(8,128)(2,1)}, u32[]{:S(2)}, u32[]{:S(2)}) %collective-permute-start.44) | collective-permute-done | bytes 1146912 | tf_op jit(solution)/shard_map/ppermute | solution.py:36
  352.6 4.3 %collective-permute-done.40 = bf16[1,896,224]{1,2,0:T(8,128)(2,1)S(1)} collective-permute-done((bf16[1,896,224]{1,2,0:T(8,128)(2,1)S(1)}, bf16[1,896,224]{1,2,0:T(8,128)(2,1)S(1)}, u32[]{:S(2)}, u32[]{:S(2)}) %collective-permute-start.40) | collective-permute-done | bytes 401440 | tf_op jit(solution)/shard_map/ppermute | solution.py:36
  360.3 7.7 %collective-permute-done.45 = bf16[2,160,896]{2,1,0:T(8,128)(2,1)} collective-permute-done((bf16[2,160,896]{2,1,0:T(8,128)(2,1)}, bf16[2,160,896]{2,1,0:T(8,128)(2,1)}, u32[]{:S(2)}, u32[]{:S(2)}) %collective-permute-start.45) | collective-permute-done | bytes 573472 | tf_op jit(solution)/shard_map/ppermute | solution.py:36
  369.7 15.5 %collective-permute-done.38 = bf16[1,8,160,224]{3,2,1,0:T(8,128)(2,1)} collective-permute-done((bf16[1,8,160,224]{3,2,1,0:T(8,128)(2,1)}, bf16[1,8,160,224]{3,2,1,0:T(8,128)(2,1)}, u32[]{:S(2)}, u32[]{:S(2)}) %collective-permute-start.38) | collective-permute-done | bytes 573472 | tf_op jit(solution)/shard_map/ppermute | solution.py:36
  392.2 8.5 %collective-permute-done.43 = bf16[4,272,224]{2,1,0:T(8,128)(2,1)S(1)} collective-permute-done((bf16[4,272,224]{2,1,0:T(8,128)(2,1)S(1)}, bf16[4,272,224]{2,1,0:T(8,128)(2,1)S(1)}, u32[]{:S(2)}, u32[]{:S(2)}) %collective-permute-start.43) | collective-permute-done | bytes 487456 | tf_op jit(solution)/shard_map/ppermute | solution.py:36
  (345 shorter events, 151.2 us)
Async XLA Ops:
  31.3 41.1 %collective-permute-start.13 = (bf16[480,896]{1,0:T(8,128)(2,1)S(1)}, bf16[480,896]{1,0:T(8,128)(2,1)}, u32[]{:S(2)}, u32[]{:S(2)}) collective-permute-start(bf16[480,896]{1,0:T(8,128)(2,1)S(1)} %join_lanes.1.refs_0_), channel_id=1, source_target_pairs={{0,4},{1,5},{2,6},{3,7},{4,0},{5,1},{6,2},{7,3},{8,12},{9,13},{10,... | collective-permute-start | bytes 2580488 | tf_op jit(solution)/shard_map/ppermute | solution.py:36
  33.0 39.5 %collective-permute-start.14 = (bf16[480,896]{1,0:T(8,128)(2,1)S(1)}, bf16[480,896]{1,0:T(8,128)(2,1)}, u32[]{:S(2)}, u32[]{:S(2)}) collective-permute-start(bf16[480,896]{1,0:T(8,128)(2,1)S(1)} %join_lanes.1.refs_0_), channel_id=1, source_target_pairs={{0,2},{1,3},{2,0},{3,1},{4,6},{5,7},{6,4},{7,5},{8,10},{9,11},{10,... | collective-permute-start | bytes 2580488 | tf_op jit(solution)/shard_map/ppermute | solution.py:36
  39.3 33.2 %collective-permute-start.15 = (bf16[480,896]{1,0:T(8,128)(2,1)S(1)}, bf16[480,896]{1,0:T(8,128)(2,1)}, u32[]{:S(2)}, u32[]{:S(2)}) collective-permute-start(bf16[480,896]{1,0:T(8,128)(2,1)S(1)} %join_lanes.1.refs_0_), channel_id=1, source_target_pairs={{0,1},{1,0},{2,3},{3,2},{4,5},{5,4},{6,7},{7,6},{8,9},{9,8},{10,11... | collective-permute-start | bytes 2580488 | tf_op jit(solution)/shard_map/ppermute | solution.py:36
  60.8 28.7 %collective-permute-start.19 = (bf16[8,112,224]{2,1,0:T(8,128)(2,1)S(1)}, bf16[8,112,224]{2,1,0:T(8,128)(2,1)S(1)}, u32[]{:S(2)}, u32[]{:S(2)}) collective-permute-start(bf16[8,112,224]{2,1,0:T(8,128)(2,1)S(1)} %pad_maximum_fusion.5.refs_0_), channel_id=1, source_target_pairs={{0,16},{8,24},{16,0},{24,8},{1,17},{9,25},{17,1},{25,9},{2,18},{10... | collective-permute-start | bytes 1204232 | tf_op jit(solution)/shard_map/ppermute | solution.py:36
  87.8 22.3 %collective-permute-start.17 = (bf16[480,896]{1,0:T(8,128)(2,1)}, bf16[480,896]{1,0:T(8,128)(2,1)}, u32[]{:S(2)}, u32[]{:S(2)}) collective-permute-start(bf16[480,896]{1,0:T(8,128)(2,1)} %collective-permute-done.14.refs_2_), channel_id=1, source_target_pairs={{0,1},{1,0},{2,3},{3,2},{4,5},{5,4},{6,7},{7,6},{8,9},{9,8},{10,11... | collective-permute-start | bytes 2580488 | tf_op jit(solution)/shard_map/ppermute | solution.py:36
  88.3 21.2 %collective-permute-start.16 = (bf16[384,896]{1,0:T(8,128)(2,1)}, bf16[384,896]{1,0:T(8,128)(2,1)S(1)}, u32[]{:S(2)}, u32[]{:S(2)}) collective-permute-start(bf16[384,896]{1,0:T(8,128)(2,1)} %cot_ref.1), channel_id=1, source_target_pairs={{0,16},{8,24},{16,0},{24,8},{1,17},{9,25},{17,1},{25,9},{2,18},{10... | collective-permute-start | bytes 2064392 | tf_op jit(solution)/shard_map/ppermute | solution.py:36
  103.7 43.0 %collective-permute-start.21 = (bf16[480,896]{1,0:T(8,128)(2,1)}, bf16[480,896]{1,0:T(8,128)(2,1)S(1)}, u32[]{:S(2)}, u32[]{:S(2)}) collective-permute-start(bf16[480,896]{1,0:T(8,128)(2,1)} %collective-permute-done.13.refs_4_), channel_id=1, source_target_pairs={{0,1},{1,0},{2,3},{3,2},{4,5},{5,4},{6,7},{7,6},{8,9},{9,8},{10,11... | collective-permute-start | bytes 2580488 | tf_op jit(solution)/shard_map/ppermute | solution.py:36
  105.2 40.4 %collective-permute-start.22 = (bf16[480,896]{1,0:T(8,128)(2,1)}, bf16[480,896]{1,0:T(8,128)(2,1)S(1)}, u32[]{:S(2)}, u32[]{:S(2)}) collective-permute-start(bf16[480,896]{1,0:T(8,128)(2,1)} %collective-permute-done.14.refs_2_), channel_id=1, source_target_pairs={{0,4},{1,5},{2,6},{3,7},{4,0},{5,1},{6,2},{7,3},{8,12},{9,13},{10,... | collective-permute-start | bytes 2580488 | tf_op jit(solution)/shard_map/ppermute | solution.py:36
  121.4 25.4 %collective-permute-start.25 = (bf16[384,896]{1,0:T(8,128)(2,1)S(1)}, bf16[384,896]{1,0:T(8,128)(2,1)S(1)}, u32[]{:S(2)}, u32[]{:S(2)}) collective-permute-start(bf16[384,896]{1,0:T(8,128)(2,1)S(1)} %multiply_convert_fusion.refs_8_), channel_id=1, source_target_pairs={{0,16},{8,24},{16,0},{24,8},{1,17},{9,25},{17,1},{25,9},{2,18},{10... | collective-permute-start | bytes 2064392 | tf_op jit(solution)/shard_map/ppermute | solution.py:36
  145.7 20.9 %collective-permute-start.23 = (bf16[480,896]{1,0:T(8,128)(2,1)S(1)}, bf16[480,896]{1,0:T(8,128)(2,1)S(1)}, u32[]{:S(2)}, u32[]{:S(2)}) collective-permute-start(bf16[480,896]{1,0:T(8,128)(2,1)S(1)} %collective-permute-done.22.refs_6_), channel_id=1, source_target_pairs={{0,1},{1,0},{2,3},{3,2},{4,5},{5,4},{6,7},{7,6},{8,9},{9,8},{10,11... | collective-permute-start | bytes 2580488 | tf_op jit(solution)/shard_map/ppermute | solution.py:36
  146.8 19.8 %collective-permute-start.26 = (bf16[384,896]{1,0:T(8,128)(2,1)S(1)}, bf16[384,896]{1,0:T(8,128)(2,1)S(1)}, u32[]{:S(2)}, u32[]{:S(2)}) collective-permute-start(bf16[384,896]{1,0:T(8,128)(2,1)S(1)} %collective-permute-done.25.refs_10_), channel_id=1, source_target_pairs={{0,8},{8,0},{16,24},{24,16},{1,9},{9,1},{17,25},{25,17},{2,10},{10... | collective-permute-start | bytes 2064392 | tf_op jit(solution)/shard_map/ppermute | solution.py:36
  207.8 36.7 %collective-permute-start.30 = (bf16[1,384,896]{2,1,0:T(8,128)(2,1)S(1)}, bf16[1,384,896]{2,1,0:T(8,128)(2,1)S(1)}, u32[]{:S(2)}, u32[]{:S(2)}) collective-permute-start(bf16[1,384,896]{2,1,0:T(8,128)(2,1)S(1)} %dynamic-slice_convert_fusion.1), channel_id=1, source_target_pairs={{0,16},{8,24},{16,0},{24,8},{1,17},{9,25},{17,1},{25,9},{2,18},{10... | collective-permute-start | bytes 2064392 | tf_op jit(solution)/shard_map/ppermute | solution.py:36
  215.0 27.7 %collective-permute-start.31 = (bf16[4,160,896]{2,1,0:T(8,128)(2,1)S(1)}, bf16[4,160,896]{2,1,0:T(8,128)(2,1)S(1)}, u32[]{:S(2)}, u32[]{:S(2)}) collective-permute-start(bf16[4,160,896]{2,1,0:T(8,128)(2,1)S(1)} %dynamic-slice_bitcast_fusion.3), channel_id=1, source_target_pairs={{0,1},{1,0},{2,3},{3,2},{4,5},{5,4},{6,7},{7,6},{8,9},{9,8},{10,11... | collective-permute-start | bytes 3440648 | tf_op jit(solution)/shard_map/ppermute | solution.py:36
  243.0 38.5 %collective-permute-start.32 = (bf16[2,160,896]{2,1,0:T(8,128)(2,1)S(1)}, bf16[2,160,896]{2,1,0:T(8,128)(2,1)S(1)}, u32[]{:S(2)}, u32[]{:S(2)}) collective-permute-start(bf16[2,160,896]{2,1,0:T(8,128)(2,1)S(1)} %fusion.8), channel_id=1, source_target_pairs={{0,4},{1,5},{2,6},{3,7},{4,0},{5,1},{6,2},{7,3},{8,12},{9,13},{10,... | collective-permute-start | bytes 1720328 | tf_op jit(solution)/shard_map/ppermute | solution.py:36
  284.5 28.4 %collective-permute-start.41 = (bf16[4,160,896]{2,1,0:T(8,128)(2,1)}, bf16[4,160,896]{2,1,0:T(8,128)(2,1)}, u32[]{:S(2)}, u32[]{:S(2)}) collective-permute-start(bf16[4,160,896]{2,1,0:T(8,128)(2,1)} %dynamic-slice_bitcast_fusion.2), channel_id=1, source_target_pairs={{0,1},{1,0},{2,3},{3,2},{4,5},{5,4},{6,7},{7,6},{8,9},{9,8},{10,11... | collective-permute-start | bytes 3440648 | tf_op jit(solution)/shard_map/ppermute | solution.py:36
  287.1 35.4 %collective-permute-start.34 = (bf16[2,384,896]{2,1,0:T(8,128)(2,1)}, bf16[2,384,896]{2,1,0:T(8,128)(2,1)}, u32[]{:S(2)}, u32[]{:S(2)}) collective-permute-start(bf16[2,384,896]{2,1,0:T(8,128)(2,1)} %slice_bitcast_fusion.1), channel_id=1, source_target_pairs={{0,8},{8,0},{16,24},{24,16},{1,9},{9,1},{17,25},{25,17},{2,10},{10... | collective-permute-start | bytes 4128776 | tf_op jit(solution)/shard_map/ppermute | solution.py:36
  290.0 27.5 %collective-permute-start.39 = (bf16[2,896,224]{1,2,0:T(8,128)(2,1)}, bf16[2,896,224]{1,2,0:T(8,128)(2,1)}, u32[]{:S(2)}, u32[]{:S(2)}) collective-permute-start(bf16[2,896,224]{1,2,0:T(8,128)(2,1)} %dynamic-slice_bitcast_fusion.4), channel_id=1, source_target_pairs={{0,8},{8,0},{16,24},{24,16},{1,9},{9,1},{17,25},{25,17},{2,10},{10... | collective-permute-start | bytes 2408456 | tf_op jit(solution)/shard_map/ppermute | solution.py:36
  291.3 45.7 %collective-permute-start.44 = (bf16[4,160,896]{2,1,0:T(8,128)(2,1)}, bf16[4,160,896]{2,1,0:T(8,128)(2,1)}, u32[]{:S(2)}, u32[]{:S(2)}) collective-permute-start(bf16[4,160,896]{2,1,0:T(8,128)(2,1)} %dynamic-slice_bitcast_fusion.1), channel_id=1, source_target_pairs={{0,1},{1,0},{2,3},{3,2},{4,5},{5,4},{6,7},{7,6},{8,9},{9,8},{10,11... | collective-permute-start | bytes 3440648 | tf_op jit(solution)/shard_map/ppermute | solution.py:36
  314.8 27.4 %collective-permute-start.42 = (bf16[2,160,896]{2,1,0:T(8,128)(2,1)S(1)}, bf16[2,160,896]{2,1,0:T(8,128)(2,1)S(1)}, u32[]{:S(2)}, u32[]{:S(2)}) collective-permute-start(bf16[2,160,896]{2,1,0:T(8,128)(2,1)S(1)} %fusion.9), channel_id=1, source_target_pairs={{0,4},{1,5},{2,6},{3,7},{4,0},{5,1},{6,2},{7,3},{8,12},{9,13},{10,... | collective-permute-start | bytes 1720328 | tf_op jit(solution)/shard_map/ppermute | solution.py:36
  339.8 28.2 %collective-permute-start.45 = (bf16[2,160,896]{2,1,0:T(8,128)(2,1)}, bf16[2,160,896]{2,1,0:T(8,128)(2,1)}, u32[]{:S(2)}, u32[]{:S(2)}) collective-permute-start(bf16[2,160,896]{2,1,0:T(8,128)(2,1)} %fusion.10), channel_id=1, source_target_pairs={{0,4},{1,5},{2,6},{3,7},{4,0},{5,1},{6,2},{7,3},{8,12},{9,13},{10,... | collective-permute-start | bytes 1720328 | tf_op jit(solution)/shard_map/ppermute | solution.py:36
  343.8 43.5 %collective-permute-start.49 = (bf16[2,160,896]{2,1,0:T(8,128)(2,1)}, bf16[2,160,896]{2,1,0:T(8,128)(2,1)}, u32[]{:S(2)}, u32[]{:S(2)}) collective-permute-start(bf16[2,160,896]{2,1,0:T(8,128)(2,1)} %pad_maximum_fusion.3), channel_id=1, source_target_pairs={{0,2},{1,3},{2,0},{3,1},{4,6},{5,7},{6,4},{7,5},{8,10},{9,11},{10,... | collective-permute-start | bytes 1720328 | tf_op jit(solution)/shard_map/ppermute | solution.py:36
  347.8 55.8 %collective-permute-start.36 = (bf16[1,384,896]{2,1,0:T(8,128)(2,1)S(1)}, bf16[1,384,896]{2,1,0:T(8,128)(2,1)}, u32[]{:S(2)}, u32[]{:S(2)}) collective-permute-start(bf16[1,384,896]{2,1,0:T(8,128)(2,1)S(1)} %dynamic-slice_convert_fusion), channel_id=1, source_target_pairs={{0,16},{8,24},{16,0},{24,8},{1,17},{9,25},{17,1},{25,9},{2,18},{10... | collective-permute-start | bytes 2064392 | tf_op jit(solution)/shard_map/ppermute | solution.py:36
  351.7 33.4 %collective-permute-start.38 = (bf16[1,8,160,224]{3,2,1,0:T(8,128)(2,1)}, bf16[1,8,160,224]{3,2,1,0:T(8,128)(2,1)}, u32[]{:S(2)}, u32[]{:S(2)}) collective-permute-start(bf16[1,8,160,224]{3,2,1,0:T(8,128)(2,1)} %dynamic-slice_convert_fusion.2), channel_id=1, source_target_pairs={{0,16},{8,24},{16,0},{24,8},{1,17},{9,25},{17,1},{25,9},{2,18},{10... | collective-permute-start | bytes 1720328 | tf_op jit(solution)/shard_map/ppermute | solution.py:36
  369.6 19.6 %collective-permute-start.50 = (bf16[1,160,896]{2,1,0:T(8,128)(2,1)S(1)}, bf16[1,160,896]{2,1,0:T(8,128)(2,1)S(1)}, u32[]{:S(2)}, u32[]{:S(2)}) collective-permute-start(bf16[1,160,896]{2,1,0:T(8,128)(2,1)S(1)} %dynamic-slice_convert_fusion.8), channel_id=1, source_target_pairs={{0,2},{1,3},{2,0},{3,1},{4,6},{5,7},{6,4},{7,5},{8,10},{9,11},{10,... | collective-permute-start | bytes 860168 | tf_op jit(solution)/shard_map/ppermute | solution.py:36
  (97 other events, 838.0 us)

commit v9 on v7

--- a/solution.py
+++ b/solution.py
@@ -56,7 +56,7 @@
     while bit < size:
         (outer_bits if bit >= inner else inner_bits).append(bit)
         bit *= 2
-    return outer_bits + inner_bits
+    return outer_bits[::-1] + inner_bits
 
 
 def column_gather(block, size):
@@ -274,7 +274,7 @@
         xs, gs = refs[count : count + size], refs[count + size : count + 2 * size]
         outs = refs[count + 2 * size : count + 2 * size + 9]
         hid, gg, gu, gn_kept, gn_given, part_kept, part_given, x_out, g_out = outs
-        gu_w, d_w, x_all, g_all, sems = refs[count + 2 * size + 9 :]
+        gu_w, d_w, x_all, g_all, held, sems = refs[count + 2 * size + 9 :]
         step = pl.program_id(0)
         core = me_ref[0] % 2
         handed = [
@@ -302,8 +302,8 @@
             for copy in handed:
                 copy.start()
 
-        x = x_all[step]
-        g = g_all[step]
+        x = x_all[pl.ds(2 * step, 2)].reshape(2 * rows, width)
+        g = g_all[pl.ds(2 * step, 2)].reshape(2 * rows, width)
         gate_w = gu_w[: count // 2].reshape(units, width)
         up_w = gu_w[count // 2 :].reshape(units, width)
         down_w = d_w[...].reshape(units, width)
@@ -318,34 +318,26 @@
             gg[:, at] = (grad_hidden * up * (sigmoid + silu * (1.0 - sigmoid))).astype(BF16)
             gu[:, at] = (grad_hidden * silu).astype(BF16)
 
-        mine = step % 2 == core
-
         def hand_out(value, kept, given):
-            low = value.astype(BF16)
-
-            @pl.when(mine)
-            def _():
-                kept[0] = low
-
-            @pl.when(jnp.logical_not(mine))
-            def _():
-                given[0] = low
+            held[...] = value.astype(BF16).reshape(2, rows, width)
+            kept[0] = held[core]
+            given[0] = held[1 - core]
 
         hand_out(dot(gg[...], gate_w, 1, 0) + dot(gu[...], up_w, 1, 0), gn_kept, gn_given)
         hand_out(dot(hid[...], down_w, 1, 0), part_kept, part_given)
 
-        @pl.when(step == size - 1)
+        @pl.when(step == size // 2 - 1)
         def _():
             for copy in handed:
                 copy.wait()
 
     hbm = pl.BlockSpec(memory_space=pl.ANY)
-    by_rows = pl.BlockSpec((rows, units), lambda i: (i, 0))
-    by_pair = pl.BlockSpec((1, rows, width), lambda i: (i // 2, 0, 0))
+    by_rows = pl.BlockSpec((2 * rows, units), lambda i: (i, 0))
+    by_pair = pl.BlockSpec((1, rows, width), lambda i: (i, 0, 0))
     like = jax.ShapeDtypeStruct
     return pl.pallas_call(
         body,
-        grid=(size,),
+        grid=(size // 2,),
         in_specs=[pl.BlockSpec(memory_space=pltpu.SMEM)]
         + [hbm] * (count + 2 * size),
         out_specs=[by_rows] * 3 + [by_pair] * 4 + [hbm] * 2,
@@ -357,6 +349,7 @@
             pltpu.VMEM((count, tall, width), BF16),
             pltpu.VMEM((size, rows, width), BF16),
             pltpu.VMEM((size, rows, width), BF16),
+            pltpu.VMEM((2, rows, width), BF16),
             pltpu.SemaphoreType.DMA((2 * count + 2 * size + 2,)),
         ],
         compiler_params=pltpu.CompilerParams(vmem_limit_bytes=VMEM_LIMIT),
@@ -736,7 +729,7 @@
     out_blocks = seq_gather(out_stack, seq_size)
 
     own_x = ff_spread(ff_block, fsdp_size)
-    last = swap(after(near, qkv_t), "fsdp", fsdp_size, 2 * inner)
+    last = swap(after(far, qkv_t), "fsdp", fsdp_size, inner)
     qkv_t = after(qkv_t, far, near, *own_x.values())[:, :qkv_rows].reshape(fsdp_size * qkv_rows, -1)
     gain_one = vectors[:, 0, : norm_one.shape[0]].reshape(-1).astype(F32)
     bias_full = vectors[:, 1, : qkv_bias.shape[0]].reshape(-1).astype(F32)
@@ -764,7 +757,7 @@
         low, high, place, after(queries, far), kv_all, 0, split
     )
     far_x = spread(after(far, kv_all))
-    queries_two = after(queries, attn_one, last, cot_blocks[seq_size // 2], *near_x.values())
+    queries_two = after(queries, attn_one, cot_blocks[seq_size // 2], *near_x.values())
     attn_two, lse_two = attend(low, high, place, queries_two, kv_all, split, PAIRS - split)
     last_x = spread(last)
     for base, row in ((0, own_x), (inner, near_x), (2 * inner, far_x), (3 * inner, last_x)):
@@ -783,7 +776,7 @@
     while bit:
         if bit == 1:
             top = seq_size // 2
-            normed_blocks[top] = after(normed_blocks[top], *far_x.values())
+            normed_blocks[top] = after(normed_blocks[top], last, *far_x.values())
         normed_blocks.update(
             {o ^ bit: swap(b, "seq", seq_size, bit) for o, b in normed_blocks.items()}
         )
@@ -869,25 +862,26 @@
     out_term = stack_from_lanes(dot(attn_late, grad_branch, 0, 0).astype(BF16), seq_size)
     kept, given = halve(out_term, 1, my_seq)
     out_sum = add(kept, swap(given, "seq", seq_size, 1))
-    layer_sum = add(kept_layer, swap(after(given_layer, dq_two), "seq", seq_size, 1))
+    layer_got = swap(after(given_layer, dq_two), "seq", seq_size, 1)
+    layer_sum = add(kept_layer, layer_got)
     kept_layer, given_layer = halve(layer_sum, 1, my_seq // 2)
+    grad_tokens, kept, given = joined_back(
+        me, dq_one, dq_two, kv_kept[0], after(kv_got[0], layer_got), cosine, sine, qkv_t, tokens, scale_one,
+        gain_one, grad_residual, normed_one, norm_two_term, seq_size, fsdp_size,
+    )
+
+    got_three = after(got_three, grad_tokens)
+    kept_three, given_last = give(add(kept_three, got_three), 1)
+    next_three = send(given_last, 1)
+    next_one, next_two = after(next_one, grad_tokens), after(next_two, grad_tokens)
+    down_sum = finish(kept_one, next_one, 1)
+
     bit = 2
     while bit < seq_size:
-        kept, given = halve(out_sum, 1, my_seq // bit)
-        out_sum = add(kept, swap(after(given, kv_mine), "seq", seq_size, bit))
+        kept_out, given_out = halve(out_sum, 1, my_seq // bit)
+        out_sum = add(kept_out, swap(after(given_out, grad_tokens), "seq", seq_size, bit))
         bit *= 2
     out_mine = out_sum[0].reshape(fsdp_size, -1, width)
-    got_three = after(got_three, kv_mine)
-    kept_three, given = give(add(kept_three, got_three), 1)
-    next_three = send(given, 1)
-    grad_tokens, kept, given = joined_back(
-        me, dq_one, dq_two, kv_kept[0], kv_got[0], cosine, sine, qkv_t, tokens, scale_one,
-        gain_one, grad_residual, normed_one, norm_two_term, seq_size, fsdp_size,
-    )
-
-    next_one, next_two = after(next_one, grad_tokens), after(next_two, grad_tokens)
-    down_sum = finish(kept_one, next_one, 1)
-
     tail_sum = add(kept, swap(given, "seq", seq_size, 1))
     bit = 2
     while bit < seq_size:

time: 380 us -> 367 us (0.966)
  waiting for transfers between devices: 120 us -> 104 us
    ppermute x55, waiting for transfers between devices: 120 us -> 104 us  [swap(): return lax.ppermute(block, axis, [(i, i ^ bits) for i in range(size)])]
    unnamed x115 -> x123, local copies, waits for them, and re-layouts: 11.1 us -> 9.08 us
  transfers between devices with their start and end apart: 55 -> 55, of which waited for: 23 -> 22; matrix products, arithmetic and copies ran while one was open for 16% -> 18% of each run, Pallas kernels for 21% -> 22%
where the time goes in v9:
time: 367 us; the launch traced here: 359 us
  Pallas kernels  114 us (31%)
  waiting for transfers between devices  104 us (28%)
  starting transfers between devices  48.9 us (13%)
  local copies, waits for them, and re-layouts  39.8 us (11%)
  other arithmetic  22.4 us (6%)
  matrix products  20 us (5%)
  blocking collectives  8.18 us (2%)
    ppermute x55, waiting for transfers between devices, swap(): return lax.ppermute(block, axis, [(i, i ^ bits) for i in range(size)])  104 us
    ppermute x55, starting transfers between devices, swap(): return lax.ppermute(block, axis, [(i, i ^ bits) for i in range(size)])  48.9 us
    pallas_call x1, Pallas kernels, feed_forward(): pl.pallas_call(body, grid=(size // 2,), in_specs=[pl.BlockSpec(memory_spa...  34.4 us
    pallas_call x2, Pallas kernels, attend_back(): pl.pallas_call(functools.partial(attend_back_kernel, begin), grid=(pairs,...  32.1 us
    pallas_call x8, Pallas kernels, on_device(): pl.pallas_call(body, in_specs=[pl.BlockSpec(memory_space=pltpu.SMEM)] + [...  23.8 us
    pallas_call x2, Pallas kernels, attend(): pl.pallas_call(functools.partial(attend_kernel, begin), grid=(pairs,), in...  23.4 us
    dot_general x6, matrix products, dot(): lax.dot_general(left, right, (((left_dim,), (right_dim,)), ((), ())), pre...  20 us
    add x13, other arithmetic, add(): return kept.astype(F32) + got.astype(F32)  12.4 us
  transfers between devices with their start and end apart: 55, of which 22 were waited for; matrix products, arithmetic and copies ran while one was open for 18% of the time, Pallas kernels for 22%

profile of v9, /device:TPU:0, one launch (start us, length us, event | category | flops | bytes accessed | tf_op | source)
XLA Modules:
  0.0 359.5 jit_solution(16796849557735118671)
XLA Ops:
  15.4 8.0 %collective-permute-done.1 = bf16[272,224]{1,0:T(8,128)(2,1)S(1)} collective-permute-done((bf16[272,224]{1,0:T(8,128)(2,1)S(1)}, bf16[272,224]{1,0:T(8,128)(2,1)S(1)}, u32[]{:S(2)}, u32[]{:S(2)}) %collective-permute-start.1) | collective-permute-done | bytes 121888 | tf_op jit(solution)/shard_map/ppermute | solution.py:36
  35.5 3.8 %collective-permute-done.9.refs_4_ = bf16[4,160,224]{2,1,0:T(8,128)(2,1)S(1)} collective-permute-done((bf16[4,160,224]{2,1,0:T(8,128)(2,1)S(1)}, bf16[4,160,224]{2,1,0:T(8,128)(2,1)S(1)}, u32[]{:S(2)}, u32[]{:S(2)}) %collective-permute-start.9) | collective-permute-done | bytes 286752 | tf_op jit(solution)/shard_map/ppermute | solution.py:36
  46.1 6.6 %collective-permute-done.10.refs_5_ = bf16[4,160,224]{2,1,0:T(8,128)(2,1)} collective-permute-done((bf16[4,160,224]{2,1,0:T(8,128)(2,1)S(1)}, bf16[4,160,224]{2,1,0:T(8,128)(2,1)}, u32[]{:S(2)}, u32[]{:S(2)}) %collective-permute-start.10) | collective-permute-done | bytes 286752 | tf_op jit(solution)/shard_map/ppermute | solution.py:36
  62.6 3.3 join_both.2
  65.9 6.5 %collective-permute-done.13.refs_4_ = bf16[480,896]{1,0:T(8,128)(2,1)} collective-permute-done((bf16[480,896]{1,0:T(8,128)(2,1)S(1)}, bf16[480,896]{1,0:T(8,128)(2,1)}, u32[]{:S(2)}, u32[]{:S(2)}) %collective-permute-start.13) | collective-permute-done | bytes 860192 | tf_op jit(solution)/shard_map/ppermute | solution.py:36
  79.4 8.2 %all_gather.3.kv_ref = bf16[1536,256]{1,0:T(8,128)(2,1)S(1)} all-gather(bf16[384,256]{1,0:T(8,128)(2,1)S(1)} %pad_maximum_fusion.5), channel_id=1, replica_groups=mesh['seq'=4,'fsdp'=8] {'seq'}, dimensions={0}, use_global_device_ids=true | all-gather | bytes 983040 | tf_op jit(solution)/shard_map/all_gather | solution.py:746
  89.9 13.4 %attend.2 = (bf16[384,512]{1,0:T(8,128)(2,1)S(1)}, f32[4,1,768]{2,1,0:T(1,128)S(1)}) custom-call(s32[1,384]{1,0:T(1,128)S(1)} %broadcast_in_dim.10.low_ref, s32[1,384]{1,0:T(1,128)S(1)} %iota_add_fusion.high_ref, s32[1536,1]{1,0:T(8,128)S(1)} %iota.33.place_ref, bf16[384,896]{1,0:T(8,128)(2,1)S(1)} %slice_multiply_fusion.1.q_ref, ...), custom_call_target="tpu_custom_call" | custom-call | flops 1 | bytes 1 | tf_op jit(solution)/shard_map/attend/pallas_call | solution.py:507
  109.9 10.0 %attend.3 = (bf16[384,384]{1,0:T(8,128)(2,1)S(1)}, f32[3,1,768]{2,1,0:T(1,128)S(1)}) custom-call(s32[1,384]{1,0:T(1,128)S(1)} %broadcast_in_dim.10.low_ref, s32[1,384]{1,0:T(1,128)S(1)} %iota_add_fusion.high_ref, s32[1536,1]{1,0:T(8,128)S(1)} %iota.39.place_ref, bf16[384,896]{1,0:T(8,128)(2,1)S(1)} %slice_multiply_fusion.1.q_ref, ...), custom_call_target="tpu_custom_call" | custom-call | flops 1 | bytes 1 | tf_op jit(solution)/shard_map/attend/pallas_call | solution.py:507
  122.5 3.6 %collective-permute-done.22.refs_6_ = bf16[480,896]{1,0:T(8,128)(2,1)S(1)} collective-permute-done((bf16[480,896]{1,0:T(8,128)(2,1)}, bf16[480,896]{1,0:T(8,128)(2,1)S(1)}, u32[]{:S(2)}, u32[]{:S(2)}) %collective-permute-start.22) | collective-permute-done | bytes 860192 | tf_op jit(solution)/shard_map/ppermute | solution.py:36
  127.6 10.1 %collective-permute-done.25.refs_10_ = bf16[384,896]{1,0:T(8,128)(2,1)S(1)} collective-permute-done((bf16[384,896]{1,0:T(8,128)(2,1)S(1)}, bf16[384,896]{1,0:T(8,128)(2,1)S(1)}, u32[]{:S(2)}, u32[]{:S(2)}) %collective-permute-start.25) | collective-permute-done | bytes 688160 | tf_op jit(solution)/shard_map/ppermute | solution.py:36
  137.7 8.4 %collective-permute-done.23.refs_7_ = bf16[480,896]{1,0:T(8,128)(2,1)S(1)} collective-permute-done((bf16[480,896]{1,0:T(8,128)(2,1)S(1)}, bf16[480,896]{1,0:T(8,128)(2,1)S(1)}, u32[]{:S(2)}, u32[]{:S(2)}) %collective-permute-start.23) | collective-permute-done | bytes 860192 | tf_op jit(solution)/shard_map/ppermute | solution.py:36
  147.0 34.4 %feed_forward.1 = (bf16[1536,1280]{1,0:T(8,128)(2,1)}, bf16[1536,1280]{1,0:T(8,128)(2,1)}, bf16[1536,1280]{1,0:T(8,128)(2,1)}, bf16[2,384,896]{2,1,0:T(8,128)(2,...) custom-call(s32[2]{0:T(128)S(1)} %pad_add_fusion.me_ref, ...), custom_call_target="tpu_custom_call" | custom-call | flops 1 | bytes 1 | tf_op jit(solution)/shard_map/feed_forward/pallas_call | solution.py:338
  188.4 4.5 %convolution_convert_fusion.2 = bf16[1280,896]{1,0:T(8,128)(2,1)S(1)} fusion(bf16[1536,1280]{1,0:T(8,128)(2,1)S(1)} %copy-done.56, bf16[1536,896]{1,0:T(8,128)(2,1)S(1)} %bitcast.193), kind=kOutput, calls=%fused_computation.2 | convolution fusion | flops 3524362240 | bytes 8978432 | tf_op jit(solution)/shard_map/dot_general | solution.py:30
  192.9 4.7 %convolution_convert_fusion = bf16[1280,896]{1,0:T(8,128)(2,1)S(1)} fusion(bf16[1536,1280]{1,0:T(8,128)(2,1)S(1)} %copy-done.55, bf16[1536,896]{1,0:T(8,128)(2,1)S(1)} %bitcast.191), kind=kOutput, calls=%fused_computation | convolution fusion | flops 3524362240 | bytes 8978432 | tf_op jit(solution)/shard_map/dot_general | solution.py:30
  197.7 4.5 %convolution_convert_fusion.1 = bf16[1280,896]{1,0:T(8,128)(2,1)S(1)} fusion(bf16[1536,1280]{1,0:T(8,128)(2,1)S(1)} %copy-done.54, bf16[1536,896]{1,0:T(8,128)(2,1)S(1)} %bitcast.192), kind=kOutput, calls=%fused_computation.1 | convolution fusion | flops 3524362240 | bytes 8978432 | tf_op jit(solution)/shard_map/dot_general | solution.py:30
  209.6 4.7 %residual_back.1 = (f32[384,896]{1,0:T(8,128)}, bf16[384,896]{1,0:T(8,128)(2,1)S(1)}, bf16[384,896]{1,0:T(8,128)(2,1)S(1)}, f32[1,896]{1,0:T(1,128)S(1)}) custom-call(s32[2]{0:T(128)S(1)} %pad_add_fusion.me_ref, f32[384,896]{1,0:T(8,128)} %dynamic-slice_bitcast_fusion.kept_ref, bf16[384,896]{1,0:T(8,128)(2,1)S(1)} %bitcast.159, f32[384,896]{1,0:T(8,128)} %copy-done.25, ...), custom_call_target="tpu_custom_call" | custom-call | tf_op jit(solution)/shard_map/residual_back/pallas_call | solution.py:125
  214.4 17.9 %attend_back.2 = (f32[384,512]{1,0:T(8,128)S(1)}, f32[1536,256]{1,0:T(8,128)}) custom-call(s32[1,384]{1,0:T(1,128)S(1)} %broadcast_in_dim.10.low_ref, s32[1,384]{1,0:T(1,128)S(1)} %iota_add_fusion.high_ref, s32[1536,1]{1,0:T(8,128)S(1)} %iota.41.place_ref, bf16[384,896]{1,0:T(8,128)(2,1)S(1)} %slice_multiply_fusion.1.q_ref, ...), custom_call_target="tpu_custom_call" | custom-call | flops 1 | bytes 1 | tf_op jit(solution)/shard_map/attend_back/pallas_call | solution.py:533
  235.5 14.2 %attend_back.3 = (f32[384,384]{1,0:T(8,128)S(1)}, f32[1536,256]{1,0:T(8,128)}) custom-call(s32[1,384]{1,0:T(1,128)S(1)} %broadcast_in_dim.10.low_ref, s32[1,384]{1,0:T(1,128)S(1)} %iota_add_fusion.high_ref, s32[1536,1]{1,0:T(8,128)S(1)} %iota.40.place_ref, bf16[384,896]{1,0:T(8,128)(2,1)S(1)} %slice_multiply_fusion.1.q_ref, ...), custom_call_target="tpu_custom_call" | custom-call | flops 1 | bytes 1 | tf_op jit(solution)/shard_map/attend_back/pallas_call | solution.py:533
  260.4 3.3 collective-permute-done.35
  263.7 9.3 %joined_back.1 = (f32[384,896]{1,0:T(8,128)}, bf16[2,8,160,224]{3,2,1,0:T(8,128)(2,1)}, bf16[2,8,160,224]{3,2,1,0:T(8,128)(2,1)}) custom-call(s32[2]{0:T(128)S(1)} %pad_add_fusion.me_ref, f32[384,512]{1,0:T(8,128)S(1)} %get-tuple-element.120.dq1_ref, f32[384,384]{1,0:T(8,128)S(1)} %get-tuple-element.124.dq2_ref, ...), custom_call_target="tpu_custom_call" | custom-call | tf_op jit(solution)/shard_map/joined_back/pallas_call | solution.py:125
  294.2 6.3 %collective-permute-done.40 = bf16[1,896,224]{1,2,0:T(8,128)(2,1)S(1)} collective-permute-done((bf16[1,896,224]{1,2,0:T(8,128)(2,1)S(1)}, bf16[1,896,224]{1,2,0:T(8,128)(2,1)S(1)}, u32[]{:S(2)}, u32[]{:S(2)}) %collective-permute-start.40) | collective-permute-done | bytes 401440 | tf_op jit(solution)/shard_map/ppermute | solution.py:36
  303.9 4.6 %collective-permute-done.44 = bf16[2,160,896]{2,1,0:T(8,128)(2,1)} collective-permute-done((bf16[2,160,896]{2,1,0:T(8,128)(2,1)}, bf16[2,160,896]{2,1,0:T(8,128)(2,1)}, u32[]{:S(2)}, u32[]{:S(2)}) %collective-permute-start.44) | collective-permute-done | bytes 573472 | tf_op jit(solution)/shard_map/ppermute | solution.py:36
  310.2 18.2 %collective-permute-done.38 = bf16[1,8,160,224]{3,2,1,0:T(8,128)(2,1)} collective-permute-done((bf16[1,8,160,224]{3,2,1,0:T(8,128)(2,1)}, bf16[1,8,160,224]{3,2,1,0:T(8,128)(2,1)}, u32[]{:S(2)}, u32[]{:S(2)}) %collective-permute-start.38) | collective-permute-done | bytes 573472 | tf_op jit(solution)/shard_map/ppermute | solution.py:36
  334.9 8.7 %collective-permute-done.42 = bf16[4,272,224]{2,1,0:T(8,128)(2,1)S(1)} collective-permute-done((bf16[4,272,224]{2,1,0:T(8,128)(2,1)S(1)}, bf16[4,272,224]{2,1,0:T(8,128)(2,1)S(1)}, u32[]{:S(2)}, u32[]{:S(2)}) %collective-permute-start.42) | collective-permute-done | bytes 487456 | tf_op jit(solution)/shard_map/ppermute | solution.py:36
  (331 shorter events, 139.9 us)
Async XLA Ops:
  31.3 41.1 %collective-permute-start.13 = (bf16[480,896]{1,0:T(8,128)(2,1)S(1)}, bf16[480,896]{1,0:T(8,128)(2,1)}, u32[]{:S(2)}, u32[]{:S(2)}) collective-permute-start(bf16[480,896]{1,0:T(8,128)(2,1)S(1)} %join_lanes.1.refs_0_), channel_id=1, source_target_pairs={{0,4},{1,5},{2,6},{3,7},{4,0},{5,1},{6,2},{7,3},{8,12},{9,13},{10,... | collective-permute-start | bytes 2580488 | tf_op jit(solution)/shard_map/ppermute | solution.py:36
  33.0 39.5 %collective-permute-start.14 = (bf16[480,896]{1,0:T(8,128)(2,1)S(1)}, bf16[480,896]{1,0:T(8,128)(2,1)}, u32[]{:S(2)}, u32[]{:S(2)}) collective-permute-start(bf16[480,896]{1,0:T(8,128)(2,1)S(1)} %join_lanes.1.refs_0_), channel_id=1, source_target_pairs={{0,2},{1,3},{2,0},{3,1},{4,6},{5,7},{6,4},{7,5},{8,10},{9,11},{10,... | collective-permute-start | bytes 2580488 | tf_op jit(solution)/shard_map/ppermute | solution.py:36
  39.3 33.2 %collective-permute-start.15 = (bf16[480,896]{1,0:T(8,128)(2,1)S(1)}, bf16[480,896]{1,0:T(8,128)(2,1)}, u32[]{:S(2)}, u32[]{:S(2)}) collective-permute-start(bf16[480,896]{1,0:T(8,128)(2,1)S(1)} %join_lanes.1.refs_0_), channel_id=1, source_target_pairs={{0,1},{1,0},{2,3},{3,2},{4,5},{5,4},{6,7},{7,6},{8,9},{9,8},{10,11... | collective-permute-start | bytes 2580488 | tf_op jit(solution)/shard_map/ppermute | solution.py:36
  60.8 28.4 %collective-permute-start.19 = (bf16[8,112,224]{2,1,0:T(8,128)(2,1)S(1)}, bf16[8,112,224]{2,1,0:T(8,128)(2,1)S(1)}, u32[]{:S(2)}, u32[]{:S(2)}) collective-permute-start(bf16[8,112,224]{2,1,0:T(8,128)(2,1)S(1)} %pad_maximum_fusion.4.refs_0_), channel_id=1, source_target_pairs={{0,16},{8,24},{16,0},{24,8},{1,17},{9,25},{17,1},{25,9},{2,18},{10... | collective-permute-start | bytes 1204232 | tf_op jit(solution)/shard_map/ppermute | solution.py:36
  87.5 22.3 %collective-permute-start.17 = (bf16[480,896]{1,0:T(8,128)(2,1)}, bf16[480,896]{1,0:T(8,128)(2,1)}, u32[]{:S(2)}, u32[]{:S(2)}) collective-permute-start(bf16[480,896]{1,0:T(8,128)(2,1)} %collective-permute-done.14.refs_2_), channel_id=1, source_target_pairs={{0,1},{1,0},{2,3},{3,2},{4,5},{5,4},{6,7},{7,6},{8,9},{9,8},{10,11... | collective-permute-start | bytes 2580488 | tf_op jit(solution)/shard_map/ppermute | solution.py:36
  88.1 20.5 %collective-permute-start.16 = (bf16[384,896]{1,0:T(8,128)(2,1)}, bf16[384,896]{1,0:T(8,128)(2,1)S(1)}, u32[]{:S(2)}, u32[]{:S(2)}) collective-permute-start(bf16[384,896]{1,0:T(8,128)(2,1)} %cot_ref.1), channel_id=1, source_target_pairs={{0,16},{8,24},{16,0},{24,8},{1,17},{9,25},{17,1},{25,9},{2,18},{10... | collective-permute-start | bytes 2064392 | tf_op jit(solution)/shard_map/ppermute | solution.py:36
  89.2 16.5 %collective-permute-start.20 = (bf16[8,112,224]{2,1,0:T(8,128)(2,1)S(1)}, bf16[8,112,224]{2,1,0:T(8,128)(2,1)}, u32[]{:S(2)}, u32[]{:S(2)}) collective-permute-start(bf16[8,112,224]{2,1,0:T(8,128)(2,1)S(1)} %collective-permute-done.19.refs_2_), channel_id=1, source_target_pairs={{0,8},{8,0},{16,24},{24,16},{1,9},{9,1},{17,25},{25,17},{2,10},{10... | collective-permute-start | bytes 1204232 | tf_op jit(solution)/shard_map/ppermute | solution.py:36
  103.5 24.1 %collective-permute-start.21 = (bf16[480,896]{1,0:T(8,128)(2,1)}, bf16[480,896]{1,0:T(8,128)(2,1)S(1)}, u32[]{:S(2)}, u32[]{:S(2)}) collective-permute-start(bf16[480,896]{1,0:T(8,128)(2,1)} %collective-permute-done.13.refs_4_), channel_id=1, source_target_pairs={{0,1},{1,0},{2,3},{3,2},{4,5},{5,4},{6,7},{7,6},{8,9},{9,8},{10,11... | collective-permute-start | bytes 2580488 | tf_op jit(solution)/shard_map/ppermute | solution.py:36
  105.0 21.1 %collective-permute-start.22 = (bf16[480,896]{1,0:T(8,128)(2,1)}, bf16[480,896]{1,0:T(8,128)(2,1)S(1)}, u32[]{:S(2)}, u32[]{:S(2)}) collective-permute-start(bf16[480,896]{1,0:T(8,128)(2,1)} %collective-permute-done.13.refs_4_), channel_id=1, source_target_pairs={{0,2},{1,3},{2,0},{3,1},{4,6},{5,7},{6,4},{7,5},{8,10},{9,11},{10,... | collective-permute-start | bytes 2580488 | tf_op jit(solution)/shard_map/ppermute | solution.py:36
  121.2 16.4 %collective-permute-start.25 = (bf16[384,896]{1,0:T(8,128)(2,1)S(1)}, bf16[384,896]{1,0:T(8,128)(2,1)S(1)}, u32[]{:S(2)}, u32[]{:S(2)}) collective-permute-start(bf16[384,896]{1,0:T(8,128)(2,1)S(1)} %multiply_convert_fusion.refs_8_), channel_id=1, source_target_pairs={{0,16},{8,24},{16,0},{24,8},{1,17},{9,25},{17,1},{25,9},{2,18},{10... | collective-permute-start | bytes 2064392 | tf_op jit(solution)/shard_map/ppermute | solution.py:36
  126.1 19.9 %collective-permute-start.23 = (bf16[480,896]{1,0:T(8,128)(2,1)S(1)}, bf16[480,896]{1,0:T(8,128)(2,1)S(1)}, u32[]{:S(2)}, u32[]{:S(2)}) collective-permute-start(bf16[480,896]{1,0:T(8,128)(2,1)S(1)} %collective-permute-done.22.refs_6_), channel_id=1, source_target_pairs={{0,1},{1,0},{2,3},{3,2},{4,5},{5,4},{6,7},{7,6},{8,9},{9,8},{10,11... | collective-permute-start | bytes 2580488 | tf_op jit(solution)/shard_map/ppermute | solution.py:36
  186.8 21.3 %collective-permute-start.30 = (bf16[1,384,896]{2,1,0:T(8,128)(2,1)S(1)}, bf16[1,384,896]{2,1,0:T(8,128)(2,1)S(1)}, u32[]{:S(2)}, u32[]{:S(2)}) collective-permute-start(bf16[1,384,896]{2,1,0:T(8,128)(2,1)S(1)} %dynamic-slice_convert_fusion.1), channel_id=1, source_target_pairs={{0,16},{8,24},{16,0},{24,8},{1,17},{9,25},{17,1},{25,9},{2,18},{10... | collective-permute-start | bytes 2064392 | tf_op jit(solution)/shard_map/ppermute | solution.py:36
  203.3 28.9 %collective-permute-start.31 = (bf16[4,160,896]{2,1,0:T(8,128)(2,1)}, bf16[4,160,896]{2,1,0:T(8,128)(2,1)S(1)}, u32[]{:S(2)}, u32[]{:S(2)}) collective-permute-start(bf16[4,160,896]{2,1,0:T(8,128)(2,1)} %dynamic-slice_bitcast_fusion.3), channel_id=1, source_target_pairs={{0,1},{1,0},{2,3},{3,2},{4,5},{5,4},{6,7},{7,6},{8,9},{9,8},{10,11... | collective-permute-start | bytes 3440648 | tf_op jit(solution)/shard_map/ppermute | solution.py:36
  208.2 48.2 %collective-permute-start.34 = (bf16[4,160,896]{2,1,0:T(8,128)(2,1)}, bf16[4,160,896]{2,1,0:T(8,128)(2,1)}, u32[]{:S(2)}, u32[]{:S(2)}) collective-permute-start(bf16[4,160,896]{2,1,0:T(8,128)(2,1)} %dynamic-slice_bitcast_fusion.2), channel_id=1, source_target_pairs={{0,1},{1,0},{2,3},{3,2},{4,5},{5,4},{6,7},{7,6},{8,9},{9,8},{10,11... | collective-permute-start | bytes 3440648 | tf_op jit(solution)/shard_map/ppermute | solution.py:36
  234.7 38.3 %collective-permute-start.50 = (bf16[2,160,896]{2,1,0:T(8,128)(2,1)}, bf16[2,160,896]{2,1,0:T(8,128)(2,1)}, u32[]{:S(2)}, u32[]{:S(2)}) collective-permute-start(bf16[2,160,896]{2,1,0:T(8,128)(2,1)} %fusion.8), channel_id=1, source_target_pairs={{0,2},{1,3},{2,0},{3,1},{4,6},{5,7},{6,4},{7,5},{8,10},{9,11},{10,... | collective-permute-start | bytes 1720328 | tf_op jit(solution)/shard_map/ppermute | solution.py:36
  251.5 28.6 %collective-permute-start.43 = (bf16[4,160,896]{2,1,0:T(8,128)(2,1)}, bf16[4,160,896]{2,1,0:T(8,128)(2,1)}, u32[]{:S(2)}, u32[]{:S(2)}) collective-permute-start(bf16[4,160,896]{2,1,0:T(8,128)(2,1)} %dynamic-slice_bitcast_fusion.1), channel_id=1, source_target_pairs={{0,1},{1,0},{2,3},{3,2},{4,5},{5,4},{6,7},{7,6},{8,9},{9,8},{10,11... | collective-permute-start | bytes 3440648 | tf_op jit(solution)/shard_map/ppermute | solution.py:36
  260.0 23.6 %collective-permute-start.41 = (bf16[2,160,896]{2,1,0:T(8,128)(2,1)}, bf16[2,160,896]{2,1,0:T(8,128)(2,1)}, u32[]{:S(2)}, u32[]{:S(2)}) collective-permute-start(bf16[2,160,896]{2,1,0:T(8,128)(2,1)} %fusion.9), channel_id=1, source_target_pairs={{0,2},{1,3},{2,0},{3,1},{4,6},{5,7},{6,4},{7,5},{8,10},{9,11},{10,... | collective-permute-start | bytes 1720328 | tf_op jit(solution)/shard_map/ppermute | solution.py:36
  282.8 25.7 %collective-permute-start.44 = (bf16[2,160,896]{2,1,0:T(8,128)(2,1)}, bf16[2,160,896]{2,1,0:T(8,128)(2,1)}, u32[]{:S(2)}, u32[]{:S(2)}) collective-permute-start(bf16[2,160,896]{2,1,0:T(8,128)(2,1)} %fusion.10), channel_id=1, source_target_pairs={{0,2},{1,3},{2,0},{3,1},{4,6},{5,7},{6,4},{7,5},{8,10},{9,11},{10,... | collective-permute-start | bytes 1720328 | tf_op jit(solution)/shard_map/ppermute | solution.py:36
  285.6 44.9 %collective-permute-start.48 = (bf16[1,160,896]{2,1,0:T(8,128)(2,1)}, bf16[1,160,896]{2,1,0:T(8,128)(2,1)}, u32[]{:S(2)}, u32[]{:S(2)}) collective-permute-start(bf16[1,160,896]{2,1,0:T(8,128)(2,1)} %dynamic-slice_convert_fusion.7), channel_id=1, source_target_pairs={{0,4},{1,5},{2,6},{3,7},{4,0},{5,1},{6,2},{7,3},{8,12},{9,13},{10,... | collective-permute-start | bytes 860168 | tf_op jit(solution)/shard_map/ppermute | solution.py:36
  290.4 53.8 %collective-permute-start.36 = (bf16[1,384,896]{2,1,0:T(8,128)(2,1)}, bf16[1,384,896]{2,1,0:T(8,128)(2,1)}, u32[]{:S(2)}, u32[]{:S(2)}) collective-permute-start(bf16[1,384,896]{2,1,0:T(8,128)(2,1)} %dynamic-slice_convert_fusion), channel_id=1, source_target_pairs={{0,16},{8,24},{16,0},{24,8},{1,17},{9,25},{17,1},{25,9},{2,18},{10... | collective-permute-start | bytes 2064392 | tf_op jit(solution)/shard_map/ppermute | solution.py:36
  293.0 35.3 %collective-permute-start.38 = (bf16[1,8,160,224]{3,2,1,0:T(8,128)(2,1)}, bf16[1,8,160,224]{3,2,1,0:T(8,128)(2,1)}, u32[]{:S(2)}, u32[]{:S(2)}) collective-permute-start(bf16[1,8,160,224]{3,2,1,0:T(8,128)(2,1)} %dynamic-slice_convert_fusion.2), channel_id=1, source_target_pairs={{0,16},{8,24},{16,0},{24,8},{1,17},{9,25},{17,1},{25,9},{2,18},{10... | collective-permute-start | bytes 1720328 | tf_op jit(solution)/shard_map/ppermute | solution.py:36
  310.1 21.8 %collective-permute-start.49 = (bf16[1,160,896]{2,1,0:T(8,128)(2,1)S(1)}, bf16[1,160,896]{2,1,0:T(8,128)(2,1)S(1)}, u32[]{:S(2)}, u32[]{:S(2)}) collective-permute-start(bf16[1,160,896]{2,1,0:T(8,128)(2,1)S(1)} %dynamic-slice_convert_fusion.6), channel_id=1, source_target_pairs={{0,4},{1,5},{2,6},{3,7},{4,0},{5,1},{6,2},{7,3},{8,12},{9,13},{10,... | collective-permute-start | bytes 860168 | tf_op jit(solution)/shard_map/ppermute | solution.py:36
  333.0 17.4 %collective-permute-start.53 = (bf16[480,224]{1,0:T(8,128)(2,1)S(1)}, bf16[480,224]{1,0:T(8,128)(2,1)S(1)}, u32[]{:S(2)}, u32[]{:S(2)}) collective-permute-start(bf16[480,224]{1,0:T(8,128)(2,1)S(1)} %get-tuple-element.148), channel_id=1, source_target_pairs={{0,16},{8,24},{16,0},{24,8},{1,17},{9,25},{17,1},{25,9},{2,18},{10... | collective-permute-start | bytes 645128 | tf_op jit(solution)/shard_map/ppermute | solution.py:36
  334.0 16.4 %collective-permute-start.54 = (bf16[480,224]{1,0:T(8,128)(2,1)S(1)}, bf16[480,224]{1,0:T(8,128)(2,1)S(1)}, u32[]{:S(2)}, u32[]{:S(2)}) collective-permute-start(bf16[480,224]{1,0:T(8,128)(2,1)S(1)} %get-tuple-element.149), channel_id=1, source_target_pairs={{0,24},{8,16},{16,8},{24,0},{1,25},{9,17},{17,9},{25,1},{2,26},{10... | collective-permute-start | bytes 645128 | tf_op jit(solution)/shard_map/ppermute | solution.py:36
  (91 other events, 872.4 us)

commit v10 on v9

--- a/solution.py
+++ b/solution.py
@@ -801,6 +801,9 @@
         normed_sum = add(kept, got)
         bit *= 2
     normed_kept, normed_got = kept[0], got[0]
+    layer_sum = add(kept_layer, swap(after(given_layer, given), "seq", seq_size, 1))
+    kept_layer, given_layer = halve(layer_sum, 1, my_seq // 2)
+    got_layer = swap(after(given_layer, normed_got), "seq", seq_size, 2)
     hidden = after(hidden, given)
     down_term = dot(hidden, cot_all, 0, 0).astype(BF16).reshape(fsdp_size, tall, -1)
     grad_gate, grad_up = after(grad_gate, down_term), after(grad_up, down_term)
@@ -832,7 +835,7 @@
     grad_residual, grad_branch, grad_attn, norm_two_term = residual_back(
         me, normed_kept, normed_got, residual, scale_two, gain_two, cotangent, out_full
     )
-    grad_attn = after(grad_attn, gate_term, up_term)
+    grad_attn = after(grad_attn, gate_term, up_term, given_layer)
     dq_one, kv_terms = attend_back(
         low, high, place, queries, grad_attn, attn_one, lse_one, kv_all, 0, split, ()
     )
@@ -848,25 +851,23 @@
     got_two = after(got_two, dq_two)
     kept_two, given = give(add(kept_two, got_two), 1)
     next_two = send(given, 1)
-    kept, given = halve(by_seq(kv_terms), 1, my_seq)
+    kept, given = halve(after(by_seq(kv_terms), got_layer), 1, my_seq)
     kv_sum = add(kept, swap(given, "seq", seq_size, 1))
     bit = 2
     while bit < seq_size:
         kv_kept, given = halve(kv_sum, 1, my_seq // bit)
-        kv_got = swap(after(given, got_two), "seq", seq_size, bit)
+        given_kv = given
+        kv_got = swap(given_kv, "seq", seq_size, bit)
         kv_sum = add(kv_kept, kv_got)
         bit *= 2
     kv_mine = kv_got
 
-    attn_late = after(attn_flat, dq_two)
+    attn_late = after(attn_flat, given_kv)
     out_term = stack_from_lanes(dot(attn_late, grad_branch, 0, 0).astype(BF16), seq_size)
     kept, given = halve(out_term, 1, my_seq)
     out_sum = add(kept, swap(given, "seq", seq_size, 1))
-    layer_got = swap(after(given_layer, dq_two), "seq", seq_size, 1)
-    layer_sum = add(kept_layer, layer_got)
-    kept_layer, given_layer = halve(layer_sum, 1, my_seq // 2)
     grad_tokens, kept, given = joined_back(
-        me, dq_one, dq_two, kv_kept[0], after(kv_got[0], layer_got), cosine, sine, qkv_t, tokens, scale_one,
+        me, dq_one, dq_two, kv_kept[0], kv_got[0], cosine, sine, qkv_t, tokens, scale_one,
         gain_one, grad_residual, normed_one, norm_two_term, seq_size, fsdp_size,
     )
 
@@ -879,7 +880,7 @@
     bit = 2
     while bit < seq_size:
         kept_out, given_out = halve(out_sum, 1, my_seq // bit)
-        out_sum = add(kept_out, swap(after(given_out, grad_tokens), "seq", seq_size, bit))
+        out_sum = add(kept_out, swap(after(given_out, kv_got), "seq", seq_size, bit))
         bit *= 2
     out_mine = out_sum[0].reshape(fsdp_size, -1, width)
     tail_sum = add(kept, swap(given, "seq", seq_size, 1))
@@ -889,7 +890,6 @@
         tail_sum = add(kept, swap(given, "seq", seq_size, bit))
         bit *= 2
     tail_mine = tail_sum[0]
-    got_layer = swap(after(given_layer, kv_mine), "seq", seq_size, 2)
     layer_sum = add(kept_layer, got_layer)
     bit = 4
     while bit < seq_size:

time: 367 us -> 359 us (0.978)
  waiting for transfers between devices: 104 us -> 97.8 us
    ppermute x55, waiting for transfers between devices: 104 us -> 97.8 us  [swap(): return lax.ppermute(block, axis, [(i, i ^ bits) for i in range(size)])]
    unnamed x123 -> x129, local copies, waits for them, and re-layouts: 9.08 us -> 10.5 us
  transfers between devices with their start and end apart: 55 -> 55, of which waited for: 22 -> 23; matrix products, arithmetic and copies ran while one was open for 18% -> 18% of each run, Pallas kernels for 22% -> 22%
where the time goes in v10:
time: 359 us; the launch traced here: 353 us
  Pallas kernels  114 us (32%)
  waiting for transfers between devices  97.8 us (27%)
  starting transfers between devices  49.7 us (14%)
  local copies, waits for them, and re-layouts  40.1 us (11%)
  other arithmetic  21.7 us (6%)
  matrix products  18.7 us (5%)
  blocking collectives  8.18 us (2%)
    ppermute x55, waiting for transfers between devices, swap(): return lax.ppermute(block, axis, [(i, i ^ bits) for i in range(size)])  97.8 us
    ppermute x55, starting transfers between devices, swap(): return lax.ppermute(block, axis, [(i, i ^ bits) for i in range(size)])  49.7 us
    pallas_call x1, Pallas kernels, feed_forward(): pl.pallas_call(body, grid=(size // 2,), in_specs=[pl.BlockSpec(memory_spa...  34.4 us
    pallas_call x2, Pallas kernels, attend_back(): pl.pallas_call(functools.partial(attend_back_kernel, begin), grid=(pairs,...  32.4 us
    pallas_call x8, Pallas kernels, on_device(): pl.pallas_call(body, in_specs=[pl.BlockSpec(memory_space=pltpu.SMEM)] + [...  23.8 us
    pallas_call x2, Pallas kernels, attend(): pl.pallas_call(functools.partial(attend_kernel, begin), grid=(pairs,), in...  23.4 us
    dot_general x6, matrix products, dot(): lax.dot_general(left, right, (((left_dim,), (right_dim,)), ((), ())), pre...  18.7 us
    add x13, other arithmetic, add(): return kept.astype(F32) + got.astype(F32)  11.6 us
  transfers between devices with their start and end apart: 55, of which 23 were waited for; matrix products, arithmetic and copies ran while one was open for 18% of the time, Pallas kernels for 22%

profile of v10, /device:TPU:0, one launch (start us, length us, event | category | flops | bytes accessed | tf_op | source)
XLA Modules:
  0.0 352.6 jit_solution(12654572556922449831)
XLA Ops:
  15.4 8.0 %collective-permute-done.1 = bf16[272,224]{1,0:T(8,128)(2,1)S(1)} collective-permute-done((bf16[272,224]{1,0:T(8,128)(2,1)S(1)}, bf16[272,224]{1,0:T(8,128)(2,1)S(1)}, u32[]{:S(2)}, u32[]{:S(2)}) %collective-permute-start.1) | collective-permute-done | bytes 121888 | tf_op jit(solution)/shard_map/ppermute | solution.py:36
  35.5 3.8 %collective-permute-done.9.refs_4_ = bf16[4,160,224]{2,1,0:T(8,128)(2,1)S(1)} collective-permute-done((bf16[4,160,224]{2,1,0:T(8,128)(2,1)S(1)}, bf16[4,160,224]{2,1,0:T(8,128)(2,1)S(1)}, u32[]{:S(2)}, u32[]{:S(2)}) %collective-permute-start.9) | collective-permute-done | bytes 286752 | tf_op jit(solution)/shard_map/ppermute | solution.py:36
  46.1 6.6 %collective-permute-done.10.refs_5_ = bf16[4,160,224]{2,1,0:T(8,128)(2,1)} collective-permute-done((bf16[4,160,224]{2,1,0:T(8,128)(2,1)S(1)}, bf16[4,160,224]{2,1,0:T(8,128)(2,1)}, u32[]{:S(2)}, u32[]{:S(2)}) %collective-permute-start.10) | collective-permute-done | bytes 286752 | tf_op jit(solution)/shard_map/ppermute | solution.py:36
  65.9 6.5 %collective-permute-done.13.refs_4_ = bf16[480,896]{1,0:T(8,128)(2,1)} collective-permute-done((bf16[480,896]{1,0:T(8,128)(2,1)S(1)}, bf16[480,896]{1,0:T(8,128)(2,1)}, u32[]{:S(2)}, u32[]{:S(2)}) %collective-permute-start.13) | collective-permute-done | bytes 860192 | tf_op jit(solution)/shard_map/ppermute | solution.py:36
  79.4 8.2 %all_gather.3.kv_ref = bf16[1536,256]{1,0:T(8,128)(2,1)S(1)} all-gather(bf16[384,256]{1,0:T(8,128)(2,1)S(1)} %pad_maximum_fusion.5), channel_id=1, replica_groups=mesh['seq'=4,'fsdp'=8] {'seq'}, dimensions={0}, use_global_device_ids=true | all-gather | bytes 983040 | tf_op jit(solution)/shard_map/all_gather | solution.py:746
  90.0 13.4 %attend.2 = (bf16[384,512]{1,0:T(8,128)(2,1)S(1)}, f32[4,1,768]{2,1,0:T(1,128)S(1)}) custom-call(s32[1,384]{1,0:T(1,128)S(1)} %broadcast_in_dim.10.low_ref, s32[1,384]{1,0:T(1,128)S(1)} %iota_add_fusion.high_ref, s32[1536,1]{1,0:T(8,128)S(1)} %iota.33.place_ref, bf16[384,896]{1,0:T(8,128)(2,1)S(1)} %slice_multiply_fusion.1.q_ref, ...), custom_call_target="tpu_custom_call" | custom-call | flops 1 | bytes 1 | tf_op jit(solution)/shard_map/attend/pallas_call | solution.py:507
  109.9 10.0 %attend.3 = (bf16[384,384]{1,0:T(8,128)(2,1)S(1)}, f32[3,1,768]{2,1,0:T(1,128)S(1)}) custom-call(s32[1,384]{1,0:T(1,128)S(1)} %broadcast_in_dim.10.low_ref, s32[1,384]{1,0:T(1,128)S(1)} %iota_add_fusion.high_ref, s32[1536,1]{1,0:T(8,128)S(1)} %iota.39.place_ref, bf16[384,896]{1,0:T(8,128)(2,1)S(1)} %slice_multiply_fusion.1.q_ref, ...), custom_call_target="tpu_custom_call" | custom-call | flops 1 | bytes 1 | tf_op jit(solution)/shard_map/attend/pallas_call | solution.py:507
  122.5 3.6 %collective-permute-done.22.refs_6_ = bf16[480,896]{1,0:T(8,128)(2,1)S(1)} collective-permute-done((bf16[480,896]{1,0:T(8,128)(2,1)}, bf16[480,896]{1,0:T(8,128)(2,1)S(1)}, u32[]{:S(2)}, u32[]{:S(2)}) %collective-permute-start.22) | collective-permute-done | bytes 860192 | tf_op jit(solution)/shard_map/ppermute | solution.py:36
  127.6 10.1 %collective-permute-done.25.refs_10_ = bf16[384,896]{1,0:T(8,128)(2,1)S(1)} collective-permute-done((bf16[384,896]{1,0:T(8,128)(2,1)S(1)}, bf16[384,896]{1,0:T(8,128)(2,1)S(1)}, u32[]{:S(2)}, u32[]{:S(2)}) %collective-permute-start.25) | collective-permute-done | bytes 688160 | tf_op jit(solution)/shard_map/ppermute | solution.py:36
  137.7 8.4 %collective-permute-done.23.refs_7_ = bf16[480,896]{1,0:T(8,128)(2,1)S(1)} collective-permute-done((bf16[480,896]{1,0:T(8,128)(2,1)S(1)}, bf16[480,896]{1,0:T(8,128)(2,1)S(1)}, u32[]{:S(2)}, u32[]{:S(2)}) %collective-permute-start.23) | collective-permute-done | bytes 860192 | tf_op jit(solution)/shard_map/ppermute | solution.py:36
  147.0 34.4 %feed_forward.1 = (bf16[1536,1280]{1,0:T(8,128)(2,1)}, bf16[1536,1280]{1,0:T(8,128)(2,1)}, bf16[1536,1280]{1,0:T(8,128)(2,1)}, bf16[2,384,896]{2,1,0:T(8,128)(2,...) custom-call(s32[2]{0:T(128)S(1)} %pad_add_fusion.me_ref, ...), custom_call_target="tpu_custom_call" | custom-call | flops 1 | bytes 1 | tf_op jit(solution)/shard_map/feed_forward/pallas_call | solution.py:338
  188.4 4.5 %convolution_convert_fusion.2 = bf16[1280,896]{1,0:T(8,128)(2,1)S(1)} fusion(bf16[1536,1280]{1,0:T(8,128)(2,1)S(1)} %copy-done.58, bf16[1536,896]{1,0:T(8,128)(2,1)S(1)} %bitcast.194), kind=kOutput, calls=%fused_computation.2 | convolution fusion | flops 3524362240 | bytes 8978432 | tf_op jit(solution)/shard_map/dot_general | solution.py:30
  193.1 4.7 %convolution_convert_fusion = bf16[1280,896]{1,0:T(8,128)(2,1)S(1)} fusion(bf16[1536,1280]{1,0:T(8,128)(2,1)S(1)} %copy-done.57, bf16[1536,896]{1,0:T(8,128)(2,1)S(1)} %bitcast.192), kind=kOutput, calls=%fused_computation | convolution fusion | flops 3524362240 | bytes 8978432 | tf_op jit(solution)/shard_map/dot_general | solution.py:30
  197.8 4.5 %convolution_convert_fusion.1 = bf16[1280,896]{1,0:T(8,128)(2,1)S(1)} fusion(bf16[1536,1280]{1,0:T(8,128)(2,1)S(1)} %copy-done.56, bf16[1536,896]{1,0:T(8,128)(2,1)S(1)} %bitcast.193), kind=kOutput, calls=%fused_computation.1 | convolution fusion | flops 3524362240 | bytes 8978432 | tf_op jit(solution)/shard_map/dot_general | solution.py:30
  211.3 4.7 %residual_back.1 = (f32[384,896]{1,0:T(8,128)}, bf16[384,896]{1,0:T(8,128)(2,1)S(1)}, bf16[384,896]{1,0:T(8,128)(2,1)S(1)}, f32[1,896]{1,0:T(1,128)S(1)}) custom-call(s32[2]{0:T(128)S(1)} %pad_add_fusion.me_ref, f32[384,896]{1,0:T(8,128)} %dynamic-slice_bitcast_fusion.kept_ref, bf16[384,896]{1,0:T(8,128)(2,1)S(1)} %bitcast.160, f32[384,896]{1,0:T(8,128)} %copy-done.25, ...), custom_call_target="tpu_custom_call" | custom-call | tf_op jit(solution)/shard_map/residual_back/pallas_call | solution.py:125
  216.0 18.1 %attend_back.2 = (f32[384,512]{1,0:T(8,128)S(1)}, f32[1536,256]{1,0:T(8,128)}) custom-call(s32[1,384]{1,0:T(1,128)S(1)} %broadcast_in_dim.10.low_ref, s32[1,384]{1,0:T(1,128)S(1)} %iota_add_fusion.high_ref, s32[1536,1]{1,0:T(8,128)S(1)} %iota.40.place_ref, bf16[384,896]{1,0:T(8,128)(2,1)S(1)} %slice_multiply_fusion.1.q_ref, ...), custom_call_target="tpu_custom_call" | custom-call | flops 1 | bytes 1 | tf_op jit(solution)/shard_map/attend_back/pallas_call | solution.py:533
  238.6 14.3 %attend_back.3 = (f32[384,384]{1,0:T(8,128)S(1)}, f32[1536,256]{1,0:T(8,128)}) custom-call(s32[1,384]{1,0:T(1,128)S(1)} %broadcast_in_dim.10.low_ref, s32[1,384]{1,0:T(1,128)S(1)} %iota_add_fusion.high_ref, s32[1536,1]{1,0:T(8,128)S(1)} %iota.41.place_ref, bf16[384,896]{1,0:T(8,128)(2,1)S(1)} %slice_multiply_fusion.1.q_ref, ...), custom_call_target="tpu_custom_call" | custom-call | flops 1 | bytes 1 | tf_op jit(solution)/shard_map/attend_back/pallas_call | solution.py:533
  264.4 3.8 %collective-permute-done.35 = bf16[1,384,256]{2,1,0:T(8,128)(2,1)S(1)} collective-permute-done((bf16[1,384,256]{2,1,0:T(8,128)(2,1)S(1)}, bf16[1,384,256]{2,1,0:T(8,128)(2,1)S(1)}, u32[]{:S(2)}, u32[]{:S(2)}) %collective-permute-start.35) | collective-permute-done | bytes 196640 | tf_op jit(solution)/shard_map/ppermute | solution.py:36
  268.2 9.2 %joined_back.1 = (f32[384,896]{1,0:T(8,128)}, bf16[2,8,160,224]{3,2,1,0:T(8,128)(2,1)}, bf16[2,8,160,224]{3,2,1,0:T(8,128)(2,1)}) custom-call(s32[2]{0:T(128)S(1)} %pad_add_fusion.me_ref, f32[384,512]{1,0:T(8,128)S(1)} %get-tuple-element.120.dq1_ref, f32[384,384]{1,0:T(8,128)S(1)} %get-tuple-element.125.dq2_ref, ...), custom_call_target="tpu_custom_call" | custom-call | tf_op jit(solution)/shard_map/joined_back/pallas_call | solution.py:125
  286.9 7.9 %collective-permute-done.51 = bf16[1,160,896]{2,1,0:T(8,128)(2,1)S(1)} collective-permute-done((bf16[1,160,896]{2,1,0:T(8,128)(2,1)S(1)}, bf16[1,160,896]{2,1,0:T(8,128)(2,1)S(1)}, u32[]{:S(2)}, u32[]{:S(2)}) %collective-permute-start.51) | collective-permute-done | bytes 286752 | tf_op jit(solution)/shard_map/ppermute | solution.py:36
  299.7 10.5 %collective-permute-done.44 = bf16[2,160,896]{2,1,0:T(8,128)(2,1)S(1)} collective-permute-done((bf16[2,160,896]{2,1,0:T(8,128)(2,1)S(1)}, bf16[2,160,896]{2,1,0:T(8,128)(2,1)S(1)}, u32[]{:S(2)}, u32[]{:S(2)}) %collective-permute-start.44) | collective-permute-done | bytes 573472 | tf_op jit(solution)/shard_map/ppermute | solution.py:36
  316.3 4.9 %collective-permute-done.37 = bf16[1,8,160,224]{3,2,1,0:T(8,128)(2,1)} collective-permute-done((bf16[1,8,160,224]{3,2,1,0:T(8,128)(2,1)}, bf16[1,8,160,224]{3,2,1,0:T(8,128)(2,1)}, u32[]{:S(2)}, u32[]{:S(2)}) %collective-permute-start.37) | collective-permute-done | bytes 573472 | tf_op jit(solution)/shard_map/ppermute | solution.py:36
  323.8 4.2 %collective-permute-done.49 = bf16[1,160,896]{2,1,0:T(8,128)(2,1)} collective-permute-done((bf16[1,160,896]{2,1,0:T(8,128)(2,1)}, bf16[1,160,896]{2,1,0:T(8,128)(2,1)}, u32[]{:S(2)}, u32[]{:S(2)}) %collective-permute-start.49) | collective-permute-done | bytes 286752 | tf_op jit(solution)/shard_map/ppermute | solution.py:36
  332.0 3.9 %collective-permute-done.42 = bf16[4,272,224]{2,1,0:T(8,128)(2,1)S(1)} collective-permute-done((bf16[4,272,224]{2,1,0:T(8,128)(2,1)S(1)}, bf16[4,272,224]{2,1,0:T(8,128)(2,1)S(1)}, u32[]{:S(2)}, u32[]{:S(2)}) %collective-permute-start.42) | collective-permute-done | bytes 487456 | tf_op jit(solution)/shard_map/ppermute | solution.py:36
  (337 shorter events, 142.0 us)
Async XLA Ops:
  31.3 41.1 %collective-permute-start.13 = (bf16[480,896]{1,0:T(8,128)(2,1)S(1)}, bf16[480,896]{1,0:T(8,128)(2,1)}, u32[]{:S(2)}, u32[]{:S(2)}) collective-permute-start(bf16[480,896]{1,0:T(8,128)(2,1)S(1)} %join_lanes.1.refs_0_), channel_id=1, source_target_pairs={{0,4},{1,5},{2,6},{3,7},{4,0},{5,1},{6,2},{7,3},{8,12},{9,13},{10,... | collective-permute-start | bytes 2580488 | tf_op jit(solution)/shard_map/ppermute | solution.py:36
  33.0 39.5 %collective-permute-start.14 = (bf16[480,896]{1,0:T(8,128)(2,1)S(1)}, bf16[480,896]{1,0:T(8,128)(2,1)}, u32[]{:S(2)}, u32[]{:S(2)}) collective-permute-start(bf16[480,896]{1,0:T(8,128)(2,1)S(1)} %join_lanes.1.refs_0_), channel_id=1, source_target_pairs={{0,2},{1,3},{2,0},{3,1},{4,6},{5,7},{6,4},{7,5},{8,10},{9,11},{10,... | collective-permute-start | bytes 2580488 | tf_op jit(solution)/shard_map/ppermute | solution.py:36
  39.3 33.2 %collective-permute-start.15 = (bf16[480,896]{1,0:T(8,128)(2,1)S(1)}, bf16[480,896]{1,0:T(8,128)(2,1)}, u32[]{:S(2)}, u32[]{:S(2)}) collective-permute-start(bf16[480,896]{1,0:T(8,128)(2,1)S(1)} %join_lanes.1.refs_0_), channel_id=1, source_target_pairs={{0,1},{1,0},{2,3},{3,2},{4,5},{5,4},{6,7},{7,6},{8,9},{9,8},{10,11... | collective-permute-start | bytes 2580488 | tf_op jit(solution)/shard_map/ppermute | solution.py:36
  60.8 28.5 %collective-permute-start.19 = (bf16[8,112,224]{2,1,0:T(8,128)(2,1)S(1)}, bf16[8,112,224]{2,1,0:T(8,128)(2,1)S(1)}, u32[]{:S(2)}, u32[]{:S(2)}) collective-permute-start(bf16[8,112,224]{2,1,0:T(8,128)(2,1)S(1)} %pad_maximum_fusion.4.refs_0_), channel_id=1, source_target_pairs={{0,16},{8,24},{16,0},{24,8},{1,17},{9,25},{17,1},{25,9},{2,18},{10... | collective-permute-start | bytes 1204232 | tf_op jit(solution)/shard_map/ppermute | solution.py:36
  87.6 22.3 %collective-permute-start.17 = (bf16[480,896]{1,0:T(8,128)(2,1)}, bf16[480,896]{1,0:T(8,128)(2,1)}, u32[]{:S(2)}, u32[]{:S(2)}) collective-permute-start(bf16[480,896]{1,0:T(8,128)(2,1)} %collective-permute-done.14.refs_2_), channel_id=1, source_target_pairs={{0,1},{1,0},{2,3},{3,2},{4,5},{5,4},{6,7},{7,6},{8,9},{9,8},{10,11... | collective-permute-start | bytes 2580488 | tf_op jit(solution)/shard_map/ppermute | solution.py:36
  88.1 20.5 %collective-permute-start.16 = (bf16[384,896]{1,0:T(8,128)(2,1)}, bf16[384,896]{1,0:T(8,128)(2,1)S(1)}, u32[]{:S(2)}, u32[]{:S(2)}) collective-permute-start(bf16[384,896]{1,0:T(8,128)(2,1)} %cot_ref.1), channel_id=1, source_target_pairs={{0,16},{8,24},{16,0},{24,8},{1,17},{9,25},{17,1},{25,9},{2,18},{10... | collective-permute-start | bytes 2064392 | tf_op jit(solution)/shard_map/ppermute | solution.py:36
  89.3 16.5 %collective-permute-start.20 = (bf16[8,112,224]{2,1,0:T(8,128)(2,1)S(1)}, bf16[8,112,224]{2,1,0:T(8,128)(2,1)}, u32[]{:S(2)}, u32[]{:S(2)}) collective-permute-start(bf16[8,112,224]{2,1,0:T(8,128)(2,1)S(1)} %collective-permute-done.19.refs_2_), channel_id=1, source_target_pairs={{0,8},{8,0},{16,24},{24,16},{1,9},{9,1},{17,25},{25,17},{2,10},{10... | collective-permute-start | bytes 1204232 | tf_op jit(solution)/shard_map/ppermute | solution.py:36
  103.5 24.1 %collective-permute-start.21 = (bf16[480,896]{1,0:T(8,128)(2,1)}, bf16[480,896]{1,0:T(8,128)(2,1)S(1)}, u32[]{:S(2)}, u32[]{:S(2)}) collective-permute-start(bf16[480,896]{1,0:T(8,128)(2,1)} %collective-permute-done.13.refs_4_), channel_id=1, source_target_pairs={{0,1},{1,0},{2,3},{3,2},{4,5},{5,4},{6,7},{7,6},{8,9},{9,8},{10,11... | collective-permute-start | bytes 2580488 | tf_op jit(solution)/shard_map/ppermute | solution.py:36
  105.1 21.1 %collective-permute-start.22 = (bf16[480,896]{1,0:T(8,128)(2,1)}, bf16[480,896]{1,0:T(8,128)(2,1)S(1)}, u32[]{:S(2)}, u32[]{:S(2)}) collective-permute-start(bf16[480,896]{1,0:T(8,128)(2,1)} %collective-permute-done.13.refs_4_), channel_id=1, source_target_pairs={{0,2},{1,3},{2,0},{3,1},{4,6},{5,7},{6,4},{7,5},{8,10},{9,11},{10,... | collective-permute-start | bytes 2580488 | tf_op jit(solution)/shard_map/ppermute | solution.py:36
  121.3 16.4 %collective-permute-start.25 = (bf16[384,896]{1,0:T(8,128)(2,1)S(1)}, bf16[384,896]{1,0:T(8,128)(2,1)S(1)}, u32[]{:S(2)}, u32[]{:S(2)}) collective-permute-start(bf16[384,896]{1,0:T(8,128)(2,1)S(1)} %multiply_convert_fusion.refs_8_), channel_id=1, source_target_pairs={{0,16},{8,24},{16,0},{24,8},{1,17},{9,25},{17,1},{25,9},{2,18},{10... | collective-permute-start | bytes 2064392 | tf_op jit(solution)/shard_map/ppermute | solution.py:36
  126.2 19.9 %collective-permute-start.23 = (bf16[480,896]{1,0:T(8,128)(2,1)S(1)}, bf16[480,896]{1,0:T(8,128)(2,1)S(1)}, u32[]{:S(2)}, u32[]{:S(2)}) collective-permute-start(bf16[480,896]{1,0:T(8,128)(2,1)S(1)} %collective-permute-done.22.refs_6_), channel_id=1, source_target_pairs={{0,1},{1,0},{2,3},{3,2},{4,5},{5,4},{6,7},{7,6},{8,9},{9,8},{10,11... | collective-permute-start | bytes 2580488 | tf_op jit(solution)/shard_map/ppermute | solution.py:36
  186.8 19.2 %collective-permute-start.31 = (bf16[1,384,896]{2,1,0:T(8,128)(2,1)S(1)}, bf16[1,384,896]{2,1,0:T(8,128)(2,1)S(1)}, u32[]{:S(2)}, u32[]{:S(2)}) collective-permute-start(bf16[1,384,896]{2,1,0:T(8,128)(2,1)S(1)} %dynamic-slice_convert_fusion.1), channel_id=1, source_target_pairs={{0,16},{8,24},{16,0},{24,8},{1,17},{9,25},{17,1},{25,9},{2,18},{10... | collective-permute-start | bytes 2064392 | tf_op jit(solution)/shard_map/ppermute | solution.py:36
  203.5 30.6 %collective-permute-start.33 = (bf16[4,160,896]{2,1,0:T(8,128)(2,1)}, bf16[4,160,896]{2,1,0:T(8,128)(2,1)}, u32[]{:S(2)}, u32[]{:S(2)}) collective-permute-start(bf16[4,160,896]{2,1,0:T(8,128)(2,1)} %dynamic-slice_bitcast_fusion.3), channel_id=1, source_target_pairs={{0,1},{1,0},{2,3},{3,2},{4,5},{5,4},{6,7},{7,6},{8,9},{9,8},{10,11... | collective-permute-start | bytes 3440648 | tf_op jit(solution)/shard_map/ppermute | solution.py:36
  206.0 50.5 %collective-permute-start.40 = (bf16[4,160,896]{2,1,0:T(8,128)(2,1)}, bf16[4,160,896]{2,1,0:T(8,128)(2,1)}, u32[]{:S(2)}, u32[]{:S(2)}) collective-permute-start(bf16[4,160,896]{2,1,0:T(8,128)(2,1)} %dynamic-slice_bitcast_fusion.2), channel_id=1, source_target_pairs={{0,1},{1,0},{2,3},{3,2},{4,5},{5,4},{6,7},{7,6},{8,9},{9,8},{10,11... | collective-permute-start | bytes 3440648 | tf_op jit(solution)/shard_map/ppermute | solution.py:36
  208.9 47.6 %collective-permute-start.32 = (bf16[1,384,896]{2,1,0:T(8,128)(2,1)}, bf16[1,384,896]{2,1,0:T(8,128)(2,1)}, u32[]{:S(2)}, u32[]{:S(2)}) collective-permute-start(bf16[1,384,896]{2,1,0:T(8,128)(2,1)} %dynamic-slice_convert_fusion), channel_id=1, source_target_pairs={{0,16},{8,24},{16,0},{24,8},{1,17},{9,25},{17,1},{25,9},{2,18},{10... | collective-permute-start | bytes 2064392 | tf_op jit(solution)/shard_map/ppermute | solution.py:36
  236.9 40.6 %collective-permute-start.50 = (bf16[2,160,896]{2,1,0:T(8,128)(2,1)}, bf16[2,160,896]{2,1,0:T(8,128)(2,1)}, u32[]{:S(2)}, u32[]{:S(2)}) collective-permute-start(bf16[2,160,896]{2,1,0:T(8,128)(2,1)} %fusion.8), channel_id=1, source_target_pairs={{0,2},{1,3},{2,0},{3,1},{4,6},{5,7},{6,4},{7,5},{8,10},{9,11},{10,... | collective-permute-start | bytes 1720328 | tf_op jit(solution)/shard_map/ppermute | solution.py:36
  237.5 43.3 %collective-permute-start.43 = (bf16[4,160,896]{2,1,0:T(8,128)(2,1)S(1)}, bf16[4,160,896]{2,1,0:T(8,128)(2,1)}, u32[]{:S(2)}, u32[]{:S(2)}) collective-permute-start(bf16[4,160,896]{2,1,0:T(8,128)(2,1)S(1)} %dynamic-slice_bitcast_fusion.1), channel_id=1, source_target_pairs={{0,1},{1,0},{2,3},{3,2},{4,5},{5,4},{6,7},{7,6},{8,9},{9,8},{10,11... | collective-permute-start | bytes 3440648 | tf_op jit(solution)/shard_map/ppermute | solution.py:36
  259.6 24.6 %collective-permute-start.41 = (bf16[2,160,896]{2,1,0:T(8,128)(2,1)S(1)}, bf16[2,160,896]{2,1,0:T(8,128)(2,1)S(1)}, u32[]{:S(2)}, u32[]{:S(2)}) collective-permute-start(bf16[2,160,896]{2,1,0:T(8,128)(2,1)S(1)} %fusion.9), channel_id=1, source_target_pairs={{0,2},{1,3},{2,0},{3,1},{4,6},{5,7},{6,4},{7,5},{8,10},{9,11},{10,... | collective-permute-start | bytes 1720328 | tf_op jit(solution)/shard_map/ppermute | solution.py:36
  264.1 30.7 %collective-permute-start.38 = (bf16[2,896,224]{1,2,0:T(8,128)(2,1)}, bf16[2,896,224]{1,2,0:T(8,128)(2,1)}, u32[]{:S(2)}, u32[]{:S(2)}) collective-permute-start(bf16[2,896,224]{1,2,0:T(8,128)(2,1)} %dynamic-slice_bitcast_fusion.4), channel_id=1, source_target_pairs={{0,8},{8,0},{16,24},{24,16},{1,9},{9,1},{17,25},{25,17},{2,10},{10... | collective-permute-start | bytes 2408456 | tf_op jit(solution)/shard_map/ppermute | solution.py:36
  278.7 16.1 %collective-permute-start.51 = (bf16[1,160,896]{2,1,0:T(8,128)(2,1)S(1)}, bf16[1,160,896]{2,1,0:T(8,128)(2,1)S(1)}, u32[]{:S(2)}, u32[]{:S(2)}) collective-permute-start(bf16[1,160,896]{2,1,0:T(8,128)(2,1)S(1)} %dynamic-slice_convert_fusion.5), channel_id=1, source_target_pairs={{0,4},{1,5},{2,6},{3,7},{4,0},{5,1},{6,2},{7,3},{8,12},{9,13},{10,... | collective-permute-start | bytes 860168 | tf_op jit(solution)/shard_map/ppermute | solution.py:36
  282.8 27.4 %collective-permute-start.44 = (bf16[2,160,896]{2,1,0:T(8,128)(2,1)S(1)}, bf16[2,160,896]{2,1,0:T(8,128)(2,1)S(1)}, u32[]{:S(2)}, u32[]{:S(2)}) collective-permute-start(bf16[2,160,896]{2,1,0:T(8,128)(2,1)S(1)} %fusion.10), channel_id=1, source_target_pairs={{0,2},{1,3},{2,0},{3,1},{4,6},{5,7},{6,4},{7,5},{8,10},{9,11},{10,... | collective-permute-start | bytes 1720328 | tf_op jit(solution)/shard_map/ppermute | solution.py:36
  285.2 38.2 %collective-permute-start.48 = (bf16[1,160,896]{2,1,0:T(8,128)(2,1)}, bf16[1,160,896]{2,1,0:T(8,128)(2,1)S(1)}, u32[]{:S(2)}, u32[]{:S(2)}) collective-permute-start(bf16[1,160,896]{2,1,0:T(8,128)(2,1)} %dynamic-slice_convert_fusion.7), channel_id=1, source_target_pairs={{0,4},{1,5},{2,6},{3,7},{4,0},{5,1},{6,2},{7,3},{8,12},{9,13},{10,... | collective-permute-start | bytes 860168 | tf_op jit(solution)/shard_map/ppermute | solution.py:36
  296.4 16.6 %collective-permute-start.39 = (bf16[1,896,224]{1,2,0:T(8,128)(2,1)S(1)}, bf16[1,896,224]{1,2,0:T(8,128)(2,1)S(1)}, u32[]{:S(2)}, u32[]{:S(2)}) collective-permute-start(bf16[1,896,224]{1,2,0:T(8,128)(2,1)S(1)} %dynamic-slice_convert_fusion.4), channel_id=1, source_target_pairs={{0,16},{8,24},{16,0},{24,8},{1,17},{9,25},{17,1},{25,9},{2,18},{10... | collective-permute-start | bytes 1204232 | tf_op jit(solution)/shard_map/ppermute | solution.py:36
  298.6 22.6 %collective-permute-start.37 = (bf16[1,8,160,224]{3,2,1,0:T(8,128)(2,1)}, bf16[1,8,160,224]{3,2,1,0:T(8,128)(2,1)}, u32[]{:S(2)}, u32[]{:S(2)}) collective-permute-start(bf16[1,8,160,224]{3,2,1,0:T(8,128)(2,1)} %dynamic-slice_convert_fusion.2), channel_id=1, source_target_pairs={{0,16},{8,24},{16,0},{24,8},{1,17},{9,25},{17,1},{25,9},{2,18},{10... | collective-permute-start | bytes 1720328 | tf_op jit(solution)/shard_map/ppermute | solution.py:36
  (94 other events, 867.7 us)
